TPU v7x, 32 devices: a whole 2x2x4 slice. The times are simulated.
32 devices in a mesh: ctx: 4 (over y, x), exp: 8 (over z, core).
Axes of the slice: x: 2, y: 2, z: 4, core: 2. Of those that a mesh axis runs over, the one named last changes fastest.
Arguments:
- queries: bfloat16 [8, 512, 2048], P('exp', 'ctx')
- key_rows: bfloat16 [8, 512, 2048], P('exp', 'ctx')
- value_rows: bfloat16 [8, 512, 2048], P('exp', 'ctx'), may hold values from -6 to 6
- out_grad: bfloat16 [8, 512, 2048], P('exp', 'ctx'), may hold values from -6 to 6
- moe_input: bfloat16 [8, 512, 2048], P('exp', 'ctx'), may hold values from -6 to 6
- routes: int32 [8, 512, 4], P('exp', 'ctx'), may hold values from 0 to 31, all different within a row; in each aligned block of 128 rows (0 to 127, 128 to 255, ..., all dimensions but the last counted through in order) at most 24 rows name the same one
- route_gates: float32 [8, 512, 4], P('exp', 'ctx'), may hold values from 0.1 to 1
- up_weight: bfloat16 [32, 2048, 768], P('exp'), may hold values from -0.125 to 0.125
- down_weight: bfloat16 [32, 768, 2048], P('exp'), may hold values from -0.21875 to 0.21875
Outputs:
- query_grad: bfloat16 [8, 512, 2048], P('exp', 'ctx')
- key_grad: bfloat16 [8, 512, 2048], P('exp', 'ctx')
- value_grad: bfloat16 [8, 512, 2048], P('exp', 'ctx')
- input_grad: bfloat16 [8, 512, 2048], P('exp', 'ctx')
Inputs may be any that keep to these rules, and one draw needn't show every extreme that they name: In the bins of one device no expert is named by more than 24 routes, a bound that some block reaches; the 4 experts of a bin differ.
All inputs are finite; a program needn't handle non-finite values.
Results may differ from a plain program's by a relative error of at most 0.0064.
Values may be sent and summed in bfloat16 or wider, within the bound.
No kernel may reach another device: no remote copies, remote signals or barrier semaphores. Data moves between devices by JAX's collectives and lax.ppermute only.
A program may use at most 128 MiB of HBM per device.

v0:
```python
import functools

import jax
import jax.numpy as jnp
from jax import lax
from jax.experimental import pallas as pl
from jax.experimental.pallas import tpu as pltpu
from jax.sharding import PartitionSpec as P

HD = 128
CAP = 24
NOTES = 16
PARTS = 4
VMEM_BYTES = 36 * 1024 * 1024
VMEM_EXPERTS = 45 * 1024 * 1024
SMALL = pl.CostEstimate(flops=1, bytes_accessed=1, transcendentals=0)
NT = (((1,), (1,)), ((), ()))
TN = (((0,), (0,)), ((), ()))


def dot_nt(left, right):
    return lax.dot_general(left, right, NT, preferred_element_type=jnp.float32)


def dot_tn(left, right):
    return lax.dot_general(left, right, TN, preferred_element_type=jnp.float32)


def dot_nn(left, right):
    return jnp.dot(left, right, preferred_element_type=jnp.float32)


def silu_slope(preact):
    sigmoid = jax.nn.sigmoid(preact)
    return sigmoid * (1.0 + preact * (1.0 - sigmoid))


def pack_kernel(*refs):
    *members, packed = refs
    groups, _, _, width = packed.shape
    for group in range(groups):
        for row, member in enumerate(members):
            packed[group, row] = member[:, group * width : (group + 1) * width]


def pack_groups(members, groups):
    bins, width = members[0].shape
    return pl.pallas_call(
        pack_kernel,
        out_shape=jax.ShapeDtypeStruct((groups, 4, bins, width // groups), jnp.bfloat16),
        compiler_params=pltpu.CompilerParams(vmem_limit_bytes=VMEM_BYTES),
        cost_estimate=SMALL,
        name="pack_groups",
    )(*members)


def unpack_kernel(packed, *outs):
    groups, _, _, width = packed.shape
    for group in range(groups):
        for row, out in enumerate(outs):
            out[:, group * width : (group + 1) * width] = packed[group, row]


def unpack_groups(packed):
    groups, count, bins, width = packed.shape
    out = jax.ShapeDtypeStruct((bins, width * groups), jnp.bfloat16)
    return pl.pallas_call(
        unpack_kernel,
        out_shape=[out] * count,
        compiler_params=pltpu.CompilerParams(vmem_limit_bytes=VMEM_BYTES),
        cost_estimate=SMALL,
        name="unpack_groups",
    )(packed)


def heads_kernel(packed, out):
    groups, _, bins, _ = packed.shape
    rows = groups * bins
    scale = HD ** (-0.5)
    query, key, value, grad = (packed[:, row].reshape(rows, HD) for row in range(4))
    scores = dot_nt(key, query) * scale
    powers = jnp.exp(scores - jnp.max(scores, axis=0, keepdims=True))
    probs = powers * (1.0 / jnp.sum(powers, axis=0, keepdims=True))
    prob_grad = dot_nt(value, grad)
    row_delta = jnp.sum(probs * prob_grad, axis=0, keepdims=True)
    score_grad = (probs * (prob_grad - row_delta)).astype(jnp.bfloat16)
    results = (
        dot_tn(score_grad, key) * scale,
        dot_nn(score_grad, query) * scale,
        dot_nn(probs.astype(jnp.bfloat16), grad),
    )
    for row, result in enumerate(results):
        out[:, row] = result.astype(jnp.bfloat16).reshape(groups, bins, HD)


def heads_back(packed):
    groups, _, bins, width = packed.shape
    rows = bins * groups
    heads = width // HD
    return pl.pallas_call(
        heads_kernel,
        grid=(heads,),
        out_shape=jax.ShapeDtypeStruct((groups, 3, bins, width), jnp.bfloat16),
        in_specs=[pl.BlockSpec((groups, 4, bins, HD), lambda h: (0, 0, 0, h))],
        out_specs=pl.BlockSpec((groups, 3, bins, HD), lambda h: (0, 0, 0, h)),
        compiler_params=pltpu.CompilerParams(vmem_limit_bytes=VMEM_BYTES),
        cost_estimate=SMALL,
        name="heads_back",
    )(packed)


def exchange(packed):
    return lax.all_to_all(packed, "ctx", split_axis=0, concat_axis=0, tiled=True)


def rows_kernel(tokens_ref, routes_ref, gates_ref, rows_ref):
    bins, width = tokens_ref.shape
    rows_ref[:bins] = tokens_ref[...]
    rest = gates_ref[...]
    pieces = [(routes_ref[...] + 1).astype(jnp.float32)]
    for _ in range(3):
        piece = rest.astype(jnp.bfloat16).astype(jnp.float32)
        rest = rest - piece
        pieces.append(piece)
    rows_ref[bins:, bins:] = jnp.zeros((NOTES, width - bins), jnp.bfloat16)
    rows_ref[bins:, :bins] = jnp.concatenate(pieces, axis=0).astype(jnp.bfloat16)


def add_notes(tokens, routes, gates):
    bins, width = tokens.shape
    return pl.pallas_call(
        rows_kernel,
        out_shape=jax.ShapeDtypeStruct((bins + NOTES, width), jnp.bfloat16),
        compiler_params=pltpu.CompilerParams(vmem_limit_bytes=VMEM_BYTES),
        cost_estimate=SMALL,
        name="add_notes",
    )(tokens, routes.T, gates.T)


def expert_kernel(sources, top, base_ref, *refs):
    token_refs, grad_refs = refs[:sources], refs[sources : 2 * sources]
    up_hbm, down_hbm = refs[2 * sources : 2 * sources + 2]
    keep_refs = refs[2 * sources + 2 : -8]
    give_ref, pick_ref, token_rows, gated_rows, back_rows, up_ref, down_ref, sems = refs[-8:]
    bins = keep_refs[0].shape[0]
    slots = sources * CAP
    experts = pick_ref.shape[0] // slots

    def copies(expert):
        place = expert % 2
        return [
            pltpu.make_async_copy(
                hbm.at[expert, pl.ds(part * (hbm.shape[1] // PARTS), hbm.shape[1] // PARTS)],
                vmem.at[place, pl.ds(part * (hbm.shape[1] // PARTS), hbm.shape[1] // PARTS)],
                sems.at[place, PARTS * which + part],
            )
            for which, (hbm, vmem) in enumerate(((up_hbm, up_ref), (down_hbm, down_ref)))
            for part in range(PARTS)
        ]

    for copy in copies(0):
        copy.start()

    def pick_rows():
        earlier = lax.broadcasted_iota(jnp.int32, (bins, bins), 0)
        later = lax.broadcasted_iota(jnp.int32, (bins, bins), 1)
        before = (earlier < later).astype(jnp.bfloat16)
        slot = lax.broadcasted_iota(jnp.int32, (slots, bins), 0).astype(jnp.float32)
        base = base_ref[0].astype(jnp.float32)
        gates = [jnp.zeros((slots, 1), jnp.float32)] * experts
        for source, token_ref in enumerate(token_refs):
            notes = token_ref[bins:, :bins].astype(jnp.float32)
            named = notes[:top] - base
            weights = notes[top : 2 * top] + notes[2 * top : 3 * top] + notes[3 * top : 4 * top]
            hits = [(named == float(local + 1)).astype(jnp.float32) for local in range(experts)]
            chosen = [jnp.sum(hit, axis=0, keepdims=True) for hit in hits]
            stacked = jnp.concatenate(chosen, axis=0)
            position = dot_nn(stacked.astype(jnp.bfloat16), before)
            for local in range(experts):
                place = jnp.where(
                    chosen[local] > 0.0, position[local : local + 1] + float(source * CAP), -1.0
                )
                pick = (slot == place).astype(jnp.float32)
                gate = jnp.sum(hits[local] * weights, axis=0, keepdims=True)
                gates[local] = gates[local] + jnp.sum(pick * gate, axis=1, keepdims=True)
                pick_ref[
                    local * slots : (local + 1) * slots, source * bins : (source + 1) * bins
                ] = pick.astype(jnp.bfloat16)
        picks = pick_ref[...]
        tokens = jnp.concatenate([ref[:bins] for ref in token_refs], axis=0)
        token_rows[...] = dot_nn(picks, tokens).astype(jnp.bfloat16)
        grads = jnp.concatenate([ref[...] for ref in grad_refs], axis=0)
        gate_column = jnp.concatenate(gates, axis=0)
        gated_rows[...] = (gate_column * dot_nn(picks, grads)).astype(jnp.bfloat16)

    pick_rows()

    @pl.loop(0, experts)
    def _(expert):
        @pl.when(expert + 1 < experts)
        def _():
            for copy in copies(expert + 1):
                copy.start()

        for copy in copies(expert):
            copy.wait()
        place = expert % 2
        rows = pl.ds(pl.multiple_of(expert * slots, 16), slots)
        preact = dot_nn(token_rows[rows, :], up_ref[place])
        back_grad = dot_nt(gated_rows[rows, :], down_ref[place])
        hidden_grad = (back_grad * silu_slope(preact)).astype(jnp.bfloat16)
        back_rows[rows, :] = dot_nt(hidden_grad, up_ref[place]).astype(jnp.bfloat16)

    sums = dot_tn(pick_ref[...], back_rows[...])
    for pair, keep in enumerate(keep_refs):
        mine, other = 2 * pair * bins, (2 * pair + 1) * bins
        keep[...] = sums[mine : mine + bins].astype(jnp.bfloat16)
        give_ref[pair * bins : (pair + 1) * bins] = sums[other : other + bins].astype(jnp.bfloat16)


def expert_back(base, tokens, grads, up_weight, down_weight, top):
    sources = len(tokens)
    bins = grads[0].shape[0]
    experts, width, hidden = up_weight.shape
    slots = sources * CAP
    pairs = sources // 2
    return pl.pallas_call(
        functools.partial(expert_kernel, sources, top),
        out_shape=[jax.ShapeDtypeStruct((bins, width), jnp.bfloat16)] * pairs
        + [jax.ShapeDtypeStruct((pairs * bins, width), jnp.bfloat16)],
        in_specs=[pl.BlockSpec(memory_space=pltpu.SMEM)]
        + [pl.BlockSpec(memory_space=pltpu.VMEM)] * (2 * sources)
        + [pl.BlockSpec(memory_space=pltpu.HBM)] * 2,
        out_specs=[pl.BlockSpec(memory_space=pltpu.VMEM)] * (pairs + 1),
        scratch_shapes=[
            pltpu.VMEM((experts * slots, sources * bins), jnp.bfloat16),
            pltpu.VMEM((experts * slots, width), jnp.bfloat16),
            pltpu.VMEM((experts * slots, width), jnp.bfloat16),
            pltpu.VMEM((experts * slots, width), jnp.bfloat16),
            pltpu.VMEM((2, width, hidden), jnp.bfloat16),
            pltpu.VMEM((2, hidden, width), jnp.bfloat16),
            pltpu.SemaphoreType.DMA((2, 2 * PARTS)),
        ],
        compiler_params=pltpu.CompilerParams(vmem_limit_bytes=VMEM_EXPERTS),
        cost_estimate=SMALL,
        name="expert_back",
    )(base, *tokens, *grads, up_weight, down_weight)


def per_device(
    queries, key_rows, value_rows, out_grad, moe_input, routes, route_gates, up_weight, down_weight
):
    members = lax.axis_size("exp")
    me = lax.axis_index("exp")
    groups = lax.axis_size("ctx")
    chips = members // 2
    half = chips // 2
    _, bins, top = routes.shape
    base = (me * up_weight.shape[0]).astype(jnp.int32).reshape(1)

    def swap(block):
        return lax.ppermute(block, "exp", [(i, i ^ 1) for i in range(members)])

    def hop(block, step):
        return lax.ppermute(
            block, "exp", [(i, (i + 2 * step) % members) for i in range(members)]
        )

    def work(tokens, grads):
        all_tokens, all_grads = [], []
        for token_rows, grad_rows in zip(tokens, grads):
            all_tokens += [token_rows, swap(token_rows)]
            all_grads += [grad_rows, swap(grad_rows)]
        *kept, give = expert_back(base, all_tokens, all_grads, up_weight, down_weight, top)
        return kept, give

    def both_cores(kept, given):
        return [
            (own.astype(jnp.float32) + given[place * bins : (place + 1) * bins]).astype(
                jnp.bfloat16
            )
            for place, own in enumerate(kept)
        ]

    barrier = lax.optimization_barrier
    grads = out_grad[0]
    tokens = add_notes(moe_input[0], routes[0], route_gates[0])
    left_grads, right_grads = hop(grads, -1), hop(grads, 1)
    right_tokens, left_tokens = hop(tokens, 1), hop(tokens, -1)
    packed = pack_groups((queries[0], key_rows[0], value_rows[0], grads), groups)
    heads = exchange(packed)
    kept, give = work([tokens], [grads])
    given = swap(give)
    right_tokens, left_grads, kept, given = barrier((right_tokens, left_grads, kept, given))
    total = kept[0].astype(jnp.float32) + given
    heads, right_tokens, left_grads = barrier((heads, right_tokens, left_grads))
    results = heads_back(heads)
    distances, parts, sums, arrived = [], [], [], []
    for d in range(1, half + 1):
        if d < half:
            near = (right_tokens, left_tokens, right_grads, left_grads)
            steps = [-d, d]
        else:
            near = (right_tokens, left_grads)
            steps = [half]
        if d > 1:
            near, kept, given, results = barrier((near, kept, given, results))
            sums = both_cores(kept, given)
            near, sums = barrier((near, sums))
            arrived = [hop(part, step) for part, step in zip(sums, distances)]
        else:
            near, results = barrier((near, results))
            results = exchange(results)
        if d < half:
            right_tokens, left_tokens, right_grads, left_grads = near
            kept, give = work([right_tokens, left_tokens], [right_grads, left_grads])
            right_tokens = hop(right_tokens, 1)
            left_grads = hop(left_grads, -1)
            if d + 1 < half:
                left_tokens = hop(left_tokens, -1)
                right_grads = hop(right_grads, 1)
        else:
            right_tokens, left_grads = near
            kept, give = work([right_tokens], [left_grads])
        give, arrived = barrier((give, arrived))
        parts += arrived
        given = swap(give)
        distances = steps
    outs = unpack_groups(results)
    for part, step in zip(both_cores(kept, given), distances):
        parts.append(hop(part, step))
    for part in parts:
        total = total + part
    return tuple(out[None] for out in outs) + (total.astype(jnp.bfloat16)[None],)


def solution(mesh):
    rows = P("exp", "ctx", None)
    experts = P("exp", None, None)
    return jax.shard_map(
        per_device,
        mesh=mesh,
        in_specs=(rows,) * 7 + (experts,) * 2,
        out_specs=(rows,) * 4,
        check_vma=False,
    )
```

profile of v0, /device:TPU:0, one launch (start us, length us, event | category | flops | bytes accessed | tf_op | source)
XLA Modules:
  0.0 178.0 jit_solution(2656981290484870227)
XLA Ops:
  0.6 0.0 copy-start.2
  0.6 1.0 copy-done.2
  1.7 1.0 copy-done.9
  2.7 1.0 copy-done.10
  3.8 1.0 copy-done.11
  4.8 0.2 pack_groups.1
  5.0 1.3 copy-done
  6.3 5.3 %all-to-all-start = ((bf16[4,4,128,512]{3,2,1,0:T(8,128)(2,1)}), bf16[4,4,128,512]{3,2,1,0:T(8,128)(2,1)S(1)}, u32[]{:S(2)}, u32[]{:S(2)}) async-start(bf16[4,4,128,512]{3,2,1,0:T(8,128)(2,1)} %copy-done), calls=%async_computation | async-start | bytes 4194304 | tf_op jit(solution)/shard_map/all_to_all | solution.py:113
  11.6 1.0 copy-done.4
  12.7 0.1 collective-permute-start.2
  12.8 0.5 collective-permute-start.3
  13.3 1.6 collective-permute-start
  14.9 2.2 %collective-permute-start.5 = (bf16[144,2048]{1,0:T(8,128)(2,1)S(1)}, bf16[144,2048]{1,0:T(8,128)(2,1)}, u32[]{:S(2)}, u32[]{:S(2)}) collective-permute-start(bf16[144,2048]{1,0:T(8,128)(2,1)S(1)} %add_notes.1.refs_0_), channel_id=1, source_target_pairs={{0,6},{1,7},{2,0},{3,1},{4,2},{5,3},{6,4},{7,5},{8,14},{9,15},{10,... | collective-permute-start | bytes 1769480 | tf_op jit(solution)/shard_map/ppermute | solution.py:265
  17.1 1.8 %collective-permute-start.1 = (bf16[128,2048]{1,0:T(8,128)(2,1)S(1)}, bf16[128,2048]{1,0:T(8,128)(2,1)}, u32[]{:S(2)}, u32[]{:S(2)}) collective-permute-start(bf16[128,2048]{1,0:T(8,128)(2,1)S(1)} %bitcast.19), channel_id=1, source_target_pairs={{0,6},{1,7},{2,0},{3,1},{4,2},{5,3},{6,4},{7,5},{8,14},{9,15},{10,... | collective-permute-start | bytes 1572872 | tf_op jit(solution)/shard_map/ppermute | solution.py:265
  18.9 16.0 %expert_back.3 = (bf16[128,2048]{1,0:T(8,128)(2,1)S(1)}, bf16[128,2048]{1,0:T(8,128)(2,1)S(1)}) custom-call(s32[1]{0:T(128)} %bitcast.9.base_ref, bf16[144,2048]{1,0:T(8,128)(2,1)S(1)} %add_notes.1.refs_0_, bf16[144,2048]{1,0:T(8,128)(2,1)} %collective-permute-done.2.refs_1_, bf16[128,2048]{1,0:T(8,128)(2,1)S(1)} %bitcast.20, ...), custom_call_target="tpu_custom_call" | custom-call | flops 1 | bytes 1 | tf_op jit(solution)/shard_map/expert_back/pallas_call | solution.py:227
  34.9 0.8 copy-done.5
  35.7 0.0 collective-permute-start.4
  35.7 0.2 collective-permute-start.6
  35.9 18.1 %collective-permute-done.1.refs_6_ = bf16[128,2048]{1,0:T(8,128)(2,1)} collective-permute-done((bf16[128,2048]{1,0:T(8,128)(2,1)S(1)}, bf16[128,2048]{1,0:T(8,128)(2,1)}, u32[]{:S(2)}, u32[]{:S(2)}) %collective-permute-start.1) | collective-permute-done | bytes 524320 | tf_op jit(solution)/shard_map/ppermute | solution.py:265
  54.1 0.8 copy-done.14
  54.9 0.0 all-to-all-done.packed
  54.9 6.2 %heads_back.1 = bf16[4,3,128,512]{3,2,1,0:T(8,128)(2,1)S(1)} custom-call(bf16[4,4,128,512]{3,2,1,0:T(8,128)(2,1)S(1)} %all-to-all-done.packed), custom_call_target="tpu_custom_call" | custom-call | flops 1 | bytes 1 | tf_op jit(solution)/shard_map/heads_back/pallas_call | solution.py:100
  61.2 1.2 copy-done.1
  62.3 3.4 %collective-permute-done.6.refs_4_ = bf16[128,2048]{1,0:T(8,128)(2,1)} collective-permute-done((bf16[128,2048]{1,0:T(8,128)(2,1)S(1)}, bf16[128,2048]{1,0:T(8,128)(2,1)}, u32[]{:S(2)}, u32[]{:S(2)}) %collective-permute-start.6) | collective-permute-done | bytes 524320 | tf_op jit(solution)/shard_map/ppermute | solution.py:265
  65.7 0.5 collective-permute-start.9
  66.2 0.0 collective-permute-start.11
  66.2 0.5 collective-permute-start.12
  66.7 4.2 %all-to-all-start.1 = ((bf16[4,3,128,512]{3,2,1,0:T(8,128)(2,1)}), bf16[4,3,128,512]{3,2,1,0:T(8,128)(2,1)S(1)}, u32[]{:S(2)}, u32[]{:S(2)}) async-start(bf16[4,3,128,512]{3,2,1,0:T(8,128)(2,1)} %copy-done.1), calls=%async_computation.1 | async-start | bytes 3145728 | tf_op jit(solution)/shard_map/all_to_all | solution.py:113
  71.0 19.6 %expert_back.4 = (bf16[128,2048]{1,0:T(8,128)(2,1)S(1)}, bf16[128,2048]{1,0:T(8,128)(2,1)S(1)}, bf16[256,2048]{1,0:T(8,128)(2,1)}) custom-call(s32[1]{0:T(128)} %bitcast.9.base_ref, bf16[144,2048]{1,0:T(8,128)(2,1)} %collective-permute-done.refs_0_, bf16[144,2048]{1,0:T(8,128)(2,1)S(1)} %collective-permute-done.9.refs_1_, ...), custom_call_target="tpu_custom_call" | custom-call | flops 1 | bytes 1 | tf_op jit(solution)/shard_map/expert_back/pallas_call | solution.py:227
  90.5 0.0 copy-start.7
  90.5 0.8 copy-done.7
  91.3 0.8 copy-done.8
  92.1 3.8 %collective-permute-start.8 = (bf16[128,2048]{1,0:T(8,128)(2,1)}, bf16[128,2048]{1,0:T(8,128)(2,1)S(1)}, u32[]{:S(2)}, u32[]{:S(2)}) collective-permute-start(bf16[128,2048]{1,0:T(8,128)(2,1)} %collective-permute-done.1.refs_6_), channel_id=1, source_target_pairs={{0,6},{1,7},{2,0},{3,1},{4,2},{5,3},{6,4},{7,5},{8,14},{9,15},{10,... | collective-permute-start | bytes 1572872 | tf_op jit(solution)/shard_map/ppermute | solution.py:265
  95.9 23.4 %collective-permute-done.8.refs_2_ = bf16[128,2048]{1,0:T(8,128)(2,1)S(1)} collective-permute-done((bf16[128,2048]{1,0:T(8,128)(2,1)}, bf16[128,2048]{1,0:T(8,128)(2,1)S(1)}, u32[]{:S(2)}, u32[]{:S(2)}) %collective-permute-start.8) | collective-permute-done | bytes 524320 | tf_op jit(solution)/shard_map/ppermute | solution.py:265
  119.3 2.0 %add_convert_fusion.2 = (bf16[128,2048]{1,0:T(8,128)(2,1)S(1)}, bf16[128,2048]{1,0:T(8,128)(2,1)S(1)}) fusion(bf16[128,2048]{1,0:T(8,128)(2,1)} %copy-done.8, bf16[256,2048]{1,0:T(8,128)(2,1)} %collective-permute-done.13, bf16[128,2048]{1,0:T(8,128)(2,1)} %copy-done.7), kind=kLoop, calls=%fused_computation.2 | loop fusion | flops 2097152 | bytes 3145728 | tf_op jit(solution)/shard_map/convert_element_type | solution.py:279
  121.3 0.1 collective-permute-start.14
  121.4 0.5 collective-permute-start.15
  121.9 2.1 %collective-permute-start.16 = (bf16[128,2048]{1,0:T(8,128)(2,1)S(1)}, bf16[128,2048]{1,0:T(8,128)(2,1)S(1)}, u32[]{:S(2)}, u32[]{:S(2)}) collective-permute-start(bf16[128,2048]{1,0:T(8,128)(2,1)S(1)} %get-tuple-element.68), channel_id=1, source_target_pairs={{0,6},{1,7},{2,0},{3,1},{4,2},{5,3},{6,4},{7,5},{8,14},{9,15},{10,... | collective-permute-start | bytes 1572872 | tf_op jit(solution)/shard_map/ppermute | solution.py:265
  124.0 0.0 collective-permute-start.17
  124.0 0.2 collective-permute-done.15.refs_3_
  124.1 14.8 %expert_back.5 = (bf16[128,2048]{1,0:T(8,128)(2,1)S(1)}, bf16[128,2048]{1,0:T(8,128)(2,1)S(1)}) custom-call(s32[1]{0:T(128)} %bitcast.9.base_ref, bf16[144,2048]{1,0:T(8,128)(2,1)S(1)} %collective-permute-done.7.refs_0_, bf16[144,2048]{1,0:T(8,128)(2,1)S(1)} %collective-permute-done.14.refs_1_, bf16[128,2048]{1,0:T(8,128)(2,1)S(1)} %collective-permute-done.8.refs_2_, ...), custom_call_target="tpu_custom_call" | custom-call | flops 1 | bytes 1 | tf_op jit(solution)/shard_map/expert_back/pallas_call | solution.py:227
  139.0 9.9 %collective-permute-done.17 = bf16[128,2048]{1,0:T(8,128)(2,1)S(1)} collective-permute-done((bf16[128,2048]{1,0:T(8,128)(2,1)S(1)}, bf16[128,2048]{1,0:T(8,128)(2,1)S(1)}, u32[]{:S(2)}, u32[]{:S(2)}) %collective-permute-start.17) | collective-permute-done | bytes 524320 | tf_op jit(solution)/shard_map/ppermute | solution.py:265
  148.9 1.9 %collective-permute-done.18 = bf16[128,2048]{1,0:T(8,128)(2,1)S(1)} collective-permute-done((bf16[128,2048]{1,0:T(8,128)(2,1)S(1)}, bf16[128,2048]{1,0:T(8,128)(2,1)S(1)}, u32[]{:S(2)}, u32[]{:S(2)}) %collective-permute-start.18) | collective-permute-done | bytes 524320 | tf_op jit(solution)/shard_map/ppermute | solution.py:262
  150.8 0.1 add_convert_fusion.1
  150.9 0.6 collective-permute-start.19
  151.6 1.2 unpack_groups.1
  152.8 24.0 %collective-permute-done.19 = bf16[128,2048]{1,0:T(8,128)(2,1)S(1)} collective-permute-done((bf16[128,2048]{1,0:T(8,128)(2,1)S(1)}, bf16[128,2048]{1,0:T(8,128)(2,1)S(1)}, u32[]{:S(2)}, u32[]{:S(2)}) %collective-permute-start.19) | collective-permute-done | bytes 524320 | tf_op jit(solution)/shard_map/ppermute | solution.py:265
  176.8 1.2 fusion
  (38 shorter events, 0.1 us)
Async XLA Ops:
  0.6 1.0 copy-start.2
  1.7 1.0 copy-start.9
  2.7 1.0 copy-start.10
  3.8 1.0 copy-start.11
  5.0 1.3 copy-start
  6.3 5.3 %copy-start.12 = (s32[1,128,4]{1,2,0:T(4,128)S(1)}, s32[1,128,4]{1,2,0:T(4,128)}, u32[]{:S(2)}) copy-start(s32[1,128,4]{1,2,0:T(4,128)} %param.14) | copy-start | bytes 6148
  6.3 5.3 %copy-start.13 = (f32[1,128,4]{1,2,0:T(4,128)S(1)}, f32[1,128,4]{1,2,0:T(4,128)}, u32[]{:S(2)}) copy-start(f32[1,128,4]{1,2,0:T(4,128)} %param.15) | copy-start | bytes 6148
  6.3 6.5 %copy-start.3 = (bf16[1,128,2048]{2,1,0:T(8,128)(2,1)S(1)}, bf16[1,128,2048]{2,1,0:T(8,128)(2,1)}, u32[]{:S(2)}) copy-start(bf16[1,128,2048]{2,1,0:T(8,128)(2,1)} %param.12) | copy-start | bytes 1572868
  6.3 48.6 %all-to-all-start = ((bf16[4,4,128,512]{3,2,1,0:T(8,128)(2,1)}), bf16[4,4,128,512]{3,2,1,0:T(8,128)(2,1)S(1)}, u32[]{:S(2)}, u32[]{:S(2)}) async-start(bf16[4,4,128,512]{3,2,1,0:T(8,128)(2,1)} %copy-done), calls=%async_computation | async-start | bytes 4194304 | tf_op jit(solution)/shard_map/all_to_all | solution.py:113
  11.6 1.0 copy-start.4
  12.7 6.2 %collective-permute-start.2 = (bf16[144,2048]{1,0:T(8,128)(2,1)S(1)}, bf16[144,2048]{1,0:T(8,128)(2,1)}, u32[]{:S(2)}, u32[]{:S(2)}) collective-permute-start(bf16[144,2048]{1,0:T(8,128)(2,1)S(1)} %add_notes.1.refs_0_), channel_id=1, source_target_pairs={{0,1},{1,0},{2,3},{3,2},{4,5},{5,4},{6,7},{7,6},{8,9},{9,8},{10,11... | collective-permute-start | bytes 1769480 | tf_op jit(solution)/shard_map/ppermute | solution.py:262
  12.8 6.1 %collective-permute-start.3 = (bf16[128,2048]{1,0:T(8,128)(2,1)S(1)}, bf16[128,2048]{1,0:T(8,128)(2,1)}, u32[]{:S(2)}, u32[]{:S(2)}) collective-permute-start(bf16[128,2048]{1,0:T(8,128)(2,1)S(1)} %bitcast.18), channel_id=1, source_target_pairs={{0,1},{1,0},{2,3},{3,2},{4,5},{5,4},{6,7},{7,6},{8,9},{9,8},{10,11... | collective-permute-start | bytes 1572872 | tf_op jit(solution)/shard_map/ppermute | solution.py:262
  13.3 40.8 %collective-permute-start = (bf16[144,2048]{1,0:T(8,128)(2,1)S(1)}, bf16[144,2048]{1,0:T(8,128)(2,1)}, u32[]{:S(2)}, u32[]{:S(2)}) collective-permute-start(bf16[144,2048]{1,0:T(8,128)(2,1)S(1)} %add_notes.1.refs_0_), channel_id=1, source_target_pairs={{0,2},{1,3},{2,4},{3,5},{4,6},{5,7},{6,0},{7,1},{8,10},{9,11},{10,... | collective-permute-start | bytes 1769480 | tf_op jit(solution)/shard_map/ppermute | solution.py:265
  14.9 50.9 %collective-permute-start.5 = (bf16[144,2048]{1,0:T(8,128)(2,1)S(1)}, bf16[144,2048]{1,0:T(8,128)(2,1)}, u32[]{:S(2)}, u32[]{:S(2)}) collective-permute-start(bf16[144,2048]{1,0:T(8,128)(2,1)S(1)} %add_notes.1.refs_0_), channel_id=1, source_target_pairs={{0,6},{1,7},{2,0},{3,1},{4,2},{5,3},{6,4},{7,5},{8,14},{9,15},{10,... | collective-permute-start | bytes 1769480 | tf_op jit(solution)/shard_map/ppermute | solution.py:265
  17.1 37.0 %collective-permute-start.1 = (bf16[128,2048]{1,0:T(8,128)(2,1)S(1)}, bf16[128,2048]{1,0:T(8,128)(2,1)}, u32[]{:S(2)}, u32[]{:S(2)}) collective-permute-start(bf16[128,2048]{1,0:T(8,128)(2,1)S(1)} %bitcast.19), channel_id=1, source_target_pairs={{0,6},{1,7},{2,0},{3,1},{4,2},{5,3},{6,4},{7,5},{8,14},{9,15},{10,... | collective-permute-start | bytes 1572872 | tf_op jit(solution)/shard_map/ppermute | solution.py:265
  34.9 0.8 copy-start.5
  35.7 18.3 %collective-permute-start.4 = (bf16[128,2048]{1,0:T(8,128)(2,1)S(1)}, bf16[128,2048]{1,0:T(8,128)(2,1)S(1)}, u32[]{:S(2)}, u32[]{:S(2)}) collective-permute-start(bf16[128,2048]{1,0:T(8,128)(2,1)S(1)} %get-tuple-element.40), channel_id=1, source_target_pairs={{0,1},{1,0},{2,3},{3,2},{4,5},{5,4},{6,7},{7,6},{8,9},{9,8},{10,11... | collective-permute-start | bytes 1572872 | tf_op jit(solution)/shard_map/ppermute | solution.py:262
  35.7 30.0 %collective-permute-start.6 = (bf16[128,2048]{1,0:T(8,128)(2,1)S(1)}, bf16[128,2048]{1,0:T(8,128)(2,1)}, u32[]{:S(2)}, u32[]{:S(2)}) collective-permute-start(bf16[128,2048]{1,0:T(8,128)(2,1)S(1)} %bitcast.21), channel_id=1, source_target_pairs={{0,2},{1,3},{2,4},{3,5},{4,6},{5,7},{6,0},{7,1},{8,10},{9,11},{10,... | collective-permute-start | bytes 1572872 | tf_op jit(solution)/shard_map/ppermute | solution.py:265
  54.1 0.8 copy-start.14
  61.1 1.2 copy-start.1
  65.7 5.2 %collective-permute-start.10 = (bf16[144,2048]{1,0:T(8,128)(2,1)}, bf16[144,2048]{1,0:T(8,128)(2,1)S(1)}, u32[]{:S(2)}, u32[]{:S(2)}) collective-permute-start(bf16[144,2048]{1,0:T(8,128)(2,1)} %collective-permute-done.5.refs_2_), channel_id=1, source_target_pairs={{0,1},{1,0},{2,3},{3,2},{4,5},{5,4},{6,7},{7,6},{8,9},{9,8},{10,11... | collective-permute-start | bytes 1769480 | tf_op jit(solution)/shard_map/ppermute | solution.py:262
  65.7 5.2 %collective-permute-start.9 = (bf16[144,2048]{1,0:T(8,128)(2,1)}, bf16[144,2048]{1,0:T(8,128)(2,1)S(1)}, u32[]{:S(2)}, u32[]{:S(2)}) collective-permute-start(bf16[144,2048]{1,0:T(8,128)(2,1)} %collective-permute-done.refs_0_), channel_id=1, source_target_pairs={{0,1},{1,0},{2,3},{3,2},{4,5},{5,4},{6,7},{7,6},{8,9},{9,8},{10,11... | collective-permute-start | bytes 1769480 | tf_op jit(solution)/shard_map/ppermute | solution.py:262
  66.2 4.7 %collective-permute-start.11 = (bf16[128,2048]{1,0:T(8,128)(2,1)}, bf16[128,2048]{1,0:T(8,128)(2,1)S(1)}, u32[]{:S(2)}, u32[]{:S(2)}) collective-permute-start(bf16[128,2048]{1,0:T(8,128)(2,1)} %collective-permute-done.6.refs_4_), channel_id=1, source_target_pairs={{0,1},{1,0},{2,3},{3,2},{4,5},{5,4},{6,7},{7,6},{8,9},{9,8},{10,11... | collective-permute-start | bytes 1572872 | tf_op jit(solution)/shard_map/ppermute | solution.py:262
  66.2 4.7 %collective-permute-start.12 = (bf16[128,2048]{1,0:T(8,128)(2,1)}, bf16[128,2048]{1,0:T(8,128)(2,1)}, u32[]{:S(2)}, u32[]{:S(2)}) collective-permute-start(bf16[128,2048]{1,0:T(8,128)(2,1)} %collective-permute-done.1.refs_6_), channel_id=1, source_target_pairs={{0,1},{1,0},{2,3},{3,2},{4,5},{5,4},{6,7},{7,6},{8,9},{9,8},{10,11... | collective-permute-start | bytes 1572872 | tf_op jit(solution)/shard_map/ppermute | solution.py:262
  66.7 52.6 %all-to-all-start.1 = ((bf16[4,3,128,512]{3,2,1,0:T(8,128)(2,1)}), bf16[4,3,128,512]{3,2,1,0:T(8,128)(2,1)S(1)}, u32[]{:S(2)}, u32[]{:S(2)}) async-start(bf16[4,3,128,512]{3,2,1,0:T(8,128)(2,1)} %copy-done.1), calls=%async_computation.1 | async-start | bytes 3145728 | tf_op jit(solution)/shard_map/all_to_all | solution.py:113
  90.5 0.8 copy-start.7
  91.3 0.8 copy-start.8
  92.1 27.2 %collective-permute-start.13 = (bf16[256,2048]{1,0:T(8,128)(2,1)}, bf16[256,2048]{1,0:T(8,128)(2,1)}, u32[]{:S(2)}, u32[]{:S(2)}) collective-permute-start(bf16[256,2048]{1,0:T(8,128)(2,1)} %get-tuple-element.52), channel_id=1, source_target_pairs={{0,1},{1,0},{2,3},{3,2},{4,5},{5,4},{6,7},{7,6},{8,9},{9,8},{10,11... | collective-permute-start | bytes 3145736 | tf_op jit(solution)/shard_map/ppermute | solution.py:262
  92.1 27.2 %collective-permute-start.7 = (bf16[144,2048]{1,0:T(8,128)(2,1)}, bf16[144,2048]{1,0:T(8,128)(2,1)S(1)}, u32[]{:S(2)}, u32[]{:S(2)}) collective-permute-start(bf16[144,2048]{1,0:T(8,128)(2,1)} %collective-permute-done.refs_0_), channel_id=1, source_target_pairs={{0,2},{1,3},{2,4},{3,5},{4,6},{5,7},{6,0},{7,1},{8,10},{9,11},{10,... | collective-permute-start | bytes 1769480 | tf_op jit(solution)/shard_map/ppermute | solution.py:265
  92.1 27.2 %collective-permute-start.8 = (bf16[128,2048]{1,0:T(8,128)(2,1)}, bf16[128,2048]{1,0:T(8,128)(2,1)S(1)}, u32[]{:S(2)}, u32[]{:S(2)}) collective-permute-start(bf16[128,2048]{1,0:T(8,128)(2,1)} %collective-permute-done.1.refs_6_), channel_id=1, source_target_pairs={{0,6},{1,7},{2,0},{3,1},{4,2},{5,3},{6,4},{7,5},{8,14},{9,15},{10,... | collective-permute-start | bytes 1572872 | tf_op jit(solution)/shard_map/ppermute | solution.py:265
  121.3 2.8 %collective-permute-start.14 = (bf16[144,2048]{1,0:T(8,128)(2,1)S(1)}, bf16[144,2048]{1,0:T(8,128)(2,1)S(1)}, u32[]{:S(2)}, u32[]{:S(2)}) collective-permute-start(bf16[144,2048]{1,0:T(8,128)(2,1)S(1)} %collective-permute-done.7.refs_0_), channel_id=1, source_target_pairs={{0,1},{1,0},{2,3},{3,2},{4,5},{5,4},{6,7},{7,6},{8,9},{9,8},{10,11... | collective-permute-start | bytes 1769480 | tf_op jit(solution)/shard_map/ppermute | solution.py:262
  121.4 2.7 %collective-permute-start.15 = (bf16[128,2048]{1,0:T(8,128)(2,1)S(1)}, bf16[128,2048]{1,0:T(8,128)(2,1)S(1)}, u32[]{:S(2)}, u32[]{:S(2)}) collective-permute-start(bf16[128,2048]{1,0:T(8,128)(2,1)S(1)} %collective-permute-done.8.refs_2_), channel_id=1, source_target_pairs={{0,1},{1,0},{2,3},{3,2},{4,5},{5,4},{6,7},{7,6},{8,9},{9,8},{10,11... | collective-permute-start | bytes 1572872 | tf_op jit(solution)/shard_map/ppermute | solution.py:262
  121.9 17.1 %collective-permute-start.16 = (bf16[128,2048]{1,0:T(8,128)(2,1)S(1)}, bf16[128,2048]{1,0:T(8,128)(2,1)S(1)}, u32[]{:S(2)}, u32[]{:S(2)}) collective-permute-start(bf16[128,2048]{1,0:T(8,128)(2,1)S(1)} %get-tuple-element.68), channel_id=1, source_target_pairs={{0,6},{1,7},{2,0},{3,1},{4,2},{5,3},{6,4},{7,5},{8,14},{9,15},{10,... | collective-permute-start | bytes 1572872 | tf_op jit(solution)/shard_map/ppermute | solution.py:265
  124.0 24.9 %collective-permute-start.17 = (bf16[128,2048]{1,0:T(8,128)(2,1)S(1)}, bf16[128,2048]{1,0:T(8,128)(2,1)S(1)}, u32[]{:S(2)}, u32[]{:S(2)}) collective-permute-start(bf16[128,2048]{1,0:T(8,128)(2,1)S(1)} %get-tuple-element.69), channel_id=1, source_target_pairs={{0,2},{1,3},{2,4},{3,5},{4,6},{5,7},{6,0},{7,1},{8,10},{9,11},{10,... | collective-permute-start | bytes 1572872 | tf_op jit(solution)/shard_map/ppermute | solution.py:265
  138.9 37.9 %copy-start.6 = (bf16[128,2048]{1,0:T(8,128)(2,1)S(1)}, bf16[128,2048]{1,0:T(8,128)(2,1)}, u32[]{:S(2)}) copy-start(bf16[128,2048]{1,0:T(8,128)(2,1)} %copy-done.5) | copy-start | bytes 1572868
  138.9 37.9 %copy-start.15 = (bf16[128,2048]{1,0:T(8,128)(2,1)S(1)}, bf16[128,2048]{1,0:T(8,128)(2,1)}, u32[]{:S(2)}) copy-start(bf16[128,2048]{1,0:T(8,128)(2,1)} %copy-done.14) | copy-start | bytes 1572868
  148.9 1.9 %collective-permute-start.18 = (bf16[128,2048]{1,0:T(8,128)(2,1)S(1)}, bf16[128,2048]{1,0:T(8,128)(2,1)S(1)}, u32[]{:S(2)}, u32[]{:S(2)}) collective-permute-start(bf16[128,2048]{1,0:T(8,128)(2,1)S(1)} %get-tuple-element.73), channel_id=1, source_target_pairs={{0,1},{1,0},{2,3},{3,2},{4,5},{5,4},{6,7},{7,6},{8,9},{9,8},{10,11... | collective-permute-start | bytes 1572872 | tf_op jit(solution)/shard_map/ppermute | solution.py:262
  150.9 25.9 %collective-permute-start.19 = (bf16[128,2048]{1,0:T(8,128)(2,1)S(1)}, bf16[128,2048]{1,0:T(8,128)(2,1)S(1)}, u32[]{:S(2)}, u32[]{:S(2)}) collective-permute-start(bf16[128,2048]{1,0:T(8,128)(2,1)S(1)} %add_convert_fusion.1), channel_id=1, source_target_pairs={{0,4},{1,5},{2,6},{3,7},{4,0},{5,1},{6,2},{7,3},{8,12},{9,13},{10,... | collective-permute-start | bytes 1572872 | tf_op jit(solution)/shard_map/ppermute | solution.py:265
where the time goes:
time: 179 us; the launch traced here: 178 us
  waiting for transfers between devices  80.9 us (45%)
  Pallas kernels  58 us (32%)
  starting transfers between devices  24 us (13%)
  local copies, waits for them, and re-layouts  10.9 us (6%)
  other arithmetic  3.33 us (2%)
    ppermute x9, waiting for transfers between devices, hop(): lax.ppermute(block, 'exp', [(i, (i + 2 * step) % members) for i in range(...  78.8 us
    pallas_call x3, Pallas kernels, expert_back(): pl.pallas_call(functools.partial(expert_kernel, sources, top), out_shape=...  50.3 us
    ppermute x9, starting transfers between devices, hop(): lax.ppermute(block, 'exp', [(i, (i + 2 * step) % members) for i in range(...  12.4 us
    unnamed x32, local copies, waits for them, and re-layouts  10.9 us
    all_to_all x2, starting transfers between devices, exchange(): lax.all_to_all(packed, 'ctx', split_axis=0, concat_axis=0, tiled=True)  9.49 us
    pallas_call x1, Pallas kernels, heads_back(): pl.pallas_call(heads_kernel, grid=(heads,), out_shape=jax.ShapeDtypeStruc...  6.24 us
  transfers between devices with their start and end apart: 22, of which 7 were waited for; matrix products, arithmetic and copies ran while one was open for 0% of the time, Pallas kernels for 33%

commit v1 on v0

v1 whole, which is shorter than its diff:
```python
import functools

import jax
import jax.numpy as jnp
from jax import lax
from jax.experimental import pallas as pl
from jax.experimental.pallas import tpu as pltpu
from jax.sharding import PartitionSpec as P

HD = 128
CAP = 24
NOTES = 16
PARTS = 4
VMEM_BYTES = 36 * 1024 * 1024
VMEM_EXPERTS = 45 * 1024 * 1024
SMALL = pl.CostEstimate(flops=1, bytes_accessed=1, transcendentals=0)
LARGE = pl.CostEstimate(flops=30 * 10**9, bytes_accessed=50 * 10**6, transcendentals=0)
NT = (((1,), (1,)), ((), ()))
TN = (((0,), (0,)), ((), ()))


def dot_nt(left, right):
    return lax.dot_general(left, right, NT, preferred_element_type=jnp.float32)


def dot_tn(left, right):
    return lax.dot_general(left, right, TN, preferred_element_type=jnp.float32)


def dot_nn(left, right):
    return jnp.dot(left, right, preferred_element_type=jnp.float32)


def silu_slope(preact):
    sigmoid = jax.nn.sigmoid(preact)
    return sigmoid * (1.0 + preact * (1.0 - sigmoid))


def pack_kernel(group_ref, *refs):
    members, blocks = refs[:4], refs[4:]
    width = blocks[0].shape[2]
    for place, block in enumerate(blocks):
        first = pl.multiple_of(group_ref[place] * width, 128)
        for row, member in enumerate(members):
            block[row] = member[:, pl.ds(first, width)]


def pack_groups(group_ids, members, groups):
    bins, width = members[0].shape
    block = jax.ShapeDtypeStruct((4, bins, width // groups), jnp.bfloat16)
    return pl.pallas_call(
        pack_kernel,
        out_shape=[block] * groups,
        in_specs=[pl.BlockSpec(memory_space=pltpu.SMEM)]
        + [pl.BlockSpec(memory_space=pltpu.VMEM)] * 4,
        out_specs=[pl.BlockSpec(memory_space=pltpu.VMEM)] * groups,
        compiler_params=pltpu.CompilerParams(vmem_limit_bytes=VMEM_BYTES),
        cost_estimate=SMALL,
        name="pack_groups",
    )(group_ids, *members)


def unpack_kernel(group_ref, *refs):
    blocks, outs = refs[:-3], refs[-3:]
    width = blocks[0].shape[2]
    for place, block in enumerate(blocks):
        first = pl.multiple_of(group_ref[place] * width, 128)
        for row, out in enumerate(outs):
            out[:, pl.ds(first, width)] = block[row]


def unpack_groups(group_ids, blocks):
    groups = len(blocks)
    bins, width = blocks[0].shape[1], blocks[0].shape[2] * groups
    out = jax.ShapeDtypeStruct((bins, width), jnp.bfloat16)
    return pl.pallas_call(
        unpack_kernel,
        out_shape=[out] * 3,
        in_specs=[pl.BlockSpec(memory_space=pltpu.SMEM)]
        + [pl.BlockSpec(memory_space=pltpu.VMEM)] * groups,
        out_specs=[pl.BlockSpec(memory_space=pltpu.VMEM)] * 3,
        compiler_params=pltpu.CompilerParams(vmem_limit_bytes=VMEM_BYTES),
        cost_estimate=SMALL,
        name="unpack_groups",
    )(group_ids, *blocks)


def heads_kernel(*refs):
    count = len(refs) // 2
    blocks, outs = refs[:count], refs[count:]
    bins = blocks[0].shape[1]
    scale = HD ** (-0.5)
    query, key, value, grad = (
        jnp.concatenate([block[row] for block in blocks], axis=0) for row in range(4)
    )
    scores = dot_nt(key, query) * scale
    powers = jnp.exp(scores - jnp.max(scores, axis=0, keepdims=True))
    probs = powers * (1.0 / jnp.sum(powers, axis=0, keepdims=True))
    prob_grad = dot_nt(value, grad)
    row_delta = jnp.sum(probs * prob_grad, axis=0, keepdims=True)
    score_grad = (probs * (prob_grad - row_delta)).astype(jnp.bfloat16)
    results = (
        dot_tn(score_grad, key) * scale,
        dot_nn(score_grad, query) * scale,
        dot_nn(probs.astype(jnp.bfloat16), grad),
    )
    for row, result in enumerate(results):
        result = result.astype(jnp.bfloat16)
        for place, out in enumerate(outs):
            out[row] = result[place * bins : (place + 1) * bins]


def heads_back(blocks):
    groups = len(blocks)
    bins, width = blocks[0].shape[1:]
    rows = bins * groups
    heads = width // HD
    return pl.pallas_call(
        heads_kernel,
        grid=(heads,),
        out_shape=[jax.ShapeDtypeStruct((3, bins, width), jnp.bfloat16)] * groups,
        in_specs=[pl.BlockSpec((4, bins, HD), lambda h: (0, 0, h))] * groups,
        out_specs=[pl.BlockSpec((3, bins, HD), lambda h: (0, 0, h))] * groups,
        compiler_params=pltpu.CompilerParams(vmem_limit_bytes=VMEM_BYTES),
        cost_estimate=SMALL,
        name="heads_back",
    )(*blocks)


def exchange(blocks):
    groups = len(blocks)
    return [blocks[0]] + [
        lax.ppermute(blocks[place], "ctx", [(i, i ^ place) for i in range(groups)])
        for place in range(1, groups)
    ]


def block_kernel(tokens_ref, grads_ref, routes_ref, gates_ref, block_ref):
    bins, width = tokens_ref.shape
    block_ref[:bins] = tokens_ref[...]
    block_ref[bins : 2 * bins] = grads_ref[...]
    rest = gates_ref[...]
    pieces = [(routes_ref[...] + 1).astype(jnp.float32)]
    for _ in range(3):
        piece = rest.astype(jnp.bfloat16).astype(jnp.float32)
        rest = rest - piece
        pieces.append(piece)
    block_ref[2 * bins :, bins:] = jnp.zeros((NOTES, width - bins), jnp.bfloat16)
    block_ref[2 * bins :, :bins] = jnp.concatenate(pieces, axis=0).astype(jnp.bfloat16)


def make_block(tokens, grads, routes, gates):
    bins, width = tokens.shape
    return pl.pallas_call(
        block_kernel,
        out_shape=jax.ShapeDtypeStruct((2 * bins + NOTES, width), jnp.bfloat16),
        compiler_params=pltpu.CompilerParams(vmem_limit_bytes=VMEM_BYTES),
        cost_estimate=SMALL,
        name="make_block",
    )(tokens, grads, routes.T, gates.T)


def expert_kernel(sources, top, base_ref, *refs):
    block_refs = refs[:sources]
    up_hbm, down_hbm = refs[sources : sources + 2]
    keep_refs = refs[sources + 2 : -8]
    give_ref, pick_ref, token_rows, gated_rows, back_rows, up_ref, down_ref, sems = refs[-8:]
    bins = keep_refs[0].shape[0]
    slots = sources * CAP
    experts = pick_ref.shape[0] // slots

    def copies(expert):
        place = expert % 2
        return [
            pltpu.make_async_copy(
                hbm.at[expert, pl.ds(part * (hbm.shape[1] // PARTS), hbm.shape[1] // PARTS)],
                vmem.at[place, pl.ds(part * (hbm.shape[1] // PARTS), hbm.shape[1] // PARTS)],
                sems.at[place, PARTS * which + part],
            )
            for which, (hbm, vmem) in enumerate(((up_hbm, up_ref), (down_hbm, down_ref)))
            for part in range(PARTS)
        ]

    for copy in copies(0):
        copy.start()

    def pick_rows():
        earlier = lax.broadcasted_iota(jnp.int32, (bins, bins), 0)
        later = lax.broadcasted_iota(jnp.int32, (bins, bins), 1)
        before = (earlier < later).astype(jnp.bfloat16)
        slot = lax.broadcasted_iota(jnp.int32, (slots, bins), 0).astype(jnp.float32)
        base = base_ref[0].astype(jnp.float32)
        gates = [jnp.zeros((slots, 1), jnp.float32)] * experts
        for source, block in enumerate(block_refs):
            notes = block[2 * bins :, :bins].astype(jnp.float32)
            named = notes[:top] - base
            weights = notes[top : 2 * top] + notes[2 * top : 3 * top] + notes[3 * top : 4 * top]
            hits = [(named == float(local + 1)).astype(jnp.float32) for local in range(experts)]
            chosen = [jnp.sum(hit, axis=0, keepdims=True) for hit in hits]
            stacked = jnp.concatenate(chosen, axis=0)
            position = dot_nn(stacked.astype(jnp.bfloat16), before)
            for local in range(experts):
                place = jnp.where(
                    chosen[local] > 0.0, position[local : local + 1] + float(source * CAP), -1.0
                )
                pick = (slot == place).astype(jnp.float32)
                gate = jnp.sum(hits[local] * weights, axis=0, keepdims=True)
                gates[local] = gates[local] + jnp.sum(pick * gate, axis=1, keepdims=True)
                pick_ref[
                    local * slots : (local + 1) * slots, source * bins : (source + 1) * bins
                ] = pick.astype(jnp.bfloat16)
        picks = pick_ref[...]
        tokens = jnp.concatenate([block[:bins] for block in block_refs], axis=0)
        token_rows[...] = dot_nn(picks, tokens).astype(jnp.bfloat16)
        grads = jnp.concatenate([block[bins : 2 * bins] for block in block_refs], axis=0)
        gate_column = jnp.concatenate(gates, axis=0)
        gated_rows[...] = (gate_column * dot_nn(picks, grads)).astype(jnp.bfloat16)

    pick_rows()

    @pl.loop(0, experts)
    def _(expert):
        @pl.when(expert + 1 < experts)
        def _():
            for copy in copies(expert + 1):
                copy.start()

        for copy in copies(expert):
            copy.wait()
        place = expert % 2
        rows = pl.ds(pl.multiple_of(expert * slots, 16), slots)
        preact = dot_nn(token_rows[rows, :], up_ref[place])
        back_grad = dot_nt(gated_rows[rows, :], down_ref[place])
        hidden_grad = (back_grad * silu_slope(preact)).astype(jnp.bfloat16)
        back_rows[rows, :] = dot_nt(hidden_grad, up_ref[place]).astype(jnp.bfloat16)

    sums = dot_tn(pick_ref[...], back_rows[...])
    for pair, keep in enumerate(keep_refs):
        mine, other = 2 * pair * bins, (2 * pair + 1) * bins
        keep[...] = sums[mine : mine + bins].astype(jnp.bfloat16)
        give_ref[pair * bins : (pair + 1) * bins] = sums[other : other + bins].astype(jnp.bfloat16)


def expert_back(base, blocks, up_weight, down_weight, bins, top):
    sources = len(blocks)
    experts, width, hidden = up_weight.shape
    slots = sources * CAP
    pairs = sources // 2
    return pl.pallas_call(
        functools.partial(expert_kernel, sources, top),
        out_shape=[jax.ShapeDtypeStruct((bins, width), jnp.bfloat16)] * pairs
        + [jax.ShapeDtypeStruct((pairs * bins, width), jnp.bfloat16)],
        in_specs=[pl.BlockSpec(memory_space=pltpu.SMEM)]
        + [pl.BlockSpec(memory_space=pltpu.VMEM)] * sources
        + [pl.BlockSpec(memory_space=pltpu.HBM)] * 2,
        out_specs=[pl.BlockSpec(memory_space=pltpu.VMEM)] * (pairs + 1),
        scratch_shapes=[
            pltpu.VMEM((experts * slots, sources * bins), jnp.bfloat16),
            pltpu.VMEM((experts * slots, width), jnp.bfloat16),
            pltpu.VMEM((experts * slots, width), jnp.bfloat16),
            pltpu.VMEM((experts * slots, width), jnp.bfloat16),
            pltpu.VMEM((2, width, hidden), jnp.bfloat16),
            pltpu.VMEM((2, hidden, width), jnp.bfloat16),
            pltpu.SemaphoreType.DMA((2, 2 * PARTS)),
        ],
        compiler_params=pltpu.CompilerParams(vmem_limit_bytes=VMEM_EXPERTS),
        cost_estimate=LARGE,
        name="expert_back",
    )(base, *blocks, up_weight, down_weight)


def per_device(
    queries, key_rows, value_rows, out_grad, moe_input, routes, route_gates, up_weight, down_weight
):
    members = lax.axis_size("exp")
    me = lax.axis_index("exp")
    groups = lax.axis_size("ctx")
    chips = members // 2
    half = chips // 2
    _, bins, top = routes.shape
    base = (me * up_weight.shape[0]).astype(jnp.int32).reshape(1)

    def swap(block):
        return lax.ppermute(block, "exp", [(i, i ^ 1) for i in range(members)])

    def hop(block, step):
        return lax.ppermute(
            block, "exp", [(i, (i + 2 * step) % members) for i in range(members)]
        )

    def work(blocks):
        *kept, give = expert_back(base, blocks, up_weight, down_weight, bins, top)
        return kept, give

    def both_cores(kept, given):
        return [
            (own.astype(jnp.float32) + given[place * bins : (place + 1) * bins]).astype(
                jnp.bfloat16
            )
            for place, own in enumerate(kept)
        ]

    barrier = lax.optimization_barrier
    own = make_block(moe_input[0], out_grad[0], routes[0], route_gates[0])
    right, left = hop(own, 1), hop(own, -1)
    pair = [own, swap(own)]
    table = [[group ^ place for place in range(groups)] for group in range(groups)]
    group_ids = jnp.asarray(table, jnp.int32)[lax.axis_index("ctx")]
    rows = (queries[0], key_rows[0], value_rows[0], out_grad[0])
    packed = pack_groups(group_ids, rows, groups)
    pair, packed = barrier((pair, packed))
    heads = exchange(packed)
    kept, give = work(pair)
    heads, kept, give = barrier((heads, kept, give))
    results = heads_back(heads)
    right, kept, give, results = barrier((right, kept, give, results))
    total = kept[0].astype(jnp.float32) + swap(give)
    results = exchange(results)
    steps, parts, arrived = [], [], []
    for d in range(1, half + 1):
        blocks = [right, swap(right)]
        following = []
        if d < half:
            following.append(hop(right, 1))
            blocks += [left, swap(left)]
            if d + 1 < half:
                following.append(hop(left, -1))
        if d > 1:
            sums = both_cores(kept, swap(give))
            sums, blocks = barrier((sums, blocks))
            arrived = [hop(part, step) for part, step in zip(sums, steps)]
        kept, give = work(blocks)
        following, arrived, results, kept, give = barrier(
            (following, arrived, results, kept, give)
        )
        right, left = (following + [None, None])[:2]
        parts += arrived
        steps = [-d, d] if d < half else [half]
    outs = unpack_groups(group_ids, results)
    for part, step in zip(both_cores(kept, swap(give)), steps):
        parts.append(hop(part, step))
    for part in parts:
        total = total + part
    return tuple(out[None] for out in outs) + (total.astype(jnp.bfloat16)[None],)


def solution(mesh):
    rows = P("exp", "ctx", None)
    experts = P("exp", None, None)
    return jax.shard_map(
        per_device,
        mesh=mesh,
        in_specs=(rows,) * 7 + (experts,) * 2,
        out_specs=(rows,) * 4,
        check_vma=False,
    )
```

time: 179 us -> 147 us (0.82)
  waiting for transfers between devices: 80.9 us -> 60.1 us
  starting transfers between devices: 24 us -> 18.1 us
  local copies, waits for them, and re-layouts: 10.9 us -> 7.31 us
    ppermute x9 -> x6, waiting for transfers between devices: 78.8 us -> 49 us  [hop(): lax.ppermute(block, 'exp', [(i, (i + 2 * step) % members) for i in range(...]
    all_to_all x2 -> x0, starting transfers between devices: 9.49 us -> none  [exchange(): lax.all_to_all(packed, 'ctx', split_axis=0, concat_axis=0, tiled=True)]
    ppermute x0 -> x6, starting transfers between devices: none -> 6.98 us  [exchange(): lax.ppermute(blocks[place], 'ctx', [(i, i ^ place) for i in range(groups)])]
    ppermute x0 -> x6, waiting for transfers between devices: none -> 6.32 us  [exchange(): lax.ppermute(blocks[place], 'ctx', [(i, i ^ place) for i in range(groups)])]
    unnamed x32 -> x26, local copies, waits for them, and re-layouts: 10.9 us -> 6.62 us
    ppermute x9 -> x6, starting transfers between devices: 12.4 us -> 9.56 us  [hop(): lax.ppermute(block, 'exp', [(i, (i + 2 * step) % members) for i in range(...]
    ppermute x11 -> x7, waiting for transfers between devices: 2.09 us -> 4.76 us  [swap(): return lax.ppermute(block, 'exp', [(i, i ^ 1) for i in range(members)])]
  transfers between devices with their start and end apart: 22 -> 19, of which waited for: 7 -> 9; matrix products, arithmetic and copies ran while one was open for 0% -> 1% of each run, Pallas kernels for 33% -> 40%
where the time goes in v1:
time: 147 us; the launch traced here: 146 us
  waiting for transfers between devices  60.1 us (41%)
  Pallas kernels  58.3 us (40%)
  starting transfers between devices  18.1 us (12%)
  local copies, waits for them, and re-layouts  7.31 us (5%)
  other arithmetic  1.74 us (1%)
    pallas_call x3, Pallas kernels, expert_back(): pl.pallas_call(functools.partial(expert_kernel, sources, top), out_shape=...  49.4 us
    ppermute x6, waiting for transfers between devices, hop(): lax.ppermute(block, 'exp', [(i, (i + 2 * step) % members) for i in range(...  49 us
    ppermute x6, starting transfers between devices, hop(): lax.ppermute(block, 'exp', [(i, (i + 2 * step) % members) for i in range(...  9.56 us
    ppermute x6, starting transfers between devices, exchange(): lax.ppermute(blocks[place], 'ctx', [(i, i ^ place) for i in range(groups)])  6.98 us
    unnamed x26, local copies, waits for them, and re-layouts  6.62 us
    pallas_call x1, Pallas kernels, heads_back(): pl.pallas_call(heads_kernel, grid=(heads,), out_shape=[jax.ShapeDtypeStru...  6.37 us
    ppermute x6, waiting for transfers between devices, exchange(): lax.ppermute(blocks[place], 'ctx', [(i, i ^ place) for i in range(groups)])  6.32 us
    ppermute x7, waiting for transfers between devices, swap(): return lax.ppermute(block, 'exp', [(i, i ^ 1) for i in range(members)])  4.76 us
  transfers between devices with their start and end apart: 19, of which 9 were waited for; matrix products, arithmetic and copies ran while one was open for 1% of the time, Pallas kernels for 40%

profile of v1, /device:TPU:0, one launch (start us, length us, event | category | flops | bytes accessed | tf_op | source)
XLA Modules:
  0.0 146.3 jit_solution(13802028722139601825)
XLA Ops:
  0.6 1.0 copy-done
  1.7 1.0 copy-done.5
  2.7 0.7 copy-done.8
  3.4 0.7 copy-done.9
  4.1 0.1 make_block.1.refs_0_
  4.2 0.5 collective-permute-start.1
  4.7 4.7 %collective-permute-start.10 = (bf16[272,2048]{1,0:T(8,128)(2,1)S(1)}, bf16[272,2048]{1,0:T(8,128)(2,1)}, u32[]{:S(2)}, u32[]{:S(2)}) collective-permute-start(bf16[272,2048]{1,0:T(8,128)(2,1)S(1)} %make_block.1.refs_0_), channel_id=1, source_target_pairs={{0,6},{1,7},{2,0},{3,1},{4,2},{5,3},{6,4},{7,5},{8,14},{9,15},{10,... | collective-permute-start | bytes 3342344 | tf_op jit(solution)/shard_map/ppermute | solution.py:287
  9.4 0.0 collective-permute-start
  9.4 0.7 dynamic-slice_bitcast_fusion.group_ref
  10.1 0.7 pack_groups.1
  10.8 0.0 copy-start.6
  10.8 0.8 copy-done.6
  11.6 0.8 copy-done.10
  12.4 0.8 copy-done.11
  13.2 0.8 copy-done.12
  14.0 0.0 collective-permute-done.1.refs_1_
  14.0 1.5 %collective-permute-start.2 = (bf16[4,128,512]{2,1,0:T(8,128)(2,1)}, bf16[4,128,512]{2,1,0:T(8,128)(2,1)S(1)}, u32[]{:S(2)}, u32[]{:S(2)}) collective-permute-start(bf16[4,128,512]{2,1,0:T(8,128)(2,1)} %copy-done.12), channel_id=1, source_target_pairs={{0,8},{8,0},{16,24},{24,16},{1,9},{9,1},{17,25},{25,17},{2,10},{10... | collective-permute-start | bytes 1572872 | tf_op jit(solution)/shard_map/ppermute | solution.py:133
  15.5 1.5 %collective-permute-start.3 = (bf16[4,128,512]{2,1,0:T(8,128)(2,1)}, bf16[4,128,512]{2,1,0:T(8,128)(2,1)S(1)}, u32[]{:S(2)}, u32[]{:S(2)}) collective-permute-start(bf16[4,128,512]{2,1,0:T(8,128)(2,1)} %copy-done.11), channel_id=1, source_target_pairs={{0,16},{8,24},{16,0},{24,8},{1,17},{9,25},{17,1},{25,9},{2,18},{10... | collective-permute-start | bytes 1572872 | tf_op jit(solution)/shard_map/ppermute | solution.py:133
  17.0 0.5 collective-permute-start.4
  17.5 16.1 %expert_back.3 = (bf16[128,2048]{1,0:T(8,128)(2,1)S(1)}, bf16[128,2048]{1,0:T(8,128)(2,1)S(1)}) custom-call(s32[1]{0:T(128)} %bitcast.10.base_ref, bf16[272,2048]{1,0:T(8,128)(2,1)S(1)} %make_block.1.refs_0_, bf16[272,2048]{1,0:T(8,128)(2,1)} %collective-permute-done.1.refs_1_, bf16[4,2048,768]{2,1,0:T(8,128)(2,1)} %refs_2_.3, bf16[4,768,2048]{2,1,0:T(8,128)(2,1)} %refs_3_.3), custom_call_target="tpu_custom_call" | custom-call | flops 30000001024 | bytes 50000000 | tf_op jit(solution)/shard_map/expert_back/pallas_call | solution.py:249
  33.5 0.8 collective-permute-done.10.refs_2_
  34.3 0.0 collective-permute-start.11
  34.3 6.3 %collective-permute-done.3.refs_2_ = bf16[4,128,512]{2,1,0:T(8,128)(2,1)S(1)} collective-permute-done((bf16[4,128,512]{2,1,0:T(8,128)(2,1)}, bf16[4,128,512]{2,1,0:T(8,128)(2,1)S(1)}, u32[]{:S(2)}, u32[]{:S(2)}) %collective-permute-start.3) | collective-permute-done | bytes 524320 | tf_op jit(solution)/shard_map/ppermute | solution.py:133
  40.6 6.4 %heads_back.1 = (bf16[3,128,512]{2,1,0:T(8,128)(2,1)S(1)}, bf16[3,128,512]{2,1,0:T(8,128)(2,1)S(1)}, bf16[3,128,512]{2,1,0:T(8,128)(2,1)S(1)}, bf16[3,128,512]{2,1,0:T(8,128)(2,1)S(1)}) custom-call(bf16[4,128,512]{2,1,0:T(8,128)(2,1)S(1)} %copy-done.7, bf16[4,128,512]{2,1,0:T(8,128)(2,1)S(1)} %collective-permute-done.2.refs_1_, ...), custom_call_target="tpu_custom_call" | custom-call | flops 1 | bytes 1 | tf_op jit(solution)/shard_map/heads_back/pallas_call | solution.py:118
  47.0 11.7 %collective-permute-done.refs_0_ = bf16[272,2048]{1,0:T(8,128)(2,1)} collective-permute-done((bf16[272,2048]{1,0:T(8,128)(2,1)S(1)}, bf16[272,2048]{1,0:T(8,128)(2,1)}, u32[]{:S(2)}, u32[]{:S(2)}) %collective-permute-start) | collective-permute-done | bytes 1114144 | tf_op jit(solution)/shard_map/ppermute | solution.py:287
  58.7 1.6 %collective-permute-start.5 = (bf16[272,2048]{1,0:T(8,128)(2,1)}, bf16[272,2048]{1,0:T(8,128)(2,1)S(1)}, u32[]{:S(2)}, u32[]{:S(2)}) collective-permute-start(bf16[272,2048]{1,0:T(8,128)(2,1)} %collective-permute-done.refs_0_), channel_id=1, source_target_pairs={{0,2},{1,3},{2,4},{3,5},{4,6},{5,7},{6,0},{7,1},{8,10},{9,11},{10,... | collective-permute-start | bytes 3342344 | tf_op jit(solution)/shard_map/ppermute | solution.py:287
  60.3 1.5 %collective-permute-start.6 = (bf16[3,128,512]{2,1,0:T(8,128)(2,1)S(1)}, bf16[3,128,512]{2,1,0:T(8,128)(2,1)S(1)}, u32[]{:S(2)}, u32[]{:S(2)}) collective-permute-start(bf16[3,128,512]{2,1,0:T(8,128)(2,1)S(1)} %get-tuple-element.85), channel_id=1, source_target_pairs={{0,8},{8,0},{16,24},{24,16},{1,9},{9,1},{17,25},{25,17},{2,10},{10... | collective-permute-start | bytes 1179656 | tf_op jit(solution)/shard_map/ppermute | solution.py:133
  61.8 1.5 %collective-permute-start.7 = (bf16[3,128,512]{2,1,0:T(8,128)(2,1)S(1)}, bf16[3,128,512]{2,1,0:T(8,128)(2,1)S(1)}, u32[]{:S(2)}, u32[]{:S(2)}) collective-permute-start(bf16[3,128,512]{2,1,0:T(8,128)(2,1)S(1)} %get-tuple-element.86), channel_id=1, source_target_pairs={{0,16},{8,24},{16,0},{24,8},{1,17},{9,25},{17,1},{25,9},{2,18},{10... | collective-permute-start | bytes 1179656 | tf_op jit(solution)/shard_map/ppermute | solution.py:133
  63.3 0.5 collective-permute-start.8
  63.8 18.5 %expert_back.4 = (bf16[128,2048]{1,0:T(8,128)(2,1)S(1)}, bf16[128,2048]{1,0:T(8,128)(2,1)S(1)}, bf16[256,2048]{1,0:T(8,128)(2,1)S(1)}) custom-call(s32[1]{0:T(128)} %bitcast.10.base_ref, bf16[272,2048]{1,0:T(8,128)(2,1)} %collective-permute-done.refs_0_, bf16[272,2048]{1,0:T(8,128)(2,1)S(1)} %collective-permute-done.9.refs_1_, ...), custom_call_target="tpu_custom_call" | custom-call | flops 30000001024 | bytes 50000000 | tf_op jit(solution)/shard_map/expert_back/pallas_call | solution.py:249
  82.3 0.0 collective-permute-done.6.refs_1_
  82.4 0.0 collective-permute-done.7.refs_2_
  82.4 5.3 %collective-permute-done.5.refs_0_ = bf16[272,2048]{1,0:T(8,128)(2,1)S(1)} collective-permute-done((bf16[272,2048]{1,0:T(8,128)(2,1)}, bf16[272,2048]{1,0:T(8,128)(2,1)S(1)}, u32[]{:S(2)}, u32[]{:S(2)}) %collective-permute-start.5) | collective-permute-done | bytes 1114144 | tf_op jit(solution)/shard_map/ppermute | solution.py:287
  87.7 0.0 collective-permute-start.12
  87.7 0.5 collective-permute-start.13
  88.2 2.1 %collective-permute-done.12 = bf16[256,2048]{1,0:T(8,128)(2,1)S(1)} collective-permute-done((bf16[256,2048]{1,0:T(8,128)(2,1)S(1)}, bf16[256,2048]{1,0:T(8,128)(2,1)S(1)}, u32[]{:S(2)}, u32[]{:S(2)}) %collective-permute-start.12) | collective-permute-done | bytes 1048608 | tf_op jit(solution)/shard_map/ppermute | solution.py:284
  90.3 0.4 add_convert_fusion.2
  90.7 1.2 collective-permute-done.13.refs_1_
  91.9 2.0 %collective-permute-start.15 = (bf16[128,2048]{1,0:T(8,128)(2,1)S(1)}, bf16[128,2048]{1,0:T(8,128)(2,1)S(1)}, u32[]{:S(2)}, u32[]{:S(2)}) collective-permute-start(bf16[128,2048]{1,0:T(8,128)(2,1)S(1)} %get-tuple-element.96), channel_id=1, source_target_pairs={{0,2},{1,3},{2,4},{3,5},{4,6},{5,7},{6,0},{7,1},{8,10},{9,11},{10,... | collective-permute-start | bytes 1572872 | tf_op jit(solution)/shard_map/ppermute | solution.py:287
  93.9 14.8 %expert_back.5 = (bf16[128,2048]{1,0:T(8,128)(2,1)S(1)}, bf16[128,2048]{1,0:T(8,128)(2,1)S(1)}) custom-call(s32[1]{0:T(128)} %bitcast.10.base_ref, bf16[272,2048]{1,0:T(8,128)(2,1)S(1)} %collective-permute-done.5.refs_0_, bf16[272,2048]{1,0:T(8,128)(2,1)S(1)} %collective-permute-done.13.refs_1_, bf16[4,2048,768]{2,1,0:T(8,128)(2,1)} %refs_2_.3, ...), custom_call_target="tpu_custom_call" | custom-call | flops 30000001024 | bytes 50000000 | tf_op jit(solution)/shard_map/expert_back/pallas_call | solution.py:249
  108.7 8.4 %collective-permute-done.14 = bf16[128,2048]{1,0:T(8,128)(2,1)S(1)} collective-permute-done((bf16[128,2048]{1,0:T(8,128)(2,1)S(1)}, bf16[128,2048]{1,0:T(8,128)(2,1)S(1)}, u32[]{:S(2)}, u32[]{:S(2)}) %collective-permute-start.14) | collective-permute-done | bytes 524320 | tf_op jit(solution)/shard_map/ppermute | solution.py:287
  117.1 0.5 collective-permute-start.16
  117.6 1.4 collective-permute-done.17
  119.0 0.1 add_convert_fusion.1
  119.2 1.2 collective-permute-start.18
  120.4 1.8 %unpack_groups.1 = (bf16[128,2048]{1,0:T(8,128)(2,1)}, bf16[128,2048]{1,0:T(8,128)(2,1)}, bf16[128,2048]{1,0:T(8,128)(2,1)}) custom-call(s32[4]{0:T(128)S(1)} %dynamic-slice_bitcast_fusion.group_ref, bf16[3,128,512]{2,1,0:T(8,128)(2,1)S(1)} %get-tuple-element.105.refs_0_, bf16[3,128,512]{2,1,0:T(8,128)(2,1)S(1)} %collective-permute-done.6.refs_1_, ...), custom_call_target="tpu_custom_call" | custom-call | flops 1 | bytes 1 | tf_op jit(solution)/shard_map/unpack_groups/pallas_call | solution.py:76
  122.2 22.9 %collective-permute-done.18 = bf16[128,2048]{1,0:T(8,128)(2,1)S(1)} collective-permute-done((bf16[128,2048]{1,0:T(8,128)(2,1)S(1)}, bf16[128,2048]{1,0:T(8,128)(2,1)S(1)}, u32[]{:S(2)}, u32[]{:S(2)}) %collective-permute-start.18) | collective-permute-done | bytes 524320 | tf_op jit(solution)/shard_map/ppermute | solution.py:287
  145.1 1.2 fusion
  (27 shorter events, 0.1 us)
Async XLA Ops:
  0.6 1.0 copy-start
  1.7 1.0 copy-start.5
  2.7 0.7 copy-start.8
  3.4 0.7 copy-start.9
  4.1 6.0 %copy-start.1 = (bf16[1,128,2048]{2,1,0:T(8,128)(2,1)S(1)}, bf16[1,128,2048]{2,1,0:T(8,128)(2,1)}, u32[]{:S(2)}) copy-start(bf16[1,128,2048]{2,1,0:T(8,128)(2,1)} %param.13) | copy-start | bytes 1572868
  4.1 6.0 %copy-start.2 = (bf16[1,128,2048]{2,1,0:T(8,128)(2,1)S(1)}, bf16[1,128,2048]{2,1,0:T(8,128)(2,1)}, u32[]{:S(2)}) copy-start(bf16[1,128,2048]{2,1,0:T(8,128)(2,1)} %param.10) | copy-start | bytes 1572868
  4.1 6.0 %copy-start.3 = (bf16[1,128,2048]{2,1,0:T(8,128)(2,1)S(1)}, bf16[1,128,2048]{2,1,0:T(8,128)(2,1)}, u32[]{:S(2)}) copy-start(bf16[1,128,2048]{2,1,0:T(8,128)(2,1)} %param.11) | copy-start | bytes 1572868
  4.1 6.0 %copy-start.4 = (bf16[1,128,2048]{2,1,0:T(8,128)(2,1)S(1)}, bf16[1,128,2048]{2,1,0:T(8,128)(2,1)}, u32[]{:S(2)}) copy-start(bf16[1,128,2048]{2,1,0:T(8,128)(2,1)} %param.12) | copy-start | bytes 1572868
  4.2 9.8 %collective-permute-start.1 = (bf16[272,2048]{1,0:T(8,128)(2,1)S(1)}, bf16[272,2048]{1,0:T(8,128)(2,1)}, u32[]{:S(2)}, u32[]{:S(2)}) collective-permute-start(bf16[272,2048]{1,0:T(8,128)(2,1)S(1)} %make_block.1.refs_0_), channel_id=1, source_target_pairs={{0,1},{1,0},{2,3},{3,2},{4,5},{5,4},{6,7},{7,6},{8,9},{9,8},{10,11... | collective-permute-start | bytes 3342344 | tf_op jit(solution)/shard_map/ppermute | solution.py:284
  4.7 29.6 %collective-permute-start.10 = (bf16[272,2048]{1,0:T(8,128)(2,1)S(1)}, bf16[272,2048]{1,0:T(8,128)(2,1)}, u32[]{:S(2)}, u32[]{:S(2)}) collective-permute-start(bf16[272,2048]{1,0:T(8,128)(2,1)S(1)} %make_block.1.refs_0_), channel_id=1, source_target_pairs={{0,6},{1,7},{2,0},{3,1},{4,2},{5,3},{6,4},{7,5},{8,14},{9,15},{10,... | collective-permute-start | bytes 3342344 | tf_op jit(solution)/shard_map/ppermute | solution.py:287
  9.4 49.3 %collective-permute-start = (bf16[272,2048]{1,0:T(8,128)(2,1)S(1)}, bf16[272,2048]{1,0:T(8,128)(2,1)}, u32[]{:S(2)}, u32[]{:S(2)}) collective-permute-start(bf16[272,2048]{1,0:T(8,128)(2,1)S(1)} %make_block.1.refs_0_), channel_id=1, source_target_pairs={{0,2},{1,3},{2,4},{3,5},{4,6},{5,7},{6,0},{7,1},{8,10},{9,11},{10,... | collective-permute-start | bytes 3342344 | tf_op jit(solution)/shard_map/ppermute | solution.py:287
  10.8 0.8 copy-start.6
  11.6 0.8 copy-start.10
  12.4 0.8 copy-start.11
  13.2 0.8 copy-start.12
  14.0 20.3 %collective-permute-start.2 = (bf16[4,128,512]{2,1,0:T(8,128)(2,1)}, bf16[4,128,512]{2,1,0:T(8,128)(2,1)S(1)}, u32[]{:S(2)}, u32[]{:S(2)}) collective-permute-start(bf16[4,128,512]{2,1,0:T(8,128)(2,1)} %copy-done.12), channel_id=1, source_target_pairs={{0,8},{8,0},{16,24},{24,16},{1,9},{9,1},{17,25},{25,17},{2,10},{10... | collective-permute-start | bytes 1572872 | tf_op jit(solution)/shard_map/ppermute | solution.py:133
  15.5 25.2 %collective-permute-start.3 = (bf16[4,128,512]{2,1,0:T(8,128)(2,1)}, bf16[4,128,512]{2,1,0:T(8,128)(2,1)S(1)}, u32[]{:S(2)}, u32[]{:S(2)}) collective-permute-start(bf16[4,128,512]{2,1,0:T(8,128)(2,1)} %copy-done.11), channel_id=1, source_target_pairs={{0,16},{8,24},{16,0},{24,8},{1,17},{9,25},{17,1},{25,9},{2,18},{10... | collective-permute-start | bytes 1572872 | tf_op jit(solution)/shard_map/ppermute | solution.py:133
  17.0 23.6 %collective-permute-start.4 = (bf16[4,128,512]{2,1,0:T(8,128)(2,1)}, bf16[4,128,512]{2,1,0:T(8,128)(2,1)S(1)}, u32[]{:S(2)}, u32[]{:S(2)}) collective-permute-start(bf16[4,128,512]{2,1,0:T(8,128)(2,1)} %copy-done.10), channel_id=1, source_target_pairs={{0,24},{8,16},{16,8},{24,0},{1,25},{9,17},{17,9},{25,1},{2,26},{10... | collective-permute-start | bytes 1572872 | tf_op jit(solution)/shard_map/ppermute | solution.py:133
  17.5 23.2 %copy-start.7 = (bf16[4,128,512]{2,1,0:T(8,128)(2,1)S(1)}, bf16[4,128,512]{2,1,0:T(8,128)(2,1)}, u32[]{:S(2)}) copy-start(bf16[4,128,512]{2,1,0:T(8,128)(2,1)} %copy-done.6) | copy-start | bytes 1572868
  34.3 29.0 %collective-permute-start.11 = (bf16[272,2048]{1,0:T(8,128)(2,1)}, bf16[272,2048]{1,0:T(8,128)(2,1)S(1)}, u32[]{:S(2)}, u32[]{:S(2)}) collective-permute-start(bf16[272,2048]{1,0:T(8,128)(2,1)} %collective-permute-done.10.refs_2_), channel_id=1, source_target_pairs={{0,1},{1,0},{2,3},{3,2},{4,5},{5,4},{6,7},{7,6},{8,9},{9,8},{10,11... | collective-permute-start | bytes 3342344 | tf_op jit(solution)/shard_map/ppermute | solution.py:284
  58.7 5.1 %collective-permute-start.9 = (bf16[272,2048]{1,0:T(8,128)(2,1)}, bf16[272,2048]{1,0:T(8,128)(2,1)S(1)}, u32[]{:S(2)}, u32[]{:S(2)}) collective-permute-start(bf16[272,2048]{1,0:T(8,128)(2,1)} %collective-permute-done.refs_0_), channel_id=1, source_target_pairs={{0,1},{1,0},{2,3},{3,2},{4,5},{5,4},{6,7},{7,6},{8,9},{9,8},{10,11... | collective-permute-start | bytes 3342344 | tf_op jit(solution)/shard_map/ppermute | solution.py:284
  58.7 29.0 %collective-permute-start.5 = (bf16[272,2048]{1,0:T(8,128)(2,1)}, bf16[272,2048]{1,0:T(8,128)(2,1)S(1)}, u32[]{:S(2)}, u32[]{:S(2)}) collective-permute-start(bf16[272,2048]{1,0:T(8,128)(2,1)} %collective-permute-done.refs_0_), channel_id=1, source_target_pairs={{0,2},{1,3},{2,4},{3,5},{4,6},{5,7},{6,0},{7,1},{8,10},{9,11},{10,... | collective-permute-start | bytes 3342344 | tf_op jit(solution)/shard_map/ppermute | solution.py:287
  60.3 22.0 %collective-permute-start.6 = (bf16[3,128,512]{2,1,0:T(8,128)(2,1)S(1)}, bf16[3,128,512]{2,1,0:T(8,128)(2,1)S(1)}, u32[]{:S(2)}, u32[]{:S(2)}) collective-permute-start(bf16[3,128,512]{2,1,0:T(8,128)(2,1)S(1)} %get-tuple-element.85), channel_id=1, source_target_pairs={{0,8},{8,0},{16,24},{24,16},{1,9},{9,1},{17,25},{25,17},{2,10},{10... | collective-permute-start | bytes 1179656 | tf_op jit(solution)/shard_map/ppermute | solution.py:133
  61.8 20.6 %collective-permute-start.7 = (bf16[3,128,512]{2,1,0:T(8,128)(2,1)S(1)}, bf16[3,128,512]{2,1,0:T(8,128)(2,1)S(1)}, u32[]{:S(2)}, u32[]{:S(2)}) collective-permute-start(bf16[3,128,512]{2,1,0:T(8,128)(2,1)S(1)} %get-tuple-element.86), channel_id=1, source_target_pairs={{0,16},{8,24},{16,0},{24,8},{1,17},{9,25},{17,1},{25,9},{2,18},{10... | collective-permute-start | bytes 1179656 | tf_op jit(solution)/shard_map/ppermute | solution.py:133
  63.3 19.0 %collective-permute-start.8 = (bf16[3,128,512]{2,1,0:T(8,128)(2,1)S(1)}, bf16[3,128,512]{2,1,0:T(8,128)(2,1)S(1)}, u32[]{:S(2)}, u32[]{:S(2)}) collective-permute-start(bf16[3,128,512]{2,1,0:T(8,128)(2,1)S(1)} %get-tuple-element.87), channel_id=1, source_target_pairs={{0,24},{8,16},{16,8},{24,0},{1,25},{9,17},{17,9},{25,1},{2,26},{10... | collective-permute-start | bytes 1179656 | tf_op jit(solution)/shard_map/ppermute | solution.py:133
  87.7 2.7 %collective-permute-start.12 = (bf16[256,2048]{1,0:T(8,128)(2,1)S(1)}, bf16[256,2048]{1,0:T(8,128)(2,1)S(1)}, u32[]{:S(2)}, u32[]{:S(2)}) collective-permute-start(bf16[256,2048]{1,0:T(8,128)(2,1)S(1)} %get-tuple-element.92), channel_id=1, source_target_pairs={{0,1},{1,0},{2,3},{3,2},{4,5},{5,4},{6,7},{7,6},{8,9},{9,8},{10,11... | collective-permute-start | bytes 3145736 | tf_op jit(solution)/shard_map/ppermute | solution.py:284
  87.7 4.3 %collective-permute-start.13 = (bf16[272,2048]{1,0:T(8,128)(2,1)S(1)}, bf16[272,2048]{1,0:T(8,128)(2,1)S(1)}, u32[]{:S(2)}, u32[]{:S(2)}) collective-permute-start(bf16[272,2048]{1,0:T(8,128)(2,1)S(1)} %collective-permute-done.5.refs_0_), channel_id=1, source_target_pairs={{0,1},{1,0},{2,3},{3,2},{4,5},{5,4},{6,7},{7,6},{8,9},{9,8},{10,11... | collective-permute-start | bytes 3342344 | tf_op jit(solution)/shard_map/ppermute | solution.py:284
  91.9 25.2 %collective-permute-start.14 = (bf16[128,2048]{1,0:T(8,128)(2,1)S(1)}, bf16[128,2048]{1,0:T(8,128)(2,1)S(1)}, u32[]{:S(2)}, u32[]{:S(2)}) collective-permute-start(bf16[128,2048]{1,0:T(8,128)(2,1)S(1)} %get-tuple-element.95), channel_id=1, source_target_pairs={{0,6},{1,7},{2,0},{3,1},{4,2},{5,3},{6,4},{7,5},{8,14},{9,15},{10,... | collective-permute-start | bytes 1572872 | tf_op jit(solution)/shard_map/ppermute | solution.py:287
  91.9 25.2 %collective-permute-start.15 = (bf16[128,2048]{1,0:T(8,128)(2,1)S(1)}, bf16[128,2048]{1,0:T(8,128)(2,1)S(1)}, u32[]{:S(2)}, u32[]{:S(2)}) collective-permute-start(bf16[128,2048]{1,0:T(8,128)(2,1)S(1)} %get-tuple-element.96), channel_id=1, source_target_pairs={{0,2},{1,3},{2,4},{3,5},{4,6},{5,7},{6,0},{7,1},{8,10},{9,11},{10,... | collective-permute-start | bytes 1572872 | tf_op jit(solution)/shard_map/ppermute | solution.py:287
  117.1 1.9 %collective-permute-start.17 = (bf16[128,2048]{1,0:T(8,128)(2,1)S(1)}, bf16[128,2048]{1,0:T(8,128)(2,1)S(1)}, u32[]{:S(2)}, u32[]{:S(2)}) collective-permute-start(bf16[128,2048]{1,0:T(8,128)(2,1)S(1)} %get-tuple-element.117), channel_id=1, source_target_pairs={{0,1},{1,0},{2,3},{3,2},{4,5},{5,4},{6,7},{7,6},{8,9},{9,8},{10,11... | collective-permute-start | bytes 1572872 | tf_op jit(solution)/shard_map/ppermute | solution.py:284
  117.1 5.1 %collective-permute-start.16 = (bf16[128,2048]{1,0:T(8,128)(2,1)S(1)}, bf16[128,2048]{1,0:T(8,128)(2,1)S(1)}, u32[]{:S(2)}, u32[]{:S(2)}) collective-permute-start(bf16[128,2048]{1,0:T(8,128)(2,1)S(1)} %get-tuple-element.113), channel_id=1, source_target_pairs={{0,1},{1,0},{2,3},{3,2},{4,5},{5,4},{6,7},{7,6},{8,9},{9,8},{10,11... | collective-permute-start | bytes 1572872 | tf_op jit(solution)/shard_map/ppermute | solution.py:284
  119.2 25.9 %collective-permute-start.18 = (bf16[128,2048]{1,0:T(8,128)(2,1)S(1)}, bf16[128,2048]{1,0:T(8,128)(2,1)S(1)}, u32[]{:S(2)}, u32[]{:S(2)}) collective-permute-start(bf16[128,2048]{1,0:T(8,128)(2,1)S(1)} %add_convert_fusion.1), channel_id=1, source_target_pairs={{0,4},{1,5},{2,6},{3,7},{4,0},{5,1},{6,2},{7,3},{8,12},{9,13},{10,... | collective-permute-start | bytes 1572872 | tf_op jit(solution)/shard_map/ppermute | solution.py:287

commit v2 on v1

--- a/solution.py
+++ b/solution.py
@@ -13,8 +13,14 @@
 PARTS = 4
 VMEM_BYTES = 36 * 1024 * 1024
 VMEM_EXPERTS = 45 * 1024 * 1024
-SMALL = pl.CostEstimate(flops=1, bytes_accessed=1, transcendentals=0)
-LARGE = pl.CostEstimate(flops=30 * 10**9, bytes_accessed=50 * 10**6, transcendentals=0)
+def cost(units):
+    return pl.CostEstimate(
+        flops=units * 10**9, bytes_accessed=units * 10**6, transcendentals=0
+    )
+
+
+SMALL = cost(0)
+OWN_COST, HEADS_COST, NEAR_COST, FAR_COST = 30, 5, 0, 30
 NT = (((1,), (1,)), ((), ()))
 TN = (((0,), (0,)), ((), ()))
 
@@ -122,7 +128,7 @@
         in_specs=[pl.BlockSpec((4, bins, HD), lambda h: (0, 0, h))] * groups,
         out_specs=[pl.BlockSpec((3, bins, HD), lambda h: (0, 0, h))] * groups,
         compiler_params=pltpu.CompilerParams(vmem_limit_bytes=VMEM_BYTES),
-        cost_estimate=SMALL,
+        cost_estimate=cost(HEADS_COST),
         name="heads_back",
     )(*blocks)
 
@@ -160,11 +166,13 @@
     )(tokens, grads, routes.T, gates.T)
 
 
-def expert_kernel(sources, top, base_ref, *refs):
-    block_refs = refs[:sources]
-    up_hbm, down_hbm = refs[sources : sources + 2]
-    keep_refs = refs[sources + 2 : -8]
-    give_ref, pick_ref, token_rows, gated_rows, back_rows, up_ref, down_ref, sems = refs[-8:]
+def expert_kernel(layout, pieces, top, base_ref, *refs):
+    sources, count = len(layout), sum(layout)
+    block_refs, refs = refs[:count], refs[count:]
+    up_hbm, down_hbm = refs[:2]
+    keep_refs = refs[2 : 2 + sources // 2]
+    give_refs = refs[2 + sources // 2 : -7]
+    pick_ref, token_rows, gated_rows, back_rows, up_ref, down_ref, sems = refs[-7:]
     bins = keep_refs[0].shape[0]
     slots = sources * CAP
     experts = pick_ref.shape[0] // slots
@@ -185,13 +193,18 @@
         copy.start()
 
     def pick_rows():
+        blocks, first = [], 0
+        for length in layout:
+            members = [ref[...] for ref in block_refs[first : first + length]]
+            blocks.append(jnp.concatenate(members, axis=0) if length > 1 else members[0])
+            first += length
         earlier = lax.broadcasted_iota(jnp.int32, (bins, bins), 0)
         later = lax.broadcasted_iota(jnp.int32, (bins, bins), 1)
         before = (earlier < later).astype(jnp.bfloat16)
         slot = lax.broadcasted_iota(jnp.int32, (slots, bins), 0).astype(jnp.float32)
         base = base_ref[0].astype(jnp.float32)
         gates = [jnp.zeros((slots, 1), jnp.float32)] * experts
-        for source, block in enumerate(block_refs):
+        for source, block in enumerate(blocks):
             notes = block[2 * bins :, :bins].astype(jnp.float32)
             named = notes[:top] - base
             weights = notes[top : 2 * top] + notes[2 * top : 3 * top] + notes[3 * top : 4 * top]
@@ -210,9 +223,9 @@
                     local * slots : (local + 1) * slots, source * bins : (source + 1) * bins
                 ] = pick.astype(jnp.bfloat16)
         picks = pick_ref[...]
-        tokens = jnp.concatenate([block[:bins] for block in block_refs], axis=0)
+        tokens = jnp.concatenate([block[:bins] for block in blocks], axis=0)
         token_rows[...] = dot_nn(picks, tokens).astype(jnp.bfloat16)
-        grads = jnp.concatenate([block[bins : 2 * bins] for block in block_refs], axis=0)
+        grads = jnp.concatenate([block[bins : 2 * bins] for block in blocks], axis=0)
         gate_column = jnp.concatenate(gates, axis=0)
         gated_rows[...] = (gate_column * dot_nn(picks, grads)).astype(jnp.bfloat16)
 
@@ -238,22 +251,27 @@
     for pair, keep in enumerate(keep_refs):
         mine, other = 2 * pair * bins, (2 * pair + 1) * bins
         keep[...] = sums[mine : mine + bins].astype(jnp.bfloat16)
-        give_ref[pair * bins : (pair + 1) * bins] = sums[other : other + bins].astype(jnp.bfloat16)
-
-
-def expert_back(base, blocks, up_weight, down_weight, bins, top):
+        for piece in range(pieces):
+            rows = bins // pieces
+            give_refs[pair * pieces + piece][...] = sums[
+                other + piece * rows : other + (piece + 1) * rows
+            ].astype(jnp.bfloat16)
+
+
+def expert_back(base, blocks, up_weight, down_weight, bins, top, units, pieces):
     sources = len(blocks)
+    layout = [len(block) for block in blocks]
     experts, width, hidden = up_weight.shape
     slots = sources * CAP
     pairs = sources // 2
     return pl.pallas_call(
-        functools.partial(expert_kernel, sources, top),
+        functools.partial(expert_kernel, layout, pieces, top),
         out_shape=[jax.ShapeDtypeStruct((bins, width), jnp.bfloat16)] * pairs
-        + [jax.ShapeDtypeStruct((pairs * bins, width), jnp.bfloat16)],
+        + [jax.ShapeDtypeStruct((bins // pieces, width), jnp.bfloat16)] * (pairs * pieces),
         in_specs=[pl.BlockSpec(memory_space=pltpu.SMEM)]
-        + [pl.BlockSpec(memory_space=pltpu.VMEM)] * sources
+        + [pl.BlockSpec(memory_space=pltpu.VMEM)] * sum(layout)
         + [pl.BlockSpec(memory_space=pltpu.HBM)] * 2,
-        out_specs=[pl.BlockSpec(memory_space=pltpu.VMEM)] * (pairs + 1),
+        out_specs=[pl.BlockSpec(memory_space=pltpu.VMEM)] * (pairs * (1 + pieces)),
         scratch_shapes=[
             pltpu.VMEM((experts * slots, sources * bins), jnp.bfloat16),
             pltpu.VMEM((experts * slots, width), jnp.bfloat16),
@@ -264,9 +282,9 @@
             pltpu.SemaphoreType.DMA((2, 2 * PARTS)),
         ],
         compiler_params=pltpu.CompilerParams(vmem_limit_bytes=VMEM_EXPERTS),
-        cost_estimate=LARGE,
+        cost_estimate=cost(units),
         name="expert_back",
-    )(base, *blocks, up_weight, down_weight)
+    )(base, *[piece for block in blocks for piece in block], up_weight, down_weight)
 
 
 def per_device(
@@ -288,59 +306,71 @@
             block, "exp", [(i, (i + 2 * step) % members) for i in range(members)]
         )
 
-    def work(blocks):
-        *kept, give = expert_back(base, blocks, up_weight, down_weight, bins, top)
-        return kept, give
+    def pair(block):
+        return [[block], [swap(block)]]
+
+    def pair_in_pieces(block):
+        cuts = [0, bins // 2, bins, bins + bins // 2, block.shape[0]]
+        return [[block], [swap(block[a:b]) for a, b in zip(cuts, cuts[1:])]]
+
+    def work(blocks, units, pieces=1):
+        outs = expert_back(base, blocks, up_weight, down_weight, bins, top, units, pieces)
+        return outs[: len(blocks) // 2], outs[len(blocks) // 2 :]
 
     def both_cores(kept, given):
+        pieces = len(given) // len(kept)
         return [
-            (own.astype(jnp.float32) + given[place * bins : (place + 1) * bins]).astype(
-                jnp.bfloat16
-            )
+            (
+                own.astype(jnp.float32)
+                + jnp.concatenate(given[place * pieces : (place + 1) * pieces], axis=0)
+            ).astype(jnp.bfloat16)
             for place, own in enumerate(kept)
         ]
 
     barrier = lax.optimization_barrier
     own = make_block(moe_input[0], out_grad[0], routes[0], route_gates[0])
     right, left = hop(own, 1), hop(own, -1)
-    pair = [own, swap(own)]
+    own_pair = pair(own)
     table = [[group ^ place for place in range(groups)] for group in range(groups)]
     group_ids = jnp.asarray(table, jnp.int32)[lax.axis_index("ctx")]
     rows = (queries[0], key_rows[0], value_rows[0], out_grad[0])
     packed = pack_groups(group_ids, rows, groups)
-    pair, packed = barrier((pair, packed))
+    own_pair, packed = barrier((own_pair, packed))
     heads = exchange(packed)
-    kept, give = work(pair)
-    heads, kept, give = barrier((heads, kept, give))
+    kept, give = work(own_pair, OWN_COST)
+    heads, kept, give, left = barrier((heads, kept, give, left))
     results = heads_back(heads)
     right, kept, give, results = barrier((right, kept, give, results))
-    total = kept[0].astype(jnp.float32) + swap(give)
+    total = both_cores(kept, [swap(part) for part in give])[0].astype(jnp.float32)
     results = exchange(results)
     steps, parts, arrived = [], [], []
-    for d in range(1, half + 1):
-        blocks = [right, swap(right)]
-        following = []
-        if d < half:
+    for d in range(1, half):
+        blocks = pair(left) + pair_in_pieces(right)
+        following = [hop(left, -1)]
+        if d + 1 < half:
             following.append(hop(right, 1))
-            blocks += [left, swap(left)]
-            if d + 1 < half:
-                following.append(hop(left, -1))
         if d > 1:
-            sums = both_cores(kept, swap(give))
-            sums, blocks = barrier((sums, blocks))
+            blocks, sums = barrier((blocks, sums))
             arrived = [hop(part, step) for part, step in zip(sums, steps)]
-        kept, give = work(blocks)
+        kept, give = work(blocks, NEAR_COST)
         following, arrived, results, kept, give = barrier(
             (following, arrived, results, kept, give)
         )
-        right, left = (following + [None, None])[:2]
         parts += arrived
-        steps = [-d, d] if d < half else [half]
-    outs = unpack_groups(group_ids, results)
-    for part, step in zip(both_cores(kept, swap(give)), steps):
-        parts.append(hop(part, step))
+        sums = both_cores(kept, [swap(part) for part in give])
+        left, right = (following + [None])[:2]
+        steps = [d, -d]
+    blocks, sums = barrier((pair(left), sums))
+    arrived = [hop(part, step) for part, step in zip(sums, steps)]
+    kept, give = work(blocks, FAR_COST, 2)
+    given = [swap(part) for part in give]
+    kept, given, arrived = barrier((kept, given, arrived))
+    parts += arrived
     for part in parts:
         total = total + part
+    far = hop(both_cores(kept, given)[0], half)
+    outs = unpack_groups(group_ids, results)
+    total = total + far
     return tuple(out[None] for out in outs) + (total.astype(jnp.bfloat16)[None],)
 
 

time: 147 us -> 142 us (0.966)
  waiting for transfers between devices: 60.1 us -> 52 us
  starting transfers between devices: 18.1 us -> 23 us
    ppermute x6, waiting for transfers between devices: 49 us -> 40.5 us  [hop(): lax.ppermute(block, 'exp', [(i, (i + 2 * step) % members) for i in range(...]
    ppermute x6, starting transfers between devices: 9.56 us -> 13.3 us  [hop(): lax.ppermute(block, 'exp', [(i, (i + 2 * step) % members) for i in range(...]
    pallas_call x3, Pallas kernels: 49.4 us -> 47.5 us  [expert_back(): pl.pallas_call(functools.partial(expert_kernel, layout, pieces, top), out...]
    ppermute x7 -> x12, waiting for transfers between devices: 4.76 us -> 6.43 us  [swap(): return lax.ppermute(block, 'exp', [(i, i ^ 1) for i in range(members)])]
    unnamed x26 -> x16, local copies, waits for them, and re-layouts: 6.62 us -> 5.52 us
  transfers between devices with their start and end apart: 19 -> 24, of which waited for: 9 -> 13; matrix products, arithmetic and copies ran while one was open for 1% -> 1% of each run, Pallas kernels for 40% -> 40%
where the time goes in v2:
time: 142 us; the launch traced here: 141 us
  Pallas kernels  57.5 us (40%)
  waiting for transfers between devices  52 us (37%)
  starting transfers between devices  23 us (16%)
  local copies, waits for them, and re-layouts  6.29 us (4%)
  other arithmetic  1.59 us (1%)
    pallas_call x3, Pallas kernels, expert_back(): pl.pallas_call(functools.partial(expert_kernel, layout, pieces, top), out...  47.5 us
    ppermute x6, waiting for transfers between devices, hop(): lax.ppermute(block, 'exp', [(i, (i + 2 * step) % members) for i in range(...  40.5 us
    ppermute x6, starting transfers between devices, hop(): lax.ppermute(block, 'exp', [(i, (i + 2 * step) % members) for i in range(...  13.3 us
    ppermute x6, starting transfers between devices, exchange(): lax.ppermute(blocks[place], 'ctx', [(i, i ^ place) for i in range(groups)])  7.2 us
    ppermute x12, waiting for transfers between devices, swap(): return lax.ppermute(block, 'exp', [(i, i ^ 1) for i in range(members)])  6.43 us
    pallas_call x1, Pallas kernels, heads_back(): pl.pallas_call(heads_kernel, grid=(heads,), out_shape=[jax.ShapeDtypeStru...  6.37 us
    unnamed x16, local copies, waits for them, and re-layouts  5.52 us
    ppermute x6, waiting for transfers between devices, exchange(): lax.ppermute(blocks[place], 'ctx', [(i, i ^ place) for i in range(groups)])  5.11 us
  transfers between devices with their start and end apart: 24, of which 13 were waited for; matrix products, arithmetic and copies ran while one was open for 1% of the time, Pallas kernels for 40%

profile of v2, /device:TPU:0, one launch (start us, length us, event | category | flops | bytes accessed | tf_op | source)
XLA Modules:
  0.0 141.3 jit_solution(12892570627708131412)
XLA Ops:
  0.6 1.0 copy-done
  1.7 1.0 copy-done.5
  2.7 0.7 copy-done.6
  3.4 0.7 copy-done.7
  4.1 1.1 make_block.1.refs_0_
  5.2 0.5 collective-permute-start
  5.6 4.6 %collective-permute-start.4 = (bf16[272,2048]{1,0:T(8,128)(2,1)}, bf16[272,2048]{1,0:T(8,128)(2,1)S(1)}, u32[]{:S(2)}, u32[]{:S(2)}) collective-permute-start(bf16[272,2048]{1,0:T(8,128)(2,1)} %make_block.1.refs_0_), channel_id=1, source_target_pairs={{0,6},{1,7},{2,0},{3,1},{4,2},{5,3},{6,4},{7,5},{8,14},{9,15},{10,... | collective-permute-start | bytes 3342344 | tf_op jit(solution)/shard_map/ppermute | solution.py:305
  10.2 0.7 dynamic-slice_bitcast_fusion.group_ref
  10.9 1.0 copy-done.3
  12.0 1.0 copy-done.4
  13.0 0.7 pack_groups.1
  13.7 1.6 %collective-permute-start.1 = (bf16[4,128,512]{2,1,0:T(8,128)(2,1)S(1)}, bf16[4,128,512]{2,1,0:T(8,128)(2,1)S(1)}, u32[]{:S(2)}, u32[]{:S(2)}) collective-permute-start(bf16[4,128,512]{2,1,0:T(8,128)(2,1)S(1)} %get-tuple-element.67), channel_id=1, source_target_pairs={{0,8},{8,0},{16,24},{24,16},{1,9},{9,1},{17,25},{25,17},{2,10},{10... | collective-permute-start | bytes 1572872 | tf_op jit(solution)/shard_map/ppermute | solution.py:139
  15.3 1.5 %collective-permute-start.2 = (bf16[4,128,512]{2,1,0:T(8,128)(2,1)S(1)}, bf16[4,128,512]{2,1,0:T(8,128)(2,1)S(1)}, u32[]{:S(2)}, u32[]{:S(2)}) collective-permute-start(bf16[4,128,512]{2,1,0:T(8,128)(2,1)S(1)} %get-tuple-element.68), channel_id=1, source_target_pairs={{0,16},{8,24},{16,0},{24,8},{1,17},{9,25},{17,1},{25,9},{2,18},{10... | collective-permute-start | bytes 1572872 | tf_op jit(solution)/shard_map/ppermute | solution.py:139
  16.8 0.5 collective-permute-start.3
  17.3 15.8 %expert_back.3 = (bf16[128,2048]{1,0:T(8,128)(2,1)S(1)}, bf16[128,2048]{1,0:T(8,128)(2,1)S(1)}) custom-call(s32[1]{0:T(128)} %bitcast.10.base_ref, bf16[272,2048]{1,0:T(8,128)(2,1)} %make_block.1.refs_0_, bf16[272,2048]{1,0:T(8,128)(2,1)} %collective-permute-done.refs_1_, bf16[4,2048,768]{2,1,0:T(8,128)(2,1)} %refs_2_.3, bf16[4,768,2048]{2,1,0:T(8,128)(2,1)} %refs_3_.3), custom_call_target="tpu_custom_call" | custom-call | flops 30000001024 | bytes 30000000 | tf_op jit(solution)/shard_map/expert_back/pallas_call | solution.py:267
  33.1 2.4 %collective-permute-done.4.refs_0_ = bf16[272,2048]{1,0:T(8,128)(2,1)S(1)} collective-permute-done((bf16[272,2048]{1,0:T(8,128)(2,1)}, bf16[272,2048]{1,0:T(8,128)(2,1)S(1)}, u32[]{:S(2)}, u32[]{:S(2)}) %collective-permute-start.4) | collective-permute-done | bytes 1114144 | tf_op jit(solution)/shard_map/ppermute | solution.py:305
  35.5 4.8 %collective-permute-done.2.refs_2_ = bf16[4,128,512]{2,1,0:T(8,128)(2,1)S(1)} collective-permute-done((bf16[4,128,512]{2,1,0:T(8,128)(2,1)S(1)}, bf16[4,128,512]{2,1,0:T(8,128)(2,1)S(1)}, u32[]{:S(2)}, u32[]{:S(2)}) %collective-permute-start.2) | collective-permute-done | bytes 524320 | tf_op jit(solution)/shard_map/ppermute | solution.py:139
  40.3 3.5 %collective-permute-start.5 = (bf16[272,2048]{1,0:T(8,128)(2,1)S(1)}, bf16[272,2048]{1,0:T(8,128)(2,1)S(1)}, u32[]{:S(2)}, u32[]{:S(2)}) collective-permute-start(bf16[272,2048]{1,0:T(8,128)(2,1)S(1)} %collective-permute-done.4.refs_0_), channel_id=1, source_target_pairs={{0,6},{1,7},{2,0},{3,1},{4,2},{5,3},{6,4},{7,5},{8,14},{9,15},{10,... | collective-permute-start | bytes 3342344 | tf_op jit(solution)/shard_map/ppermute | solution.py:305
  43.8 6.4 %heads_back.1 = (bf16[3,128,512]{2,1,0:T(8,128)(2,1)S(1)}, bf16[3,128,512]{2,1,0:T(8,128)(2,1)S(1)}, bf16[3,128,512]{2,1,0:T(8,128)(2,1)S(1)}, bf16[3,128,512]{2,1,0:T(8,128)(2,1)S(1)}) custom-call(bf16[4,128,512]{2,1,0:T(8,128)(2,1)S(1)} %get-tuple-element.77.refs_0_, bf16[4,128,512]{2,1,0:T(8,128)(2,1)S(1)} %collective-permute-done.1.refs_1_, ...), custom_call_target="tpu_custom_call" | custom-call | flops 5000000000 | bytes 5000000 | tf_op jit(solution)/shard_map/heads_back/pallas_call | solution.py:124
  50.2 9.9 %collective-permute-done.6.refs_2_ = bf16[272,2048]{1,0:T(8,128)(2,1)S(1)} collective-permute-done((bf16[272,2048]{1,0:T(8,128)(2,1)}, bf16[272,2048]{1,0:T(8,128)(2,1)S(1)}, u32[]{:S(2)}, u32[]{:S(2)}) %collective-permute-start.6) | collective-permute-done | bytes 1114144 | tf_op jit(solution)/shard_map/ppermute | solution.py:305
  60.3 0.6 collective-permute-start.14
  60.9 0.1 collective-permute-start.12
  61.0 0.9 collective-permute-done.11.refs_3_
  61.8 0.1 collective-permute-start.13
  62.0 0.7 collective-permute-done.12.refs_4_
  62.7 1.5 %collective-permute-start.7 = (bf16[3,128,512]{2,1,0:T(8,128)(2,1)S(1)}, bf16[3,128,512]{2,1,0:T(8,128)(2,1)S(1)}, u32[]{:S(2)}, u32[]{:S(2)}) collective-permute-start(bf16[3,128,512]{2,1,0:T(8,128)(2,1)S(1)} %get-tuple-element.86), channel_id=1, source_target_pairs={{0,8},{8,0},{16,24},{24,16},{1,9},{9,1},{17,25},{25,17},{2,10},{10... | collective-permute-start | bytes 1179656 | tf_op jit(solution)/shard_map/ppermute | solution.py:139
  64.2 1.5 %collective-permute-start.8 = (bf16[3,128,512]{2,1,0:T(8,128)(2,1)S(1)}, bf16[3,128,512]{2,1,0:T(8,128)(2,1)S(1)}, u32[]{:S(2)}, u32[]{:S(2)}) collective-permute-start(bf16[3,128,512]{2,1,0:T(8,128)(2,1)S(1)} %get-tuple-element.87), channel_id=1, source_target_pairs={{0,16},{8,24},{16,0},{24,8},{1,17},{9,25},{17,1},{25,9},{2,18},{10... | collective-permute-start | bytes 1179656 | tf_op jit(solution)/shard_map/ppermute | solution.py:139
  65.7 0.6 collective-permute-start.9
  66.3 16.9 %expert_back.4 = (bf16[128,2048]{1,0:T(8,128)(2,1)S(1)}, bf16[128,2048]{1,0:T(8,128)(2,1)S(1)}, bf16[128,2048]{1,0:T(8,128)(2,1)S(1)}, bf16[128,2048]{1,0:T(8,128)(2,1)S(1)}) custom-call(s32[1]{0:T(128)} %bitcast.10.base_ref, bf16[272,2048]{1,0:T(8,128)(2,1)S(1)} %collective-permute-done.4.refs_0_, bf16[272,2048]{1,0:T(8,128)(2,1)S(1)} %collective-permute-done.10.refs_1_, ...), custom_call_target="tpu_custom_call" | custom-call | tf_op jit(solution)/shard_map/expert_back/pallas_call | solution.py:267
  83.3 0.3 collective-permute-done.8.refs_2_
  83.6 0.1 collective-permute-done.5.refs_0_
  83.7 0.4 collective-permute-start.16
  84.3 1.3 collective-permute-done.18
  85.6 0.1 add_convert_fusion.2
  85.7 2.2 %collective-permute-done.17 = bf16[128,2048]{1,0:T(8,128)(2,1)S(1)} collective-permute-done((bf16[128,2048]{1,0:T(8,128)(2,1)S(1)}, bf16[128,2048]{1,0:T(8,128)(2,1)S(1)}, u32[]{:S(2)}, u32[]{:S(2)}) %collective-permute-start.17) | collective-permute-done | bytes 524320 | tf_op jit(solution)/shard_map/ppermute | solution.py:302
  87.9 0.1 add_convert_fusion.3
  88.1 1.5 %collective-permute-start.21 = (bf16[128,2048]{1,0:T(8,128)(2,1)S(1)}, bf16[128,2048]{1,0:T(8,128)(2,1)S(1)}, u32[]{:S(2)}, u32[]{:S(2)}) collective-permute-start(bf16[128,2048]{1,0:T(8,128)(2,1)S(1)} %add_convert_fusion.3), channel_id=1, source_target_pairs={{0,2},{1,3},{2,4},{3,5},{4,6},{5,7},{6,0},{7,1},{8,10},{9,11},{10,... | collective-permute-start | bytes 1572872 | tf_op jit(solution)/shard_map/ppermute | solution.py:305
  89.6 2.4 %collective-permute-start.22 = (bf16[128,2048]{1,0:T(8,128)(2,1)S(1)}, bf16[128,2048]{1,0:T(8,128)(2,1)S(1)}, u32[]{:S(2)}, u32[]{:S(2)}) collective-permute-start(bf16[128,2048]{1,0:T(8,128)(2,1)S(1)} %add_convert_fusion.2), channel_id=1, source_target_pairs={{0,6},{1,7},{2,0},{3,1},{4,2},{5,3},{6,4},{7,5},{8,14},{9,15},{10,... | collective-permute-start | bytes 1572872 | tf_op jit(solution)/shard_map/ppermute | solution.py:305
  92.0 14.8 %expert_back.5 = (bf16[128,2048]{1,0:T(8,128)(2,1)S(1)}, bf16[64,2048]{1,0:T(8,128)(2,1)S(1)}, bf16[64,2048]{1,0:T(8,128)(2,1)S(1)}) custom-call(s32[1]{0:T(128)} %bitcast.10.base_ref, bf16[272,2048]{1,0:T(8,128)(2,1)S(1)} %collective-permute-done.5.refs_0_, bf16[272,2048]{1,0:T(8,128)(2,1)S(1)} %collective-permute-done.16.refs_1_, ...), custom_call_target="tpu_custom_call" | custom-call | flops 30000001024 | bytes 30000000 | tf_op jit(solution)/shard_map/expert_back/pallas_call | solution.py:267
  106.8 0.5 collective-permute-start.20
  107.4 0.9 collective-permute-done.19
  108.3 0.4 collective-permute-done.20
  108.7 5.8 %collective-permute-done.22 = bf16[128,2048]{1,0:T(8,128)(2,1)S(1)} collective-permute-done((bf16[128,2048]{1,0:T(8,128)(2,1)S(1)}, bf16[128,2048]{1,0:T(8,128)(2,1)S(1)}, u32[]{:S(2)}, u32[]{:S(2)}) %collective-permute-start.22) | collective-permute-done | bytes 524320 | tf_op jit(solution)/shard_map/ppermute | solution.py:305
  114.5 0.1 add_convert_fusion.1
  114.6 1.3 collective-permute-start.23
  115.9 1.8 %unpack_groups.1 = (bf16[128,2048]{1,0:T(8,128)(2,1)}, bf16[128,2048]{1,0:T(8,128)(2,1)}, bf16[128,2048]{1,0:T(8,128)(2,1)}) custom-call(s32[4]{0:T(128)S(1)} %dynamic-slice_bitcast_fusion.group_ref, bf16[3,128,512]{2,1,0:T(8,128)(2,1)S(1)} %get-tuple-element.94.refs_0_, bf16[3,128,512]{2,1,0:T(8,128)(2,1)S(1)} %collective-permute-done.7.refs_1_, ...), custom_call_target="tpu_custom_call" | custom-call | tf_op jit(solution)/shard_map/unpack_groups/pallas_call | solution.py:82
  117.7 22.3 %collective-permute-done.23 = bf16[128,2048]{1,0:T(8,128)(2,1)S(1)} collective-permute-done((bf16[128,2048]{1,0:T(8,128)(2,1)S(1)}, bf16[128,2048]{1,0:T(8,128)(2,1)S(1)}, u32[]{:S(2)}, u32[]{:S(2)}) %collective-permute-start.23) | collective-permute-done | bytes 524320 | tf_op jit(solution)/shard_map/ppermute | solution.py:305
  140.0 1.2 fusion
  (30 shorter events, 0.5 us)
Async XLA Ops:
  0.6 1.0 copy-start
  1.7 1.0 copy-start.5
  2.7 0.7 copy-start.6
  3.4 0.7 copy-start.7
  4.1 6.8 %copy-start.1 = (bf16[1,128,2048]{2,1,0:T(8,128)(2,1)S(1)}, bf16[1,128,2048]{2,1,0:T(8,128)(2,1)}, u32[]{:S(2)}) copy-start(bf16[1,128,2048]{2,1,0:T(8,128)(2,1)} %param.13) | copy-start | bytes 1572868
  4.1 6.8 %copy-start.2 = (bf16[1,128,2048]{2,1,0:T(8,128)(2,1)S(1)}, bf16[1,128,2048]{2,1,0:T(8,128)(2,1)}, u32[]{:S(2)}) copy-start(bf16[1,128,2048]{2,1,0:T(8,128)(2,1)} %param.10) | copy-start | bytes 1572868
  5.2 8.5 %collective-permute-start = (bf16[272,2048]{1,0:T(8,128)(2,1)}, bf16[272,2048]{1,0:T(8,128)(2,1)}, u32[]{:S(2)}, u32[]{:S(2)}) collective-permute-start(bf16[272,2048]{1,0:T(8,128)(2,1)} %make_block.1.refs_0_), channel_id=1, source_target_pairs={{0,1},{1,0},{2,3},{3,2},{4,5},{5,4},{6,7},{7,6},{8,9},{9,8},{10,11... | collective-permute-start | bytes 3342344 | tf_op jit(solution)/shard_map/ppermute | solution.py:302
  5.6 29.8 %collective-permute-start.4 = (bf16[272,2048]{1,0:T(8,128)(2,1)}, bf16[272,2048]{1,0:T(8,128)(2,1)S(1)}, u32[]{:S(2)}, u32[]{:S(2)}) collective-permute-start(bf16[272,2048]{1,0:T(8,128)(2,1)} %make_block.1.refs_0_), channel_id=1, source_target_pairs={{0,6},{1,7},{2,0},{3,1},{4,2},{5,3},{6,4},{7,5},{8,14},{9,15},{10,... | collective-permute-start | bytes 3342344 | tf_op jit(solution)/shard_map/ppermute | solution.py:305
  10.2 49.9 %collective-permute-start.6 = (bf16[272,2048]{1,0:T(8,128)(2,1)}, bf16[272,2048]{1,0:T(8,128)(2,1)S(1)}, u32[]{:S(2)}, u32[]{:S(2)}) collective-permute-start(bf16[272,2048]{1,0:T(8,128)(2,1)} %make_block.1.refs_0_), channel_id=1, source_target_pairs={{0,2},{1,3},{2,4},{3,5},{4,6},{5,7},{6,0},{7,1},{8,10},{9,11},{10,... | collective-permute-start | bytes 3342344 | tf_op jit(solution)/shard_map/ppermute | solution.py:305
  10.9 1.0 copy-start.3
  12.0 1.0 copy-start.4
  13.7 21.7 %collective-permute-start.1 = (bf16[4,128,512]{2,1,0:T(8,128)(2,1)S(1)}, bf16[4,128,512]{2,1,0:T(8,128)(2,1)S(1)}, u32[]{:S(2)}, u32[]{:S(2)}) collective-permute-start(bf16[4,128,512]{2,1,0:T(8,128)(2,1)S(1)} %get-tuple-element.67), channel_id=1, source_target_pairs={{0,8},{8,0},{16,24},{24,16},{1,9},{9,1},{17,25},{25,17},{2,10},{10... | collective-permute-start | bytes 1572872 | tf_op jit(solution)/shard_map/ppermute | solution.py:139
  15.3 25.0 %collective-permute-start.2 = (bf16[4,128,512]{2,1,0:T(8,128)(2,1)S(1)}, bf16[4,128,512]{2,1,0:T(8,128)(2,1)S(1)}, u32[]{:S(2)}, u32[]{:S(2)}) collective-permute-start(bf16[4,128,512]{2,1,0:T(8,128)(2,1)S(1)} %get-tuple-element.68), channel_id=1, source_target_pairs={{0,16},{8,24},{16,0},{24,8},{1,17},{9,25},{17,1},{25,9},{2,18},{10... | collective-permute-start | bytes 1572872 | tf_op jit(solution)/shard_map/ppermute | solution.py:139
  16.8 23.5 %collective-permute-start.3 = (bf16[4,128,512]{2,1,0:T(8,128)(2,1)S(1)}, bf16[4,128,512]{2,1,0:T(8,128)(2,1)S(1)}, u32[]{:S(2)}, u32[]{:S(2)}) collective-permute-start(bf16[4,128,512]{2,1,0:T(8,128)(2,1)S(1)} %get-tuple-element.69), channel_id=1, source_target_pairs={{0,24},{8,16},{16,8},{24,0},{1,25},{9,17},{17,9},{25,1},{2,26},{10... | collective-permute-start | bytes 1572872 | tf_op jit(solution)/shard_map/ppermute | solution.py:139
  40.3 26.0 %collective-permute-start.10 = (bf16[272,2048]{1,0:T(8,128)(2,1)S(1)}, bf16[272,2048]{1,0:T(8,128)(2,1)S(1)}, u32[]{:S(2)}, u32[]{:S(2)}) collective-permute-start(bf16[272,2048]{1,0:T(8,128)(2,1)S(1)} %collective-permute-done.4.refs_0_), channel_id=1, source_target_pairs={{0,1},{1,0},{2,3},{3,2},{4,5},{5,4},{6,7},{7,6},{8,9},{9,8},{10,11... | collective-permute-start | bytes 3342344 | tf_op jit(solution)/shard_map/ppermute | solution.py:302
  40.3 43.4 %collective-permute-start.5 = (bf16[272,2048]{1,0:T(8,128)(2,1)S(1)}, bf16[272,2048]{1,0:T(8,128)(2,1)S(1)}, u32[]{:S(2)}, u32[]{:S(2)}) collective-permute-start(bf16[272,2048]{1,0:T(8,128)(2,1)S(1)} %collective-permute-done.4.refs_0_), channel_id=1, source_target_pairs={{0,6},{1,7},{2,0},{3,1},{4,2},{5,3},{6,4},{7,5},{8,14},{9,15},{10,... | collective-permute-start | bytes 3342344 | tf_op jit(solution)/shard_map/ppermute | solution.py:305
  60.2 1.6 %collective-permute-start.11 = (bf16[64,2048]{1,0:T(8,128)(2,1)S(1)}, bf16[64,2048]{1,0:T(8,128)(2,1)S(1)}, u32[]{:S(2)}, u32[]{:S(2)}) collective-permute-start(bf16[64,2048]{1,0:T(8,128)(2,1)S(1)} %get-tuple-element.122), channel_id=1, source_target_pairs={{0,1},{1,0},{2,3},{3,2},{4,5},{5,4},{6,7},{7,6},{8,9},{9,8},{10,11... | collective-permute-start | bytes 786440 | tf_op jit(solution)/shard_map/ppermute | solution.py:302
  60.3 5.4 %collective-permute-start.14 = (bf16[80,2048]{1,0:T(8,128)(2,1)S(1)}, bf16[80,2048]{1,0:T(8,128)(2,1)S(1)}, u32[]{:S(2)}, u32[]{:S(2)}) collective-permute-start(bf16[80,2048]{1,0:T(8,128)(2,1)S(1)} %slice.15), channel_id=1, source_target_pairs={{0,1},{1,0},{2,3},{3,2},{4,5},{5,4},{6,7},{7,6},{8,9},{9,8},{10,11... | collective-permute-start | bytes 983048 | tf_op jit(solution)/shard_map/ppermute | solution.py:302
  60.9 1.8 %collective-permute-start.12 = (bf16[64,2048]{1,0:T(8,128)(2,1)S(1)}, bf16[64,2048]{1,0:T(8,128)(2,1)S(1)}, u32[]{:S(2)}, u32[]{:S(2)}) collective-permute-start(bf16[64,2048]{1,0:T(8,128)(2,1)S(1)} %get-tuple-element.121), channel_id=1, source_target_pairs={{0,1},{1,0},{2,3},{3,2},{4,5},{5,4},{6,7},{7,6},{8,9},{9,8},{10,11... | collective-permute-start | bytes 786440 | tf_op jit(solution)/shard_map/ppermute | solution.py:302
  61.8 2.3 %collective-permute-start.13 = (bf16[64,2048]{1,0:T(8,128)(2,1)S(1)}, bf16[64,2048]{1,0:T(8,128)(2,1)S(1)}, u32[]{:S(2)}, u32[]{:S(2)}) collective-permute-start(bf16[64,2048]{1,0:T(8,128)(2,1)S(1)} %get-tuple-element.120), channel_id=1, source_target_pairs={{0,1},{1,0},{2,3},{3,2},{4,5},{5,4},{6,7},{7,6},{8,9},{9,8},{10,11... | collective-permute-start | bytes 786440 | tf_op jit(solution)/shard_map/ppermute | solution.py:302
  62.7 20.6 %collective-permute-start.7 = (bf16[3,128,512]{2,1,0:T(8,128)(2,1)S(1)}, bf16[3,128,512]{2,1,0:T(8,128)(2,1)S(1)}, u32[]{:S(2)}, u32[]{:S(2)}) collective-permute-start(bf16[3,128,512]{2,1,0:T(8,128)(2,1)S(1)} %get-tuple-element.86), channel_id=1, source_target_pairs={{0,8},{8,0},{16,24},{24,16},{1,9},{9,1},{17,25},{25,17},{2,10},{10... | collective-permute-start | bytes 1179656 | tf_op jit(solution)/shard_map/ppermute | solution.py:139
  64.2 19.4 %collective-permute-start.8 = (bf16[3,128,512]{2,1,0:T(8,128)(2,1)S(1)}, bf16[3,128,512]{2,1,0:T(8,128)(2,1)S(1)}, u32[]{:S(2)}, u32[]{:S(2)}) collective-permute-start(bf16[3,128,512]{2,1,0:T(8,128)(2,1)S(1)} %get-tuple-element.87), channel_id=1, source_target_pairs={{0,16},{8,24},{16,0},{24,8},{1,17},{9,25},{17,1},{25,9},{2,18},{10... | collective-permute-start | bytes 1179656 | tf_op jit(solution)/shard_map/ppermute | solution.py:139
  65.7 17.9 %collective-permute-start.9 = (bf16[3,128,512]{2,1,0:T(8,128)(2,1)S(1)}, bf16[3,128,512]{2,1,0:T(8,128)(2,1)S(1)}, u32[]{:S(2)}, u32[]{:S(2)}) collective-permute-start(bf16[3,128,512]{2,1,0:T(8,128)(2,1)S(1)} %get-tuple-element.88), channel_id=1, source_target_pairs={{0,24},{8,16},{16,8},{24,0},{1,25},{9,17},{17,9},{25,1},{2,26},{10... | collective-permute-start | bytes 1179656 | tf_op jit(solution)/shard_map/ppermute | solution.py:139
  83.7 1.9 %collective-permute-start.18 = (bf16[128,2048]{1,0:T(8,128)(2,1)S(1)}, bf16[128,2048]{1,0:T(8,128)(2,1)S(1)}, u32[]{:S(2)}, u32[]{:S(2)}) collective-permute-start(bf16[128,2048]{1,0:T(8,128)(2,1)S(1)} %get-tuple-element.107), channel_id=1, source_target_pairs={{0,1},{1,0},{2,3},{3,2},{4,5},{5,4},{6,7},{7,6},{8,9},{9,8},{10,11... | collective-permute-start | bytes 1572872 | tf_op jit(solution)/shard_map/ppermute | solution.py:302
  83.7 4.3 %collective-permute-start.16 = (bf16[272,2048]{1,0:T(8,128)(2,1)S(1)}, bf16[272,2048]{1,0:T(8,128)(2,1)S(1)}, u32[]{:S(2)}, u32[]{:S(2)}) collective-permute-start(bf16[272,2048]{1,0:T(8,128)(2,1)S(1)} %collective-permute-done.5.refs_0_), channel_id=1, source_target_pairs={{0,1},{1,0},{2,3},{3,2},{4,5},{5,4},{6,7},{7,6},{8,9},{9,8},{10,11... | collective-permute-start | bytes 3342344 | tf_op jit(solution)/shard_map/ppermute | solution.py:302
  84.2 3.7 %collective-permute-start.17 = (bf16[128,2048]{1,0:T(8,128)(2,1)S(1)}, bf16[128,2048]{1,0:T(8,128)(2,1)S(1)}, u32[]{:S(2)}, u32[]{:S(2)}) collective-permute-start(bf16[128,2048]{1,0:T(8,128)(2,1)S(1)} %get-tuple-element.105), channel_id=1, source_target_pairs={{0,1},{1,0},{2,3},{3,2},{4,5},{5,4},{6,7},{7,6},{8,9},{9,8},{10,11... | collective-permute-start | bytes 1572872 | tf_op jit(solution)/shard_map/ppermute | solution.py:302
  88.1 20.7 %collective-permute-start.21 = (bf16[128,2048]{1,0:T(8,128)(2,1)S(1)}, bf16[128,2048]{1,0:T(8,128)(2,1)S(1)}, u32[]{:S(2)}, u32[]{:S(2)}) collective-permute-start(bf16[128,2048]{1,0:T(8,128)(2,1)S(1)} %add_convert_fusion.3), channel_id=1, source_target_pairs={{0,2},{1,3},{2,4},{3,5},{4,6},{5,7},{6,0},{7,1},{8,10},{9,11},{10,... | collective-permute-start | bytes 1572872 | tf_op jit(solution)/shard_map/ppermute | solution.py:305
  89.6 24.9 %collective-permute-start.22 = (bf16[128,2048]{1,0:T(8,128)(2,1)S(1)}, bf16[128,2048]{1,0:T(8,128)(2,1)S(1)}, u32[]{:S(2)}, u32[]{:S(2)}) collective-permute-start(bf16[128,2048]{1,0:T(8,128)(2,1)S(1)} %add_convert_fusion.2), channel_id=1, source_target_pairs={{0,6},{1,7},{2,0},{3,1},{4,2},{5,3},{6,4},{7,5},{8,14},{9,15},{10,... | collective-permute-start | bytes 1572872 | tf_op jit(solution)/shard_map/ppermute | solution.py:305
  106.7 1.6 %collective-permute-start.19 = (bf16[64,2048]{1,0:T(8,128)(2,1)S(1)}, bf16[64,2048]{1,0:T(8,128)(2,1)S(1)}, u32[]{:S(2)}, u32[]{:S(2)}) collective-permute-start(bf16[64,2048]{1,0:T(8,128)(2,1)S(1)} %get-tuple-element.111), channel_id=1, source_target_pairs={{0,1},{1,0},{2,3},{3,2},{4,5},{5,4},{6,7},{7,6},{8,9},{9,8},{10,11... | collective-permute-start | bytes 786440 | tf_op jit(solution)/shard_map/ppermute | solution.py:302
  106.8 1.9 %collective-permute-start.20 = (bf16[64,2048]{1,0:T(8,128)(2,1)S(1)}, bf16[64,2048]{1,0:T(8,128)(2,1)S(1)}, u32[]{:S(2)}, u32[]{:S(2)}) collective-permute-start(bf16[64,2048]{1,0:T(8,128)(2,1)S(1)} %get-tuple-element.112), channel_id=1, source_target_pairs={{0,1},{1,0},{2,3},{3,2},{4,5},{5,4},{6,7},{7,6},{8,9},{9,8},{10,11... | collective-permute-start | bytes 786440 | tf_op jit(solution)/shard_map/ppermute | solution.py:302
  107.3 10.4 %collective-permute-start.15 = (bf16[128,2048]{1,0:T(8,128)(2,1)S(1)}, bf16[128,2048]{1,0:T(8,128)(2,1)S(1)}, u32[]{:S(2)}, u32[]{:S(2)}) collective-permute-start(bf16[128,2048]{1,0:T(8,128)(2,1)S(1)} %get-tuple-element.102), channel_id=1, source_target_pairs={{0,1},{1,0},{2,3},{3,2},{4,5},{5,4},{6,7},{7,6},{8,9},{9,8},{10,11... | collective-permute-start | bytes 1572872 | tf_op jit(solution)/shard_map/ppermute | solution.py:302
  114.6 25.4 %collective-permute-start.23 = (bf16[128,2048]{1,0:T(8,128)(2,1)S(1)}, bf16[128,2048]{1,0:T(8,128)(2,1)S(1)}, u32[]{:S(2)}, u32[]{:S(2)}) collective-permute-start(bf16[128,2048]{1,0:T(8,128)(2,1)S(1)} %add_convert_fusion.1), channel_id=1, source_target_pairs={{0,4},{1,5},{2,6},{3,7},{4,0},{5,1},{6,2},{7,3},{8,12},{9,13},{10,... | collective-permute-start | bytes 1572872 | tf_op jit(solution)/shard_map/ppermute | solution.py:305

commit v3 on v2

--- a/solution.py
+++ b/solution.py
@@ -20,7 +20,7 @@
 
 
 SMALL = cost(0)
-OWN_COST, HEADS_COST, NEAR_COST, FAR_COST = 30, 5, 0, 30
+OWN_COST, HEADS_COST, LEFT_COST, FAR_COST, RIGHT_COST = 30, 30, 0, 0, 30
 NT = (((1,), (1,)), ((), ()))
 TN = (((0,), (0,)), ((), ()))
 
@@ -141,25 +141,30 @@
     ]
 
 
-def block_kernel(tokens_ref, grads_ref, routes_ref, gates_ref, block_ref):
+def block_kernel(tokens_ref, grads_ref, routes_ref, gates_ref, block_ref, rows_ref):
     bins, width = tokens_ref.shape
-    block_ref[:bins] = tokens_ref[...]
-    block_ref[bins : 2 * bins] = grads_ref[...]
     rest = gates_ref[...]
     pieces = [(routes_ref[...] + 1).astype(jnp.float32)]
     for _ in range(3):
         piece = rest.astype(jnp.bfloat16).astype(jnp.float32)
         rest = rest - piece
         pieces.append(piece)
-    block_ref[2 * bins :, bins:] = jnp.zeros((NOTES, width - bins), jnp.bfloat16)
-    block_ref[2 * bins :, :bins] = jnp.concatenate(pieces, axis=0).astype(jnp.bfloat16)
+    notes = jnp.concatenate(pieces, axis=0).astype(jnp.bfloat16)
+    for out in (block_ref, rows_ref):
+        out[:bins] = tokens_ref[...]
+        out[bins : bins + NOTES, bins:] = jnp.zeros((NOTES, width - bins), jnp.bfloat16)
+        out[bins : bins + NOTES, :bins] = notes
+    block_ref[bins + NOTES :] = grads_ref[...]
 
 
 def make_block(tokens, grads, routes, gates):
     bins, width = tokens.shape
     return pl.pallas_call(
         block_kernel,
-        out_shape=jax.ShapeDtypeStruct((2 * bins + NOTES, width), jnp.bfloat16),
+        out_shape=[
+            jax.ShapeDtypeStruct((2 * bins + NOTES, width), jnp.bfloat16),
+            jax.ShapeDtypeStruct((bins + NOTES, width), jnp.bfloat16),
+        ],
         compiler_params=pltpu.CompilerParams(vmem_limit_bytes=VMEM_BYTES),
         cost_estimate=SMALL,
         name="make_block",
@@ -205,7 +210,7 @@
         base = base_ref[0].astype(jnp.float32)
         gates = [jnp.zeros((slots, 1), jnp.float32)] * experts
         for source, block in enumerate(blocks):
-            notes = block[2 * bins :, :bins].astype(jnp.float32)
+            notes = block[bins : bins + NOTES, :bins].astype(jnp.float32)
             named = notes[:top] - base
             weights = notes[top : 2 * top] + notes[2 * top : 3 * top] + notes[3 * top : 4 * top]
             hits = [(named == float(local + 1)).astype(jnp.float32) for local in range(experts)]
@@ -225,7 +230,7 @@
         picks = pick_ref[...]
         tokens = jnp.concatenate([block[:bins] for block in blocks], axis=0)
         token_rows[...] = dot_nn(picks, tokens).astype(jnp.bfloat16)
-        grads = jnp.concatenate([block[bins : 2 * bins] for block in blocks], axis=0)
+        grads = jnp.concatenate([block[bins + NOTES :] for block in blocks], axis=0)
         gate_column = jnp.concatenate(gates, axis=0)
         gated_rows[...] = (gate_column * dot_nn(picks, grads)).astype(jnp.bfloat16)
 
@@ -306,30 +311,22 @@
             block, "exp", [(i, (i + 2 * step) % members) for i in range(members)]
         )
 
-    def pair(block):
-        return [[block], [swap(block)]]
-
-    def pair_in_pieces(block):
-        cuts = [0, bins // 2, bins, bins + bins // 2, block.shape[0]]
-        return [[block], [swap(block[a:b]) for a, b in zip(cuts, cuts[1:])]]
+    def pair(*pieces):
+        return [list(pieces), [swap(piece) for piece in pieces]]
 
     def work(blocks, units, pieces=1):
-        outs = expert_back(base, blocks, up_weight, down_weight, bins, top, units, pieces)
-        return outs[: len(blocks) // 2], outs[len(blocks) // 2 :]
-
-    def both_cores(kept, given):
-        pieces = len(given) // len(kept)
-        return [
-            (
-                own.astype(jnp.float32)
-                + jnp.concatenate(given[place * pieces : (place + 1) * pieces], axis=0)
-            ).astype(jnp.bfloat16)
-            for place, own in enumerate(kept)
-        ]
+        kept, *give = expert_back(base, blocks, up_weight, down_weight, bins, top, units, pieces)
+        return kept, give
+
+    def add_up(*members):
+        return functools.reduce(jnp.add, [member.astype(jnp.float32) for member in members])
+
+    def joined(pieces):
+        return pieces[0] if len(pieces) == 1 else jnp.concatenate(pieces, axis=0)
 
     barrier = lax.optimization_barrier
-    own = make_block(moe_input[0], out_grad[0], routes[0], route_gates[0])
-    right, left = hop(own, 1), hop(own, -1)
+    own, own_rows = make_block(moe_input[0], out_grad[0], routes[0], route_gates[0])
+    left, right_rows = hop(own, -1), hop(own_rows, 1)
     own_pair = pair(own)
     table = [[group ^ place for place in range(groups)] for group in range(groups)]
     group_ids = jnp.asarray(table, jnp.int32)[lax.axis_index("ctx")]
@@ -339,39 +336,40 @@
     heads = exchange(packed)
     kept, give = work(own_pair, OWN_COST)
     heads, kept, give, left = barrier((heads, kept, give, left))
+    total = add_up(kept, joined([swap(piece) for piece in give]))
+    left_pair, right_grads = pair(left), out_grad[0]
     results = heads_back(heads)
-    right, kept, give, results = barrier((right, kept, give, results))
-    total = both_cores(kept, [swap(part) for part in give])[0].astype(jnp.float32)
+    left_pair, results = barrier((left_pair, results))
     results = exchange(results)
-    steps, parts, arrived = [], [], []
+    left_sums = []
     for d in range(1, half):
-        blocks = pair(left) + pair_in_pieces(right)
-        following = [hop(left, -1)]
-        if d + 1 < half:
-            following.append(hop(right, 1))
-        if d > 1:
-            blocks, sums = barrier((blocks, sums))
-            arrived = [hop(part, step) for part, step in zip(sums, steps)]
-        kept, give = work(blocks, NEAR_COST)
-        following, arrived, results, kept, give = barrier(
-            (following, arrived, results, kept, give)
-        )
-        parts += arrived
-        sums = both_cores(kept, [swap(part) for part in give])
-        left, right = (following + [None])[:2]
-        steps = [d, -d]
-    blocks, sums = barrier((pair(left), sums))
-    arrived = [hop(part, step) for part, step in zip(sums, steps)]
-    kept, give = work(blocks, FAR_COST, 2)
-    given = [swap(part) for part in give]
-    kept, given, arrived = barrier((kept, given, arrived))
-    parts += arrived
-    for part in parts:
-        total = total + part
-    far = hop(both_cores(kept, given)[0], half)
+        left = hop(left, -1)
+        kept, give = work(left_pair, LEFT_COST)
+        left, right_rows, results, kept, give = barrier((left, right_rows, results, kept, give))
+        left_sums.append(add_up(kept, joined([swap(piece) for piece in give])))
+        left_pair = pair(left)
+    carried = None
+    for sums in reversed(left_sums):
+        if carried is not None:
+            sums = add_up(sums, carried)
+        carried = hop(sums.astype(jnp.bfloat16), 1)
+    rights = [(right_rows, hop(right_grads, 1))]
+    for d in range(2, half):
+        rights.append(tuple(hop(member, 1) for member in rights[-1]))
+    kept, give = work(left_pair, FAR_COST)
+    carried, rights, kept, give = barrier((carried, rights, kept, give))
+    total = add_up(total, carried)
+    carried = add_up(kept, joined([swap(piece) for piece in give]))
+    for right in reversed(rights):
+        carried = hop(carried.astype(jnp.bfloat16), -1)
+        kept, give = work(pair(*right), RIGHT_COST, 2)
+        given = [swap(piece) for piece in give]
+        kept, given, carried = barrier((kept, given, carried))
+        carried = add_up(kept, joined(given), carried)
+    carried = hop(carried.astype(jnp.bfloat16), -1)
     outs = unpack_groups(group_ids, results)
-    total = total + far
-    return tuple(out[None] for out in outs) + (total.astype(jnp.bfloat16)[None],)
+    total = add_up(total, carried).astype(jnp.bfloat16)
+    return tuple(out[None] for out in outs) + (total[None],)
 
 
 def solution(mesh):

time: 142 us -> 138 us (0.972)
  waiting for transfers between devices: 52 us -> 36.7 us
  Pallas kernels: 57.5 us -> 71.2 us
  starting transfers between devices: 23 us -> 20.8 us
    ppermute x6 -> x7, waiting for transfers between devices: 40.5 us -> 26.3 us  [hop(): lax.ppermute(block, 'exp', [(i, (i + 2 * step) % members) for i in range(...]
    pallas_call x3 -> x4, Pallas kernels: 47.5 us -> 61.5 us  [expert_back(): pl.pallas_call(functools.partial(expert_kernel, layout, pieces, top), out...]
    ppermute x6 -> x7, starting transfers between devices: 13.3 us -> 11.5 us  [hop(): lax.ppermute(block, 'exp', [(i, (i + 2 * step) % members) for i in range(...]
    ppermute x12 -> x10, waiting for transfers between devices: 6.43 us -> 5.28 us  [swap(): return lax.ppermute(block, 'exp', [(i, i ^ 1) for i in range(members)])]
  transfers between devices with their start and end apart: 24 -> 23, of which waited for: 13 -> 10; matrix products, arithmetic and copies ran while one was open for 1% -> 1% of each run, Pallas kernels for 40% -> 51%
where the time goes in v3:
time: 138 us; the launch traced here: 137 us
  Pallas kernels  71.2 us (52%)
  waiting for transfers between devices  36.7 us (27%)
  starting transfers between devices  20.8 us (15%)
  local copies, waits for them, and re-layouts  6.21 us (4%)
  other arithmetic  1.62 us (1%)
    pallas_call x4, Pallas kernels, expert_back(): pl.pallas_call(functools.partial(expert_kernel, layout, pieces, top), out...  61.5 us
    ppermute x7, waiting for transfers between devices, hop(): lax.ppermute(block, 'exp', [(i, (i + 2 * step) % members) for i in range(...  26.3 us
    ppermute x7, starting transfers between devices, hop(): lax.ppermute(block, 'exp', [(i, (i + 2 * step) % members) for i in range(...  11.5 us
    ppermute x6, starting transfers between devices, exchange(): lax.ppermute(blocks[place], 'ctx', [(i, i ^ place) for i in range(groups)])  7.11 us
    pallas_call x1, Pallas kernels, heads_back(): pl.pallas_call(heads_kernel, grid=(heads,), out_shape=[jax.ShapeDtypeStru...  6.37 us
    unnamed x16, local copies, waits for them, and re-layouts  5.52 us
    ppermute x10, waiting for transfers between devices, swap(): return lax.ppermute(block, 'exp', [(i, i ^ 1) for i in range(members)])  5.28 us
    ppermute x6, waiting for transfers between devices, exchange(): lax.ppermute(blocks[place], 'ctx', [(i, i ^ place) for i in range(groups)])  5.15 us
  transfers between devices with their start and end apart: 23, of which 10 were waited for; matrix products, arithmetic and copies ran while one was open for 1% of the time, Pallas kernels for 51%

profile of v3, /device:TPU:0, one launch (start us, length us, event | category | flops | bytes accessed | tf_op | source)
XLA Modules:
  0.0 137.4 jit_solution(17165159564680091390)
XLA Ops:
  0.6 1.0 copy-done
  1.7 1.0 copy-done.5
  2.7 0.7 copy-done.6
  3.4 0.7 copy-done.7
  4.1 0.9 make_block.1
  5.0 0.5 collective-permute-start
  5.5 4.6 %collective-permute-start.4 = (bf16[272,2048]{1,0:T(8,128)(2,1)S(1)}, bf16[272,2048]{1,0:T(8,128)(2,1)S(1)}, u32[]{:S(2)}, u32[]{:S(2)}) collective-permute-start(bf16[272,2048]{1,0:T(8,128)(2,1)S(1)} %get-tuple-element.71.refs_0_), channel_id=1, source_target_pairs={{0,6},{1,7},{2,0},{3,1},{4,2},{5,3},{6,4},{7,5},{8,14},{9,15},{10,... | collective-permute-start | bytes 3342344 | tf_op jit(solution)/shard_map/ppermute | solution.py:310
  10.1 0.7 dynamic-slice_bitcast_fusion.group_ref
  10.8 1.0 copy-done.3
  11.8 1.0 copy-done.4
  12.8 0.7 pack_groups.1
  13.6 1.6 %collective-permute-start.1 = (bf16[4,128,512]{2,1,0:T(8,128)(2,1)S(1)}, bf16[4,128,512]{2,1,0:T(8,128)(2,1)S(1)}, u32[]{:S(2)}, u32[]{:S(2)}) collective-permute-start(bf16[4,128,512]{2,1,0:T(8,128)(2,1)S(1)} %get-tuple-element.68), channel_id=1, source_target_pairs={{0,8},{8,0},{16,24},{24,16},{1,9},{9,1},{17,25},{25,17},{2,10},{10... | collective-permute-start | bytes 1572872 | tf_op jit(solution)/shard_map/ppermute | solution.py:139
  15.1 1.5 %collective-permute-start.2 = (bf16[4,128,512]{2,1,0:T(8,128)(2,1)S(1)}, bf16[4,128,512]{2,1,0:T(8,128)(2,1)S(1)}, u32[]{:S(2)}, u32[]{:S(2)}) collective-permute-start(bf16[4,128,512]{2,1,0:T(8,128)(2,1)S(1)} %get-tuple-element.69), channel_id=1, source_target_pairs={{0,16},{8,24},{16,0},{24,8},{1,17},{9,25},{17,1},{25,9},{2,18},{10... | collective-permute-start | bytes 1572872 | tf_op jit(solution)/shard_map/ppermute | solution.py:139
  16.6 0.5 collective-permute-start.3
  17.1 16.0 %expert_back.4 = (bf16[128,2048]{1,0:T(8,128)(2,1)S(1)}, bf16[128,2048]{1,0:T(8,128)(2,1)S(1)}) custom-call(s32[1]{0:T(128)} %bitcast.10.base_ref, bf16[272,2048]{1,0:T(8,128)(2,1)S(1)} %get-tuple-element.71.refs_0_, bf16[272,2048]{1,0:T(8,128)(2,1)} %collective-permute-done.refs_1_, bf16[4,2048,768]{2,1,0:T(8,128)(2,1)} %refs_4_.1, ...), custom_call_target="tpu_custom_call" | custom-call | flops 30000001024 | bytes 30000000 | tf_op jit(solution)/shard_map/expert_back/pallas_call | solution.py:272
  33.1 1.9 %collective-permute-done.4.refs_0_ = bf16[272,2048]{1,0:T(8,128)(2,1)S(1)} collective-permute-done((bf16[272,2048]{1,0:T(8,128)(2,1)S(1)}, bf16[272,2048]{1,0:T(8,128)(2,1)S(1)}, u32[]{:S(2)}, u32[]{:S(2)}) %collective-permute-start.4) | collective-permute-done | bytes 1114144 | tf_op jit(solution)/shard_map/ppermute | solution.py:310
  35.0 5.1 %collective-permute-done.2.refs_2_ = bf16[4,128,512]{2,1,0:T(8,128)(2,1)S(1)} collective-permute-done((bf16[4,128,512]{2,1,0:T(8,128)(2,1)S(1)}, bf16[4,128,512]{2,1,0:T(8,128)(2,1)S(1)}, u32[]{:S(2)}, u32[]{:S(2)}) %collective-permute-start.2) | collective-permute-done | bytes 524320 | tf_op jit(solution)/shard_map/ppermute | solution.py:139
  40.1 3.5 %collective-permute-start.5 = (bf16[272,2048]{1,0:T(8,128)(2,1)S(1)}, bf16[272,2048]{1,0:T(8,128)(2,1)S(1)}, u32[]{:S(2)}, u32[]{:S(2)}) collective-permute-start(bf16[272,2048]{1,0:T(8,128)(2,1)S(1)} %collective-permute-done.4.refs_0_), channel_id=1, source_target_pairs={{0,6},{1,7},{2,0},{3,1},{4,2},{5,3},{6,4},{7,5},{8,14},{9,15},{10,... | collective-permute-start | bytes 3342344 | tf_op jit(solution)/shard_map/ppermute | solution.py:310
  43.7 6.4 %heads_back.1 = (bf16[3,128,512]{2,1,0:T(8,128)(2,1)S(1)}, bf16[3,128,512]{2,1,0:T(8,128)(2,1)S(1)}, bf16[3,128,512]{2,1,0:T(8,128)(2,1)S(1)}, bf16[3,128,512]{2,1,0:T(8,128)(2,1)S(1)}) custom-call(bf16[4,128,512]{2,1,0:T(8,128)(2,1)S(1)} %get-tuple-element.77.refs_0_, bf16[4,128,512]{2,1,0:T(8,128)(2,1)S(1)} %collective-permute-done.1.refs_1_, ...), custom_call_target="tpu_custom_call" | custom-call | flops 30000001024 | bytes 30000000 | tf_op jit(solution)/shard_map/heads_back/pallas_call | solution.py:124
  50.1 1.6 %collective-permute-start.10 = (bf16[3,128,512]{2,1,0:T(8,128)(2,1)S(1)}, bf16[3,128,512]{2,1,0:T(8,128)(2,1)S(1)}, u32[]{:S(2)}, u32[]{:S(2)}) collective-permute-start(bf16[3,128,512]{2,1,0:T(8,128)(2,1)S(1)} %get-tuple-element.88), channel_id=1, source_target_pairs={{0,24},{8,16},{16,8},{24,0},{1,25},{9,17},{17,9},{25,1},{2,26},{10... | collective-permute-start | bytes 1179656 | tf_op jit(solution)/shard_map/ppermute | solution.py:139
  51.6 1.5 %collective-permute-start.8 = (bf16[3,128,512]{2,1,0:T(8,128)(2,1)S(1)}, bf16[3,128,512]{2,1,0:T(8,128)(2,1)S(1)}, u32[]{:S(2)}, u32[]{:S(2)}) collective-permute-start(bf16[3,128,512]{2,1,0:T(8,128)(2,1)S(1)} %get-tuple-element.86), channel_id=1, source_target_pairs={{0,8},{8,0},{16,24},{24,16},{1,9},{9,1},{17,25},{25,17},{2,10},{10... | collective-permute-start | bytes 1179656 | tf_op jit(solution)/shard_map/ppermute | solution.py:139
  53.1 0.5 collective-permute-start.9
  53.6 14.8 %expert_back.5 = (bf16[128,2048]{1,0:T(8,128)(2,1)S(1)}, bf16[128,2048]{1,0:T(8,128)(2,1)S(1)}) custom-call(s32[1]{0:T(128)} %bitcast.10.base_ref, bf16[272,2048]{1,0:T(8,128)(2,1)S(1)} %collective-permute-done.4.refs_0_, bf16[272,2048]{1,0:T(8,128)(2,1)S(1)} %collective-permute-done.7.refs_1_, bf16[4,2048,768]{2,1,0:T(8,128)(2,1)} %refs_4_.1, ...), custom_call_target="tpu_custom_call" | custom-call | tf_op jit(solution)/shard_map/expert_back/pallas_call | solution.py:272
  68.4 3.6 %collective-permute-done.5.refs_0_ = bf16[272,2048]{1,0:T(8,128)(2,1)S(1)} collective-permute-done((bf16[272,2048]{1,0:T(8,128)(2,1)S(1)}, bf16[272,2048]{1,0:T(8,128)(2,1)S(1)}, u32[]{:S(2)}, u32[]{:S(2)}) %collective-permute-start.5) | collective-permute-done | bytes 1114144 | tf_op jit(solution)/shard_map/ppermute | solution.py:310
  72.1 0.1 collective-permute-start.12
  72.2 0.4 collective-permute-start.15
  72.7 0.5 collective-permute-start.14
  73.1 0.9 collective-permute-done.12
  74.1 0.1 add_convert_fusion.3
  74.2 0.5 collective-permute-start.13
  74.7 0.9 collective-permute-done.15.refs_1_
  75.6 14.8 %expert_back.6 = (bf16[128,2048]{1,0:T(8,128)(2,1)S(1)}, bf16[128,2048]{1,0:T(8,128)(2,1)S(1)}) custom-call(s32[1]{0:T(128)} %bitcast.10.base_ref, bf16[272,2048]{1,0:T(8,128)(2,1)S(1)} %collective-permute-done.5.refs_0_, bf16[272,2048]{1,0:T(8,128)(2,1)S(1)} %collective-permute-done.15.refs_1_, bf16[4,2048,768]{2,1,0:T(8,128)(2,1)} %refs_4_.1, ...), custom_call_target="tpu_custom_call" | custom-call | tf_op jit(solution)/shard_map/expert_back/pallas_call | solution.py:272
  90.5 9.1 %collective-permute-done.13 = bf16[128,2048]{1,0:T(8,128)(2,1)S(1)} collective-permute-done((bf16[128,2048]{1,0:T(8,128)(2,1)S(1)}, bf16[128,2048]{1,0:T(8,128)(2,1)S(1)}, u32[]{:S(2)}, u32[]{:S(2)}) %collective-permute-start.13) | collective-permute-done | bytes 524320 | tf_op jit(solution)/shard_map/ppermute | solution.py:310
  99.6 0.5 collective-permute-start.16
  100.1 2.1 %collective-permute-done.20 = bf16[128,2048]{1,0:T(8,128)(2,1)S(1)} collective-permute-done((bf16[128,2048]{1,0:T(8,128)(2,1)S(1)}, bf16[128,2048]{1,0:T(8,128)(2,1)S(1)}, u32[]{:S(2)}, u32[]{:S(2)}) %collective-permute-start.20) | collective-permute-done | bytes 524320 | tf_op jit(solution)/shard_map/ppermute | solution.py:307
  102.2 0.1 add_convert_fusion.2
  102.3 1.8 %collective-permute-start.21 = (bf16[128,2048]{1,0:T(8,128)(2,1)S(1)}, bf16[128,2048]{1,0:T(8,128)(2,1)S(1)}, u32[]{:S(2)}, u32[]{:S(2)}) collective-permute-start(bf16[128,2048]{1,0:T(8,128)(2,1)S(1)} %add_convert_fusion.2), channel_id=1, source_target_pairs={{0,6},{1,7},{2,0},{3,1},{4,2},{5,3},{6,4},{7,5},{8,14},{9,15},{10,... | collective-permute-start | bytes 1572872 | tf_op jit(solution)/shard_map/ppermute | solution.py:310
  104.1 15.9 %expert_back.7 = (bf16[128,2048]{1,0:T(8,128)(2,1)S(1)}, bf16[64,2048]{1,0:T(8,128)(2,1)S(1)}, bf16[64,2048]{1,0:T(8,128)(2,1)S(1)}) custom-call(s32[1]{0:T(128)} %bitcast.10.base_ref, bf16[144,2048]{1,0:T(8,128)(2,1)} %collective-permute-done.6.refs_0_, bf16[128,2048]{1,0:T(8,128)(2,1)S(1)} %collective-permute-done.14.refs_1_, ...), custom_call_target="tpu_custom_call" | custom-call | flops 30000001024 | bytes 30000000 | tf_op jit(solution)/shard_map/expert_back/pallas_call | solution.py:272
  120.0 0.1 collective-permute-start.18
  120.1 0.5 collective-permute-start.19
  120.6 0.1 collective-permute-start.11
  120.7 0.9 collective-permute-done.18
  121.6 0.4 collective-permute-done.19
  122.0 0.2 add_convert_fusion.1
  122.2 0.6 collective-permute-start.22
  122.8 1.8 %unpack_groups.1 = (bf16[128,2048]{1,0:T(8,128)(2,1)}, bf16[128,2048]{1,0:T(8,128)(2,1)}, bf16[128,2048]{1,0:T(8,128)(2,1)}) custom-call(s32[4]{0:T(128)S(1)} %dynamic-slice_bitcast_fusion.group_ref, bf16[3,128,512]{2,1,0:T(8,128)(2,1)S(1)} %get-tuple-element.93.refs_0_, bf16[3,128,512]{2,1,0:T(8,128)(2,1)S(1)} %collective-permute-done.8.refs_1_, ...), custom_call_target="tpu_custom_call" | custom-call | tf_op jit(solution)/shard_map/unpack_groups/pallas_call | solution.py:82
  124.6 11.7 %collective-permute-done.22 = bf16[128,2048]{1,0:T(8,128)(2,1)S(1)} collective-permute-done((bf16[128,2048]{1,0:T(8,128)(2,1)S(1)}, bf16[128,2048]{1,0:T(8,128)(2,1)S(1)}, u32[]{:S(2)}, u32[]{:S(2)}) %collective-permute-start.22) | collective-permute-done | bytes 524320 | tf_op jit(solution)/shard_map/ppermute | solution.py:310
  136.3 1.1 fusion
  (27 shorter events, 0.1 us)
Async XLA Ops:
  0.6 1.0 copy-start
  1.7 1.0 copy-start.5
  2.7 0.7 copy-start.6
  3.4 0.7 copy-start.7
  4.1 6.7 %copy-start.1 = (bf16[1,128,2048]{2,1,0:T(8,128)(2,1)S(1)}, bf16[1,128,2048]{2,1,0:T(8,128)(2,1)}, u32[]{:S(2)}) copy-start(bf16[1,128,2048]{2,1,0:T(8,128)(2,1)} %param.13) | copy-start | bytes 1572868
  4.1 6.7 %copy-start.2 = (bf16[1,128,2048]{2,1,0:T(8,128)(2,1)S(1)}, bf16[1,128,2048]{2,1,0:T(8,128)(2,1)}, u32[]{:S(2)}) copy-start(bf16[1,128,2048]{2,1,0:T(8,128)(2,1)} %param.10) | copy-start | bytes 1572868
  5.0 8.5 %collective-permute-start = (bf16[272,2048]{1,0:T(8,128)(2,1)S(1)}, bf16[272,2048]{1,0:T(8,128)(2,1)}, u32[]{:S(2)}, u32[]{:S(2)}) collective-permute-start(bf16[272,2048]{1,0:T(8,128)(2,1)S(1)} %get-tuple-element.71.refs_0_), channel_id=1, source_target_pairs={{0,1},{1,0},{2,3},{3,2},{4,5},{5,4},{6,7},{7,6},{8,9},{9,8},{10,11... | collective-permute-start | bytes 3342344 | tf_op jit(solution)/shard_map/ppermute | solution.py:307
  5.5 29.5 %collective-permute-start.4 = (bf16[272,2048]{1,0:T(8,128)(2,1)S(1)}, bf16[272,2048]{1,0:T(8,128)(2,1)S(1)}, u32[]{:S(2)}, u32[]{:S(2)}) collective-permute-start(bf16[272,2048]{1,0:T(8,128)(2,1)S(1)} %get-tuple-element.71.refs_0_), channel_id=1, source_target_pairs={{0,6},{1,7},{2,0},{3,1},{4,2},{5,3},{6,4},{7,5},{8,14},{9,15},{10,... | collective-permute-start | bytes 3342344 | tf_op jit(solution)/shard_map/ppermute | solution.py:310
  10.1 58.4 %collective-permute-start.6 = (bf16[144,2048]{1,0:T(8,128)(2,1)}, bf16[144,2048]{1,0:T(8,128)(2,1)}, u32[]{:S(2)}, u32[]{:S(2)}) collective-permute-start(bf16[144,2048]{1,0:T(8,128)(2,1)} %get-tuple-element.76), channel_id=1, source_target_pairs={{0,2},{1,3},{2,4},{3,5},{4,6},{5,7},{6,0},{7,1},{8,10},{9,11},{10,... | collective-permute-start | bytes 1769480 | tf_op jit(solution)/shard_map/ppermute | solution.py:310
  10.8 1.0 copy-start.3
  11.8 1.0 copy-start.4
  13.6 21.4 %collective-permute-start.1 = (bf16[4,128,512]{2,1,0:T(8,128)(2,1)S(1)}, bf16[4,128,512]{2,1,0:T(8,128)(2,1)S(1)}, u32[]{:S(2)}, u32[]{:S(2)}) collective-permute-start(bf16[4,128,512]{2,1,0:T(8,128)(2,1)S(1)} %get-tuple-element.68), channel_id=1, source_target_pairs={{0,8},{8,0},{16,24},{24,16},{1,9},{9,1},{17,25},{25,17},{2,10},{10... | collective-permute-start | bytes 1572872 | tf_op jit(solution)/shard_map/ppermute | solution.py:139
  15.1 25.0 %collective-permute-start.2 = (bf16[4,128,512]{2,1,0:T(8,128)(2,1)S(1)}, bf16[4,128,512]{2,1,0:T(8,128)(2,1)S(1)}, u32[]{:S(2)}, u32[]{:S(2)}) collective-permute-start(bf16[4,128,512]{2,1,0:T(8,128)(2,1)S(1)} %get-tuple-element.69), channel_id=1, source_target_pairs={{0,16},{8,24},{16,0},{24,8},{1,17},{9,25},{17,1},{25,9},{2,18},{10... | collective-permute-start | bytes 1572872 | tf_op jit(solution)/shard_map/ppermute | solution.py:139
  16.6 23.5 %collective-permute-start.3 = (bf16[4,128,512]{2,1,0:T(8,128)(2,1)S(1)}, bf16[4,128,512]{2,1,0:T(8,128)(2,1)S(1)}, u32[]{:S(2)}, u32[]{:S(2)}) collective-permute-start(bf16[4,128,512]{2,1,0:T(8,128)(2,1)S(1)} %get-tuple-element.70), channel_id=1, source_target_pairs={{0,24},{8,16},{16,8},{24,0},{1,25},{9,17},{17,9},{25,1},{2,26},{10... | collective-permute-start | bytes 1572872 | tf_op jit(solution)/shard_map/ppermute | solution.py:139
  40.1 9.9 %collective-permute-start.7 = (bf16[272,2048]{1,0:T(8,128)(2,1)S(1)}, bf16[272,2048]{1,0:T(8,128)(2,1)S(1)}, u32[]{:S(2)}, u32[]{:S(2)}) collective-permute-start(bf16[272,2048]{1,0:T(8,128)(2,1)S(1)} %collective-permute-done.4.refs_0_), channel_id=1, source_target_pairs={{0,1},{1,0},{2,3},{3,2},{4,5},{5,4},{6,7},{7,6},{8,9},{9,8},{10,11... | collective-permute-start | bytes 3342344 | tf_op jit(solution)/shard_map/ppermute | solution.py:307
  40.1 31.9 %collective-permute-start.5 = (bf16[272,2048]{1,0:T(8,128)(2,1)S(1)}, bf16[272,2048]{1,0:T(8,128)(2,1)S(1)}, u32[]{:S(2)}, u32[]{:S(2)}) collective-permute-start(bf16[272,2048]{1,0:T(8,128)(2,1)S(1)} %collective-permute-done.4.refs_0_), channel_id=1, source_target_pairs={{0,6},{1,7},{2,0},{3,1},{4,2},{5,3},{6,4},{7,5},{8,14},{9,15},{10,... | collective-permute-start | bytes 3342344 | tf_op jit(solution)/shard_map/ppermute | solution.py:310
  50.1 22.0 %collective-permute-start.10 = (bf16[3,128,512]{2,1,0:T(8,128)(2,1)S(1)}, bf16[3,128,512]{2,1,0:T(8,128)(2,1)S(1)}, u32[]{:S(2)}, u32[]{:S(2)}) collective-permute-start(bf16[3,128,512]{2,1,0:T(8,128)(2,1)S(1)} %get-tuple-element.88), channel_id=1, source_target_pairs={{0,24},{8,16},{16,8},{24,0},{1,25},{9,17},{17,9},{25,1},{2,26},{10... | collective-permute-start | bytes 1179656 | tf_op jit(solution)/shard_map/ppermute | solution.py:139
  51.6 20.4 %collective-permute-start.8 = (bf16[3,128,512]{2,1,0:T(8,128)(2,1)S(1)}, bf16[3,128,512]{2,1,0:T(8,128)(2,1)S(1)}, u32[]{:S(2)}, u32[]{:S(2)}) collective-permute-start(bf16[3,128,512]{2,1,0:T(8,128)(2,1)S(1)} %get-tuple-element.86), channel_id=1, source_target_pairs={{0,8},{8,0},{16,24},{24,16},{1,9},{9,1},{17,25},{25,17},{2,10},{10... | collective-permute-start | bytes 1179656 | tf_op jit(solution)/shard_map/ppermute | solution.py:139
  53.1 19.0 %collective-permute-start.9 = (bf16[3,128,512]{2,1,0:T(8,128)(2,1)S(1)}, bf16[3,128,512]{2,1,0:T(8,128)(2,1)S(1)}, u32[]{:S(2)}, u32[]{:S(2)}) collective-permute-start(bf16[3,128,512]{2,1,0:T(8,128)(2,1)S(1)} %get-tuple-element.87), channel_id=1, source_target_pairs={{0,16},{8,24},{16,0},{24,8},{1,17},{9,25},{17,1},{25,9},{2,18},{10... | collective-permute-start | bytes 1179656 | tf_op jit(solution)/shard_map/ppermute | solution.py:139
  72.1 2.0 %collective-permute-start.12 = (bf16[128,2048]{1,0:T(8,128)(2,1)S(1)}, bf16[128,2048]{1,0:T(8,128)(2,1)S(1)}, u32[]{:S(2)}, u32[]{:S(2)}) collective-permute-start(bf16[128,2048]{1,0:T(8,128)(2,1)S(1)} %get-tuple-element.103), channel_id=1, source_target_pairs={{0,1},{1,0},{2,3},{3,2},{4,5},{5,4},{6,7},{7,6},{8,9},{9,8},{10,11... | collective-permute-start | bytes 1572872 | tf_op jit(solution)/shard_map/ppermute | solution.py:307
  72.2 3.4 %collective-permute-start.15 = (bf16[272,2048]{1,0:T(8,128)(2,1)S(1)}, bf16[272,2048]{1,0:T(8,128)(2,1)S(1)}, u32[]{:S(2)}, u32[]{:S(2)}) collective-permute-start(bf16[272,2048]{1,0:T(8,128)(2,1)S(1)} %collective-permute-done.5.refs_0_), channel_id=1, source_target_pairs={{0,1},{1,0},{2,3},{3,2},{4,5},{5,4},{6,7},{7,6},{8,9},{9,8},{10,11... | collective-permute-start | bytes 3342344 | tf_op jit(solution)/shard_map/ppermute | solution.py:307
  72.7 17.8 %collective-permute-start.14 = (bf16[128,2048]{1,0:T(8,128)(2,1)S(1)}, bf16[128,2048]{1,0:T(8,128)(2,1)S(1)}, u32[]{:S(2)}, u32[]{:S(2)}) collective-permute-start(bf16[128,2048]{1,0:T(8,128)(2,1)S(1)} %bitcast.21), channel_id=1, source_target_pairs={{0,2},{1,3},{2,4},{3,5},{4,6},{5,7},{6,0},{7,1},{8,10},{9,11},{10,... | collective-permute-start | bytes 1572872 | tf_op jit(solution)/shard_map/ppermute | solution.py:310
  74.2 25.4 %collective-permute-start.13 = (bf16[128,2048]{1,0:T(8,128)(2,1)S(1)}, bf16[128,2048]{1,0:T(8,128)(2,1)S(1)}, u32[]{:S(2)}, u32[]{:S(2)}) collective-permute-start(bf16[128,2048]{1,0:T(8,128)(2,1)S(1)} %add_convert_fusion.3), channel_id=1, source_target_pairs={{0,2},{1,3},{2,4},{3,5},{4,6},{5,7},{6,0},{7,1},{8,10},{9,11},{10,... | collective-permute-start | bytes 1572872 | tf_op jit(solution)/shard_map/ppermute | solution.py:310
  99.6 2.6 %collective-permute-start.20 = (bf16[128,2048]{1,0:T(8,128)(2,1)S(1)}, bf16[128,2048]{1,0:T(8,128)(2,1)S(1)}, u32[]{:S(2)}, u32[]{:S(2)}) collective-permute-start(bf16[128,2048]{1,0:T(8,128)(2,1)S(1)} %get-tuple-element.115), channel_id=1, source_target_pairs={{0,1},{1,0},{2,3},{3,2},{4,5},{5,4},{6,7},{7,6},{8,9},{9,8},{10,11... | collective-permute-start | bytes 1572872 | tf_op jit(solution)/shard_map/ppermute | solution.py:307
  99.6 4.5 %collective-permute-start.16 = (bf16[144,2048]{1,0:T(8,128)(2,1)}, bf16[144,2048]{1,0:T(8,128)(2,1)S(1)}, u32[]{:S(2)}, u32[]{:S(2)}) collective-permute-start(bf16[144,2048]{1,0:T(8,128)(2,1)} %collective-permute-done.6.refs_0_), channel_id=1, source_target_pairs={{0,1},{1,0},{2,3},{3,2},{4,5},{5,4},{6,7},{7,6},{8,9},{9,8},{10,11... | collective-permute-start | bytes 1769480 | tf_op jit(solution)/shard_map/ppermute | solution.py:307
  100.1 4.0 %collective-permute-start.17 = (bf16[128,2048]{1,0:T(8,128)(2,1)S(1)}, bf16[128,2048]{1,0:T(8,128)(2,1)S(1)}, u32[]{:S(2)}, u32[]{:S(2)}) collective-permute-start(bf16[128,2048]{1,0:T(8,128)(2,1)S(1)} %collective-permute-done.14.refs_1_), channel_id=1, source_target_pairs={{0,1},{1,0},{2,3},{3,2},{4,5},{5,4},{6,7},{7,6},{8,9},{9,8},{10,11... | collective-permute-start | bytes 1572872 | tf_op jit(solution)/shard_map/ppermute | solution.py:307
  102.3 19.6 %collective-permute-start.21 = (bf16[128,2048]{1,0:T(8,128)(2,1)S(1)}, bf16[128,2048]{1,0:T(8,128)(2,1)S(1)}, u32[]{:S(2)}, u32[]{:S(2)}) collective-permute-start(bf16[128,2048]{1,0:T(8,128)(2,1)S(1)} %add_convert_fusion.2), channel_id=1, source_target_pairs={{0,6},{1,7},{2,0},{3,1},{4,2},{5,3},{6,4},{7,5},{8,14},{9,15},{10,... | collective-permute-start | bytes 1572872 | tf_op jit(solution)/shard_map/ppermute | solution.py:310
  120.0 1.6 %collective-permute-start.18 = (bf16[64,2048]{1,0:T(8,128)(2,1)S(1)}, bf16[64,2048]{1,0:T(8,128)(2,1)S(1)}, u32[]{:S(2)}, u32[]{:S(2)}) collective-permute-start(bf16[64,2048]{1,0:T(8,128)(2,1)S(1)} %get-tuple-element.112), channel_id=1, source_target_pairs={{0,1},{1,0},{2,3},{3,2},{4,5},{5,4},{6,7},{7,6},{8,9},{9,8},{10,11... | collective-permute-start | bytes 786440 | tf_op jit(solution)/shard_map/ppermute | solution.py:307
  120.1 1.9 %collective-permute-start.19 = (bf16[64,2048]{1,0:T(8,128)(2,1)S(1)}, bf16[64,2048]{1,0:T(8,128)(2,1)S(1)}, u32[]{:S(2)}, u32[]{:S(2)}) collective-permute-start(bf16[64,2048]{1,0:T(8,128)(2,1)S(1)} %get-tuple-element.113), channel_id=1, source_target_pairs={{0,1},{1,0},{2,3},{3,2},{4,5},{5,4},{6,7},{7,6},{8,9},{9,8},{10,11... | collective-permute-start | bytes 786440 | tf_op jit(solution)/shard_map/ppermute | solution.py:307
  120.6 4.0 %collective-permute-start.11 = (bf16[128,2048]{1,0:T(8,128)(2,1)S(1)}, bf16[128,2048]{1,0:T(8,128)(2,1)S(1)}, u32[]{:S(2)}, u32[]{:S(2)}) collective-permute-start(bf16[128,2048]{1,0:T(8,128)(2,1)S(1)} %get-tuple-element.101), channel_id=1, source_target_pairs={{0,1},{1,0},{2,3},{3,2},{4,5},{5,4},{6,7},{7,6},{8,9},{9,8},{10,11... | collective-permute-start | bytes 1572872 | tf_op jit(solution)/shard_map/ppermute | solution.py:307
  122.2 14.0 %collective-permute-start.22 = (bf16[128,2048]{1,0:T(8,128)(2,1)S(1)}, bf16[128,2048]{1,0:T(8,128)(2,1)S(1)}, u32[]{:S(2)}, u32[]{:S(2)}) collective-permute-start(bf16[128,2048]{1,0:T(8,128)(2,1)S(1)} %add_convert_fusion.1), channel_id=1, source_target_pairs={{0,6},{1,7},{2,0},{3,1},{4,2},{5,3},{6,4},{7,5},{8,14},{9,15},{10,... | collective-permute-start | bytes 1572872 | tf_op jit(solution)/shard_map/ppermute | solution.py:310

commit v4 on v3

--- a/solution.py
+++ b/solution.py
@@ -141,34 +141,16 @@
     ]
 
 
-def block_kernel(tokens_ref, grads_ref, routes_ref, gates_ref, block_ref, rows_ref):
-    bins, width = tokens_ref.shape
-    rest = gates_ref[...]
-    pieces = [(routes_ref[...] + 1).astype(jnp.float32)]
+def make_block(tokens, grads, routes, gates):
+    rest = gates.T
+    pieces = [(routes.T + 1).astype(jnp.float32)]
     for _ in range(3):
-        piece = rest.astype(jnp.bfloat16).astype(jnp.float32)
+        piece = lax.reduce_precision(rest, 8, 7)
         rest = rest - piece
         pieces.append(piece)
     notes = jnp.concatenate(pieces, axis=0).astype(jnp.bfloat16)
-    for out in (block_ref, rows_ref):
-        out[:bins] = tokens_ref[...]
-        out[bins : bins + NOTES, bins:] = jnp.zeros((NOTES, width - bins), jnp.bfloat16)
-        out[bins : bins + NOTES, :bins] = notes
-    block_ref[bins + NOTES :] = grads_ref[...]
-
-
-def make_block(tokens, grads, routes, gates):
-    bins, width = tokens.shape
-    return pl.pallas_call(
-        block_kernel,
-        out_shape=[
-            jax.ShapeDtypeStruct((2 * bins + NOTES, width), jnp.bfloat16),
-            jax.ShapeDtypeStruct((bins + NOTES, width), jnp.bfloat16),
-        ],
-        compiler_params=pltpu.CompilerParams(vmem_limit_bytes=VMEM_BYTES),
-        cost_estimate=SMALL,
-        name="make_block",
-    )(tokens, grads, routes.T, gates.T)
+    notes = jnp.pad(notes, ((0, NOTES - notes.shape[0]), (0, tokens.shape[1] - notes.shape[1])))
+    return jnp.concatenate([tokens, notes, grads], axis=0)
 
 
 def expert_kernel(layout, pieces, top, base_ref, *refs):
@@ -325,8 +307,8 @@
         return pieces[0] if len(pieces) == 1 else jnp.concatenate(pieces, axis=0)
 
     barrier = lax.optimization_barrier
-    own, own_rows = make_block(moe_input[0], out_grad[0], routes[0], route_gates[0])
-    left, right_rows = hop(own, -1), hop(own_rows, 1)
+    own = make_block(moe_input[0], out_grad[0], routes[0], route_gates[0])
+    left, right_rows = hop(own, -1), hop(own[: bins + NOTES], 1)
     own_pair = pair(own)
     table = [[group ^ place for place in range(groups)] for group in range(groups)]
     group_ids = jnp.asarray(table, jnp.int32)[lax.axis_index("ctx")]
@@ -357,15 +339,16 @@
     for d in range(2, half):
         rights.append(tuple(hop(member, 1) for member in rights[-1]))
     kept, give = work(left_pair, FAR_COST)
-    carried, rights, kept, give = barrier((carried, rights, kept, give))
-    total = add_up(total, carried)
+    rights, kept, give = barrier((rights, kept, give))
+    left_carried = carried
     carried = add_up(kept, joined([swap(piece) for piece in give]))
     for right in reversed(rights):
         carried = hop(carried.astype(jnp.bfloat16), -1)
         kept, give = work(pair(*right), RIGHT_COST, 2)
         given = [swap(piece) for piece in give]
-        kept, given, carried = barrier((kept, given, carried))
+        kept, given, carried, left_carried = barrier((kept, given, carried, left_carried))
         carried = add_up(kept, joined(given), carried)
+    total = add_up(total, left_carried)
     carried = hop(carried.astype(jnp.bfloat16), -1)
     outs = unpack_groups(group_ids, results)
     total = add_up(total, carried).astype(jnp.bfloat16)

time: 138 us -> 131 us (0.949)
  waiting for transfers between devices: 36.7 us -> 27 us
  other arithmetic: 1.62 us -> 5.31 us
  starting transfers between devices: 20.8 us -> 24.3 us
  local copies, waits for them, and re-layouts: 6.21 us -> 2.78 us
    ppermute x7, waiting for transfers between devices: 26.3 us -> 17.2 us  [hop(): lax.ppermute(block, 'exp', [(i, (i + 2 * step) % members) for i in range(...]
    ppermute x7, starting transfers between devices: 11.5 us -> 15 us  [hop(): lax.ppermute(block, 'exp', [(i, (i + 2 * step) % members) for i in range(...]
    unnamed x16 -> x10, local copies, waits for them, and re-layouts: 5.52 us -> 2.1 us
    concatenate x0 -> x3, other arithmetic: none -> 2.23 us  [the longest x2 2.21 us: make_block(): return jnp.concatenate([tokens, notes, grads], axis=0)]
  transfers between devices with their start and end apart: 23 -> 23, of which waited for: 10 -> 9; matrix products, arithmetic and copies ran while one was open for 1% -> 2% of each run, Pallas kernels for 51% -> 54%
where the time goes in v4:
time: 131 us
  Pallas kernels  70.3 us (54%)
  waiting for transfers between devices  27 us (21%)
  starting transfers between devices  24.3 us (19%)
  other arithmetic  5.31 us (4%)
  local copies, waits for them, and re-layouts  2.78 us (2%)
    pallas_call x4, Pallas kernels, expert_back(): pl.pallas_call(functools.partial(expert_kernel, layout, pieces, top), out...  61.5 us
    ppermute x7, waiting for transfers between devices, hop(): lax.ppermute(block, 'exp', [(i, (i + 2 * step) % members) for i in range(...  17.2 us
    ppermute x7, starting transfers between devices, hop(): lax.ppermute(block, 'exp', [(i, (i + 2 * step) % members) for i in range(...  15 us
    ppermute x6, starting transfers between devices, exchange(): lax.ppermute(blocks[place], 'ctx', [(i, i ^ place) for i in range(groups)])  7.11 us
    pallas_call x1, Pallas kernels, heads_back(): pl.pallas_call(heads_kernel, grid=(heads,), out_shape=[jax.ShapeDtypeStru...  6.37 us
    ppermute x6, waiting for transfers between devices, exchange(): lax.ppermute(blocks[place], 'ctx', [(i, i ^ place) for i in range(groups)])  5.93 us
    ppermute x10, waiting for transfers between devices, swap(): return lax.ppermute(block, 'exp', [(i, i ^ 1) for i in range(members)])  3.94 us
  transfers between devices with their start and end apart: 23, of which 9 were waited for; matrix products, arithmetic and copies ran while one was open for 2% of the time, Pallas kernels for 54%

profile of v4, /device:TPU:0, one launch (start us, length us, event | category | flops | bytes accessed | tf_op | source)
XLA Modules:
  0.0 130.5 jit_solution(3362394287584570453)
XLA Ops:
  0.6 0.7 reduce-precision_convert_fusion.1
  1.4 0.7 fusion.10
  2.1 1.4 %pad_maximum_fusion.refs_0_ = bf16[272,2048]{1,0:T(8,128)(2,1)S(1)} fusion(bf16[128,2048]{1,0:T(8,128)(2,1)} %bitcast.26, bf16[16,2048]{1,0:T(8,128)(2,1)S(1)} %fusion.7, bf16[128,2048]{1,0:T(8,128)(2,1)} %bitcast.32), kind=kLoop, calls=%fused_computation | loop fusion | flops 3342336 | bytes 2228224 | tf_op jit(solution)/shard_map/concatenate | solution.py:153
  3.5 0.5 collective-permute-start
  4.0 4.7 %collective-permute-start.4 = (bf16[272,2048]{1,0:T(8,128)(2,1)S(1)}, bf16[272,2048]{1,0:T(8,128)(2,1)S(1)}, u32[]{:S(2)}, u32[]{:S(2)}) collective-permute-start(bf16[272,2048]{1,0:T(8,128)(2,1)S(1)} %pad_maximum_fusion.refs_0_), channel_id=1, source_target_pairs={{0,6},{1,7},{2,0},{3,1},{4,2},{5,3},{6,4},{7,5},{8,14},{9,15},{10,... | collective-permute-start | bytes 3342344 | tf_op jit(solution)/shard_map/ppermute | solution.py:292
  8.7 0.9 pad_maximum_fusion.1
  9.5 0.7 dynamic-slice_bitcast_fusion.group_ref
  10.2 1.0 copy-done.2
  11.3 1.0 copy-done.3
  12.3 0.7 pack_groups.1
  13.0 1.6 %collective-permute-start.1 = (bf16[4,128,512]{2,1,0:T(8,128)(2,1)S(1)}, bf16[4,128,512]{2,1,0:T(8,128)(2,1)S(1)}, u32[]{:S(2)}, u32[]{:S(2)}) collective-permute-start(bf16[4,128,512]{2,1,0:T(8,128)(2,1)S(1)} %get-tuple-element.65), channel_id=1, source_target_pairs={{0,8},{8,0},{16,24},{24,16},{1,9},{9,1},{17,25},{25,17},{2,10},{10... | collective-permute-start | bytes 1572872 | tf_op jit(solution)/shard_map/ppermute | solution.py:139
  14.6 1.5 %collective-permute-start.2 = (bf16[4,128,512]{2,1,0:T(8,128)(2,1)S(1)}, bf16[4,128,512]{2,1,0:T(8,128)(2,1)S(1)}, u32[]{:S(2)}, u32[]{:S(2)}) collective-permute-start(bf16[4,128,512]{2,1,0:T(8,128)(2,1)S(1)} %get-tuple-element.66), channel_id=1, source_target_pairs={{0,16},{8,24},{16,0},{24,8},{1,17},{9,25},{17,1},{25,9},{2,18},{10... | collective-permute-start | bytes 1572872 | tf_op jit(solution)/shard_map/ppermute | solution.py:139
  16.1 0.5 collective-permute-start.3
  16.6 16.0 %expert_back.4 = (bf16[128,2048]{1,0:T(8,128)(2,1)S(1)}, bf16[128,2048]{1,0:T(8,128)(2,1)S(1)}) custom-call(s32[1]{0:T(128)} %bitcast.11.base_ref, bf16[272,2048]{1,0:T(8,128)(2,1)S(1)} %pad_maximum_fusion.refs_0_, bf16[272,2048]{1,0:T(8,128)(2,1)} %collective-permute-done.refs_1_, bf16[4,2048,768]{2,1,0:T(8,128)(2,1)} %refs_4_.1, bf16[4,768,2048]{2,1,0:T(8,128)(2,1)} %refs_5_.1), custom_call_target="tpu_custom_call" | custom-call | flops 30000001024 | bytes 30000000 | tf_op jit(solution)/shard_map/expert_back/pallas_call | solution.py:254
  32.6 1.0 collective-permute-done.4.refs_0_
  33.6 5.9 %collective-permute-done.2.refs_2_ = bf16[4,128,512]{2,1,0:T(8,128)(2,1)S(1)} collective-permute-done((bf16[4,128,512]{2,1,0:T(8,128)(2,1)S(1)}, bf16[4,128,512]{2,1,0:T(8,128)(2,1)S(1)}, u32[]{:S(2)}, u32[]{:S(2)}) %collective-permute-start.2) | collective-permute-done | bytes 524320 | tf_op jit(solution)/shard_map/ppermute | solution.py:139
  39.5 3.5 %collective-permute-start.5 = (bf16[272,2048]{1,0:T(8,128)(2,1)S(1)}, bf16[272,2048]{1,0:T(8,128)(2,1)S(1)}, u32[]{:S(2)}, u32[]{:S(2)}) collective-permute-start(bf16[272,2048]{1,0:T(8,128)(2,1)S(1)} %collective-permute-done.4.refs_0_), channel_id=1, source_target_pairs={{0,6},{1,7},{2,0},{3,1},{4,2},{5,3},{6,4},{7,5},{8,14},{9,15},{10,... | collective-permute-start | bytes 3342344 | tf_op jit(solution)/shard_map/ppermute | solution.py:292
  43.1 6.4 %heads_back.1 = (bf16[3,128,512]{2,1,0:T(8,128)(2,1)S(1)}, bf16[3,128,512]{2,1,0:T(8,128)(2,1)S(1)}, bf16[3,128,512]{2,1,0:T(8,128)(2,1)S(1)}, bf16[3,128,512]{2,1,0:T(8,128)(2,1)S(1)}) custom-call(bf16[4,128,512]{2,1,0:T(8,128)(2,1)S(1)} %get-tuple-element.73.refs_0_, bf16[4,128,512]{2,1,0:T(8,128)(2,1)S(1)} %collective-permute-done.1.refs_1_, ...), custom_call_target="tpu_custom_call" | custom-call | flops 30000001024 | bytes 30000000 | tf_op jit(solution)/shard_map/heads_back/pallas_call | solution.py:124
  49.5 1.6 %collective-permute-start.10 = (bf16[3,128,512]{2,1,0:T(8,128)(2,1)S(1)}, bf16[3,128,512]{2,1,0:T(8,128)(2,1)S(1)}, u32[]{:S(2)}, u32[]{:S(2)}) collective-permute-start(bf16[3,128,512]{2,1,0:T(8,128)(2,1)S(1)} %get-tuple-element.84), channel_id=1, source_target_pairs={{0,24},{8,16},{16,8},{24,0},{1,25},{9,17},{17,9},{25,1},{2,26},{10... | collective-permute-start | bytes 1179656 | tf_op jit(solution)/shard_map/ppermute | solution.py:139
  51.0 1.5 %collective-permute-start.8 = (bf16[3,128,512]{2,1,0:T(8,128)(2,1)S(1)}, bf16[3,128,512]{2,1,0:T(8,128)(2,1)S(1)}, u32[]{:S(2)}, u32[]{:S(2)}) collective-permute-start(bf16[3,128,512]{2,1,0:T(8,128)(2,1)S(1)} %get-tuple-element.82), channel_id=1, source_target_pairs={{0,8},{8,0},{16,24},{24,16},{1,9},{9,1},{17,25},{25,17},{2,10},{10... | collective-permute-start | bytes 1179656 | tf_op jit(solution)/shard_map/ppermute | solution.py:139
  52.5 0.5 collective-permute-start.9
  53.0 14.8 %expert_back.5 = (bf16[128,2048]{1,0:T(8,128)(2,1)S(1)}, bf16[128,2048]{1,0:T(8,128)(2,1)S(1)}) custom-call(s32[1]{0:T(128)} %bitcast.11.base_ref, bf16[272,2048]{1,0:T(8,128)(2,1)S(1)} %collective-permute-done.4.refs_0_, bf16[272,2048]{1,0:T(8,128)(2,1)S(1)} %collective-permute-done.7.refs_1_, bf16[4,2048,768]{2,1,0:T(8,128)(2,1)} %refs_4_.1, ...), custom_call_target="tpu_custom_call" | custom-call | tf_op jit(solution)/shard_map/expert_back/pallas_call | solution.py:254
  67.8 2.8 %collective-permute-done.5.refs_0_ = bf16[272,2048]{1,0:T(8,128)(2,1)S(1)} collective-permute-done((bf16[272,2048]{1,0:T(8,128)(2,1)S(1)}, bf16[272,2048]{1,0:T(8,128)(2,1)S(1)}, u32[]{:S(2)}, u32[]{:S(2)}) %collective-permute-start.5) | collective-permute-done | bytes 1114144 | tf_op jit(solution)/shard_map/ppermute | solution.py:292
  70.6 0.1 collective-permute-start.13
  70.7 0.5 collective-permute-start.12
  71.2 0.2 collective-permute-start.20
  71.4 2.0 %collective-permute-done.13.refs_1_ = bf16[272,2048]{1,0:T(8,128)(2,1)S(1)} collective-permute-done((bf16[272,2048]{1,0:T(8,128)(2,1)S(1)}, bf16[272,2048]{1,0:T(8,128)(2,1)S(1)}, u32[]{:S(2)}, u32[]{:S(2)}) %collective-permute-start.13) | collective-permute-done | bytes 1114144 | tf_op jit(solution)/shard_map/ppermute | solution.py:289
  73.4 14.8 %expert_back.6 = (bf16[128,2048]{1,0:T(8,128)(2,1)S(1)}, bf16[128,2048]{1,0:T(8,128)(2,1)S(1)}) custom-call(s32[1]{0:T(128)} %bitcast.11.base_ref, bf16[272,2048]{1,0:T(8,128)(2,1)S(1)} %collective-permute-done.5.refs_0_, bf16[272,2048]{1,0:T(8,128)(2,1)S(1)} %collective-permute-done.13.refs_1_, bf16[4,2048,768]{2,1,0:T(8,128)(2,1)} %refs_4_.1, ...), custom_call_target="tpu_custom_call" | custom-call | tf_op jit(solution)/shard_map/expert_back/pallas_call | solution.py:254
  88.2 0.2 collective-permute-start.18
  88.4 0.4 collective-permute-start.14
  88.8 0.1 collective-permute-start.15
  88.9 0.1 add_convert_fusion.2
  89.1 0.5 collective-permute-start.21
  89.6 0.6 collective-permute-done.18
  90.2 0.1 add_convert_fusion.3
  90.3 3.6 %collective-permute-start.19 = (bf16[128,2048]{1,0:T(8,128)(2,1)S(1)}, bf16[128,2048]{1,0:T(8,128)(2,1)S(1)}, u32[]{:S(2)}, u32[]{:S(2)}) collective-permute-start(bf16[128,2048]{1,0:T(8,128)(2,1)S(1)} %add_convert_fusion.3), channel_id=1, source_target_pairs={{0,6},{1,7},{2,0},{3,1},{4,2},{5,3},{6,4},{7,5},{8,14},{9,15},{10,... | collective-permute-start | bytes 1572872 | tf_op jit(solution)/shard_map/ppermute | solution.py:292
  93.9 15.9 %expert_back.7 = (bf16[128,2048]{1,0:T(8,128)(2,1)S(1)}, bf16[64,2048]{1,0:T(8,128)(2,1)S(1)}, bf16[64,2048]{1,0:T(8,128)(2,1)S(1)}) custom-call(s32[1]{0:T(128)} %bitcast.11.base_ref, bf16[144,2048]{1,0:T(8,128)(2,1)} %collective-permute-done.6.refs_0_, bf16[128,2048]{1,0:T(8,128)(2,1)S(1)} %collective-permute-done.12.refs_1_, ...), custom_call_target="tpu_custom_call" | custom-call | flops 30000001024 | bytes 30000000 | tf_op jit(solution)/shard_map/expert_back/pallas_call | solution.py:254
  109.8 0.1 collective-permute-start.16
  109.9 0.5 collective-permute-start.17
  110.4 0.1 collective-permute-start.11
  110.5 0.9 collective-permute-done.16
  111.4 0.4 collective-permute-done.17
  111.8 4.0 %collective-permute-done.19 = bf16[128,2048]{1,0:T(8,128)(2,1)S(1)} collective-permute-done((bf16[128,2048]{1,0:T(8,128)(2,1)S(1)}, bf16[128,2048]{1,0:T(8,128)(2,1)S(1)}, u32[]{:S(2)}, u32[]{:S(2)}) %collective-permute-start.19) | collective-permute-done | bytes 524320 | tf_op jit(solution)/shard_map/ppermute | solution.py:292
  115.8 0.3 add_convert_fusion.1
  116.0 2.2 %collective-permute-start.22 = (bf16[128,2048]{1,0:T(8,128)(2,1)S(1)}, bf16[128,2048]{1,0:T(8,128)(2,1)S(1)}, u32[]{:S(2)}, u32[]{:S(2)}) collective-permute-start(bf16[128,2048]{1,0:T(8,128)(2,1)S(1)} %add_convert_fusion.1), channel_id=1, source_target_pairs={{0,6},{1,7},{2,0},{3,1},{4,2},{5,3},{6,4},{7,5},{8,14},{9,15},{10,... | collective-permute-start | bytes 1572872 | tf_op jit(solution)/shard_map/ppermute | solution.py:292
  118.2 1.8 %unpack_groups.1 = (bf16[128,2048]{1,0:T(8,128)(2,1)}, bf16[128,2048]{1,0:T(8,128)(2,1)}, bf16[128,2048]{1,0:T(8,128)(2,1)}) custom-call(s32[4]{0:T(128)S(1)} %dynamic-slice_bitcast_fusion.group_ref, bf16[3,128,512]{2,1,0:T(8,128)(2,1)S(1)} %get-tuple-element.89.refs_0_, bf16[3,128,512]{2,1,0:T(8,128)(2,1)S(1)} %collective-permute-done.8.refs_1_, ...), custom_call_target="tpu_custom_call" | custom-call | tf_op jit(solution)/shard_map/unpack_groups/pallas_call | solution.py:82
  120.0 9.4 %collective-permute-done.22 = bf16[128,2048]{1,0:T(8,128)(2,1)S(1)} collective-permute-done((bf16[128,2048]{1,0:T(8,128)(2,1)S(1)}, bf16[128,2048]{1,0:T(8,128)(2,1)S(1)}, u32[]{:S(2)}, u32[]{:S(2)}) %collective-permute-start.22) | collective-permute-done | bytes 524320 | tf_op jit(solution)/shard_map/ppermute | solution.py:292
  129.4 1.1 fusion
  (25 shorter events, 0.1 us)
Async XLA Ops:
  0.6 8.0 %copy-start.4 = (bf16[1,128,2048]{2,1,0:T(8,128)(2,1)S(1)}, bf16[1,128,2048]{2,1,0:T(8,128)(2,1)}, u32[]{:S(2)}) copy-start(bf16[1,128,2048]{2,1,0:T(8,128)(2,1)} %param.14) | copy-start | bytes 1572868
  2.1 8.1 %copy-start = (bf16[1,128,2048]{2,1,0:T(8,128)(2,1)S(1)}, bf16[1,128,2048]{2,1,0:T(8,128)(2,1)}, u32[]{:S(2)}) copy-start(bf16[1,128,2048]{2,1,0:T(8,128)(2,1)} %param.13) | copy-start | bytes 1572868
  2.1 8.1 %copy-start.1 = (bf16[1,128,2048]{2,1,0:T(8,128)(2,1)S(1)}, bf16[1,128,2048]{2,1,0:T(8,128)(2,1)}, u32[]{:S(2)}) copy-start(bf16[1,128,2048]{2,1,0:T(8,128)(2,1)} %param.10) | copy-start | bytes 1572868
  3.5 9.5 %collective-permute-start = (bf16[272,2048]{1,0:T(8,128)(2,1)S(1)}, bf16[272,2048]{1,0:T(8,128)(2,1)}, u32[]{:S(2)}, u32[]{:S(2)}) collective-permute-start(bf16[272,2048]{1,0:T(8,128)(2,1)S(1)} %pad_maximum_fusion.refs_0_), channel_id=1, source_target_pairs={{0,1},{1,0},{2,3},{3,2},{4,5},{5,4},{6,7},{7,6},{8,9},{9,8},{10,11... | collective-permute-start | bytes 3342344 | tf_op jit(solution)/shard_map/ppermute | solution.py:289
  4.0 29.6 %collective-permute-start.4 = (bf16[272,2048]{1,0:T(8,128)(2,1)S(1)}, bf16[272,2048]{1,0:T(8,128)(2,1)S(1)}, u32[]{:S(2)}, u32[]{:S(2)}) collective-permute-start(bf16[272,2048]{1,0:T(8,128)(2,1)S(1)} %pad_maximum_fusion.refs_0_), channel_id=1, source_target_pairs={{0,6},{1,7},{2,0},{3,1},{4,2},{5,3},{6,4},{7,5},{8,14},{9,15},{10,... | collective-permute-start | bytes 3342344 | tf_op jit(solution)/shard_map/ppermute | solution.py:292
  9.5 58.3 %collective-permute-start.6 = (bf16[144,2048]{1,0:T(8,128)(2,1)}, bf16[144,2048]{1,0:T(8,128)(2,1)}, u32[]{:S(2)}, u32[]{:S(2)}) collective-permute-start(bf16[144,2048]{1,0:T(8,128)(2,1)} %pad_maximum_fusion.1), channel_id=1, source_target_pairs={{0,2},{1,3},{2,4},{3,5},{4,6},{5,7},{6,0},{7,1},{8,10},{9,11},{10,... | collective-permute-start | bytes 1769480 | tf_op jit(solution)/shard_map/ppermute | solution.py:292
  10.2 1.0 copy-start.2
  11.3 1.0 copy-start.3
  13.0 20.6 %collective-permute-start.1 = (bf16[4,128,512]{2,1,0:T(8,128)(2,1)S(1)}, bf16[4,128,512]{2,1,0:T(8,128)(2,1)S(1)}, u32[]{:S(2)}, u32[]{:S(2)}) collective-permute-start(bf16[4,128,512]{2,1,0:T(8,128)(2,1)S(1)} %get-tuple-element.65), channel_id=1, source_target_pairs={{0,8},{8,0},{16,24},{24,16},{1,9},{9,1},{17,25},{25,17},{2,10},{10... | collective-permute-start | bytes 1572872 | tf_op jit(solution)/shard_map/ppermute | solution.py:139
  14.6 24.9 %collective-permute-start.2 = (bf16[4,128,512]{2,1,0:T(8,128)(2,1)S(1)}, bf16[4,128,512]{2,1,0:T(8,128)(2,1)S(1)}, u32[]{:S(2)}, u32[]{:S(2)}) collective-permute-start(bf16[4,128,512]{2,1,0:T(8,128)(2,1)S(1)} %get-tuple-element.66), channel_id=1, source_target_pairs={{0,16},{8,24},{16,0},{24,8},{1,17},{9,25},{17,1},{25,9},{2,18},{10... | collective-permute-start | bytes 1572872 | tf_op jit(solution)/shard_map/ppermute | solution.py:139
  16.1 23.4 %collective-permute-start.3 = (bf16[4,128,512]{2,1,0:T(8,128)(2,1)S(1)}, bf16[4,128,512]{2,1,0:T(8,128)(2,1)S(1)}, u32[]{:S(2)}, u32[]{:S(2)}) collective-permute-start(bf16[4,128,512]{2,1,0:T(8,128)(2,1)S(1)} %get-tuple-element.67), channel_id=1, source_target_pairs={{0,24},{8,16},{16,8},{24,0},{1,25},{9,17},{17,9},{25,1},{2,26},{10... | collective-permute-start | bytes 1572872 | tf_op jit(solution)/shard_map/ppermute | solution.py:139
  39.5 9.9 %collective-permute-start.7 = (bf16[272,2048]{1,0:T(8,128)(2,1)S(1)}, bf16[272,2048]{1,0:T(8,128)(2,1)S(1)}, u32[]{:S(2)}, u32[]{:S(2)}) collective-permute-start(bf16[272,2048]{1,0:T(8,128)(2,1)S(1)} %collective-permute-done.4.refs_0_), channel_id=1, source_target_pairs={{0,1},{1,0},{2,3},{3,2},{4,5},{5,4},{6,7},{7,6},{8,9},{9,8},{10,11... | collective-permute-start | bytes 3342344 | tf_op jit(solution)/shard_map/ppermute | solution.py:289
  39.5 31.1 %collective-permute-start.5 = (bf16[272,2048]{1,0:T(8,128)(2,1)S(1)}, bf16[272,2048]{1,0:T(8,128)(2,1)S(1)}, u32[]{:S(2)}, u32[]{:S(2)}) collective-permute-start(bf16[272,2048]{1,0:T(8,128)(2,1)S(1)} %collective-permute-done.4.refs_0_), channel_id=1, source_target_pairs={{0,6},{1,7},{2,0},{3,1},{4,2},{5,3},{6,4},{7,5},{8,14},{9,15},{10,... | collective-permute-start | bytes 3342344 | tf_op jit(solution)/shard_map/ppermute | solution.py:292
  49.5 21.1 %collective-permute-start.10 = (bf16[3,128,512]{2,1,0:T(8,128)(2,1)S(1)}, bf16[3,128,512]{2,1,0:T(8,128)(2,1)S(1)}, u32[]{:S(2)}, u32[]{:S(2)}) collective-permute-start(bf16[3,128,512]{2,1,0:T(8,128)(2,1)S(1)} %get-tuple-element.84), channel_id=1, source_target_pairs={{0,24},{8,16},{16,8},{24,0},{1,25},{9,17},{17,9},{25,1},{2,26},{10... | collective-permute-start | bytes 1179656 | tf_op jit(solution)/shard_map/ppermute | solution.py:139
  51.0 19.6 %collective-permute-start.8 = (bf16[3,128,512]{2,1,0:T(8,128)(2,1)S(1)}, bf16[3,128,512]{2,1,0:T(8,128)(2,1)S(1)}, u32[]{:S(2)}, u32[]{:S(2)}) collective-permute-start(bf16[3,128,512]{2,1,0:T(8,128)(2,1)S(1)} %get-tuple-element.82), channel_id=1, source_target_pairs={{0,8},{8,0},{16,24},{24,16},{1,9},{9,1},{17,25},{25,17},{2,10},{10... | collective-permute-start | bytes 1179656 | tf_op jit(solution)/shard_map/ppermute | solution.py:139
  52.5 18.1 %collective-permute-start.9 = (bf16[3,128,512]{2,1,0:T(8,128)(2,1)S(1)}, bf16[3,128,512]{2,1,0:T(8,128)(2,1)S(1)}, u32[]{:S(2)}, u32[]{:S(2)}) collective-permute-start(bf16[3,128,512]{2,1,0:T(8,128)(2,1)S(1)} %get-tuple-element.83), channel_id=1, source_target_pairs={{0,16},{8,24},{16,0},{24,8},{1,17},{9,25},{17,1},{25,9},{2,18},{10... | collective-permute-start | bytes 1179656 | tf_op jit(solution)/shard_map/ppermute | solution.py:139
  70.6 2.8 %collective-permute-start.13 = (bf16[272,2048]{1,0:T(8,128)(2,1)S(1)}, bf16[272,2048]{1,0:T(8,128)(2,1)S(1)}, u32[]{:S(2)}, u32[]{:S(2)}) collective-permute-start(bf16[272,2048]{1,0:T(8,128)(2,1)S(1)} %collective-permute-done.5.refs_0_), channel_id=1, source_target_pairs={{0,1},{1,0},{2,3},{3,2},{4,5},{5,4},{6,7},{7,6},{8,9},{9,8},{10,11... | collective-permute-start | bytes 3342344 | tf_op jit(solution)/shard_map/ppermute | solution.py:289
  70.7 17.5 %collective-permute-start.12 = (bf16[128,2048]{1,0:T(8,128)(2,1)S(1)}, bf16[128,2048]{1,0:T(8,128)(2,1)S(1)}, u32[]{:S(2)}, u32[]{:S(2)}) collective-permute-start(bf16[128,2048]{1,0:T(8,128)(2,1)S(1)} %bitcast.28), channel_id=1, source_target_pairs={{0,2},{1,3},{2,4},{3,5},{4,6},{5,7},{6,0},{7,1},{8,10},{9,11},{10,... | collective-permute-start | bytes 1572872 | tf_op jit(solution)/shard_map/ppermute | solution.py:292
  71.2 17.7 %collective-permute-start.20 = (bf16[128,2048]{1,0:T(8,128)(2,1)S(1)}, bf16[128,2048]{1,0:T(8,128)(2,1)S(1)}, u32[]{:S(2)}, u32[]{:S(2)}) collective-permute-start(bf16[128,2048]{1,0:T(8,128)(2,1)S(1)} %get-tuple-element.110), channel_id=1, source_target_pairs={{0,1},{1,0},{2,3},{3,2},{4,5},{5,4},{6,7},{7,6},{8,9},{9,8},{10,11... | collective-permute-start | bytes 1572872 | tf_op jit(solution)/shard_map/ppermute | solution.py:289
  88.2 2.0 %collective-permute-start.18 = (bf16[128,2048]{1,0:T(8,128)(2,1)S(1)}, bf16[128,2048]{1,0:T(8,128)(2,1)S(1)}, u32[]{:S(2)}, u32[]{:S(2)}) collective-permute-start(bf16[128,2048]{1,0:T(8,128)(2,1)S(1)} %get-tuple-element.108), channel_id=1, source_target_pairs={{0,1},{1,0},{2,3},{3,2},{4,5},{5,4},{6,7},{7,6},{8,9},{9,8},{10,11... | collective-permute-start | bytes 1572872 | tf_op jit(solution)/shard_map/ppermute | solution.py:289
  88.4 5.5 %collective-permute-start.14 = (bf16[144,2048]{1,0:T(8,128)(2,1)}, bf16[144,2048]{1,0:T(8,128)(2,1)S(1)}, u32[]{:S(2)}, u32[]{:S(2)}) collective-permute-start(bf16[144,2048]{1,0:T(8,128)(2,1)} %collective-permute-done.6.refs_0_), channel_id=1, source_target_pairs={{0,1},{1,0},{2,3},{3,2},{4,5},{5,4},{6,7},{7,6},{8,9},{9,8},{10,11... | collective-permute-start | bytes 1769480 | tf_op jit(solution)/shard_map/ppermute | solution.py:289
  88.8 5.1 %collective-permute-start.15 = (bf16[128,2048]{1,0:T(8,128)(2,1)S(1)}, bf16[128,2048]{1,0:T(8,128)(2,1)S(1)}, u32[]{:S(2)}, u32[]{:S(2)}) collective-permute-start(bf16[128,2048]{1,0:T(8,128)(2,1)S(1)} %collective-permute-done.12.refs_1_), channel_id=1, source_target_pairs={{0,1},{1,0},{2,3},{3,2},{4,5},{5,4},{6,7},{7,6},{8,9},{9,8},{10,11... | collective-permute-start | bytes 1572872 | tf_op jit(solution)/shard_map/ppermute | solution.py:289
  89.1 21.4 %collective-permute-start.21 = (bf16[128,2048]{1,0:T(8,128)(2,1)S(1)}, bf16[128,2048]{1,0:T(8,128)(2,1)S(1)}, u32[]{:S(2)}, u32[]{:S(2)}) collective-permute-start(bf16[128,2048]{1,0:T(8,128)(2,1)S(1)} %add_convert_fusion.2), channel_id=1, source_target_pairs={{0,2},{1,3},{2,4},{3,5},{4,6},{5,7},{6,0},{7,1},{8,10},{9,11},{10,... | collective-permute-start | bytes 1572872 | tf_op jit(solution)/shard_map/ppermute | solution.py:292
  90.3 25.4 %collective-permute-start.19 = (bf16[128,2048]{1,0:T(8,128)(2,1)S(1)}, bf16[128,2048]{1,0:T(8,128)(2,1)S(1)}, u32[]{:S(2)}, u32[]{:S(2)}) collective-permute-start(bf16[128,2048]{1,0:T(8,128)(2,1)S(1)} %add_convert_fusion.3), channel_id=1, source_target_pairs={{0,6},{1,7},{2,0},{3,1},{4,2},{5,3},{6,4},{7,5},{8,14},{9,15},{10,... | collective-permute-start | bytes 1572872 | tf_op jit(solution)/shard_map/ppermute | solution.py:292
  109.8 1.6 %collective-permute-start.16 = (bf16[64,2048]{1,0:T(8,128)(2,1)S(1)}, bf16[64,2048]{1,0:T(8,128)(2,1)S(1)}, u32[]{:S(2)}, u32[]{:S(2)}) collective-permute-start(bf16[64,2048]{1,0:T(8,128)(2,1)S(1)} %get-tuple-element.105), channel_id=1, source_target_pairs={{0,1},{1,0},{2,3},{3,2},{4,5},{5,4},{6,7},{7,6},{8,9},{9,8},{10,11... | collective-permute-start | bytes 786440 | tf_op jit(solution)/shard_map/ppermute | solution.py:289
  109.9 1.9 %collective-permute-start.17 = (bf16[64,2048]{1,0:T(8,128)(2,1)S(1)}, bf16[64,2048]{1,0:T(8,128)(2,1)S(1)}, u32[]{:S(2)}, u32[]{:S(2)}) collective-permute-start(bf16[64,2048]{1,0:T(8,128)(2,1)S(1)} %get-tuple-element.106), channel_id=1, source_target_pairs={{0,1},{1,0},{2,3},{3,2},{4,5},{5,4},{6,7},{7,6},{8,9},{9,8},{10,11... | collective-permute-start | bytes 786440 | tf_op jit(solution)/shard_map/ppermute | solution.py:289
  110.4 9.7 %collective-permute-start.11 = (bf16[128,2048]{1,0:T(8,128)(2,1)S(1)}, bf16[128,2048]{1,0:T(8,128)(2,1)S(1)}, u32[]{:S(2)}, u32[]{:S(2)}) collective-permute-start(bf16[128,2048]{1,0:T(8,128)(2,1)S(1)} %get-tuple-element.97), channel_id=1, source_target_pairs={{0,1},{1,0},{2,3},{3,2},{4,5},{5,4},{6,7},{7,6},{8,9},{9,8},{10,11... | collective-permute-start | bytes 1572872 | tf_op jit(solution)/shard_map/ppermute | solution.py:289
  116.0 13.4 %collective-permute-start.22 = (bf16[128,2048]{1,0:T(8,128)(2,1)S(1)}, bf16[128,2048]{1,0:T(8,128)(2,1)S(1)}, u32[]{:S(2)}, u32[]{:S(2)}) collective-permute-start(bf16[128,2048]{1,0:T(8,128)(2,1)S(1)} %add_convert_fusion.1), channel_id=1, source_target_pairs={{0,6},{1,7},{2,0},{3,1},{4,2},{5,3},{6,4},{7,5},{8,14},{9,15},{10,... | collective-permute-start | bytes 1572872 | tf_op jit(solution)/shard_map/ppermute | solution.py:292

commit v5 on v4

--- a/solution.py
+++ b/solution.py
@@ -153,16 +153,57 @@
     return jnp.concatenate([tokens, notes, grads], axis=0)
 
 
-def expert_kernel(layout, pieces, top, base_ref, *refs):
-    sources, count = len(layout), sum(layout)
-    block_refs, refs = refs[:count], refs[count:]
-    up_hbm, down_hbm = refs[:2]
-    keep_refs = refs[2 : 2 + sources // 2]
-    give_refs = refs[2 + sources // 2 : -7]
-    pick_ref, token_rows, gated_rows, back_rows, up_ref, down_ref, sems = refs[-7:]
-    bins = keep_refs[0].shape[0]
+def pick_slots(notes, base, top, experts, pick_ref):
+    bins = notes[0].shape[1]
+    slots = len(notes) * CAP
+    earlier = lax.broadcasted_iota(jnp.int32, (bins, bins), 0)
+    later = lax.broadcasted_iota(jnp.int32, (bins, bins), 1)
+    before = (earlier < later).astype(jnp.bfloat16)
+    slot = lax.broadcasted_iota(jnp.int32, (slots, bins), 0).astype(jnp.float32)
+    gates = [jnp.zeros((slots, 1), jnp.float32)] * experts
+    for source, note in enumerate(notes):
+        note = note.astype(jnp.float32)
+        named = note[:top] - base
+        weights = note[top : 2 * top] + note[2 * top : 3 * top] + note[3 * top : 4 * top]
+        hits = [(named == float(local + 1)).astype(jnp.float32) for local in range(experts)]
+        chosen = [jnp.sum(hit, axis=0, keepdims=True) for hit in hits]
+        stacked = jnp.concatenate(chosen, axis=0)
+        position = dot_nn(stacked.astype(jnp.bfloat16), before)
+        for local in range(experts):
+            place = jnp.where(
+                chosen[local] > 0.0, position[local : local + 1] + float(source * CAP), -1.0
+            )
+            pick = (slot == place).astype(jnp.float32)
+            gate = jnp.sum(hits[local] * weights, axis=0, keepdims=True)
+            gates[local] = gates[local] + jnp.sum(pick * gate, axis=1, keepdims=True)
+            pick_ref[
+                local * slots : (local + 1) * slots, source * bins : (source + 1) * bins
+            ] = pick.astype(jnp.bfloat16)
+    return jnp.concatenate(gates, axis=0)
+
+
+def expert_kernel(layout, ahead, later, pieces, top, base_ref, *refs):
+    refs = list(refs)
+
+    def take(count):
+        taken = refs[:count]
+        del refs[:count]
+        return taken
+
+    sources = len(layout)
+    blocks = [take(length) for length in layout]
+    ahead_refs = take(ahead)
+    slope_refs = take(1 if later else 0)
+    up_hbm, down_hbm = take(2)
+    (keep_ref,) = take(1)
+    give_refs = take(pieces)
+    ahead_slopes = take(1 if ahead else 0)
+    pick_ref, token_rows, gated_rows, back_rows, up_ref, down_ref, sems = take(7)
+    ahead_picks = take(1 if ahead else 0)
+    bins = keep_ref.shape[0]
     slots = sources * CAP
     experts = pick_ref.shape[0] // slots
+    wide = slots + ahead * CAP
 
     def copies(expert):
         place = expert % 2
@@ -179,44 +220,32 @@
     for copy in copies(0):
         copy.start()
 
-    def pick_rows():
-        blocks, first = [], 0
-        for length in layout:
-            members = [ref[...] for ref in block_refs[first : first + length]]
-            blocks.append(jnp.concatenate(members, axis=0) if length > 1 else members[0])
-            first += length
-        earlier = lax.broadcasted_iota(jnp.int32, (bins, bins), 0)
-        later = lax.broadcasted_iota(jnp.int32, (bins, bins), 1)
-        before = (earlier < later).astype(jnp.bfloat16)
-        slot = lax.broadcasted_iota(jnp.int32, (slots, bins), 0).astype(jnp.float32)
-        base = base_ref[0].astype(jnp.float32)
-        gates = [jnp.zeros((slots, 1), jnp.float32)] * experts
-        for source, block in enumerate(blocks):
-            notes = block[bins : bins + NOTES, :bins].astype(jnp.float32)
-            named = notes[:top] - base
-            weights = notes[top : 2 * top] + notes[2 * top : 3 * top] + notes[3 * top : 4 * top]
-            hits = [(named == float(local + 1)).astype(jnp.float32) for local in range(experts)]
-            chosen = [jnp.sum(hit, axis=0, keepdims=True) for hit in hits]
-            stacked = jnp.concatenate(chosen, axis=0)
-            position = dot_nn(stacked.astype(jnp.bfloat16), before)
-            for local in range(experts):
-                place = jnp.where(
-                    chosen[local] > 0.0, position[local : local + 1] + float(source * CAP), -1.0
-                )
-                pick = (slot == place).astype(jnp.float32)
-                gate = jnp.sum(hits[local] * weights, axis=0, keepdims=True)
-                gates[local] = gates[local] + jnp.sum(pick * gate, axis=1, keepdims=True)
-                pick_ref[
-                    local * slots : (local + 1) * slots, source * bins : (source + 1) * bins
-                ] = pick.astype(jnp.bfloat16)
-        picks = pick_ref[...]
-        tokens = jnp.concatenate([block[:bins] for block in blocks], axis=0)
-        token_rows[...] = dot_nn(picks, tokens).astype(jnp.bfloat16)
-        grads = jnp.concatenate([block[bins + NOTES :] for block in blocks], axis=0)
-        gate_column = jnp.concatenate(gates, axis=0)
-        gated_rows[...] = (gate_column * dot_nn(picks, grads)).astype(jnp.bfloat16)
-
-    pick_rows()
+    values = [
+        jnp.concatenate([piece[...] for piece in block], axis=0) if len(block) > 1 else block[0]
+        for block in blocks
+    ]
+    base = base_ref[0].astype(jnp.float32)
+    notes = [value[bins : bins + NOTES, :bins] for value in values]
+    gate_column = pick_slots(notes, base, top, experts, pick_ref)
+    grads = jnp.concatenate([value[bins + NOTES :] for value in values], axis=0)
+    gated_rows[...] = (gate_column * dot_nn(pick_ref[...], grads)).astype(jnp.bfloat16)
+    if not later:
+        tokens = jnp.concatenate([value[:bins] for value in values], axis=0)
+        picked = dot_nn(pick_ref[...], tokens).astype(jnp.bfloat16)
+        for local in range(experts):
+            token_rows[local * wide : local * wide + slots] = picked[
+                local * slots : (local + 1) * slots
+            ]
+    if ahead:
+        notes = [ref[bins : bins + NOTES, :bins] for ref in ahead_refs]
+        pick_slots(notes, base, top, experts, ahead_picks[0])
+        tokens = jnp.concatenate([ref[:bins] for ref in ahead_refs], axis=0)
+        picked = dot_nn(ahead_picks[0][...], tokens).astype(jnp.bfloat16)
+        more = ahead * CAP
+        for local in range(experts):
+            token_rows[local * wide + slots : (local + 1) * wide] = picked[
+                local * more : (local + 1) * more
+            ]
 
     @pl.loop(0, experts)
     def _(expert):
@@ -229,49 +258,62 @@
             copy.wait()
         place = expert % 2
         rows = pl.ds(pl.multiple_of(expert * slots, 16), slots)
-        preact = dot_nn(token_rows[rows, :], up_ref[place])
+        if later:
+            slopes = slope_refs[0][rows, :]
+        else:
+            wide_rows = pl.ds(pl.multiple_of(expert * wide, 16), wide)
+            slopes = silu_slope(dot_nn(token_rows[wide_rows, :], up_ref[place]))
+        if ahead:
+            more = ahead * CAP
+            ahead_slopes[0][pl.ds(pl.multiple_of(expert * more, 16), more), :] = slopes[slots:]
+            slopes = slopes[:slots]
         back_grad = dot_nt(gated_rows[rows, :], down_ref[place])
-        hidden_grad = (back_grad * silu_slope(preact)).astype(jnp.bfloat16)
+        hidden_grad = (back_grad * slopes).astype(jnp.bfloat16)
         back_rows[rows, :] = dot_nt(hidden_grad, up_ref[place]).astype(jnp.bfloat16)
 
     sums = dot_tn(pick_ref[...], back_rows[...])
-    for pair, keep in enumerate(keep_refs):
-        mine, other = 2 * pair * bins, (2 * pair + 1) * bins
-        keep[...] = sums[mine : mine + bins].astype(jnp.bfloat16)
-        for piece in range(pieces):
-            rows = bins // pieces
-            give_refs[pair * pieces + piece][...] = sums[
-                other + piece * rows : other + (piece + 1) * rows
-            ].astype(jnp.bfloat16)
-
-
-def expert_back(base, blocks, up_weight, down_weight, bins, top, units, pieces):
-    sources = len(blocks)
+    keep_ref[...] = sums[:bins].astype(jnp.bfloat16)
+    rows = bins // pieces
+    for piece, give_ref in enumerate(give_refs):
+        give_ref[...] = sums[bins + piece * rows : bins + (piece + 1) * rows].astype(jnp.bfloat16)
+
+
+def expert_back(base, blocks, up_weight, down_weight, bins, top, units, pieces, ahead, slopes):
     layout = [len(block) for block in blocks]
+    later = slopes is not None
     experts, width, hidden = up_weight.shape
-    slots = sources * CAP
-    pairs = sources // 2
+    slots = len(blocks) * CAP
+    wide = slots + len(ahead) * CAP
+    operands = [piece for block in blocks for piece in block] + list(ahead)
+    operands += [slopes] if later else []
+    more = [jax.ShapeDtypeStruct((experts * len(ahead) * CAP, hidden), jnp.float32)]
+    out_shape = (
+        [jax.ShapeDtypeStruct((bins, width), jnp.bfloat16)]
+        + [jax.ShapeDtypeStruct((bins // pieces, width), jnp.bfloat16)] * pieces
+        + (more if ahead else [])
+    )
     return pl.pallas_call(
-        functools.partial(expert_kernel, layout, pieces, top),
-        out_shape=[jax.ShapeDtypeStruct((bins, width), jnp.bfloat16)] * pairs
-        + [jax.ShapeDtypeStruct((bins // pieces, width), jnp.bfloat16)] * (pairs * pieces),
+        functools.partial(expert_kernel, layout, len(ahead), later, pieces, top),
+        out_shape=out_shape,
         in_specs=[pl.BlockSpec(memory_space=pltpu.SMEM)]
-        + [pl.BlockSpec(memory_space=pltpu.VMEM)] * sum(layout)
+        + [pl.BlockSpec(memory_space=pltpu.VMEM)] * len(operands)
         + [pl.BlockSpec(memory_space=pltpu.HBM)] * 2,
-        out_specs=[pl.BlockSpec(memory_space=pltpu.VMEM)] * (pairs * (1 + pieces)),
+        out_specs=[pl.BlockSpec(memory_space=pltpu.VMEM)] * len(out_shape),
         scratch_shapes=[
-            pltpu.VMEM((experts * slots, sources * bins), jnp.bfloat16),
-            pltpu.VMEM((experts * slots, width), jnp.bfloat16),
+            pltpu.VMEM((experts * slots, len(blocks) * bins), jnp.bfloat16),
+            pltpu.VMEM((16 if later else experts * wide, width), jnp.bfloat16),
             pltpu.VMEM((experts * slots, width), jnp.bfloat16),
             pltpu.VMEM((experts * slots, width), jnp.bfloat16),
             pltpu.VMEM((2, width, hidden), jnp.bfloat16),
             pltpu.VMEM((2, hidden, width), jnp.bfloat16),
             pltpu.SemaphoreType.DMA((2, 2 * PARTS)),
-        ],
+        ]
+        + [pltpu.VMEM((experts * len(ahead) * CAP, len(ahead) * bins), jnp.bfloat16)]
+        * (1 if ahead else 0),
         compiler_params=pltpu.CompilerParams(vmem_limit_bytes=VMEM_EXPERTS),
         cost_estimate=cost(units),
         name="expert_back",
-    )(base, *[piece for block in blocks for piece in block], up_weight, down_weight)
+    )(base, *operands, up_weight, down_weight)
 
 
 def per_device(
@@ -296,9 +338,11 @@
     def pair(*pieces):
         return [list(pieces), [swap(piece) for piece in pieces]]
 
-    def work(blocks, units, pieces=1):
-        kept, *give = expert_back(base, blocks, up_weight, down_weight, bins, top, units, pieces)
-        return kept, give
+    def work(blocks, units, pieces=1, ahead=(), slopes=None):
+        kept, *rest = expert_back(
+            base, blocks, up_weight, down_weight, bins, top, units, pieces, ahead, slopes
+        )
+        return kept, rest[:pieces], rest[pieces:]
 
     def add_up(*members):
         return functools.reduce(jnp.add, [member.astype(jnp.float32) for member in members])
@@ -316,39 +360,43 @@
     packed = pack_groups(group_ids, rows, groups)
     own_pair, packed = barrier((own_pair, packed))
     heads = exchange(packed)
-    kept, give = work(own_pair, OWN_COST)
+    kept, give, _ = work(own_pair, OWN_COST)
     heads, kept, give, left = barrier((heads, kept, give, left))
     total = add_up(kept, joined([swap(piece) for piece in give]))
     left_pair, right_grads = pair(left), out_grad[0]
     results = heads_back(heads)
-    left_pair, results = barrier((left_pair, results))
+    left_pair, results, right_rows = barrier((left_pair, results, right_rows))
     results = exchange(results)
-    left_sums = []
+    right_partner = swap(right_rows)
+    left_sums, slopes = [], None
     for d in range(1, half):
         left = hop(left, -1)
-        kept, give = work(left_pair, LEFT_COST)
-        left, right_rows, results, kept, give = barrier((left, right_rows, results, kept, give))
+        ahead = () if d > 1 else (right_rows, right_partner)
+        kept, give, more = work(left_pair, LEFT_COST, ahead=ahead)
+        slopes = more[0] if d == 1 else slopes
+        left, results, kept, give = barrier((left, results, kept, give))
         left_sums.append(add_up(kept, joined([swap(piece) for piece in give])))
         left_pair = pair(left)
-    carried = None
-    for sums in reversed(left_sums):
-        if carried is not None:
-            sums = add_up(sums, carried)
-        carried = hop(sums.astype(jnp.bfloat16), 1)
+    carried = left_sums[-1].astype(jnp.bfloat16)
+    for sums in reversed(left_sums[:-1]):
+        carried = add_up(sums, hop(carried, 1)).astype(jnp.bfloat16)
+    left_halves = [hop(carried[: bins // 2], 1), hop(carried[bins // 2 :], 1)]
     rights = [(right_rows, hop(right_grads, 1))]
     for d in range(2, half):
         rights.append(tuple(hop(member, 1) for member in rights[-1]))
-    kept, give = work(left_pair, FAR_COST)
-    rights, kept, give = barrier((rights, kept, give))
-    left_carried = carried
+    kept, give, _ = work(left_pair, FAR_COST)
+    left_halves[0], rights, kept, give = barrier((left_halves[0], rights, kept, give))
     carried = add_up(kept, joined([swap(piece) for piece in give]))
-    for right in reversed(rights):
+    for d in range(half - 1, 0, -1):
         carried = hop(carried.astype(jnp.bfloat16), -1)
-        kept, give = work(pair(*right), RIGHT_COST, 2)
+        right_pair = pair(*rights[d - 1])
+        if d == 1:
+            right_pair[1][0] = right_partner
+        kept, give, _ = work(right_pair, RIGHT_COST, 2, slopes=slopes if d == 1 else None)
         given = [swap(piece) for piece in give]
-        kept, given, carried, left_carried = barrier((kept, given, carried, left_carried))
+        kept, given, carried, left_halves = barrier((kept, given, carried, left_halves))
         carried = add_up(kept, joined(given), carried)
-    total = add_up(total, left_carried)
+    total = add_up(total, joined(left_halves))
     carried = hop(carried.astype(jnp.bfloat16), -1)
     outs = unpack_groups(group_ids, results)
     total = add_up(total, carried).astype(jnp.bfloat16)

time: 131 us -> 131 us (level)
  waiting for transfers between devices: 27 us -> 32.2 us
  starting transfers between devices: 24.3 us -> 20.7 us
  Pallas kernels: 70.3 us -> 67.5 us
    ppermute x7 -> x8, starting transfers between devices: 15 us -> 11.2 us  [hop(): lax.ppermute(block, 'exp', [(i, (i + 2 * step) % members) for i in range(...]
    pallas_call x4, Pallas kernels: 61.5 us -> 58.6 us  [expert_back(): pl.pallas_call(functools.partial(expert_kernel, layout, len(ahead), later...]
    ppermute x6, waiting for transfers between devices: 5.93 us -> 7.87 us  [exchange(): lax.ppermute(blocks[place], 'ctx', [(i, i ^ place) for i in range(groups)])]
    ppermute x7 -> x8, waiting for transfers between devices: 17.2 us -> 18.9 us  [hop(): lax.ppermute(block, 'exp', [(i, (i + 2 * step) % members) for i in range(...]
    ppermute x10, waiting for transfers between devices: 3.94 us -> 5.47 us  [swap(): return lax.ppermute(block, 'exp', [(i, i ^ 1) for i in range(members)])]
  transfers between devices with their start and end apart: 23 -> 24, of which waited for: 9 -> 12; matrix products, arithmetic and copies ran while one was open for 2% -> 2% of each run, Pallas kernels for 54% -> 52%
where the time goes in v5:
time: 131 us; the launch traced here: 130 us
  Pallas kernels  67.5 us (52%)
  waiting for transfers between devices  32.2 us (25%)
  starting transfers between devices  20.7 us (16%)
  other arithmetic  5.25 us (4%)
  local copies, waits for them, and re-layouts  3.86 us (3%)
    pallas_call x4, Pallas kernels, expert_back(): pl.pallas_call(functools.partial(expert_kernel, layout, len(ahead), later...  58.6 us
    ppermute x8, waiting for transfers between devices, hop(): lax.ppermute(block, 'exp', [(i, (i + 2 * step) % members) for i in range(...  18.9 us
    ppermute x8, starting transfers between devices, hop(): lax.ppermute(block, 'exp', [(i, (i + 2 * step) % members) for i in range(...  11.2 us
    ppermute x6, waiting for transfers between devices, exchange(): lax.ppermute(blocks[place], 'ctx', [(i, i ^ place) for i in range(groups)])  7.87 us
    ppermute x6, starting transfers between devices, exchange(): lax.ppermute(blocks[place], 'ctx', [(i, i ^ place) for i in range(groups)])  7.04 us
    pallas_call x1, Pallas kernels, heads_back(): pl.pallas_call(heads_kernel, grid=(heads,), out_shape=[jax.ShapeDtypeStru...  6.37 us
    ppermute x10, waiting for transfers between devices, swap(): return lax.ppermute(block, 'exp', [(i, i ^ 1) for i in range(members)])  5.47 us
    unnamed x10, local copies, waits for them, and re-layouts  3.14 us
  transfers between devices with their start and end apart: 24, of which 12 were waited for; matrix products, arithmetic and copies ran while one was open for 2% of the time, Pallas kernels for 52%

profile of v5, /device:TPU:0, one launch (start us, length us, event | category | flops | bytes accessed | tf_op | source)
XLA Modules:
  0.0 130.3 jit_solution(13388005357971005283)
XLA Ops:
  0.6 0.7 fusion.10
  1.4 0.7 reduce-precision_convert_fusion.1
  2.1 1.3 %pad_maximum_fusion.refs_0_ = bf16[272,2048]{1,0:T(8,128)(2,1)S(1)} fusion(bf16[128,2048]{1,0:T(8,128)(2,1)} %bitcast.26, bf16[16,2048]{1,0:T(8,128)(2,1)S(1)} %fusion.7, bf16[128,2048]{1,0:T(8,128)(2,1)} %bitcast.32), kind=kLoop, calls=%fused_computation | loop fusion | flops 3342336 | bytes 2228224 | tf_op jit(solution)/shard_map/concatenate | solution.py:153
  3.4 0.5 collective-permute-start
  4.0 4.7 %collective-permute-start.4 = (bf16[272,2048]{1,0:T(8,128)(2,1)S(1)}, bf16[272,2048]{1,0:T(8,128)(2,1)S(1)}, u32[]{:S(2)}, u32[]{:S(2)}) collective-permute-start(bf16[272,2048]{1,0:T(8,128)(2,1)S(1)} %pad_maximum_fusion.refs_0_), channel_id=1, source_target_pairs={{0,6},{1,7},{2,0},{3,1},{4,2},{5,3},{6,4},{7,5},{8,14},{9,15},{10,... | collective-permute-start | bytes 3342344 | tf_op jit(solution)/shard_map/ppermute | solution.py:334
  8.6 0.9 pad_maximum_fusion.1
  9.5 0.7 dynamic-slice_bitcast_fusion.group_ref
  10.2 1.0 copy-done.1
  11.2 1.0 copy-done.2
  12.3 1.0 copy-done.3
  13.3 0.7 pack_groups.1
  14.0 1.6 %collective-permute-start.1 = (bf16[4,128,512]{2,1,0:T(8,128)(2,1)S(1)}, bf16[4,128,512]{2,1,0:T(8,128)(2,1)S(1)}, u32[]{:S(2)}, u32[]{:S(2)}) collective-permute-start(bf16[4,128,512]{2,1,0:T(8,128)(2,1)S(1)} %get-tuple-element.68), channel_id=1, source_target_pairs={{0,8},{8,0},{16,24},{24,16},{1,9},{9,1},{17,25},{25,17},{2,10},{10... | collective-permute-start | bytes 1572872 | tf_op jit(solution)/shard_map/ppermute | solution.py:139
  15.6 1.5 %collective-permute-start.2 = (bf16[4,128,512]{2,1,0:T(8,128)(2,1)S(1)}, bf16[4,128,512]{2,1,0:T(8,128)(2,1)S(1)}, u32[]{:S(2)}, u32[]{:S(2)}) collective-permute-start(bf16[4,128,512]{2,1,0:T(8,128)(2,1)S(1)} %get-tuple-element.69), channel_id=1, source_target_pairs={{0,16},{8,24},{16,0},{24,8},{1,17},{9,25},{17,1},{25,9},{2,18},{10... | collective-permute-start | bytes 1572872 | tf_op jit(solution)/shard_map/ppermute | solution.py:139
  17.1 0.5 collective-permute-start.3
  17.6 15.6 %expert_back.4 = (bf16[128,2048]{1,0:T(8,128)(2,1)S(1)}, bf16[128,2048]{1,0:T(8,128)(2,1)S(1)}) custom-call(s32[1]{0:T(128)} %bitcast.11.base_ref, bf16[272,2048]{1,0:T(8,128)(2,1)S(1)} %pad_maximum_fusion.refs_0_, bf16[272,2048]{1,0:T(8,128)(2,1)} %collective-permute-done.refs_1_, bf16[4,2048,768]{2,1,0:T(8,128)(2,1)} %refs_5_.3, bf16[4,768,2048]{2,1,0:T(8,128)(2,1)} %refs_6_.1), custom_call_target="tpu_custom_call" | custom-call | flops 30000001024 | bytes 30000000 | tf_op jit(solution)/shard_map/expert_back/pallas_call | solution.py:295
  33.2 0.4 collective-permute-done.4.refs_0_
  33.6 7.0 %collective-permute-done.2.refs_2_ = bf16[4,128,512]{2,1,0:T(8,128)(2,1)S(1)} collective-permute-done((bf16[4,128,512]{2,1,0:T(8,128)(2,1)S(1)}, bf16[4,128,512]{2,1,0:T(8,128)(2,1)S(1)}, u32[]{:S(2)}, u32[]{:S(2)}) %collective-permute-start.2) | collective-permute-done | bytes 524320 | tf_op jit(solution)/shard_map/ppermute | solution.py:139
  40.5 3.5 %collective-permute-start.5 = (bf16[272,2048]{1,0:T(8,128)(2,1)S(1)}, bf16[272,2048]{1,0:T(8,128)(2,1)S(1)}, u32[]{:S(2)}, u32[]{:S(2)}) collective-permute-start(bf16[272,2048]{1,0:T(8,128)(2,1)S(1)} %collective-permute-done.4.refs_0_), channel_id=1, source_target_pairs={{0,6},{1,7},{2,0},{3,1},{4,2},{5,3},{6,4},{7,5},{8,14},{9,15},{10,... | collective-permute-start | bytes 3342344 | tf_op jit(solution)/shard_map/ppermute | solution.py:334
  44.1 6.4 %heads_back.1 = (bf16[3,128,512]{2,1,0:T(8,128)(2,1)S(1)}, bf16[3,128,512]{2,1,0:T(8,128)(2,1)S(1)}, bf16[3,128,512]{2,1,0:T(8,128)(2,1)S(1)}, bf16[3,128,512]{2,1,0:T(8,128)(2,1)S(1)}) custom-call(bf16[4,128,512]{2,1,0:T(8,128)(2,1)S(1)} %get-tuple-element.76.refs_0_, bf16[4,128,512]{2,1,0:T(8,128)(2,1)S(1)} %collective-permute-done.1.refs_1_, ...), custom_call_target="tpu_custom_call" | custom-call | flops 30000001024 | bytes 30000000 | tf_op jit(solution)/shard_map/heads_back/pallas_call | solution.py:124
  50.5 0.3 collective-permute-start.11
  50.8 1.2 collective-permute-start.8
  52.0 0.8 collective-permute-start.9
  52.8 1.4 %collective-permute-start.10 = (bf16[3,128,512]{2,1,0:T(8,128)(2,1)S(1)}, bf16[3,128,512]{2,1,0:T(8,128)(2,1)S(1)}, u32[]{:S(2)}, u32[]{:S(2)}) collective-permute-start(bf16[3,128,512]{2,1,0:T(8,128)(2,1)S(1)} %get-tuple-element.87), channel_id=1, source_target_pairs={{0,24},{8,16},{16,8},{24,0},{1,25},{9,17},{17,9},{25,1},{2,26},{10... | collective-permute-start | bytes 1179656 | tf_op jit(solution)/shard_map/ppermute | solution.py:139
  54.3 15.1 %expert_back.5 = (bf16[128,2048]{1,0:T(8,128)(2,1)S(1)}, bf16[128,2048]{1,0:T(8,128)(2,1)S(1)}, f32[192,768]{1,0:T(8,128)S(1)}) custom-call(s32[1]{0:T(128)} %bitcast.11.base_ref, bf16[272,2048]{1,0:T(8,128)(2,1)S(1)} %collective-permute-done.4.refs_0_, bf16[272,2048]{1,0:T(8,128)(2,1)S(1)} %collective-permute-done.6.refs_1_, ...), custom_call_target="tpu_custom_call" | custom-call | tf_op jit(solution)/shard_map/expert_back/pallas_call | solution.py:295
  69.4 1.2 collective-permute-done.5.refs_0_
  70.6 0.9 collective-permute-done.10.refs_3_
  71.5 0.5 collective-permute-start.16
  72.0 1.4 %collective-permute-done.13 = bf16[128,2048]{1,0:T(8,128)(2,1)S(1)} collective-permute-done((bf16[128,2048]{1,0:T(8,128)(2,1)S(1)}, bf16[128,2048]{1,0:T(8,128)(2,1)S(1)}, u32[]{:S(2)}, u32[]{:S(2)}) %collective-permute-start.13) | collective-permute-done | bytes 524320 | tf_op jit(solution)/shard_map/ppermute | solution.py:331
  73.4 0.1 add_convert_fusion.3
  73.6 1.3 %collective-permute-done.16.refs_1_ = bf16[272,2048]{1,0:T(8,128)(2,1)S(1)} collective-permute-done((bf16[272,2048]{1,0:T(8,128)(2,1)S(1)}, bf16[272,2048]{1,0:T(8,128)(2,1)S(1)}, u32[]{:S(2)}, u32[]{:S(2)}) %collective-permute-start.16) | collective-permute-done | bytes 1114144 | tf_op jit(solution)/shard_map/ppermute | solution.py:331
  75.0 14.8 %expert_back.6 = (bf16[128,2048]{1,0:T(8,128)(2,1)S(1)}, bf16[128,2048]{1,0:T(8,128)(2,1)S(1)}) custom-call(s32[1]{0:T(128)} %bitcast.11.base_ref, bf16[272,2048]{1,0:T(8,128)(2,1)S(1)} %collective-permute-done.5.refs_0_, bf16[272,2048]{1,0:T(8,128)(2,1)S(1)} %collective-permute-done.16.refs_1_, bf16[4,2048,768]{2,1,0:T(8,128)(2,1)} %refs_5_.3, ...), custom_call_target="tpu_custom_call" | custom-call | tf_op jit(solution)/shard_map/expert_back/pallas_call | solution.py:295
  89.8 3.4 %collective-permute-done.14 = bf16[64,2048]{1,0:T(8,128)(2,1)S(1)} collective-permute-done((bf16[64,2048]{1,0:T(8,128)(2,1)S(1)}, bf16[64,2048]{1,0:T(8,128)(2,1)S(1)}, u32[]{:S(2)}, u32[]{:S(2)}) %collective-permute-start.14) | collective-permute-done | bytes 262176 | tf_op jit(solution)/shard_map/ppermute | solution.py:334
  93.2 0.5 collective-permute-start.17
  93.7 1.4 %collective-permute-done.20 = bf16[128,2048]{1,0:T(8,128)(2,1)S(1)} collective-permute-done((bf16[128,2048]{1,0:T(8,128)(2,1)S(1)}, bf16[128,2048]{1,0:T(8,128)(2,1)S(1)}, u32[]{:S(2)}, u32[]{:S(2)}) %collective-permute-start.20) | collective-permute-done | bytes 524320 | tf_op jit(solution)/shard_map/ppermute | solution.py:331
  95.1 0.1 add_convert_fusion.2
  95.2 2.7 %collective-permute-start.21 = (bf16[128,2048]{1,0:T(8,128)(2,1)S(1)}, bf16[128,2048]{1,0:T(8,128)(2,1)S(1)}, u32[]{:S(2)}, u32[]{:S(2)}) collective-permute-start(bf16[128,2048]{1,0:T(8,128)(2,1)S(1)} %add_convert_fusion.2), channel_id=1, source_target_pairs={{0,6},{1,7},{2,0},{3,1},{4,2},{5,3},{6,4},{7,5},{8,14},{9,15},{10,... | collective-permute-start | bytes 1572872 | tf_op jit(solution)/shard_map/ppermute | solution.py:334
  97.9 13.1 %expert_back.7 = (bf16[128,2048]{1,0:T(8,128)(2,1)S(1)}, bf16[64,2048]{1,0:T(8,128)(2,1)S(1)}, bf16[64,2048]{1,0:T(8,128)(2,1)S(1)}) custom-call(s32[1]{0:T(128)} %bitcast.11.base_ref, bf16[144,2048]{1,0:T(8,128)(2,1)S(1)} %collective-permute-done.7.refs_2_.refs_0_, bf16[128,2048]{1,0:T(8,128)(2,1)S(1)} %collective-permute-done.15.refs_1_, ...), custom_call_target="tpu_custom_call" | custom-call | flops 30000001024 | bytes 30000000 | tf_op jit(solution)/shard_map/expert_back/pallas_call | solution.py:295
  111.0 0.1 collective-permute-start.18
  111.1 0.5 collective-permute-start.19
  111.6 0.1 collective-permute-start.12
  111.7 0.9 collective-permute-done.18
  112.6 0.4 collective-permute-done.19
  113.0 2.1 %collective-permute-done.21 = bf16[128,2048]{1,0:T(8,128)(2,1)S(1)} collective-permute-done((bf16[128,2048]{1,0:T(8,128)(2,1)S(1)}, bf16[128,2048]{1,0:T(8,128)(2,1)S(1)}, u32[]{:S(2)}, u32[]{:S(2)}) %collective-permute-start.21) | collective-permute-done | bytes 524320 | tf_op jit(solution)/shard_map/ppermute | solution.py:334
  115.1 0.2 add_convert_fusion.1
  115.3 0.2 collective-permute-start.23
  115.5 1.8 %unpack_groups.1 = (bf16[128,2048]{1,0:T(8,128)(2,1)}, bf16[128,2048]{1,0:T(8,128)(2,1)}, bf16[128,2048]{1,0:T(8,128)(2,1)}) custom-call(s32[4]{0:T(128)S(1)} %dynamic-slice_bitcast_fusion.group_ref, bf16[3,128,512]{2,1,0:T(8,128)(2,1)S(1)} %get-tuple-element.93.refs_0_, bf16[3,128,512]{2,1,0:T(8,128)(2,1)S(1)} %collective-permute-done.8.refs_1_, ...), custom_call_target="tpu_custom_call" | custom-call | tf_op jit(solution)/shard_map/unpack_groups/pallas_call | solution.py:82
  117.3 11.8 %collective-permute-done.23 = bf16[128,2048]{1,0:T(8,128)(2,1)S(1)} collective-permute-done((bf16[128,2048]{1,0:T(8,128)(2,1)S(1)}, bf16[128,2048]{1,0:T(8,128)(2,1)S(1)}, u32[]{:S(2)}, u32[]{:S(2)}) %collective-permute-start.23) | collective-permute-done | bytes 524320 | tf_op jit(solution)/shard_map/ppermute | solution.py:334
  129.2 1.1 fusion
  (28 shorter events, 0.2 us)
Async XLA Ops:
  0.6 8.0 %copy-start.4 = (bf16[1,128,2048]{2,1,0:T(8,128)(2,1)S(1)}, bf16[1,128,2048]{2,1,0:T(8,128)(2,1)}, u32[]{:S(2)}) copy-start(bf16[1,128,2048]{2,1,0:T(8,128)(2,1)} %param.14) | copy-start | bytes 1572868
  2.1 8.1 %copy-start = (bf16[1,128,2048]{2,1,0:T(8,128)(2,1)S(1)}, bf16[1,128,2048]{2,1,0:T(8,128)(2,1)}, u32[]{:S(2)}) copy-start(bf16[1,128,2048]{2,1,0:T(8,128)(2,1)} %param.13) | copy-start | bytes 1572868
  3.4 10.6 %collective-permute-start = (bf16[272,2048]{1,0:T(8,128)(2,1)S(1)}, bf16[272,2048]{1,0:T(8,128)(2,1)}, u32[]{:S(2)}, u32[]{:S(2)}) collective-permute-start(bf16[272,2048]{1,0:T(8,128)(2,1)S(1)} %pad_maximum_fusion.refs_0_), channel_id=1, source_target_pairs={{0,1},{1,0},{2,3},{3,2},{4,5},{5,4},{6,7},{7,6},{8,9},{9,8},{10,11... | collective-permute-start | bytes 3342344 | tf_op jit(solution)/shard_map/ppermute | solution.py:331
  4.0 29.6 %collective-permute-start.4 = (bf16[272,2048]{1,0:T(8,128)(2,1)S(1)}, bf16[272,2048]{1,0:T(8,128)(2,1)S(1)}, u32[]{:S(2)}, u32[]{:S(2)}) collective-permute-start(bf16[272,2048]{1,0:T(8,128)(2,1)S(1)} %pad_maximum_fusion.refs_0_), channel_id=1, source_target_pairs={{0,6},{1,7},{2,0},{3,1},{4,2},{5,3},{6,4},{7,5},{8,14},{9,15},{10,... | collective-permute-start | bytes 3342344 | tf_op jit(solution)/shard_map/ppermute | solution.py:334
  9.5 41.0 %collective-permute-start.7 = (bf16[144,2048]{1,0:T(8,128)(2,1)}, bf16[144,2048]{1,0:T(8,128)(2,1)S(1)}, u32[]{:S(2)}, u32[]{:S(2)}) collective-permute-start(bf16[144,2048]{1,0:T(8,128)(2,1)} %pad_maximum_fusion.1), channel_id=1, source_target_pairs={{0,2},{1,3},{2,4},{3,5},{4,6},{5,7},{6,0},{7,1},{8,10},{9,11},{10,... | collective-permute-start | bytes 1769480 | tf_op jit(solution)/shard_map/ppermute | solution.py:334
  10.2 1.0 copy-start.1
  11.2 1.0 copy-start.2
  12.3 1.0 copy-start.3
  14.0 19.5 %collective-permute-start.1 = (bf16[4,128,512]{2,1,0:T(8,128)(2,1)S(1)}, bf16[4,128,512]{2,1,0:T(8,128)(2,1)S(1)}, u32[]{:S(2)}, u32[]{:S(2)}) collective-permute-start(bf16[4,128,512]{2,1,0:T(8,128)(2,1)S(1)} %get-tuple-element.68), channel_id=1, source_target_pairs={{0,8},{8,0},{16,24},{24,16},{1,9},{9,1},{17,25},{25,17},{2,10},{10... | collective-permute-start | bytes 1572872 | tf_op jit(solution)/shard_map/ppermute | solution.py:139
  15.6 24.9 %collective-permute-start.2 = (bf16[4,128,512]{2,1,0:T(8,128)(2,1)S(1)}, bf16[4,128,512]{2,1,0:T(8,128)(2,1)S(1)}, u32[]{:S(2)}, u32[]{:S(2)}) collective-permute-start(bf16[4,128,512]{2,1,0:T(8,128)(2,1)S(1)} %get-tuple-element.69), channel_id=1, source_target_pairs={{0,16},{8,24},{16,0},{24,8},{1,17},{9,25},{17,1},{25,9},{2,18},{10... | collective-permute-start | bytes 1572872 | tf_op jit(solution)/shard_map/ppermute | solution.py:139
  17.1 23.4 %collective-permute-start.3 = (bf16[4,128,512]{2,1,0:T(8,128)(2,1)S(1)}, bf16[4,128,512]{2,1,0:T(8,128)(2,1)S(1)}, u32[]{:S(2)}, u32[]{:S(2)}) collective-permute-start(bf16[4,128,512]{2,1,0:T(8,128)(2,1)S(1)} %get-tuple-element.70), channel_id=1, source_target_pairs={{0,24},{8,16},{16,8},{24,0},{1,25},{9,17},{17,9},{25,1},{2,26},{10... | collective-permute-start | bytes 1572872 | tf_op jit(solution)/shard_map/ppermute | solution.py:139
  40.5 9.9 %collective-permute-start.6 = (bf16[272,2048]{1,0:T(8,128)(2,1)S(1)}, bf16[272,2048]{1,0:T(8,128)(2,1)S(1)}, u32[]{:S(2)}, u32[]{:S(2)}) collective-permute-start(bf16[272,2048]{1,0:T(8,128)(2,1)S(1)} %collective-permute-done.4.refs_0_), channel_id=1, source_target_pairs={{0,1},{1,0},{2,3},{3,2},{4,5},{5,4},{6,7},{7,6},{8,9},{9,8},{10,11... | collective-permute-start | bytes 3342344 | tf_op jit(solution)/shard_map/ppermute | solution.py:331
  40.5 30.0 %collective-permute-start.5 = (bf16[272,2048]{1,0:T(8,128)(2,1)S(1)}, bf16[272,2048]{1,0:T(8,128)(2,1)S(1)}, u32[]{:S(2)}, u32[]{:S(2)}) collective-permute-start(bf16[272,2048]{1,0:T(8,128)(2,1)S(1)} %collective-permute-done.4.refs_0_), channel_id=1, source_target_pairs={{0,6},{1,7},{2,0},{3,1},{4,2},{5,3},{6,4},{7,5},{8,14},{9,15},{10,... | collective-permute-start | bytes 3342344 | tf_op jit(solution)/shard_map/ppermute | solution.py:334
  50.5 3.8 %collective-permute-start.11 = (bf16[144,2048]{1,0:T(8,128)(2,1)S(1)}, bf16[144,2048]{1,0:T(8,128)(2,1)S(1)}, u32[]{:S(2)}, u32[]{:S(2)}) collective-permute-start(bf16[144,2048]{1,0:T(8,128)(2,1)S(1)} %collective-permute-done.7.refs_2_.refs_0_), channel_id=1, source_target_pairs={{0,1},{1,0},{2,3},{3,2},{4,5},{5,4},{6,7},{7,6},{8,9},{9,8},{10,11... | collective-permute-start | bytes 1769480 | tf_op jit(solution)/shard_map/ppermute | solution.py:331
  50.8 19.8 %collective-permute-start.8 = (bf16[3,128,512]{2,1,0:T(8,128)(2,1)S(1)}, bf16[3,128,512]{2,1,0:T(8,128)(2,1)S(1)}, u32[]{:S(2)}, u32[]{:S(2)}) collective-permute-start(bf16[3,128,512]{2,1,0:T(8,128)(2,1)S(1)} %get-tuple-element.85), channel_id=1, source_target_pairs={{0,8},{8,0},{16,24},{24,16},{1,9},{9,1},{17,25},{25,17},{2,10},{10... | collective-permute-start | bytes 1179656 | tf_op jit(solution)/shard_map/ppermute | solution.py:139
  52.0 18.6 %collective-permute-start.9 = (bf16[3,128,512]{2,1,0:T(8,128)(2,1)S(1)}, bf16[3,128,512]{2,1,0:T(8,128)(2,1)S(1)}, u32[]{:S(2)}, u32[]{:S(2)}) collective-permute-start(bf16[3,128,512]{2,1,0:T(8,128)(2,1)S(1)} %get-tuple-element.86), channel_id=1, source_target_pairs={{0,16},{8,24},{16,0},{24,8},{1,17},{9,25},{17,1},{25,9},{2,18},{10... | collective-permute-start | bytes 1179656 | tf_op jit(solution)/shard_map/ppermute | solution.py:139
  52.8 18.6 %collective-permute-start.10 = (bf16[3,128,512]{2,1,0:T(8,128)(2,1)S(1)}, bf16[3,128,512]{2,1,0:T(8,128)(2,1)S(1)}, u32[]{:S(2)}, u32[]{:S(2)}) collective-permute-start(bf16[3,128,512]{2,1,0:T(8,128)(2,1)S(1)} %get-tuple-element.87), channel_id=1, source_target_pairs={{0,24},{8,16},{16,8},{24,0},{1,25},{9,17},{17,9},{25,1},{2,26},{10... | collective-permute-start | bytes 1179656 | tf_op jit(solution)/shard_map/ppermute | solution.py:139
  71.4 1.9 %collective-permute-start.13 = (bf16[128,2048]{1,0:T(8,128)(2,1)S(1)}, bf16[128,2048]{1,0:T(8,128)(2,1)S(1)}, u32[]{:S(2)}, u32[]{:S(2)}) collective-permute-start(bf16[128,2048]{1,0:T(8,128)(2,1)S(1)} %get-tuple-element.103), channel_id=1, source_target_pairs={{0,1},{1,0},{2,3},{3,2},{4,5},{5,4},{6,7},{7,6},{8,9},{9,8},{10,11... | collective-permute-start | bytes 1572872 | tf_op jit(solution)/shard_map/ppermute | solution.py:331
  71.5 18.3 %collective-permute-start.15 = (bf16[128,2048]{1,0:T(8,128)(2,1)S(1)}, bf16[128,2048]{1,0:T(8,128)(2,1)S(1)}, u32[]{:S(2)}, u32[]{:S(2)}) collective-permute-start(bf16[128,2048]{1,0:T(8,128)(2,1)S(1)} %bitcast.28), channel_id=1, source_target_pairs={{0,2},{1,3},{2,4},{3,5},{4,6},{5,7},{6,0},{7,1},{8,10},{9,11},{10,... | collective-permute-start | bytes 1572872 | tf_op jit(solution)/shard_map/ppermute | solution.py:334
  71.5 3.5 %collective-permute-start.16 = (bf16[272,2048]{1,0:T(8,128)(2,1)S(1)}, bf16[272,2048]{1,0:T(8,128)(2,1)S(1)}, u32[]{:S(2)}, u32[]{:S(2)}) collective-permute-start(bf16[272,2048]{1,0:T(8,128)(2,1)S(1)} %collective-permute-done.5.refs_0_), channel_id=1, source_target_pairs={{0,1},{1,0},{2,3},{3,2},{4,5},{5,4},{6,7},{7,6},{8,9},{9,8},{10,11... | collective-permute-start | bytes 3342344 | tf_op jit(solution)/shard_map/ppermute | solution.py:331
  73.5 19.7 %collective-permute-start.14 = (bf16[64,2048]{1,0:T(8,128)(2,1)S(1)}, bf16[64,2048]{1,0:T(8,128)(2,1)S(1)}, u32[]{:S(2)}, u32[]{:S(2)}) collective-permute-start(bf16[64,2048]{1,0:T(8,128)(2,1)S(1)} %get-tuple-element.123), channel_id=1, source_target_pairs={{0,2},{1,3},{2,4},{3,5},{4,6},{5,7},{6,0},{7,1},{8,10},{9,11},{10,... | collective-permute-start | bytes 786440 | tf_op jit(solution)/shard_map/ppermute | solution.py:334
  93.2 1.9 %collective-permute-start.20 = (bf16[128,2048]{1,0:T(8,128)(2,1)S(1)}, bf16[128,2048]{1,0:T(8,128)(2,1)S(1)}, u32[]{:S(2)}, u32[]{:S(2)}) collective-permute-start(bf16[128,2048]{1,0:T(8,128)(2,1)S(1)} %get-tuple-element.114), channel_id=1, source_target_pairs={{0,1},{1,0},{2,3},{3,2},{4,5},{5,4},{6,7},{7,6},{8,9},{9,8},{10,11... | collective-permute-start | bytes 1572872 | tf_op jit(solution)/shard_map/ppermute | solution.py:331
  93.2 4.7 %collective-permute-start.17 = (bf16[128,2048]{1,0:T(8,128)(2,1)S(1)}, bf16[128,2048]{1,0:T(8,128)(2,1)S(1)}, u32[]{:S(2)}, u32[]{:S(2)}) collective-permute-start(bf16[128,2048]{1,0:T(8,128)(2,1)S(1)} %collective-permute-done.15.refs_1_), channel_id=1, source_target_pairs={{0,1},{1,0},{2,3},{3,2},{4,5},{5,4},{6,7},{7,6},{8,9},{9,8},{10,11... | collective-permute-start | bytes 1572872 | tf_op jit(solution)/shard_map/ppermute | solution.py:331
  93.7 18.0 %collective-permute-start.22 = (bf16[64,2048]{1,0:T(8,128)(2,1)S(1)}, bf16[64,2048]{1,0:T(8,128)(2,1)S(1)}, u32[]{:S(2)}, u32[]{:S(2)}) collective-permute-start(bf16[64,2048]{1,0:T(8,128)(2,1)S(1)} %get-tuple-element.122), channel_id=1, source_target_pairs={{0,2},{1,3},{2,4},{3,5},{4,6},{5,7},{6,0},{7,1},{8,10},{9,11},{10,... | collective-permute-start | bytes 786440 | tf_op jit(solution)/shard_map/ppermute | solution.py:334
  95.2 19.8 %collective-permute-start.21 = (bf16[128,2048]{1,0:T(8,128)(2,1)S(1)}, bf16[128,2048]{1,0:T(8,128)(2,1)S(1)}, u32[]{:S(2)}, u32[]{:S(2)}) collective-permute-start(bf16[128,2048]{1,0:T(8,128)(2,1)S(1)} %add_convert_fusion.2), channel_id=1, source_target_pairs={{0,6},{1,7},{2,0},{3,1},{4,2},{5,3},{6,4},{7,5},{8,14},{9,15},{10,... | collective-permute-start | bytes 1572872 | tf_op jit(solution)/shard_map/ppermute | solution.py:334
  111.0 1.6 %collective-permute-start.18 = (bf16[64,2048]{1,0:T(8,128)(2,1)S(1)}, bf16[64,2048]{1,0:T(8,128)(2,1)S(1)}, u32[]{:S(2)}, u32[]{:S(2)}) collective-permute-start(bf16[64,2048]{1,0:T(8,128)(2,1)S(1)} %get-tuple-element.111), channel_id=1, source_target_pairs={{0,1},{1,0},{2,3},{3,2},{4,5},{5,4},{6,7},{7,6},{8,9},{9,8},{10,11... | collective-permute-start | bytes 786440 | tf_op jit(solution)/shard_map/ppermute | solution.py:331
  111.1 1.9 %collective-permute-start.19 = (bf16[64,2048]{1,0:T(8,128)(2,1)S(1)}, bf16[64,2048]{1,0:T(8,128)(2,1)S(1)}, u32[]{:S(2)}, u32[]{:S(2)}) collective-permute-start(bf16[64,2048]{1,0:T(8,128)(2,1)S(1)} %get-tuple-element.112), channel_id=1, source_target_pairs={{0,1},{1,0},{2,3},{3,2},{4,5},{5,4},{6,7},{7,6},{8,9},{9,8},{10,11... | collective-permute-start | bytes 786440 | tf_op jit(solution)/shard_map/ppermute | solution.py:331
  111.6 5.7 %collective-permute-start.12 = (bf16[128,2048]{1,0:T(8,128)(2,1)S(1)}, bf16[128,2048]{1,0:T(8,128)(2,1)S(1)}, u32[]{:S(2)}, u32[]{:S(2)}) collective-permute-start(bf16[128,2048]{1,0:T(8,128)(2,1)S(1)} %get-tuple-element.101), channel_id=1, source_target_pairs={{0,1},{1,0},{2,3},{3,2},{4,5},{5,4},{6,7},{7,6},{8,9},{9,8},{10,11... | collective-permute-start | bytes 1572872 | tf_op jit(solution)/shard_map/ppermute | solution.py:331
  115.3 13.9 %collective-permute-start.23 = (bf16[128,2048]{1,0:T(8,128)(2,1)S(1)}, bf16[128,2048]{1,0:T(8,128)(2,1)S(1)}, u32[]{:S(2)}, u32[]{:S(2)}) collective-permute-start(bf16[128,2048]{1,0:T(8,128)(2,1)S(1)} %add_convert_fusion.1), channel_id=1, source_target_pairs={{0,6},{1,7},{2,0},{3,1},{4,2},{5,3},{6,4},{7,5},{8,14},{9,15},{10,... | collective-permute-start | bytes 1572872 | tf_op jit(solution)/shard_map/ppermute | solution.py:334

commit v6 on v5

--- a/solution.py
+++ b/solution.py
@@ -12,6 +12,7 @@
 NOTES = 16
 PARTS = 4
 VMEM_BYTES = 36 * 1024 * 1024
+VMEM_PACK = 58 * 1024 * 1024
 VMEM_EXPERTS = 45 * 1024 * 1024
 def cost(units):
     return pl.CostEstimate(
@@ -42,16 +43,16 @@
     return sigmoid * (1.0 + preact * (1.0 - sigmoid))
 
 
-def pack_kernel(group_ref, *refs):
+def pack_kernel(mine_ref, *refs):
     members, blocks = refs[:4], refs[4:]
     width = blocks[0].shape[2]
     for place, block in enumerate(blocks):
-        first = pl.multiple_of(group_ref[place] * width, 128)
+        first = pl.multiple_of((mine_ref[0] ^ place) * width, 128)
         for row, member in enumerate(members):
             block[row] = member[:, pl.ds(first, width)]
 
 
-def pack_groups(group_ids, members, groups):
+def pack_groups(mine, members, groups):
     bins, width = members[0].shape
     block = jax.ShapeDtypeStruct((4, bins, width // groups), jnp.bfloat16)
     return pl.pallas_call(
@@ -60,22 +61,22 @@
         in_specs=[pl.BlockSpec(memory_space=pltpu.SMEM)]
         + [pl.BlockSpec(memory_space=pltpu.VMEM)] * 4,
         out_specs=[pl.BlockSpec(memory_space=pltpu.VMEM)] * groups,
-        compiler_params=pltpu.CompilerParams(vmem_limit_bytes=VMEM_BYTES),
+        compiler_params=pltpu.CompilerParams(vmem_limit_bytes=VMEM_PACK),
         cost_estimate=SMALL,
         name="pack_groups",
-    )(group_ids, *members)
-
-
-def unpack_kernel(group_ref, *refs):
+    )(mine, *members)
+
+
+def unpack_kernel(mine_ref, *refs):
     blocks, outs = refs[:-3], refs[-3:]
     width = blocks[0].shape[2]
     for place, block in enumerate(blocks):
-        first = pl.multiple_of(group_ref[place] * width, 128)
+        first = pl.multiple_of((mine_ref[0] ^ place) * width, 128)
         for row, out in enumerate(outs):
             out[:, pl.ds(first, width)] = block[row]
 
 
-def unpack_groups(group_ids, blocks):
+def unpack_groups(mine, blocks):
     groups = len(blocks)
     bins, width = blocks[0].shape[1], blocks[0].shape[2] * groups
     out = jax.ShapeDtypeStruct((bins, width), jnp.bfloat16)
@@ -88,7 +89,7 @@
         compiler_params=pltpu.CompilerParams(vmem_limit_bytes=VMEM_BYTES),
         cost_estimate=SMALL,
         name="unpack_groups",
-    )(group_ids, *blocks)
+    )(mine, *blocks)
 
 
 def heads_kernel(*refs):
@@ -354,10 +355,9 @@
     own = make_block(moe_input[0], out_grad[0], routes[0], route_gates[0])
     left, right_rows = hop(own, -1), hop(own[: bins + NOTES], 1)
     own_pair = pair(own)
-    table = [[group ^ place for place in range(groups)] for group in range(groups)]
-    group_ids = jnp.asarray(table, jnp.int32)[lax.axis_index("ctx")]
+    mine = lax.axis_index("ctx").astype(jnp.int32).reshape(1)
     rows = (queries[0], key_rows[0], value_rows[0], out_grad[0])
-    packed = pack_groups(group_ids, rows, groups)
+    packed = pack_groups(mine, rows, groups)
     own_pair, packed = barrier((own_pair, packed))
     heads = exchange(packed)
     kept, give, _ = work(own_pair, OWN_COST)
@@ -398,7 +398,7 @@
         carried = add_up(kept, joined(given), carried)
     total = add_up(total, joined(left_halves))
     carried = hop(carried.astype(jnp.bfloat16), -1)
-    outs = unpack_groups(group_ids, results)
+    outs = unpack_groups(mine, results)
     total = add_up(total, carried).astype(jnp.bfloat16)
     return tuple(out[None] for out in outs) + (total[None],)
 

time: 131 us -> 130 us (level)
  local copies, waits for them, and re-layouts: 3.86 us -> 0.06 us
  Pallas kernels: 67.5 us -> 69.3 us
    ppermute x8, waiting for transfers between devices: 18.9 us -> 23.8 us  [hop(): lax.ppermute(block, 'exp', [(i, (i + 2 * step) % members) for i in range(...]
    unnamed x10 -> x6, local copies, waits for them, and re-layouts: 3.14 us -> 0.02 us
    ppermute x6, waiting for transfers between devices: 7.87 us -> 4.85 us  [exchange(): lax.ppermute(blocks[place], 'ctx', [(i, i ^ place) for i in range(groups)])]
    pallas_call x1, Pallas kernels: 0.7 us -> 2.99 us  [pack_groups(): pl.pallas_call(pack_kernel, out_shape=[block] * groups, in_specs=[pl.Bloc...]
  transfers between devices with their start and end apart: 24 -> 24, of which waited for: 12 -> 11; matrix products, arithmetic and copies ran while one was open for 2% -> 0% of each run, Pallas kernels for 52% -> 54%
where the time goes in v6:
time: 130 us; the launch traced here: 129 us
  Pallas kernels  69.3 us (53%)
  waiting for transfers between devices  33.5 us (26%)
  starting transfers between devices  21.4 us (16%)
  other arithmetic  4.39 us (3%)
    pallas_call x4, Pallas kernels, expert_back(): pl.pallas_call(functools.partial(expert_kernel, layout, len(ahead), later...  58.7 us
    ppermute x8, waiting for transfers between devices, hop(): lax.ppermute(block, 'exp', [(i, (i + 2 * step) % members) for i in range(...  23.8 us
    ppermute x8, starting transfers between devices, hop(): lax.ppermute(block, 'exp', [(i, (i + 2 * step) % members) for i in range(...  12.2 us
    ppermute x6, starting transfers between devices, exchange(): lax.ppermute(blocks[place], 'ctx', [(i, i ^ place) for i in range(groups)])  6.98 us
    pallas_call x1, Pallas kernels, heads_back(): pl.pallas_call(heads_kernel, grid=(heads,), out_shape=[jax.ShapeDtypeStru...  6.37 us
    ppermute x6, waiting for transfers between devices, exchange(): lax.ppermute(blocks[place], 'ctx', [(i, i ^ place) for i in range(groups)])  4.85 us
    ppermute x10, waiting for transfers between devices, swap(): return lax.ppermute(block, 'exp', [(i, i ^ 1) for i in range(members)])  4.8 us
    pallas_call x1, Pallas kernels, pack_groups(): pl.pallas_call(pack_kernel, out_shape=[block] * groups, in_specs=[pl.Bloc...  2.99 us
  transfers between devices with their start and end apart: 24, of which 11 were waited for; matrix products, arithmetic and copies ran while one was open for 0% of the time, Pallas kernels for 54%

profile of v6, /device:TPU:0, one launch (start us, length us, event | category | flops | bytes accessed | tf_op | source)
XLA Modules:
  0.0 129.4 jit_solution(5696688036451834028)
XLA Ops:
  0.6 0.0 copy-start.2
  0.6 0.7 fusion.10
  1.4 0.7 reduce-precision_convert_fusion.1
  2.1 1.3 pad_maximum_fusion.refs_0_
  3.4 0.5 collective-permute-start
  3.9 4.7 %collective-permute-start.4 = (bf16[272,2048]{1,0:T(8,128)(2,1)S(1)}, bf16[272,2048]{1,0:T(8,128)(2,1)S(1)}, u32[]{:S(2)}, u32[]{:S(2)}) collective-permute-start(bf16[272,2048]{1,0:T(8,128)(2,1)S(1)} %pad_maximum_fusion.refs_0_), channel_id=1, source_target_pairs={{0,6},{1,7},{2,0},{3,1},{4,2},{5,3},{6,4},{7,5},{8,14},{9,15},{10,... | collective-permute-start | bytes 3342344 | tf_op jit(solution)/shard_map/ppermute | solution.py:335
  8.6 0.1 collective-permute-start.7
  8.7 3.0 %pack_groups.1 = (bf16[4,128,512]{2,1,0:T(8,128)(2,1)}, bf16[4,128,512]{2,1,0:T(8,128)(2,1)}, bf16[4,128,512]{2,1,0:T(8,128)(2,1)}, bf16[4,128,512]{2,1,0:T(8,128)(2,1)}) custom-call(s32[1]{0:T(128)} %bitcast.mine_ref, bf16[128,2048]{1,0:T(8,128)(2,1)} %bitcast.30, bf16[128,2048]{1,0:T(8,128)(2,1)} %bitcast.31, bf16[128,2048]{1,0:T(8,128)(2,1)} %bitcast.32, ...), custom_call_target="tpu_custom_call" | custom-call | tf_op jit(solution)/shard_map/pack_groups/pallas_call | solution.py:58
  11.7 1.5 %collective-permute-start.1 = (bf16[4,128,512]{2,1,0:T(8,128)(2,1)}, bf16[4,128,512]{2,1,0:T(8,128)(2,1)S(1)}, u32[]{:S(2)}, u32[]{:S(2)}) collective-permute-start(bf16[4,128,512]{2,1,0:T(8,128)(2,1)} %get-tuple-element.68), channel_id=1, source_target_pairs={{0,8},{8,0},{16,24},{24,16},{1,9},{9,1},{17,25},{25,17},{2,10},{10... | collective-permute-start | bytes 1572872 | tf_op jit(solution)/shard_map/ppermute | solution.py:140
  13.2 1.5 %collective-permute-start.2 = (bf16[4,128,512]{2,1,0:T(8,128)(2,1)}, bf16[4,128,512]{2,1,0:T(8,128)(2,1)S(1)}, u32[]{:S(2)}, u32[]{:S(2)}) collective-permute-start(bf16[4,128,512]{2,1,0:T(8,128)(2,1)} %get-tuple-element.69), channel_id=1, source_target_pairs={{0,16},{8,24},{16,0},{24,8},{1,17},{9,25},{17,1},{25,9},{2,18},{10... | collective-permute-start | bytes 1572872 | tf_op jit(solution)/shard_map/ppermute | solution.py:140
  14.7 0.5 collective-permute-start.3
  15.2 15.7 %expert_back.4 = (bf16[128,2048]{1,0:T(8,128)(2,1)S(1)}, bf16[128,2048]{1,0:T(8,128)(2,1)S(1)}) custom-call(s32[1]{0:T(128)} %bitcast.11.base_ref, bf16[272,2048]{1,0:T(8,128)(2,1)S(1)} %pad_maximum_fusion.refs_0_, bf16[272,2048]{1,0:T(8,128)(2,1)} %collective-permute-done.refs_1_, bf16[4,2048,768]{2,1,0:T(8,128)(2,1)} %refs_5_.3, bf16[4,768,2048]{2,1,0:T(8,128)(2,1)} %refs_6_.1), custom_call_target="tpu_custom_call" | custom-call | flops 30000001024 | bytes 30000000 | tf_op jit(solution)/shard_map/expert_back/pallas_call | solution.py:296
  30.8 2.6 %collective-permute-done.4.refs_0_ = bf16[272,2048]{1,0:T(8,128)(2,1)S(1)} collective-permute-done((bf16[272,2048]{1,0:T(8,128)(2,1)S(1)}, bf16[272,2048]{1,0:T(8,128)(2,1)S(1)}, u32[]{:S(2)}, u32[]{:S(2)}) %collective-permute-start.4) | collective-permute-done | bytes 1114144 | tf_op jit(solution)/shard_map/ppermute | solution.py:335
  33.5 4.8 %collective-permute-done.2.refs_2_ = bf16[4,128,512]{2,1,0:T(8,128)(2,1)S(1)} collective-permute-done((bf16[4,128,512]{2,1,0:T(8,128)(2,1)}, bf16[4,128,512]{2,1,0:T(8,128)(2,1)S(1)}, u32[]{:S(2)}, u32[]{:S(2)}) %collective-permute-start.2) | collective-permute-done | bytes 524320 | tf_op jit(solution)/shard_map/ppermute | solution.py:140
  38.3 3.5 %collective-permute-start.5 = (bf16[272,2048]{1,0:T(8,128)(2,1)S(1)}, bf16[272,2048]{1,0:T(8,128)(2,1)S(1)}, u32[]{:S(2)}, u32[]{:S(2)}) collective-permute-start(bf16[272,2048]{1,0:T(8,128)(2,1)S(1)} %collective-permute-done.4.refs_0_), channel_id=1, source_target_pairs={{0,6},{1,7},{2,0},{3,1},{4,2},{5,3},{6,4},{7,5},{8,14},{9,15},{10,... | collective-permute-start | bytes 3342344 | tf_op jit(solution)/shard_map/ppermute | solution.py:335
  41.9 6.4 %heads_back.1 = (bf16[3,128,512]{2,1,0:T(8,128)(2,1)S(1)}, bf16[3,128,512]{2,1,0:T(8,128)(2,1)S(1)}, bf16[3,128,512]{2,1,0:T(8,128)(2,1)S(1)}, bf16[3,128,512]{2,1,0:T(8,128)(2,1)S(1)}) custom-call(bf16[4,128,512]{2,1,0:T(8,128)(2,1)S(1)} %copy-done, bf16[4,128,512]{2,1,0:T(8,128)(2,1)S(1)} %collective-permute-done.1.refs_1_, ...), custom_call_target="tpu_custom_call" | custom-call | flops 30000001024 | bytes 30000000 | tf_op jit(solution)/shard_map/heads_back/pallas_call | solution.py:125
  48.2 0.0 copy-start.1
  48.3 0.3 collective-permute-start.11
  48.6 1.2 collective-permute-start.8
  49.8 0.8 collective-permute-start.9
  50.6 1.4 %collective-permute-start.10 = (bf16[3,128,512]{2,1,0:T(8,128)(2,1)S(1)}, bf16[3,128,512]{2,1,0:T(8,128)(2,1)S(1)}, u32[]{:S(2)}, u32[]{:S(2)}) collective-permute-start(bf16[3,128,512]{2,1,0:T(8,128)(2,1)S(1)} %get-tuple-element.87), channel_id=1, source_target_pairs={{0,24},{8,16},{16,8},{24,0},{1,25},{9,17},{17,9},{25,1},{2,26},{10... | collective-permute-start | bytes 1179656 | tf_op jit(solution)/shard_map/ppermute | solution.py:140
  52.0 15.1 %expert_back.5 = (bf16[128,2048]{1,0:T(8,128)(2,1)S(1)}, bf16[128,2048]{1,0:T(8,128)(2,1)S(1)}, f32[192,768]{1,0:T(8,128)S(1)}) custom-call(s32[1]{0:T(128)} %bitcast.11.base_ref, bf16[272,2048]{1,0:T(8,128)(2,1)S(1)} %collective-permute-done.4.refs_0_, bf16[272,2048]{1,0:T(8,128)(2,1)S(1)} %collective-permute-done.6.refs_1_, ...), custom_call_target="tpu_custom_call" | custom-call | tf_op jit(solution)/shard_map/expert_back/pallas_call | solution.py:296
  67.2 3.3 %collective-permute-done.5.refs_0_ = bf16[272,2048]{1,0:T(8,128)(2,1)S(1)} collective-permute-done((bf16[272,2048]{1,0:T(8,128)(2,1)S(1)}, bf16[272,2048]{1,0:T(8,128)(2,1)S(1)}, u32[]{:S(2)}, u32[]{:S(2)}) %collective-permute-start.5) | collective-permute-done | bytes 1114144 | tf_op jit(solution)/shard_map/ppermute | solution.py:335
  70.5 0.1 collective-permute-start.13
  70.6 0.5 collective-permute-start.15
  71.1 0.2 collective-permute-start.16
  71.3 1.2 collective-permute-done.13
  72.5 0.1 add_convert_fusion.3
  72.7 0.5 collective-permute-start.14
  73.2 0.9 collective-permute-done.16.refs_1_
  74.1 14.8 %expert_back.6 = (bf16[128,2048]{1,0:T(8,128)(2,1)S(1)}, bf16[128,2048]{1,0:T(8,128)(2,1)S(1)}) custom-call(s32[1]{0:T(128)} %bitcast.11.base_ref, bf16[272,2048]{1,0:T(8,128)(2,1)S(1)} %collective-permute-done.5.refs_0_, bf16[272,2048]{1,0:T(8,128)(2,1)S(1)} %collective-permute-done.16.refs_1_, bf16[4,2048,768]{2,1,0:T(8,128)(2,1)} %refs_5_.3, ...), custom_call_target="tpu_custom_call" | custom-call | tf_op jit(solution)/shard_map/expert_back/pallas_call | solution.py:296
  88.9 3.4 %collective-permute-done.14 = bf16[64,2048]{1,0:T(8,128)(2,1)S(1)} collective-permute-done((bf16[64,2048]{1,0:T(8,128)(2,1)S(1)}, bf16[64,2048]{1,0:T(8,128)(2,1)S(1)}, u32[]{:S(2)}, u32[]{:S(2)}) %collective-permute-start.14) | collective-permute-done | bytes 262176 | tf_op jit(solution)/shard_map/ppermute | solution.py:335
  92.3 0.5 collective-permute-start.17
  92.8 1.4 %collective-permute-done.20 = bf16[128,2048]{1,0:T(8,128)(2,1)S(1)} collective-permute-done((bf16[128,2048]{1,0:T(8,128)(2,1)S(1)}, bf16[128,2048]{1,0:T(8,128)(2,1)S(1)}, u32[]{:S(2)}, u32[]{:S(2)}) %collective-permute-start.20) | collective-permute-done | bytes 524320 | tf_op jit(solution)/shard_map/ppermute | solution.py:332
  94.2 0.1 add_convert_fusion.2
  94.4 2.7 %collective-permute-start.21 = (bf16[128,2048]{1,0:T(8,128)(2,1)S(1)}, bf16[128,2048]{1,0:T(8,128)(2,1)S(1)}, u32[]{:S(2)}, u32[]{:S(2)}) collective-permute-start(bf16[128,2048]{1,0:T(8,128)(2,1)S(1)} %add_convert_fusion.2), channel_id=1, source_target_pairs={{0,6},{1,7},{2,0},{3,1},{4,2},{5,3},{6,4},{7,5},{8,14},{9,15},{10,... | collective-permute-start | bytes 1572872 | tf_op jit(solution)/shard_map/ppermute | solution.py:335
  97.0 13.1 %expert_back.7 = (bf16[128,2048]{1,0:T(8,128)(2,1)S(1)}, bf16[64,2048]{1,0:T(8,128)(2,1)S(1)}, bf16[64,2048]{1,0:T(8,128)(2,1)S(1)}) custom-call(s32[1]{0:T(128)} %bitcast.11.base_ref, bf16[144,2048]{1,0:T(8,128)(2,1)S(1)} %collective-permute-done.7.refs_2_.refs_0_, bf16[128,2048]{1,0:T(8,128)(2,1)S(1)} %collective-permute-done.15.refs_1_, ...), custom_call_target="tpu_custom_call" | custom-call | flops 30000001024 | bytes 30000000 | tf_op jit(solution)/shard_map/expert_back/pallas_call | solution.py:296
  110.1 0.1 collective-permute-start.18
  110.2 0.5 collective-permute-start.19
  110.7 0.1 collective-permute-start.12
  110.8 0.9 collective-permute-done.18
  111.7 0.4 collective-permute-done.19
  112.1 2.1 %collective-permute-done.21 = bf16[128,2048]{1,0:T(8,128)(2,1)S(1)} collective-permute-done((bf16[128,2048]{1,0:T(8,128)(2,1)S(1)}, bf16[128,2048]{1,0:T(8,128)(2,1)S(1)}, u32[]{:S(2)}, u32[]{:S(2)}) %collective-permute-start.21) | collective-permute-done | bytes 524320 | tf_op jit(solution)/shard_map/ppermute | solution.py:335
  114.2 0.2 add_convert_fusion.1
  114.4 0.2 collective-permute-start.23
  114.7 1.3 unpack_groups.1
  115.9 12.4 %collective-permute-done.23 = bf16[128,2048]{1,0:T(8,128)(2,1)S(1)} collective-permute-done((bf16[128,2048]{1,0:T(8,128)(2,1)S(1)}, bf16[128,2048]{1,0:T(8,128)(2,1)S(1)}, u32[]{:S(2)}, u32[]{:S(2)}) %collective-permute-start.23) | collective-permute-done | bytes 524320 | tf_op jit(solution)/shard_map/ppermute | solution.py:335
  128.3 1.1 fusion
  (23 shorter events, 0.1 us)
Async XLA Ops:
  0.6 7.9 %copy-start.2 = (bf16[1,128,2048]{2,1,0:T(8,128)(2,1)S(1)}, bf16[1,128,2048]{2,1,0:T(8,128)(2,1)}, u32[]{:S(2)}) copy-start(bf16[1,128,2048]{2,1,0:T(8,128)(2,1)} %param.13) | copy-start | bytes 1572868
  3.4 8.3 %collective-permute-start = (bf16[272,2048]{1,0:T(8,128)(2,1)S(1)}, bf16[272,2048]{1,0:T(8,128)(2,1)}, u32[]{:S(2)}, u32[]{:S(2)}) collective-permute-start(bf16[272,2048]{1,0:T(8,128)(2,1)S(1)} %pad_maximum_fusion.refs_0_), channel_id=1, source_target_pairs={{0,1},{1,0},{2,3},{3,2},{4,5},{5,4},{6,7},{7,6},{8,9},{9,8},{10,11... | collective-permute-start | bytes 3342344 | tf_op jit(solution)/shard_map/ppermute | solution.py:332
  3.9 29.6 %collective-permute-start.4 = (bf16[272,2048]{1,0:T(8,128)(2,1)S(1)}, bf16[272,2048]{1,0:T(8,128)(2,1)S(1)}, u32[]{:S(2)}, u32[]{:S(2)}) collective-permute-start(bf16[272,2048]{1,0:T(8,128)(2,1)S(1)} %pad_maximum_fusion.refs_0_), channel_id=1, source_target_pairs={{0,6},{1,7},{2,0},{3,1},{4,2},{5,3},{6,4},{7,5},{8,14},{9,15},{10,... | collective-permute-start | bytes 3342344 | tf_op jit(solution)/shard_map/ppermute | solution.py:335
  8.6 39.6 %collective-permute-start.7 = (bf16[144,2048]{1,0:T(8,128)(2,1)S(1)}, bf16[144,2048]{1,0:T(8,128)(2,1)S(1)}, u32[]{:S(2)}, u32[]{:S(2)}) collective-permute-start(bf16[144,2048]{1,0:T(8,128)(2,1)S(1)} %pad_maximum_fusion.1), channel_id=1, source_target_pairs={{0,2},{1,3},{2,4},{3,5},{4,6},{5,7},{6,0},{7,1},{8,10},{9,11},{10,... | collective-permute-start | bytes 1769480 | tf_op jit(solution)/shard_map/ppermute | solution.py:335
  11.7 21.8 %collective-permute-start.1 = (bf16[4,128,512]{2,1,0:T(8,128)(2,1)}, bf16[4,128,512]{2,1,0:T(8,128)(2,1)S(1)}, u32[]{:S(2)}, u32[]{:S(2)}) collective-permute-start(bf16[4,128,512]{2,1,0:T(8,128)(2,1)} %get-tuple-element.68), channel_id=1, source_target_pairs={{0,8},{8,0},{16,24},{24,16},{1,9},{9,1},{17,25},{25,17},{2,10},{10... | collective-permute-start | bytes 1572872 | tf_op jit(solution)/shard_map/ppermute | solution.py:140
  13.2 25.2 %collective-permute-start.2 = (bf16[4,128,512]{2,1,0:T(8,128)(2,1)}, bf16[4,128,512]{2,1,0:T(8,128)(2,1)S(1)}, u32[]{:S(2)}, u32[]{:S(2)}) collective-permute-start(bf16[4,128,512]{2,1,0:T(8,128)(2,1)} %get-tuple-element.69), channel_id=1, source_target_pairs={{0,16},{8,24},{16,0},{24,8},{1,17},{9,25},{17,1},{25,9},{2,18},{10... | collective-permute-start | bytes 1572872 | tf_op jit(solution)/shard_map/ppermute | solution.py:140
  14.7 23.6 %collective-permute-start.3 = (bf16[4,128,512]{2,1,0:T(8,128)(2,1)}, bf16[4,128,512]{2,1,0:T(8,128)(2,1)S(1)}, u32[]{:S(2)}, u32[]{:S(2)}) collective-permute-start(bf16[4,128,512]{2,1,0:T(8,128)(2,1)} %get-tuple-element.70), channel_id=1, source_target_pairs={{0,24},{8,16},{16,8},{24,0},{1,25},{9,17},{17,9},{25,1},{2,26},{10... | collective-permute-start | bytes 1572872 | tf_op jit(solution)/shard_map/ppermute | solution.py:140
  15.2 26.7 %copy-start = (bf16[4,128,512]{2,1,0:T(8,128)(2,1)S(1)}, bf16[4,128,512]{2,1,0:T(8,128)(2,1)}, u32[]{:S(2)}) copy-start(bf16[4,128,512]{2,1,0:T(8,128)(2,1)} %get-tuple-element.76.refs_0_) | copy-start | bytes 1572868
  38.3 9.9 %collective-permute-start.6 = (bf16[272,2048]{1,0:T(8,128)(2,1)S(1)}, bf16[272,2048]{1,0:T(8,128)(2,1)S(1)}, u32[]{:S(2)}, u32[]{:S(2)}) collective-permute-start(bf16[272,2048]{1,0:T(8,128)(2,1)S(1)} %collective-permute-done.4.refs_0_), channel_id=1, source_target_pairs={{0,1},{1,0},{2,3},{3,2},{4,5},{5,4},{6,7},{7,6},{8,9},{9,8},{10,11... | collective-permute-start | bytes 3342344 | tf_op jit(solution)/shard_map/ppermute | solution.py:332
  38.3 32.2 %collective-permute-start.5 = (bf16[272,2048]{1,0:T(8,128)(2,1)S(1)}, bf16[272,2048]{1,0:T(8,128)(2,1)S(1)}, u32[]{:S(2)}, u32[]{:S(2)}) collective-permute-start(bf16[272,2048]{1,0:T(8,128)(2,1)S(1)} %collective-permute-done.4.refs_0_), channel_id=1, source_target_pairs={{0,6},{1,7},{2,0},{3,1},{4,2},{5,3},{6,4},{7,5},{8,14},{9,15},{10,... | collective-permute-start | bytes 3342344 | tf_op jit(solution)/shard_map/ppermute | solution.py:335
  48.2 22.4 %copy-start.1 = (bf16[1,128,2048]{2,1,0:T(8,128)(2,1)S(1)}, bf16[1,128,2048]{2,1,0:T(8,128)(2,1)}, u32[]{:S(2)}) copy-start(bf16[1,128,2048]{2,1,0:T(8,128)(2,1)} %param.12) | copy-start | bytes 1572868
  48.3 3.8 %collective-permute-start.11 = (bf16[144,2048]{1,0:T(8,128)(2,1)S(1)}, bf16[144,2048]{1,0:T(8,128)(2,1)S(1)}, u32[]{:S(2)}, u32[]{:S(2)}) collective-permute-start(bf16[144,2048]{1,0:T(8,128)(2,1)S(1)} %collective-permute-done.7.refs_2_.refs_0_), channel_id=1, source_target_pairs={{0,1},{1,0},{2,3},{3,2},{4,5},{5,4},{6,7},{7,6},{8,9},{9,8},{10,11... | collective-permute-start | bytes 1769480 | tf_op jit(solution)/shard_map/ppermute | solution.py:332
  48.6 21.9 %collective-permute-start.8 = (bf16[3,128,512]{2,1,0:T(8,128)(2,1)S(1)}, bf16[3,128,512]{2,1,0:T(8,128)(2,1)S(1)}, u32[]{:S(2)}, u32[]{:S(2)}) collective-permute-start(bf16[3,128,512]{2,1,0:T(8,128)(2,1)S(1)} %get-tuple-element.85), channel_id=1, source_target_pairs={{0,8},{8,0},{16,24},{24,16},{1,9},{9,1},{17,25},{25,17},{2,10},{10... | collective-permute-start | bytes 1179656 | tf_op jit(solution)/shard_map/ppermute | solution.py:140
  49.8 20.7 %collective-permute-start.9 = (bf16[3,128,512]{2,1,0:T(8,128)(2,1)S(1)}, bf16[3,128,512]{2,1,0:T(8,128)(2,1)S(1)}, u32[]{:S(2)}, u32[]{:S(2)}) collective-permute-start(bf16[3,128,512]{2,1,0:T(8,128)(2,1)S(1)} %get-tuple-element.86), channel_id=1, source_target_pairs={{0,16},{8,24},{16,0},{24,8},{1,17},{9,25},{17,1},{25,9},{2,18},{10... | collective-permute-start | bytes 1179656 | tf_op jit(solution)/shard_map/ppermute | solution.py:140
  50.6 19.9 %collective-permute-start.10 = (bf16[3,128,512]{2,1,0:T(8,128)(2,1)S(1)}, bf16[3,128,512]{2,1,0:T(8,128)(2,1)S(1)}, u32[]{:S(2)}, u32[]{:S(2)}) collective-permute-start(bf16[3,128,512]{2,1,0:T(8,128)(2,1)S(1)} %get-tuple-element.87), channel_id=1, source_target_pairs={{0,24},{8,16},{16,8},{24,0},{1,25},{9,17},{17,9},{25,1},{2,26},{10... | collective-permute-start | bytes 1179656 | tf_op jit(solution)/shard_map/ppermute | solution.py:140
  70.5 2.0 %collective-permute-start.13 = (bf16[128,2048]{1,0:T(8,128)(2,1)S(1)}, bf16[128,2048]{1,0:T(8,128)(2,1)S(1)}, u32[]{:S(2)}, u32[]{:S(2)}) collective-permute-start(bf16[128,2048]{1,0:T(8,128)(2,1)S(1)} %get-tuple-element.103), channel_id=1, source_target_pairs={{0,1},{1,0},{2,3},{3,2},{4,5},{5,4},{6,7},{7,6},{8,9},{9,8},{10,11... | collective-permute-start | bytes 1572872 | tf_op jit(solution)/shard_map/ppermute | solution.py:332
  70.6 18.2 %collective-permute-start.15 = (bf16[128,2048]{1,0:T(8,128)(2,1)S(1)}, bf16[128,2048]{1,0:T(8,128)(2,1)S(1)}, u32[]{:S(2)}, u32[]{:S(2)}) collective-permute-start(bf16[128,2048]{1,0:T(8,128)(2,1)S(1)} %bitcast.27), channel_id=1, source_target_pairs={{0,2},{1,3},{2,4},{3,5},{4,6},{5,7},{6,0},{7,1},{8,10},{9,11},{10,... | collective-permute-start | bytes 1572872 | tf_op jit(solution)/shard_map/ppermute | solution.py:335
  71.1 2.9 %collective-permute-start.16 = (bf16[272,2048]{1,0:T(8,128)(2,1)S(1)}, bf16[272,2048]{1,0:T(8,128)(2,1)S(1)}, u32[]{:S(2)}, u32[]{:S(2)}) collective-permute-start(bf16[272,2048]{1,0:T(8,128)(2,1)S(1)} %collective-permute-done.5.refs_0_), channel_id=1, source_target_pairs={{0,1},{1,0},{2,3},{3,2},{4,5},{5,4},{6,7},{7,6},{8,9},{9,8},{10,11... | collective-permute-start | bytes 3342344 | tf_op jit(solution)/shard_map/ppermute | solution.py:332
  72.7 19.7 %collective-permute-start.14 = (bf16[64,2048]{1,0:T(8,128)(2,1)S(1)}, bf16[64,2048]{1,0:T(8,128)(2,1)S(1)}, u32[]{:S(2)}, u32[]{:S(2)}) collective-permute-start(bf16[64,2048]{1,0:T(8,128)(2,1)S(1)} %get-tuple-element.123), channel_id=1, source_target_pairs={{0,2},{1,3},{2,4},{3,5},{4,6},{5,7},{6,0},{7,1},{8,10},{9,11},{10,... | collective-permute-start | bytes 786440 | tf_op jit(solution)/shard_map/ppermute | solution.py:335
  92.3 1.9 %collective-permute-start.20 = (bf16[128,2048]{1,0:T(8,128)(2,1)S(1)}, bf16[128,2048]{1,0:T(8,128)(2,1)S(1)}, u32[]{:S(2)}, u32[]{:S(2)}) collective-permute-start(bf16[128,2048]{1,0:T(8,128)(2,1)S(1)} %get-tuple-element.114), channel_id=1, source_target_pairs={{0,1},{1,0},{2,3},{3,2},{4,5},{5,4},{6,7},{7,6},{8,9},{9,8},{10,11... | collective-permute-start | bytes 1572872 | tf_op jit(solution)/shard_map/ppermute | solution.py:332
  92.3 4.7 %collective-permute-start.17 = (bf16[128,2048]{1,0:T(8,128)(2,1)S(1)}, bf16[128,2048]{1,0:T(8,128)(2,1)S(1)}, u32[]{:S(2)}, u32[]{:S(2)}) collective-permute-start(bf16[128,2048]{1,0:T(8,128)(2,1)S(1)} %collective-permute-done.15.refs_1_), channel_id=1, source_target_pairs={{0,1},{1,0},{2,3},{3,2},{4,5},{5,4},{6,7},{7,6},{8,9},{9,8},{10,11... | collective-permute-start | bytes 1572872 | tf_op jit(solution)/shard_map/ppermute | solution.py:332
  92.8 18.0 %collective-permute-start.22 = (bf16[64,2048]{1,0:T(8,128)(2,1)S(1)}, bf16[64,2048]{1,0:T(8,128)(2,1)S(1)}, u32[]{:S(2)}, u32[]{:S(2)}) collective-permute-start(bf16[64,2048]{1,0:T(8,128)(2,1)S(1)} %get-tuple-element.122), channel_id=1, source_target_pairs={{0,2},{1,3},{2,4},{3,5},{4,6},{5,7},{6,0},{7,1},{8,10},{9,11},{10,... | collective-permute-start | bytes 786440 | tf_op jit(solution)/shard_map/ppermute | solution.py:335
  94.4 19.8 %collective-permute-start.21 = (bf16[128,2048]{1,0:T(8,128)(2,1)S(1)}, bf16[128,2048]{1,0:T(8,128)(2,1)S(1)}, u32[]{:S(2)}, u32[]{:S(2)}) collective-permute-start(bf16[128,2048]{1,0:T(8,128)(2,1)S(1)} %add_convert_fusion.2), channel_id=1, source_target_pairs={{0,6},{1,7},{2,0},{3,1},{4,2},{5,3},{6,4},{7,5},{8,14},{9,15},{10,... | collective-permute-start | bytes 1572872 | tf_op jit(solution)/shard_map/ppermute | solution.py:335
  110.1 1.6 %collective-permute-start.18 = (bf16[64,2048]{1,0:T(8,128)(2,1)S(1)}, bf16[64,2048]{1,0:T(8,128)(2,1)S(1)}, u32[]{:S(2)}, u32[]{:S(2)}) collective-permute-start(bf16[64,2048]{1,0:T(8,128)(2,1)S(1)} %get-tuple-element.111), channel_id=1, source_target_pairs={{0,1},{1,0},{2,3},{3,2},{4,5},{5,4},{6,7},{7,6},{8,9},{9,8},{10,11... | collective-permute-start | bytes 786440 | tf_op jit(solution)/shard_map/ppermute | solution.py:332
  110.2 1.9 %collective-permute-start.19 = (bf16[64,2048]{1,0:T(8,128)(2,1)S(1)}, bf16[64,2048]{1,0:T(8,128)(2,1)S(1)}, u32[]{:S(2)}, u32[]{:S(2)}) collective-permute-start(bf16[64,2048]{1,0:T(8,128)(2,1)S(1)} %get-tuple-element.112), channel_id=1, source_target_pairs={{0,1},{1,0},{2,3},{3,2},{4,5},{5,4},{6,7},{7,6},{8,9},{9,8},{10,11... | collective-permute-start | bytes 786440 | tf_op jit(solution)/shard_map/ppermute | solution.py:332
  110.7 5.2 %collective-permute-start.12 = (bf16[128,2048]{1,0:T(8,128)(2,1)S(1)}, bf16[128,2048]{1,0:T(8,128)(2,1)S(1)}, u32[]{:S(2)}, u32[]{:S(2)}) collective-permute-start(bf16[128,2048]{1,0:T(8,128)(2,1)S(1)} %get-tuple-element.101), channel_id=1, source_target_pairs={{0,1},{1,0},{2,3},{3,2},{4,5},{5,4},{6,7},{7,6},{8,9},{9,8},{10,11... | collective-permute-start | bytes 1572872 | tf_op jit(solution)/shard_map/ppermute | solution.py:332
  114.4 13.9 %collective-permute-start.23 = (bf16[128,2048]{1,0:T(8,128)(2,1)S(1)}, bf16[128,2048]{1,0:T(8,128)(2,1)S(1)}, u32[]{:S(2)}, u32[]{:S(2)}) collective-permute-start(bf16[128,2048]{1,0:T(8,128)(2,1)S(1)} %add_convert_fusion.1), channel_id=1, source_target_pairs={{0,6},{1,7},{2,0},{3,1},{4,2},{5,3},{6,4},{7,5},{8,14},{9,15},{10,... | collective-permute-start | bytes 1572872 | tf_op jit(solution)/shard_map/ppermute | solution.py:335

commit v7 on v6

--- a/solution.py
+++ b/solution.py
@@ -199,7 +199,7 @@
     (keep_ref,) = take(1)
     give_refs = take(pieces)
     ahead_slopes = take(1 if ahead else 0)
-    pick_ref, token_rows, gated_rows, back_rows, up_ref, down_ref, sems = take(7)
+    pick_ref, token_rows, gated_rows, back_columns, up_ref, down_ref, sems = take(7)
     ahead_picks = take(1 if ahead else 0)
     bins = keep_ref.shape[0]
     slots = sources * CAP
@@ -268,11 +268,14 @@
             more = ahead * CAP
             ahead_slopes[0][pl.ds(pl.multiple_of(expert * more, 16), more), :] = slopes[slots:]
             slopes = slopes[:slots]
-        back_grad = dot_nt(gated_rows[rows, :], down_ref[place])
-        hidden_grad = (back_grad * slopes).astype(jnp.bfloat16)
-        back_rows[rows, :] = dot_nt(hidden_grad, up_ref[place]).astype(jnp.bfloat16)
-
-    sums = dot_tn(pick_ref[...], back_rows[...])
+        back_grad = dot_nt(down_ref[place], gated_rows[rows, :])
+        hidden_grad = (back_grad * slopes.T).astype(jnp.bfloat16)
+        back_columns[expert] = dot_nn(up_ref[place], hidden_grad).astype(jnp.bfloat16)
+
+    columns = jnp.concatenate([back_columns[local] for local in range(experts)], axis=1)
+    sums = lax.dot_general(
+        pick_ref[...], columns, (((0,), (1,)), ((), ())), preferred_element_type=jnp.float32
+    )
     keep_ref[...] = sums[:bins].astype(jnp.bfloat16)
     rows = bins // pieces
     for piece, give_ref in enumerate(give_refs):
@@ -304,7 +307,7 @@
             pltpu.VMEM((experts * slots, len(blocks) * bins), jnp.bfloat16),
             pltpu.VMEM((16 if later else experts * wide, width), jnp.bfloat16),
             pltpu.VMEM((experts * slots, width), jnp.bfloat16),
-            pltpu.VMEM((experts * slots, width), jnp.bfloat16),
+            pltpu.VMEM((experts, width, slots), jnp.bfloat16),
             pltpu.VMEM((2, width, hidden), jnp.bfloat16),
             pltpu.VMEM((2, hidden, width), jnp.bfloat16),
             pltpu.SemaphoreType.DMA((2, 2 * PARTS)),

time: 130 us -> 134 us (1.031)
  Pallas kernels: 69.3 us -> 85.5 us
  waiting for transfers between devices: 33.5 us -> 19.7 us
  starting transfers between devices: 21.4 us -> 23.2 us
    pallas_call x4, Pallas kernels: 58.7 us -> 74.9 us  [expert_back(): pl.pallas_call(functools.partial(expert_kernel, layout, len(ahead), later...]
    ppermute x8, waiting for transfers between devices: 23.8 us -> 11.9 us  [hop(): lax.ppermute(block, 'exp', [(i, (i + 2 * step) % members) for i in range(...]
    ppermute x8, starting transfers between devices: 12.2 us -> 13.8 us  [hop(): lax.ppermute(block, 'exp', [(i, (i + 2 * step) % members) for i in range(...]
  transfers between devices with their start and end apart: 24 -> 24, of which waited for: 11 -> 7; matrix products, arithmetic and copies ran while one was open for 0% -> 0% of each run, Pallas kernels for 54% -> 64%
where the time goes in v7:
time: 134 us
  Pallas kernels  85.5 us (64%)
  starting transfers between devices  23.2 us (17%)
  waiting for transfers between devices  19.7 us (15%)
  other arithmetic  4.39 us (3%)
    pallas_call x4, Pallas kernels, expert_back(): pl.pallas_call(functools.partial(expert_kernel, layout, len(ahead), later...  74.9 us
    ppermute x8, starting transfers between devices, hop(): lax.ppermute(block, 'exp', [(i, (i + 2 * step) % members) for i in range(...  13.8 us
    ppermute x8, waiting for transfers between devices, hop(): lax.ppermute(block, 'exp', [(i, (i + 2 * step) % members) for i in range(...  11.9 us
    ppermute x6, starting transfers between devices, exchange(): lax.ppermute(blocks[place], 'ctx', [(i, i ^ place) for i in range(groups)])  6.98 us
    pallas_call x1, Pallas kernels, heads_back(): pl.pallas_call(heads_kernel, grid=(heads,), out_shape=[jax.ShapeDtypeStru...  6.37 us
    ppermute x10, waiting for transfers between devices, swap(): return lax.ppermute(block, 'exp', [(i, i ^ 1) for i in range(members)])  4.27 us
    ppermute x6, waiting for transfers between devices, exchange(): lax.ppermute(blocks[place], 'ctx', [(i, i ^ place) for i in range(groups)])  3.57 us
    pallas_call x1, Pallas kernels, pack_groups(): pl.pallas_call(pack_kernel, out_shape=[block] * groups, in_specs=[pl.Bloc...  2.99 us
  transfers between devices with their start and end apart: 24, of which 7 were waited for; matrix products, arithmetic and copies ran while one was open for 0% of the time, Pallas kernels for 64%

profile of v7, /device:TPU:0, one launch (start us, length us, event | category | flops | bytes accessed | tf_op | source)
XLA Modules:
  0.0 133.7 jit_solution(18138786208690825969)
XLA Ops:
  0.6 0.0 copy-start.2
  0.6 0.7 fusion.10
  1.4 0.7 reduce-precision_convert_fusion.1
  2.1 1.3 pad_maximum_fusion.refs_0_
  3.4 0.5 collective-permute-start
  3.9 4.7 %collective-permute-start.4 = (bf16[272,2048]{1,0:T(8,128)(2,1)S(1)}, bf16[272,2048]{1,0:T(8,128)(2,1)S(1)}, u32[]{:S(2)}, u32[]{:S(2)}) collective-permute-start(bf16[272,2048]{1,0:T(8,128)(2,1)S(1)} %pad_maximum_fusion.refs_0_), channel_id=1, source_target_pairs={{0,6},{1,7},{2,0},{3,1},{4,2},{5,3},{6,4},{7,5},{8,14},{9,15},{10,... | collective-permute-start | bytes 3342344 | tf_op jit(solution)/shard_map/ppermute | solution.py:338
  8.6 0.1 collective-permute-start.7
  8.7 3.0 %pack_groups.1 = (bf16[4,128,512]{2,1,0:T(8,128)(2,1)}, bf16[4,128,512]{2,1,0:T(8,128)(2,1)}, bf16[4,128,512]{2,1,0:T(8,128)(2,1)}, bf16[4,128,512]{2,1,0:T(8,128)(2,1)}) custom-call(s32[1]{0:T(128)} %bitcast.mine_ref, bf16[128,2048]{1,0:T(8,128)(2,1)} %bitcast.30, bf16[128,2048]{1,0:T(8,128)(2,1)} %bitcast.31, bf16[128,2048]{1,0:T(8,128)(2,1)} %bitcast.32, ...), custom_call_target="tpu_custom_call" | custom-call | tf_op jit(solution)/shard_map/pack_groups/pallas_call | solution.py:58
  11.7 0.0 collective-permute-done.refs_1_
  11.7 1.5 %collective-permute-start.1 = (bf16[4,128,512]{2,1,0:T(8,128)(2,1)}, bf16[4,128,512]{2,1,0:T(8,128)(2,1)S(1)}, u32[]{:S(2)}, u32[]{:S(2)}) collective-permute-start(bf16[4,128,512]{2,1,0:T(8,128)(2,1)} %get-tuple-element.68), channel_id=1, source_target_pairs={{0,8},{8,0},{16,24},{24,16},{1,9},{9,1},{17,25},{25,17},{2,10},{10... | collective-permute-start | bytes 1572872 | tf_op jit(solution)/shard_map/ppermute | solution.py:140
  13.2 1.5 %collective-permute-start.2 = (bf16[4,128,512]{2,1,0:T(8,128)(2,1)}, bf16[4,128,512]{2,1,0:T(8,128)(2,1)S(1)}, u32[]{:S(2)}, u32[]{:S(2)}) collective-permute-start(bf16[4,128,512]{2,1,0:T(8,128)(2,1)} %get-tuple-element.69), channel_id=1, source_target_pairs={{0,16},{8,24},{16,0},{24,8},{1,17},{9,25},{17,1},{25,9},{2,18},{10... | collective-permute-start | bytes 1572872 | tf_op jit(solution)/shard_map/ppermute | solution.py:140
  14.7 0.5 collective-permute-start.3
  15.2 19.6 %expert_back.4 = (bf16[128,2048]{1,0:T(8,128)(2,1)S(1)}, bf16[128,2048]{1,0:T(8,128)(2,1)S(1)}) custom-call(s32[1]{0:T(128)} %bitcast.11.base_ref, bf16[272,2048]{1,0:T(8,128)(2,1)S(1)} %pad_maximum_fusion.refs_0_, bf16[272,2048]{1,0:T(8,128)(2,1)} %collective-permute-done.refs_1_, bf16[4,2048,768]{2,1,0:T(8,128)(2,1)} %refs_5_.3, bf16[4,768,2048]{2,1,0:T(8,128)(2,1)} %refs_6_.1), custom_call_target="tpu_custom_call" | custom-call | flops 30000001024 | bytes 30000000 | tf_op jit(solution)/shard_map/expert_back/pallas_call | solution.py:299
  34.7 0.0 collective-permute-done.4.refs_0_
  34.8 3.6 %collective-permute-done.2.refs_2_ = bf16[4,128,512]{2,1,0:T(8,128)(2,1)S(1)} collective-permute-done((bf16[4,128,512]{2,1,0:T(8,128)(2,1)}, bf16[4,128,512]{2,1,0:T(8,128)(2,1)S(1)}, u32[]{:S(2)}, u32[]{:S(2)}) %collective-permute-start.2) | collective-permute-done | bytes 524320 | tf_op jit(solution)/shard_map/ppermute | solution.py:140
  38.3 3.5 %collective-permute-start.5 = (bf16[272,2048]{1,0:T(8,128)(2,1)S(1)}, bf16[272,2048]{1,0:T(8,128)(2,1)S(1)}, u32[]{:S(2)}, u32[]{:S(2)}) collective-permute-start(bf16[272,2048]{1,0:T(8,128)(2,1)S(1)} %collective-permute-done.4.refs_0_), channel_id=1, source_target_pairs={{0,6},{1,7},{2,0},{3,1},{4,2},{5,3},{6,4},{7,5},{8,14},{9,15},{10,... | collective-permute-start | bytes 3342344 | tf_op jit(solution)/shard_map/ppermute | solution.py:338
  41.9 6.4 %heads_back.1 = (bf16[3,128,512]{2,1,0:T(8,128)(2,1)S(1)}, bf16[3,128,512]{2,1,0:T(8,128)(2,1)S(1)}, bf16[3,128,512]{2,1,0:T(8,128)(2,1)S(1)}, bf16[3,128,512]{2,1,0:T(8,128)(2,1)S(1)}) custom-call(bf16[4,128,512]{2,1,0:T(8,128)(2,1)S(1)} %copy-done, bf16[4,128,512]{2,1,0:T(8,128)(2,1)S(1)} %collective-permute-done.1.refs_1_, ...), custom_call_target="tpu_custom_call" | custom-call | flops 30000001024 | bytes 30000000 | tf_op jit(solution)/shard_map/heads_back/pallas_call | solution.py:125
  48.2 0.0 copy-start.1
  48.3 0.3 collective-permute-start.11
  48.6 1.2 collective-permute-start.8
  49.8 0.8 collective-permute-start.9
  50.6 1.4 %collective-permute-start.10 = (bf16[3,128,512]{2,1,0:T(8,128)(2,1)S(1)}, bf16[3,128,512]{2,1,0:T(8,128)(2,1)S(1)}, u32[]{:S(2)}, u32[]{:S(2)}) collective-permute-start(bf16[3,128,512]{2,1,0:T(8,128)(2,1)S(1)} %get-tuple-element.87), channel_id=1, source_target_pairs={{0,24},{8,16},{16,8},{24,0},{1,25},{9,17},{17,9},{25,1},{2,26},{10... | collective-permute-start | bytes 1179656 | tf_op jit(solution)/shard_map/ppermute | solution.py:140
  52.0 19.1 %expert_back.5 = (bf16[128,2048]{1,0:T(8,128)(2,1)S(1)}, bf16[128,2048]{1,0:T(8,128)(2,1)S(1)}, f32[192,768]{1,0:T(8,128)S(1)}) custom-call(s32[1]{0:T(128)} %bitcast.11.base_ref, bf16[272,2048]{1,0:T(8,128)(2,1)S(1)} %collective-permute-done.4.refs_0_, bf16[272,2048]{1,0:T(8,128)(2,1)S(1)} %collective-permute-done.6.refs_1_, ...), custom_call_target="tpu_custom_call" | custom-call | tf_op jit(solution)/shard_map/expert_back/pallas_call | solution.py:299
  71.2 0.1 collective-permute-start.13
  71.3 0.2 collective-permute-start.15
  71.5 0.3 collective-permute-start.16
  71.8 1.4 %collective-permute-done.13 = bf16[128,2048]{1,0:T(8,128)(2,1)S(1)} collective-permute-done((bf16[128,2048]{1,0:T(8,128)(2,1)S(1)}, bf16[128,2048]{1,0:T(8,128)(2,1)S(1)}, u32[]{:S(2)}, u32[]{:S(2)}) %collective-permute-start.13) | collective-permute-done | bytes 524320 | tf_op jit(solution)/shard_map/ppermute | solution.py:335
  73.2 0.1 add_convert_fusion.3
  73.4 0.4 collective-permute-start.14
  73.7 1.1 collective-permute-done.16.refs_1_
  74.8 18.7 %expert_back.6 = (bf16[128,2048]{1,0:T(8,128)(2,1)S(1)}, bf16[128,2048]{1,0:T(8,128)(2,1)S(1)}) custom-call(s32[1]{0:T(128)} %bitcast.11.base_ref, bf16[272,2048]{1,0:T(8,128)(2,1)S(1)} %collective-permute-done.5.refs_0_, bf16[272,2048]{1,0:T(8,128)(2,1)S(1)} %collective-permute-done.16.refs_1_, bf16[4,2048,768]{2,1,0:T(8,128)(2,1)} %refs_5_.3, ...), custom_call_target="tpu_custom_call" | custom-call | tf_op jit(solution)/shard_map/expert_back/pallas_call | solution.py:299
  93.5 0.2 collective-permute-start.20
  93.7 0.4 collective-permute-start.17
  94.1 0.9 collective-permute-start.22
  95.0 0.5 collective-permute-done.20
  95.5 0.1 add_convert_fusion.2
  95.6 3.2 %collective-permute-start.21 = (bf16[128,2048]{1,0:T(8,128)(2,1)S(1)}, bf16[128,2048]{1,0:T(8,128)(2,1)S(1)}, u32[]{:S(2)}, u32[]{:S(2)}) collective-permute-start(bf16[128,2048]{1,0:T(8,128)(2,1)S(1)} %add_convert_fusion.2), channel_id=1, source_target_pairs={{0,6},{1,7},{2,0},{3,1},{4,2},{5,3},{6,4},{7,5},{8,14},{9,15},{10,... | collective-permute-start | bytes 1572872 | tf_op jit(solution)/shard_map/ppermute | solution.py:338
  98.8 17.6 %expert_back.7 = (bf16[128,2048]{1,0:T(8,128)(2,1)S(1)}, bf16[64,2048]{1,0:T(8,128)(2,1)S(1)}, bf16[64,2048]{1,0:T(8,128)(2,1)S(1)}) custom-call(s32[1]{0:T(128)} %bitcast.11.base_ref, bf16[144,2048]{1,0:T(8,128)(2,1)S(1)} %collective-permute-done.7.refs_2_.refs_0_, bf16[128,2048]{1,0:T(8,128)(2,1)S(1)} %collective-permute-done.15.refs_1_, ...), custom_call_target="tpu_custom_call" | custom-call | flops 30000001024 | bytes 30000000 | tf_op jit(solution)/shard_map/expert_back/pallas_call | solution.py:299
  116.4 0.1 collective-permute-start.18
  116.4 0.5 collective-permute-start.19
  116.9 0.1 collective-permute-start.12
  117.0 0.9 collective-permute-done.18
  118.0 0.4 collective-permute-done.19
  118.3 0.2 add_convert_fusion.1
  118.6 0.9 collective-permute-start.23
  119.5 1.3 unpack_groups.1
  120.7 11.9 %collective-permute-done.23 = bf16[128,2048]{1,0:T(8,128)(2,1)S(1)} collective-permute-done((bf16[128,2048]{1,0:T(8,128)(2,1)S(1)}, bf16[128,2048]{1,0:T(8,128)(2,1)S(1)}, u32[]{:S(2)}, u32[]{:S(2)}) %collective-permute-start.23) | collective-permute-done | bytes 524320 | tf_op jit(solution)/shard_map/ppermute | solution.py:338
  132.6 1.1 fusion
  (23 shorter events, 0.1 us)
Async XLA Ops:
  0.6 7.9 %copy-start.2 = (bf16[1,128,2048]{2,1,0:T(8,128)(2,1)S(1)}, bf16[1,128,2048]{2,1,0:T(8,128)(2,1)}, u32[]{:S(2)}) copy-start(bf16[1,128,2048]{2,1,0:T(8,128)(2,1)} %param.13) | copy-start | bytes 1572868
  3.4 8.3 %collective-permute-start = (bf16[272,2048]{1,0:T(8,128)(2,1)S(1)}, bf16[272,2048]{1,0:T(8,128)(2,1)}, u32[]{:S(2)}, u32[]{:S(2)}) collective-permute-start(bf16[272,2048]{1,0:T(8,128)(2,1)S(1)} %pad_maximum_fusion.refs_0_), channel_id=1, source_target_pairs={{0,1},{1,0},{2,3},{3,2},{4,5},{5,4},{6,7},{7,6},{8,9},{9,8},{10,11... | collective-permute-start | bytes 3342344 | tf_op jit(solution)/shard_map/ppermute | solution.py:335
  3.9 30.9 %collective-permute-start.4 = (bf16[272,2048]{1,0:T(8,128)(2,1)S(1)}, bf16[272,2048]{1,0:T(8,128)(2,1)S(1)}, u32[]{:S(2)}, u32[]{:S(2)}) collective-permute-start(bf16[272,2048]{1,0:T(8,128)(2,1)S(1)} %pad_maximum_fusion.refs_0_), channel_id=1, source_target_pairs={{0,6},{1,7},{2,0},{3,1},{4,2},{5,3},{6,4},{7,5},{8,14},{9,15},{10,... | collective-permute-start | bytes 3342344 | tf_op jit(solution)/shard_map/ppermute | solution.py:338
  8.6 39.6 %collective-permute-start.7 = (bf16[144,2048]{1,0:T(8,128)(2,1)S(1)}, bf16[144,2048]{1,0:T(8,128)(2,1)S(1)}, u32[]{:S(2)}, u32[]{:S(2)}) collective-permute-start(bf16[144,2048]{1,0:T(8,128)(2,1)S(1)} %pad_maximum_fusion.1), channel_id=1, source_target_pairs={{0,2},{1,3},{2,4},{3,5},{4,6},{5,7},{6,0},{7,1},{8,10},{9,11},{10,... | collective-permute-start | bytes 1769480 | tf_op jit(solution)/shard_map/ppermute | solution.py:338
  11.7 23.1 %collective-permute-start.1 = (bf16[4,128,512]{2,1,0:T(8,128)(2,1)}, bf16[4,128,512]{2,1,0:T(8,128)(2,1)S(1)}, u32[]{:S(2)}, u32[]{:S(2)}) collective-permute-start(bf16[4,128,512]{2,1,0:T(8,128)(2,1)} %get-tuple-element.68), channel_id=1, source_target_pairs={{0,8},{8,0},{16,24},{24,16},{1,9},{9,1},{17,25},{25,17},{2,10},{10... | collective-permute-start | bytes 1572872 | tf_op jit(solution)/shard_map/ppermute | solution.py:140
  13.2 25.2 %collective-permute-start.2 = (bf16[4,128,512]{2,1,0:T(8,128)(2,1)}, bf16[4,128,512]{2,1,0:T(8,128)(2,1)S(1)}, u32[]{:S(2)}, u32[]{:S(2)}) collective-permute-start(bf16[4,128,512]{2,1,0:T(8,128)(2,1)} %get-tuple-element.69), channel_id=1, source_target_pairs={{0,16},{8,24},{16,0},{24,8},{1,17},{9,25},{17,1},{25,9},{2,18},{10... | collective-permute-start | bytes 1572872 | tf_op jit(solution)/shard_map/ppermute | solution.py:140
  14.7 23.6 %collective-permute-start.3 = (bf16[4,128,512]{2,1,0:T(8,128)(2,1)}, bf16[4,128,512]{2,1,0:T(8,128)(2,1)S(1)}, u32[]{:S(2)}, u32[]{:S(2)}) collective-permute-start(bf16[4,128,512]{2,1,0:T(8,128)(2,1)} %get-tuple-element.70), channel_id=1, source_target_pairs={{0,24},{8,16},{16,8},{24,0},{1,25},{9,17},{17,9},{25,1},{2,26},{10... | collective-permute-start | bytes 1572872 | tf_op jit(solution)/shard_map/ppermute | solution.py:140
  15.2 26.7 %copy-start = (bf16[4,128,512]{2,1,0:T(8,128)(2,1)S(1)}, bf16[4,128,512]{2,1,0:T(8,128)(2,1)}, u32[]{:S(2)}) copy-start(bf16[4,128,512]{2,1,0:T(8,128)(2,1)} %get-tuple-element.76.refs_0_) | copy-start | bytes 1572868
  38.3 9.9 %collective-permute-start.6 = (bf16[272,2048]{1,0:T(8,128)(2,1)S(1)}, bf16[272,2048]{1,0:T(8,128)(2,1)S(1)}, u32[]{:S(2)}, u32[]{:S(2)}) collective-permute-start(bf16[272,2048]{1,0:T(8,128)(2,1)S(1)} %collective-permute-done.4.refs_0_), channel_id=1, source_target_pairs={{0,1},{1,0},{2,3},{3,2},{4,5},{5,4},{6,7},{7,6},{8,9},{9,8},{10,11... | collective-permute-start | bytes 3342344 | tf_op jit(solution)/shard_map/ppermute | solution.py:335
  38.3 32.8 %collective-permute-start.5 = (bf16[272,2048]{1,0:T(8,128)(2,1)S(1)}, bf16[272,2048]{1,0:T(8,128)(2,1)S(1)}, u32[]{:S(2)}, u32[]{:S(2)}) collective-permute-start(bf16[272,2048]{1,0:T(8,128)(2,1)S(1)} %collective-permute-done.4.refs_0_), channel_id=1, source_target_pairs={{0,6},{1,7},{2,0},{3,1},{4,2},{5,3},{6,4},{7,5},{8,14},{9,15},{10,... | collective-permute-start | bytes 3342344 | tf_op jit(solution)/shard_map/ppermute | solution.py:338
  48.2 23.0 %copy-start.1 = (bf16[1,128,2048]{2,1,0:T(8,128)(2,1)S(1)}, bf16[1,128,2048]{2,1,0:T(8,128)(2,1)}, u32[]{:S(2)}) copy-start(bf16[1,128,2048]{2,1,0:T(8,128)(2,1)} %param.12) | copy-start | bytes 1572868
  48.3 3.8 %collective-permute-start.11 = (bf16[144,2048]{1,0:T(8,128)(2,1)S(1)}, bf16[144,2048]{1,0:T(8,128)(2,1)S(1)}, u32[]{:S(2)}, u32[]{:S(2)}) collective-permute-start(bf16[144,2048]{1,0:T(8,128)(2,1)S(1)} %collective-permute-done.7.refs_2_.refs_0_), channel_id=1, source_target_pairs={{0,1},{1,0},{2,3},{3,2},{4,5},{5,4},{6,7},{7,6},{8,9},{9,8},{10,11... | collective-permute-start | bytes 1769480 | tf_op jit(solution)/shard_map/ppermute | solution.py:335
  48.6 22.6 %collective-permute-start.8 = (bf16[3,128,512]{2,1,0:T(8,128)(2,1)S(1)}, bf16[3,128,512]{2,1,0:T(8,128)(2,1)S(1)}, u32[]{:S(2)}, u32[]{:S(2)}) collective-permute-start(bf16[3,128,512]{2,1,0:T(8,128)(2,1)S(1)} %get-tuple-element.85), channel_id=1, source_target_pairs={{0,8},{8,0},{16,24},{24,16},{1,9},{9,1},{17,25},{25,17},{2,10},{10... | collective-permute-start | bytes 1179656 | tf_op jit(solution)/shard_map/ppermute | solution.py:140
  49.8 21.4 %collective-permute-start.9 = (bf16[3,128,512]{2,1,0:T(8,128)(2,1)S(1)}, bf16[3,128,512]{2,1,0:T(8,128)(2,1)S(1)}, u32[]{:S(2)}, u32[]{:S(2)}) collective-permute-start(bf16[3,128,512]{2,1,0:T(8,128)(2,1)S(1)} %get-tuple-element.86), channel_id=1, source_target_pairs={{0,16},{8,24},{16,0},{24,8},{1,17},{9,25},{17,1},{25,9},{2,18},{10... | collective-permute-start | bytes 1179656 | tf_op jit(solution)/shard_map/ppermute | solution.py:140
  50.6 20.6 %collective-permute-start.10 = (bf16[3,128,512]{2,1,0:T(8,128)(2,1)S(1)}, bf16[3,128,512]{2,1,0:T(8,128)(2,1)S(1)}, u32[]{:S(2)}, u32[]{:S(2)}) collective-permute-start(bf16[3,128,512]{2,1,0:T(8,128)(2,1)S(1)} %get-tuple-element.87), channel_id=1, source_target_pairs={{0,24},{8,16},{16,8},{24,0},{1,25},{9,17},{17,9},{25,1},{2,26},{10... | collective-permute-start | bytes 1179656 | tf_op jit(solution)/shard_map/ppermute | solution.py:140
  71.2 2.0 %collective-permute-start.13 = (bf16[128,2048]{1,0:T(8,128)(2,1)S(1)}, bf16[128,2048]{1,0:T(8,128)(2,1)S(1)}, u32[]{:S(2)}, u32[]{:S(2)}) collective-permute-start(bf16[128,2048]{1,0:T(8,128)(2,1)S(1)} %get-tuple-element.103), channel_id=1, source_target_pairs={{0,1},{1,0},{2,3},{3,2},{4,5},{5,4},{6,7},{7,6},{8,9},{9,8},{10,11... | collective-permute-start | bytes 1572872 | tf_op jit(solution)/shard_map/ppermute | solution.py:335
  71.3 22.2 %collective-permute-start.15 = (bf16[128,2048]{1,0:T(8,128)(2,1)S(1)}, bf16[128,2048]{1,0:T(8,128)(2,1)S(1)}, u32[]{:S(2)}, u32[]{:S(2)}) collective-permute-start(bf16[128,2048]{1,0:T(8,128)(2,1)S(1)} %bitcast.27), channel_id=1, source_target_pairs={{0,2},{1,3},{2,4},{3,5},{4,6},{5,7},{6,0},{7,1},{8,10},{9,11},{10,... | collective-permute-start | bytes 1572872 | tf_op jit(solution)/shard_map/ppermute | solution.py:338
  71.5 3.3 %collective-permute-start.16 = (bf16[272,2048]{1,0:T(8,128)(2,1)S(1)}, bf16[272,2048]{1,0:T(8,128)(2,1)S(1)}, u32[]{:S(2)}, u32[]{:S(2)}) collective-permute-start(bf16[272,2048]{1,0:T(8,128)(2,1)S(1)} %collective-permute-done.5.refs_0_), channel_id=1, source_target_pairs={{0,1},{1,0},{2,3},{3,2},{4,5},{5,4},{6,7},{7,6},{8,9},{9,8},{10,11... | collective-permute-start | bytes 3342344 | tf_op jit(solution)/shard_map/ppermute | solution.py:335
  73.4 20.1 %collective-permute-start.14 = (bf16[64,2048]{1,0:T(8,128)(2,1)S(1)}, bf16[64,2048]{1,0:T(8,128)(2,1)S(1)}, u32[]{:S(2)}, u32[]{:S(2)}) collective-permute-start(bf16[64,2048]{1,0:T(8,128)(2,1)S(1)} %get-tuple-element.123), channel_id=1, source_target_pairs={{0,2},{1,3},{2,4},{3,5},{4,6},{5,7},{6,0},{7,1},{8,10},{9,11},{10,... | collective-permute-start | bytes 786440 | tf_op jit(solution)/shard_map/ppermute | solution.py:338
  93.5 2.0 %collective-permute-start.20 = (bf16[128,2048]{1,0:T(8,128)(2,1)S(1)}, bf16[128,2048]{1,0:T(8,128)(2,1)S(1)}, u32[]{:S(2)}, u32[]{:S(2)}) collective-permute-start(bf16[128,2048]{1,0:T(8,128)(2,1)S(1)} %get-tuple-element.114), channel_id=1, source_target_pairs={{0,1},{1,0},{2,3},{3,2},{4,5},{5,4},{6,7},{7,6},{8,9},{9,8},{10,11... | collective-permute-start | bytes 1572872 | tf_op jit(solution)/shard_map/ppermute | solution.py:335
  93.7 5.1 %collective-permute-start.17 = (bf16[128,2048]{1,0:T(8,128)(2,1)S(1)}, bf16[128,2048]{1,0:T(8,128)(2,1)S(1)}, u32[]{:S(2)}, u32[]{:S(2)}) collective-permute-start(bf16[128,2048]{1,0:T(8,128)(2,1)S(1)} %collective-permute-done.15.refs_1_), channel_id=1, source_target_pairs={{0,1},{1,0},{2,3},{3,2},{4,5},{5,4},{6,7},{7,6},{8,9},{9,8},{10,11... | collective-permute-start | bytes 1572872 | tf_op jit(solution)/shard_map/ppermute | solution.py:335
  94.1 23.0 %collective-permute-start.22 = (bf16[64,2048]{1,0:T(8,128)(2,1)S(1)}, bf16[64,2048]{1,0:T(8,128)(2,1)S(1)}, u32[]{:S(2)}, u32[]{:S(2)}) collective-permute-start(bf16[64,2048]{1,0:T(8,128)(2,1)S(1)} %get-tuple-element.122), channel_id=1, source_target_pairs={{0,2},{1,3},{2,4},{3,5},{4,6},{5,7},{6,0},{7,1},{8,10},{9,11},{10,... | collective-permute-start | bytes 786440 | tf_op jit(solution)/shard_map/ppermute | solution.py:338
  95.6 22.7 %collective-permute-start.21 = (bf16[128,2048]{1,0:T(8,128)(2,1)S(1)}, bf16[128,2048]{1,0:T(8,128)(2,1)S(1)}, u32[]{:S(2)}, u32[]{:S(2)}) collective-permute-start(bf16[128,2048]{1,0:T(8,128)(2,1)S(1)} %add_convert_fusion.2), channel_id=1, source_target_pairs={{0,6},{1,7},{2,0},{3,1},{4,2},{5,3},{6,4},{7,5},{8,14},{9,15},{10,... | collective-permute-start | bytes 1572872 | tf_op jit(solution)/shard_map/ppermute | solution.py:338
  116.4 1.6 %collective-permute-start.18 = (bf16[64,2048]{1,0:T(8,128)(2,1)S(1)}, bf16[64,2048]{1,0:T(8,128)(2,1)S(1)}, u32[]{:S(2)}, u32[]{:S(2)}) collective-permute-start(bf16[64,2048]{1,0:T(8,128)(2,1)S(1)} %get-tuple-element.111), channel_id=1, source_target_pairs={{0,1},{1,0},{2,3},{3,2},{4,5},{5,4},{6,7},{7,6},{8,9},{9,8},{10,11... | collective-permute-start | bytes 786440 | tf_op jit(solution)/shard_map/ppermute | solution.py:335
  116.4 1.9 %collective-permute-start.19 = (bf16[64,2048]{1,0:T(8,128)(2,1)S(1)}, bf16[64,2048]{1,0:T(8,128)(2,1)S(1)}, u32[]{:S(2)}, u32[]{:S(2)}) collective-permute-start(bf16[64,2048]{1,0:T(8,128)(2,1)S(1)} %get-tuple-element.112), channel_id=1, source_target_pairs={{0,1},{1,0},{2,3},{3,2},{4,5},{5,4},{6,7},{7,6},{8,9},{9,8},{10,11... | collective-permute-start | bytes 786440 | tf_op jit(solution)/shard_map/ppermute | solution.py:335
  116.9 3.8 %collective-permute-start.12 = (bf16[128,2048]{1,0:T(8,128)(2,1)S(1)}, bf16[128,2048]{1,0:T(8,128)(2,1)S(1)}, u32[]{:S(2)}, u32[]{:S(2)}) collective-permute-start(bf16[128,2048]{1,0:T(8,128)(2,1)S(1)} %get-tuple-element.101), channel_id=1, source_target_pairs={{0,1},{1,0},{2,3},{3,2},{4,5},{5,4},{6,7},{7,6},{8,9},{9,8},{10,11... | collective-permute-start | bytes 1572872 | tf_op jit(solution)/shard_map/ppermute | solution.py:335
  118.6 14.0 %collective-permute-start.23 = (bf16[128,2048]{1,0:T(8,128)(2,1)S(1)}, bf16[128,2048]{1,0:T(8,128)(2,1)S(1)}, u32[]{:S(2)}, u32[]{:S(2)}) collective-permute-start(bf16[128,2048]{1,0:T(8,128)(2,1)S(1)} %add_convert_fusion.1), channel_id=1, source_target_pairs={{0,6},{1,7},{2,0},{3,1},{4,2},{5,3},{6,4},{7,5},{8,14},{9,15},{10,... | collective-permute-start | bytes 1572872 | tf_op jit(solution)/shard_map/ppermute | solution.py:338

commit v8 on v6

--- a/solution.py
+++ b/solution.py
@@ -13,7 +13,7 @@
 PARTS = 4
 VMEM_BYTES = 36 * 1024 * 1024
 VMEM_PACK = 58 * 1024 * 1024
-VMEM_EXPERTS = 45 * 1024 * 1024
+VMEM_EXPERTS = 18 * 1024 * 1024
 def cost(units):
     return pl.CostEstimate(
         flops=units * 10**9, bytes_accessed=units * 10**6, transcendentals=0
@@ -128,7 +128,7 @@
         out_shape=[jax.ShapeDtypeStruct((3, bins, width), jnp.bfloat16)] * groups,
         in_specs=[pl.BlockSpec((4, bins, HD), lambda h: (0, 0, h))] * groups,
         out_specs=[pl.BlockSpec((3, bins, HD), lambda h: (0, 0, h))] * groups,
-        compiler_params=pltpu.CompilerParams(vmem_limit_bytes=VMEM_BYTES),
+        compiler_params=pltpu.CompilerParams(vmem_limit_bytes=6 * 1024 * 1024 + 40 * rows * rows),
         cost_estimate=cost(HEADS_COST),
         name="heads_back",
     )(*blocks)
@@ -183,7 +183,7 @@
     return jnp.concatenate(gates, axis=0)
 
 
-def expert_kernel(layout, ahead, later, pieces, top, base_ref, *refs):
+def expert_kernel(layout, ahead, later, loads, pieces, top, base_ref, *refs):
     refs = list(refs)
 
     def take(count):
@@ -195,31 +195,33 @@
     blocks = [take(length) for length in layout]
     ahead_refs = take(ahead)
     slope_refs = take(1 if later else 0)
-    up_hbm, down_hbm = take(2)
+    weights = take(2)
     (keep_ref,) = take(1)
     give_refs = take(pieces)
     ahead_slopes = take(1 if ahead else 0)
-    pick_ref, token_rows, gated_rows, back_rows, up_ref, down_ref, sems = take(7)
+    up_ref, down_ref = take(2) if loads else weights
+    pick_ref, token_rows, gated_rows, back_rows = take(4)
     ahead_picks = take(1 if ahead else 0)
+    sems = take(1)[0] if loads else None
     bins = keep_ref.shape[0]
     slots = sources * CAP
     experts = pick_ref.shape[0] // slots
     wide = slots + ahead * CAP
 
     def copies(expert):
-        place = expert % 2
-        return [
-            pltpu.make_async_copy(
-                hbm.at[expert, pl.ds(part * (hbm.shape[1] // PARTS), hbm.shape[1] // PARTS)],
-                vmem.at[place, pl.ds(part * (hbm.shape[1] // PARTS), hbm.shape[1] // PARTS)],
-                sems.at[place, PARTS * which + part],
-            )
-            for which, (hbm, vmem) in enumerate(((up_hbm, up_ref), (down_hbm, down_ref)))
-            for part in range(PARTS)
-        ]
-
-    for copy in copies(0):
-        copy.start()
+        parts = []
+        for which, (hbm, vmem) in enumerate(zip(weights, (up_ref, down_ref))):
+            length = hbm.shape[1] // PARTS
+            for part in range(PARTS):
+                rows = (expert, pl.ds(part * length, length))
+                sem = sems.at[expert, PARTS * which + part]
+                parts.append(pltpu.make_async_copy(hbm.at[rows], vmem.at[rows], sem))
+        return parts
+
+    if loads:
+        for local in range(experts):
+            for copy in copies(local):
+                copy.start()
 
     values = [
         jnp.concatenate([piece[...] for piece in block], axis=0) if len(block) > 1 else block[0]
@@ -250,27 +252,22 @@
 
     @pl.loop(0, experts)
     def _(expert):
-        @pl.when(expert + 1 < experts)
-        def _():
-            for copy in copies(expert + 1):
-                copy.start()
-
-        for copy in copies(expert):
-            copy.wait()
-        place = expert % 2
+        if loads:
+            for copy in copies(expert):
+                copy.wait()
         rows = pl.ds(pl.multiple_of(expert * slots, 16), slots)
         if later:
             slopes = slope_refs[0][rows, :]
         else:
             wide_rows = pl.ds(pl.multiple_of(expert * wide, 16), wide)
-            slopes = silu_slope(dot_nn(token_rows[wide_rows, :], up_ref[place]))
+            slopes = silu_slope(dot_nn(token_rows[wide_rows, :], up_ref[expert]))
         if ahead:
             more = ahead * CAP
             ahead_slopes[0][pl.ds(pl.multiple_of(expert * more, 16), more), :] = slopes[slots:]
             slopes = slopes[:slots]
-        back_grad = dot_nt(gated_rows[rows, :], down_ref[place])
+        back_grad = dot_nt(gated_rows[rows, :], down_ref[expert])
         hidden_grad = (back_grad * slopes).astype(jnp.bfloat16)
-        back_rows[rows, :] = dot_nt(hidden_grad, up_ref[place]).astype(jnp.bfloat16)
+        back_rows[rows, :] = dot_nt(hidden_grad, up_ref[expert]).astype(jnp.bfloat16)
 
     sums = dot_tn(pick_ref[...], back_rows[...])
     keep_ref[...] = sums[:bins].astype(jnp.bfloat16)
@@ -279,10 +276,10 @@
         give_ref[...] = sums[bins + piece * rows : bins + (piece + 1) * rows].astype(jnp.bfloat16)
 
 
-def expert_back(base, blocks, up_weight, down_weight, bins, top, units, pieces, ahead, slopes):
+def expert_back(base, blocks, weights, loads, bins, top, units, pieces, ahead, slopes):
     layout = [len(block) for block in blocks]
     later = slopes is not None
-    experts, width, hidden = up_weight.shape
+    experts, width, hidden = weights[0].shape
     slots = len(blocks) * CAP
     wide = slots + len(ahead) * CAP
     operands = [piece for block in blocks for piece in block] + list(ahead)
@@ -292,29 +289,28 @@
         [jax.ShapeDtypeStruct((bins, width), jnp.bfloat16)]
         + [jax.ShapeDtypeStruct((bins // pieces, width), jnp.bfloat16)] * pieces
         + (more if ahead else [])
+        + ([jax.ShapeDtypeStruct(weight.shape, weight.dtype) for weight in weights] if loads else [])
     )
     return pl.pallas_call(
-        functools.partial(expert_kernel, layout, len(ahead), later, pieces, top),
+        functools.partial(expert_kernel, layout, len(ahead), later, loads, pieces, top),
         out_shape=out_shape,
         in_specs=[pl.BlockSpec(memory_space=pltpu.SMEM)]
         + [pl.BlockSpec(memory_space=pltpu.VMEM)] * len(operands)
-        + [pl.BlockSpec(memory_space=pltpu.HBM)] * 2,
+        + [pl.BlockSpec(memory_space=pltpu.HBM if loads else pltpu.VMEM)] * 2,
         out_specs=[pl.BlockSpec(memory_space=pltpu.VMEM)] * len(out_shape),
         scratch_shapes=[
             pltpu.VMEM((experts * slots, len(blocks) * bins), jnp.bfloat16),
             pltpu.VMEM((16 if later else experts * wide, width), jnp.bfloat16),
             pltpu.VMEM((experts * slots, width), jnp.bfloat16),
             pltpu.VMEM((experts * slots, width), jnp.bfloat16),
-            pltpu.VMEM((2, width, hidden), jnp.bfloat16),
-            pltpu.VMEM((2, hidden, width), jnp.bfloat16),
-            pltpu.SemaphoreType.DMA((2, 2 * PARTS)),
         ]
         + [pltpu.VMEM((experts * len(ahead) * CAP, len(ahead) * bins), jnp.bfloat16)]
-        * (1 if ahead else 0),
+        * (1 if ahead else 0)
+        + [pltpu.SemaphoreType.DMA((experts, 2 * PARTS))] * (1 if loads else 0),
         compiler_params=pltpu.CompilerParams(vmem_limit_bytes=VMEM_EXPERTS),
         cost_estimate=cost(units),
         name="expert_back",
-    )(base, *operands, up_weight, down_weight)
+    )(base, *operands, *weights)
 
 
 def per_device(
@@ -339,9 +335,9 @@
     def pair(*pieces):
         return [list(pieces), [swap(piece) for piece in pieces]]
 
-    def work(blocks, units, pieces=1, ahead=(), slopes=None):
+    def work(blocks, weights, units, pieces=1, ahead=(), slopes=None, loads=False):
         kept, *rest = expert_back(
-            base, blocks, up_weight, down_weight, bins, top, units, pieces, ahead, slopes
+            base, blocks, weights, loads, bins, top, units, pieces, ahead, slopes
         )
         return kept, rest[:pieces], rest[pieces:]
 
@@ -360,7 +356,7 @@
     packed = pack_groups(mine, rows, groups)
     own_pair, packed = barrier((own_pair, packed))
     heads = exchange(packed)
-    kept, give, _ = work(own_pair, OWN_COST)
+    kept, give, weights = work(own_pair, (up_weight, down_weight), OWN_COST, loads=True)
     heads, kept, give, left = barrier((heads, kept, give, left))
     total = add_up(kept, joined([swap(piece) for piece in give]))
     left_pair, right_grads = pair(left), out_grad[0]
@@ -372,7 +368,7 @@
     for d in range(1, half):
         left = hop(left, -1)
         ahead = () if d > 1 else (right_rows, right_partner)
-        kept, give, more = work(left_pair, LEFT_COST, ahead=ahead)
+        kept, give, more = work(left_pair, weights, LEFT_COST, ahead=ahead)
         slopes = more[0] if d == 1 else slopes
         left, results, kept, give = barrier((left, results, kept, give))
         left_sums.append(add_up(kept, joined([swap(piece) for piece in give])))
@@ -384,7 +380,7 @@
     rights = [(right_rows, hop(right_grads, 1))]
     for d in range(2, half):
         rights.append(tuple(hop(member, 1) for member in rights[-1]))
-    kept, give, _ = work(left_pair, FAR_COST)
+    kept, give, _ = work(left_pair, weights, FAR_COST)
     left_halves[0], rights, kept, give = barrier((left_halves[0], rights, kept, give))
     carried = add_up(kept, joined([swap(piece) for piece in give]))
     for d in range(half - 1, 0, -1):
@@ -392,7 +388,9 @@
         right_pair = pair(*rights[d - 1])
         if d == 1:
             right_pair[1][0] = right_partner
-        kept, give, _ = work(right_pair, RIGHT_COST, 2, slopes=slopes if d == 1 else None)
+        kept, give, _ = work(
+            right_pair, weights, RIGHT_COST, 2, slopes=slopes if d == 1 else None
+        )
         given = [swap(piece) for piece in give]
         kept, given, carried, left_halves = barrier((kept, given, carried, left_halves))
         carried = add_up(kept, joined(given), carried)

time: 130 us -> 130 us (level)
  Pallas kernels: 69.3 us -> 60.3 us
  waiting for transfers between devices: 33.5 us -> 42.5 us
    ppermute x8, waiting for transfers between devices: 23.8 us -> 32.8 us  [hop(): lax.ppermute(block, 'exp', [(i, (i + 2 * step) % members) for i in range(...]
    pallas_call x4, Pallas kernels: 58.7 us -> 49.7 us  [expert_back(): pl.pallas_call(functools.partial(expert_kernel, layout, len(ahead), later...]
  transfers between devices with their start and end apart: 24 -> 24, of which waited for: 11 -> 12; matrix products, arithmetic and copies ran while one was open for 0% -> 0% of each run, Pallas kernels for 54% -> 47%
where the time goes in v8:
time: 130 us; the launch traced here: 129 us
  Pallas kernels  60.3 us (46%)
  waiting for transfers between devices  42.5 us (33%)
  starting transfers between devices  21.4 us (16%)
  other arithmetic  4.39 us (3%)
    pallas_call x4, Pallas kernels, expert_back(): pl.pallas_call(functools.partial(expert_kernel, layout, len(ahead), later...  49.7 us
    ppermute x8, waiting for transfers between devices, hop(): lax.ppermute(block, 'exp', [(i, (i + 2 * step) % members) for i in range(...  32.8 us
    ppermute x8, starting transfers between devices, hop(): lax.ppermute(block, 'exp', [(i, (i + 2 * step) % members) for i in range(...  12.2 us
    ppermute x6, starting transfers between devices, exchange(): lax.ppermute(blocks[place], 'ctx', [(i, i ^ place) for i in range(groups)])  6.98 us
    pallas_call x1, Pallas kernels, heads_back(): pl.pallas_call(heads_kernel, grid=(heads,), out_shape=[jax.ShapeDtypeStru...  6.37 us
    ppermute x6, waiting for transfers between devices, exchange(): lax.ppermute(blocks[place], 'ctx', [(i, i ^ place) for i in range(groups)])  4.85 us
    ppermute x10, waiting for transfers between devices, swap(): return lax.ppermute(block, 'exp', [(i, i ^ 1) for i in range(members)])  4.8 us
    pallas_call x1, Pallas kernels, pack_groups(): pl.pallas_call(pack_kernel, out_shape=[block] * groups, in_specs=[pl.Bloc...  2.99 us
  transfers between devices with their start and end apart: 24, of which 12 were waited for; matrix products, arithmetic and copies ran while one was open for 0% of the time, Pallas kernels for 47%

profile of v8, /device:TPU:0, one launch (start us, length us, event | category | flops | bytes accessed | tf_op | source)
XLA Modules:
  0.0 129.4 jit_solution(3713911141117586567)
XLA Ops:
  0.6 0.0 copy-start.2
  0.6 0.7 fusion.10
  1.4 0.7 reduce-precision_convert_fusion.1
  2.1 1.3 pad_maximum_fusion.refs_0_
  3.4 0.5 collective-permute-start
  3.9 4.7 %collective-permute-start.4 = (bf16[272,2048]{1,0:T(8,128)(2,1)S(1)}, bf16[272,2048]{1,0:T(8,128)(2,1)S(1)}, u32[]{:S(2)}, u32[]{:S(2)}) collective-permute-start(bf16[272,2048]{1,0:T(8,128)(2,1)S(1)} %pad_maximum_fusion.refs_0_), channel_id=1, source_target_pairs={{0,6},{1,7},{2,0},{3,1},{4,2},{5,3},{6,4},{7,5},{8,14},{9,15},{10,... | collective-permute-start | bytes 3342344 | tf_op jit(solution)/shard_map/ppermute | solution.py:331
  8.6 0.1 collective-permute-start.7
  8.7 3.0 %pack_groups.1 = (bf16[4,128,512]{2,1,0:T(8,128)(2,1)}, bf16[4,128,512]{2,1,0:T(8,128)(2,1)}, bf16[4,128,512]{2,1,0:T(8,128)(2,1)}, bf16[4,128,512]{2,1,0:T(8,128)(2,1)}) custom-call(s32[1]{0:T(128)} %bitcast.mine_ref, bf16[128,2048]{1,0:T(8,128)(2,1)} %bitcast.30, bf16[128,2048]{1,0:T(8,128)(2,1)} %bitcast.31, bf16[128,2048]{1,0:T(8,128)(2,1)} %bitcast.32, ...), custom_call_target="tpu_custom_call" | custom-call | tf_op jit(solution)/shard_map/pack_groups/pallas_call | solution.py:58
  11.7 1.5 %collective-permute-start.1 = (bf16[4,128,512]{2,1,0:T(8,128)(2,1)}, bf16[4,128,512]{2,1,0:T(8,128)(2,1)S(1)}, u32[]{:S(2)}, u32[]{:S(2)}) collective-permute-start(bf16[4,128,512]{2,1,0:T(8,128)(2,1)} %get-tuple-element.70), channel_id=1, source_target_pairs={{0,8},{8,0},{16,24},{24,16},{1,9},{9,1},{17,25},{25,17},{2,10},{10... | collective-permute-start | bytes 1572872 | tf_op jit(solution)/shard_map/ppermute | solution.py:140
  13.2 1.5 %collective-permute-start.2 = (bf16[4,128,512]{2,1,0:T(8,128)(2,1)}, bf16[4,128,512]{2,1,0:T(8,128)(2,1)S(1)}, u32[]{:S(2)}, u32[]{:S(2)}) collective-permute-start(bf16[4,128,512]{2,1,0:T(8,128)(2,1)} %get-tuple-element.71), channel_id=1, source_target_pairs={{0,16},{8,24},{16,0},{24,8},{1,17},{9,25},{17,1},{25,9},{2,18},{10... | collective-permute-start | bytes 1572872 | tf_op jit(solution)/shard_map/ppermute | solution.py:140
  14.7 0.5 collective-permute-start.3
  15.2 15.8 %expert_back.4 = (bf16[128,2048]{1,0:T(8,128)(2,1)S(1)}, bf16[128,2048]{1,0:T(8,128)(2,1)S(1)}, bf16[4,2048,768]{2,1,0:T(8,128)(2,1)S(1)}, bf16[4,768,2048]{2,1,0:T(8,128)(2,1)S(1)}) custom-call(s32[1]{0:T(128)} %bitcast.11.base_ref, bf16[272,2048]{1,0:T(8,128)(2,1)S(1)} %pad_maximum_fusion.refs_0_, bf16[272,2048]{1,0:T(8,128)(2,1)} %collective-permute-done.refs_1_, ...), custom_call_target="tpu_custom_call" | custom-call | flops 30000001024 | bytes 30000000 | tf_op jit(solution)/shard_map/expert_back/pallas_call | solution.py:294
  31.0 2.5 %collective-permute-done.4.refs_0_ = bf16[272,2048]{1,0:T(8,128)(2,1)S(1)} collective-permute-done((bf16[272,2048]{1,0:T(8,128)(2,1)S(1)}, bf16[272,2048]{1,0:T(8,128)(2,1)S(1)}, u32[]{:S(2)}, u32[]{:S(2)}) %collective-permute-start.4) | collective-permute-done | bytes 1114144 | tf_op jit(solution)/shard_map/ppermute | solution.py:331
  33.5 4.8 %collective-permute-done.2.refs_2_ = bf16[4,128,512]{2,1,0:T(8,128)(2,1)S(1)} collective-permute-done((bf16[4,128,512]{2,1,0:T(8,128)(2,1)}, bf16[4,128,512]{2,1,0:T(8,128)(2,1)S(1)}, u32[]{:S(2)}, u32[]{:S(2)}) %collective-permute-start.2) | collective-permute-done | bytes 524320 | tf_op jit(solution)/shard_map/ppermute | solution.py:140
  38.3 3.5 %collective-permute-start.5 = (bf16[272,2048]{1,0:T(8,128)(2,1)S(1)}, bf16[272,2048]{1,0:T(8,128)(2,1)S(1)}, u32[]{:S(2)}, u32[]{:S(2)}) collective-permute-start(bf16[272,2048]{1,0:T(8,128)(2,1)S(1)} %collective-permute-done.4.refs_0_), channel_id=1, source_target_pairs={{0,6},{1,7},{2,0},{3,1},{4,2},{5,3},{6,4},{7,5},{8,14},{9,15},{10,... | collective-permute-start | bytes 3342344 | tf_op jit(solution)/shard_map/ppermute | solution.py:331
  41.9 6.4 %heads_back.1 = (bf16[3,128,512]{2,1,0:T(8,128)(2,1)S(1)}, bf16[3,128,512]{2,1,0:T(8,128)(2,1)S(1)}, bf16[3,128,512]{2,1,0:T(8,128)(2,1)S(1)}, bf16[3,128,512]{2,1,0:T(8,128)(2,1)S(1)}) custom-call(bf16[4,128,512]{2,1,0:T(8,128)(2,1)S(1)} %copy-done, bf16[4,128,512]{2,1,0:T(8,128)(2,1)S(1)} %collective-permute-done.1.refs_1_, ...), custom_call_target="tpu_custom_call" | custom-call | flops 30000001024 | bytes 30000000 | tf_op jit(solution)/shard_map/heads_back/pallas_call | solution.py:125
  48.2 0.3 collective-permute-start.11
  48.5 1.2 collective-permute-start.8
  49.8 0.8 collective-permute-start.9
  50.6 1.4 %collective-permute-start.10 = (bf16[3,128,512]{2,1,0:T(8,128)(2,1)S(1)}, bf16[3,128,512]{2,1,0:T(8,128)(2,1)S(1)}, u32[]{:S(2)}, u32[]{:S(2)}) collective-permute-start(bf16[3,128,512]{2,1,0:T(8,128)(2,1)S(1)} %get-tuple-element.89), channel_id=1, source_target_pairs={{0,24},{8,16},{16,8},{24,0},{1,25},{9,17},{17,9},{25,1},{2,26},{10... | collective-permute-start | bytes 1179656 | tf_op jit(solution)/shard_map/ppermute | solution.py:140
  52.0 12.3 %expert_back.5 = (bf16[128,2048]{1,0:T(8,128)(2,1)S(1)}, bf16[128,2048]{1,0:T(8,128)(2,1)S(1)}, f32[192,768]{1,0:T(8,128)S(1)}) custom-call(s32[1]{0:T(128)} %bitcast.11.base_ref, bf16[272,2048]{1,0:T(8,128)(2,1)S(1)} %collective-permute-done.4.refs_0_, bf16[272,2048]{1,0:T(8,128)(2,1)S(1)} %collective-permute-done.6.refs_1_, ...), custom_call_target="tpu_custom_call" | custom-call | tf_op jit(solution)/shard_map/expert_back/pallas_call | solution.py:294
  64.4 6.1 %collective-permute-done.5.refs_0_ = bf16[272,2048]{1,0:T(8,128)(2,1)S(1)} collective-permute-done((bf16[272,2048]{1,0:T(8,128)(2,1)S(1)}, bf16[272,2048]{1,0:T(8,128)(2,1)S(1)}, u32[]{:S(2)}, u32[]{:S(2)}) %collective-permute-start.5) | collective-permute-done | bytes 1114144 | tf_op jit(solution)/shard_map/ppermute | solution.py:331
  70.5 0.1 collective-permute-start.13
  70.6 0.5 collective-permute-start.15
  71.1 0.2 collective-permute-start.16
  71.3 1.2 collective-permute-done.13
  72.5 0.1 add_convert_fusion.3
  72.7 0.5 collective-permute-start.14
  73.2 0.9 collective-permute-done.16.refs_1_
  74.1 12.0 %expert_back.6 = (bf16[128,2048]{1,0:T(8,128)(2,1)S(1)}, bf16[128,2048]{1,0:T(8,128)(2,1)S(1)}) custom-call(s32[1]{0:T(128)} %bitcast.11.base_ref, bf16[272,2048]{1,0:T(8,128)(2,1)S(1)} %collective-permute-done.5.refs_0_, bf16[272,2048]{1,0:T(8,128)(2,1)S(1)} %collective-permute-done.16.refs_1_, ...), custom_call_target="tpu_custom_call" | custom-call | tf_op jit(solution)/shard_map/expert_back/pallas_call | solution.py:294
  86.1 1.1 collective-permute-done.15.refs_1_
  87.2 5.2 %collective-permute-done.14 = bf16[64,2048]{1,0:T(8,128)(2,1)S(1)} collective-permute-done((bf16[64,2048]{1,0:T(8,128)(2,1)S(1)}, bf16[64,2048]{1,0:T(8,128)(2,1)S(1)}, u32[]{:S(2)}, u32[]{:S(2)}) %collective-permute-start.14) | collective-permute-done | bytes 262176 | tf_op jit(solution)/shard_map/ppermute | solution.py:331
  92.3 0.5 collective-permute-start.17
  92.8 1.4 %collective-permute-done.20 = bf16[128,2048]{1,0:T(8,128)(2,1)S(1)} collective-permute-done((bf16[128,2048]{1,0:T(8,128)(2,1)S(1)}, bf16[128,2048]{1,0:T(8,128)(2,1)S(1)}, u32[]{:S(2)}, u32[]{:S(2)}) %collective-permute-start.20) | collective-permute-done | bytes 524320 | tf_op jit(solution)/shard_map/ppermute | solution.py:328
  94.2 0.1 add_convert_fusion.2
  94.4 2.7 %collective-permute-start.21 = (bf16[128,2048]{1,0:T(8,128)(2,1)S(1)}, bf16[128,2048]{1,0:T(8,128)(2,1)S(1)}, u32[]{:S(2)}, u32[]{:S(2)}) collective-permute-start(bf16[128,2048]{1,0:T(8,128)(2,1)S(1)} %add_convert_fusion.2), channel_id=1, source_target_pairs={{0,6},{1,7},{2,0},{3,1},{4,2},{5,3},{6,4},{7,5},{8,14},{9,15},{10,... | collective-permute-start | bytes 1572872 | tf_op jit(solution)/shard_map/ppermute | solution.py:331
  97.0 9.6 %expert_back.7 = (bf16[128,2048]{1,0:T(8,128)(2,1)S(1)}, bf16[64,2048]{1,0:T(8,128)(2,1)S(1)}, bf16[64,2048]{1,0:T(8,128)(2,1)S(1)}) custom-call(s32[1]{0:T(128)} %bitcast.11.base_ref, bf16[144,2048]{1,0:T(8,128)(2,1)S(1)} %collective-permute-done.7.refs_2_.refs_0_, bf16[128,2048]{1,0:T(8,128)(2,1)S(1)} %collective-permute-done.15.refs_1_, ...), custom_call_target="tpu_custom_call" | custom-call | flops 30000001024 | bytes 30000000 | tf_op jit(solution)/shard_map/expert_back/pallas_call | solution.py:294
  106.6 0.1 collective-permute-start.18
  106.7 0.5 collective-permute-start.19
  107.2 0.1 collective-permute-start.12
  107.3 0.9 collective-permute-done.18
  108.2 0.4 collective-permute-done.19
  108.6 5.6 %collective-permute-done.21 = bf16[128,2048]{1,0:T(8,128)(2,1)S(1)} collective-permute-done((bf16[128,2048]{1,0:T(8,128)(2,1)S(1)}, bf16[128,2048]{1,0:T(8,128)(2,1)S(1)}, u32[]{:S(2)}, u32[]{:S(2)}) %collective-permute-start.21) | collective-permute-done | bytes 524320 | tf_op jit(solution)/shard_map/ppermute | solution.py:331
  114.2 0.2 add_convert_fusion.1
  114.4 0.2 collective-permute-start.23
  114.7 1.3 unpack_groups.1
  115.9 12.4 %collective-permute-done.23 = bf16[128,2048]{1,0:T(8,128)(2,1)S(1)} collective-permute-done((bf16[128,2048]{1,0:T(8,128)(2,1)S(1)}, bf16[128,2048]{1,0:T(8,128)(2,1)S(1)}, u32[]{:S(2)}, u32[]{:S(2)}) %collective-permute-start.23) | collective-permute-done | bytes 524320 | tf_op jit(solution)/shard_map/ppermute | solution.py:331
  128.3 1.1 fusion
  (23 shorter events, 0.1 us)
Async XLA Ops:
  0.6 7.9 %copy-start.2 = (bf16[1,128,2048]{2,1,0:T(8,128)(2,1)S(1)}, bf16[1,128,2048]{2,1,0:T(8,128)(2,1)}, u32[]{:S(2)}) copy-start(bf16[1,128,2048]{2,1,0:T(8,128)(2,1)} %param.13) | copy-start | bytes 1572868
  3.4 8.3 %collective-permute-start = (bf16[272,2048]{1,0:T(8,128)(2,1)S(1)}, bf16[272,2048]{1,0:T(8,128)(2,1)}, u32[]{:S(2)}, u32[]{:S(2)}) collective-permute-start(bf16[272,2048]{1,0:T(8,128)(2,1)S(1)} %pad_maximum_fusion.refs_0_), channel_id=1, source_target_pairs={{0,1},{1,0},{2,3},{3,2},{4,5},{5,4},{6,7},{7,6},{8,9},{9,8},{10,11... | collective-permute-start | bytes 3342344 | tf_op jit(solution)/shard_map/ppermute | solution.py:328
  3.9 29.6 %collective-permute-start.4 = (bf16[272,2048]{1,0:T(8,128)(2,1)S(1)}, bf16[272,2048]{1,0:T(8,128)(2,1)S(1)}, u32[]{:S(2)}, u32[]{:S(2)}) collective-permute-start(bf16[272,2048]{1,0:T(8,128)(2,1)S(1)} %pad_maximum_fusion.refs_0_), channel_id=1, source_target_pairs={{0,6},{1,7},{2,0},{3,1},{4,2},{5,3},{6,4},{7,5},{8,14},{9,15},{10,... | collective-permute-start | bytes 3342344 | tf_op jit(solution)/shard_map/ppermute | solution.py:331
  8.6 39.6 %collective-permute-start.7 = (bf16[144,2048]{1,0:T(8,128)(2,1)S(1)}, bf16[144,2048]{1,0:T(8,128)(2,1)S(1)}, u32[]{:S(2)}, u32[]{:S(2)}) collective-permute-start(bf16[144,2048]{1,0:T(8,128)(2,1)S(1)} %pad_maximum_fusion.1), channel_id=1, source_target_pairs={{0,2},{1,3},{2,4},{3,5},{4,6},{5,7},{6,0},{7,1},{8,10},{9,11},{10,... | collective-permute-start | bytes 1769480 | tf_op jit(solution)/shard_map/ppermute | solution.py:331
  11.7 21.8 %collective-permute-start.1 = (bf16[4,128,512]{2,1,0:T(8,128)(2,1)}, bf16[4,128,512]{2,1,0:T(8,128)(2,1)S(1)}, u32[]{:S(2)}, u32[]{:S(2)}) collective-permute-start(bf16[4,128,512]{2,1,0:T(8,128)(2,1)} %get-tuple-element.70), channel_id=1, source_target_pairs={{0,8},{8,0},{16,24},{24,16},{1,9},{9,1},{17,25},{25,17},{2,10},{10... | collective-permute-start | bytes 1572872 | tf_op jit(solution)/shard_map/ppermute | solution.py:140
  13.2 25.2 %collective-permute-start.2 = (bf16[4,128,512]{2,1,0:T(8,128)(2,1)}, bf16[4,128,512]{2,1,0:T(8,128)(2,1)S(1)}, u32[]{:S(2)}, u32[]{:S(2)}) collective-permute-start(bf16[4,128,512]{2,1,0:T(8,128)(2,1)} %get-tuple-element.71), channel_id=1, source_target_pairs={{0,16},{8,24},{16,0},{24,8},{1,17},{9,25},{17,1},{25,9},{2,18},{10... | collective-permute-start | bytes 1572872 | tf_op jit(solution)/shard_map/ppermute | solution.py:140
  14.7 23.6 %collective-permute-start.3 = (bf16[4,128,512]{2,1,0:T(8,128)(2,1)}, bf16[4,128,512]{2,1,0:T(8,128)(2,1)S(1)}, u32[]{:S(2)}, u32[]{:S(2)}) collective-permute-start(bf16[4,128,512]{2,1,0:T(8,128)(2,1)} %get-tuple-element.72), channel_id=1, source_target_pairs={{0,24},{8,16},{16,8},{24,0},{1,25},{9,17},{17,9},{25,1},{2,26},{10... | collective-permute-start | bytes 1572872 | tf_op jit(solution)/shard_map/ppermute | solution.py:140
  15.2 26.7 %copy-start = (bf16[4,128,512]{2,1,0:T(8,128)(2,1)S(1)}, bf16[4,128,512]{2,1,0:T(8,128)(2,1)}, u32[]{:S(2)}) copy-start(bf16[4,128,512]{2,1,0:T(8,128)(2,1)} %get-tuple-element.78.refs_0_) | copy-start | bytes 1572868
  38.3 9.9 %collective-permute-start.6 = (bf16[272,2048]{1,0:T(8,128)(2,1)S(1)}, bf16[272,2048]{1,0:T(8,128)(2,1)S(1)}, u32[]{:S(2)}, u32[]{:S(2)}) collective-permute-start(bf16[272,2048]{1,0:T(8,128)(2,1)S(1)} %collective-permute-done.4.refs_0_), channel_id=1, source_target_pairs={{0,1},{1,0},{2,3},{3,2},{4,5},{5,4},{6,7},{7,6},{8,9},{9,8},{10,11... | collective-permute-start | bytes 3342344 | tf_op jit(solution)/shard_map/ppermute | solution.py:328
  38.3 32.2 %collective-permute-start.5 = (bf16[272,2048]{1,0:T(8,128)(2,1)S(1)}, bf16[272,2048]{1,0:T(8,128)(2,1)S(1)}, u32[]{:S(2)}, u32[]{:S(2)}) collective-permute-start(bf16[272,2048]{1,0:T(8,128)(2,1)S(1)} %collective-permute-done.4.refs_0_), channel_id=1, source_target_pairs={{0,6},{1,7},{2,0},{3,1},{4,2},{5,3},{6,4},{7,5},{8,14},{9,15},{10,... | collective-permute-start | bytes 3342344 | tf_op jit(solution)/shard_map/ppermute | solution.py:331
  48.2 3.8 %collective-permute-start.11 = (bf16[144,2048]{1,0:T(8,128)(2,1)S(1)}, bf16[144,2048]{1,0:T(8,128)(2,1)S(1)}, u32[]{:S(2)}, u32[]{:S(2)}) collective-permute-start(bf16[144,2048]{1,0:T(8,128)(2,1)S(1)} %collective-permute-done.7.refs_2_.refs_0_), channel_id=1, source_target_pairs={{0,1},{1,0},{2,3},{3,2},{4,5},{5,4},{6,7},{7,6},{8,9},{9,8},{10,11... | collective-permute-start | bytes 1769480 | tf_op jit(solution)/shard_map/ppermute | solution.py:328
  48.5 21.9 %collective-permute-start.8 = (bf16[3,128,512]{2,1,0:T(8,128)(2,1)S(1)}, bf16[3,128,512]{2,1,0:T(8,128)(2,1)S(1)}, u32[]{:S(2)}, u32[]{:S(2)}) collective-permute-start(bf16[3,128,512]{2,1,0:T(8,128)(2,1)S(1)} %get-tuple-element.87), channel_id=1, source_target_pairs={{0,8},{8,0},{16,24},{24,16},{1,9},{9,1},{17,25},{25,17},{2,10},{10... | collective-permute-start | bytes 1179656 | tf_op jit(solution)/shard_map/ppermute | solution.py:140
  49.8 20.7 %collective-permute-start.9 = (bf16[3,128,512]{2,1,0:T(8,128)(2,1)S(1)}, bf16[3,128,512]{2,1,0:T(8,128)(2,1)S(1)}, u32[]{:S(2)}, u32[]{:S(2)}) collective-permute-start(bf16[3,128,512]{2,1,0:T(8,128)(2,1)S(1)} %get-tuple-element.88), channel_id=1, source_target_pairs={{0,16},{8,24},{16,0},{24,8},{1,17},{9,25},{17,1},{25,9},{2,18},{10... | collective-permute-start | bytes 1179656 | tf_op jit(solution)/shard_map/ppermute | solution.py:140
  50.6 19.9 %collective-permute-start.10 = (bf16[3,128,512]{2,1,0:T(8,128)(2,1)S(1)}, bf16[3,128,512]{2,1,0:T(8,128)(2,1)S(1)}, u32[]{:S(2)}, u32[]{:S(2)}) collective-permute-start(bf16[3,128,512]{2,1,0:T(8,128)(2,1)S(1)} %get-tuple-element.89), channel_id=1, source_target_pairs={{0,24},{8,16},{16,8},{24,0},{1,25},{9,17},{17,9},{25,1},{2,26},{10... | collective-permute-start | bytes 1179656 | tf_op jit(solution)/shard_map/ppermute | solution.py:140
  52.0 18.6 %copy-start.1 = (bf16[1,128,2048]{2,1,0:T(8,128)(2,1)S(1)}, bf16[1,128,2048]{2,1,0:T(8,128)(2,1)}, u32[]{:S(2)}) copy-start(bf16[1,128,2048]{2,1,0:T(8,128)(2,1)} %param.12) | copy-start | bytes 1572868
  70.5 2.0 %collective-permute-start.13 = (bf16[128,2048]{1,0:T(8,128)(2,1)S(1)}, bf16[128,2048]{1,0:T(8,128)(2,1)S(1)}, u32[]{:S(2)}, u32[]{:S(2)}) collective-permute-start(bf16[128,2048]{1,0:T(8,128)(2,1)S(1)} %get-tuple-element.107), channel_id=1, source_target_pairs={{0,1},{1,0},{2,3},{3,2},{4,5},{5,4},{6,7},{7,6},{8,9},{9,8},{10,11... | collective-permute-start | bytes 1572872 | tf_op jit(solution)/shard_map/ppermute | solution.py:328
  70.6 16.5 %collective-permute-start.15 = (bf16[128,2048]{1,0:T(8,128)(2,1)S(1)}, bf16[128,2048]{1,0:T(8,128)(2,1)S(1)}, u32[]{:S(2)}, u32[]{:S(2)}) collective-permute-start(bf16[128,2048]{1,0:T(8,128)(2,1)S(1)} %bitcast.27), channel_id=1, source_target_pairs={{0,2},{1,3},{2,4},{3,5},{4,6},{5,7},{6,0},{7,1},{8,10},{9,11},{10,... | collective-permute-start | bytes 1572872 | tf_op jit(solution)/shard_map/ppermute | solution.py:331
  71.1 2.9 %collective-permute-start.16 = (bf16[272,2048]{1,0:T(8,128)(2,1)S(1)}, bf16[272,2048]{1,0:T(8,128)(2,1)S(1)}, u32[]{:S(2)}, u32[]{:S(2)}) collective-permute-start(bf16[272,2048]{1,0:T(8,128)(2,1)S(1)} %collective-permute-done.5.refs_0_), channel_id=1, source_target_pairs={{0,1},{1,0},{2,3},{3,2},{4,5},{5,4},{6,7},{7,6},{8,9},{9,8},{10,11... | collective-permute-start | bytes 3342344 | tf_op jit(solution)/shard_map/ppermute | solution.py:328
  72.7 19.7 %collective-permute-start.14 = (bf16[64,2048]{1,0:T(8,128)(2,1)S(1)}, bf16[64,2048]{1,0:T(8,128)(2,1)S(1)}, u32[]{:S(2)}, u32[]{:S(2)}) collective-permute-start(bf16[64,2048]{1,0:T(8,128)(2,1)S(1)} %get-tuple-element.127), channel_id=1, source_target_pairs={{0,2},{1,3},{2,4},{3,5},{4,6},{5,7},{6,0},{7,1},{8,10},{9,11},{10,... | collective-permute-start | bytes 786440 | tf_op jit(solution)/shard_map/ppermute | solution.py:331
  92.3 1.9 %collective-permute-start.20 = (bf16[128,2048]{1,0:T(8,128)(2,1)S(1)}, bf16[128,2048]{1,0:T(8,128)(2,1)S(1)}, u32[]{:S(2)}, u32[]{:S(2)}) collective-permute-start(bf16[128,2048]{1,0:T(8,128)(2,1)S(1)} %get-tuple-element.118), channel_id=1, source_target_pairs={{0,1},{1,0},{2,3},{3,2},{4,5},{5,4},{6,7},{7,6},{8,9},{9,8},{10,11... | collective-permute-start | bytes 1572872 | tf_op jit(solution)/shard_map/ppermute | solution.py:328
  92.3 4.7 %collective-permute-start.17 = (bf16[128,2048]{1,0:T(8,128)(2,1)S(1)}, bf16[128,2048]{1,0:T(8,128)(2,1)S(1)}, u32[]{:S(2)}, u32[]{:S(2)}) collective-permute-start(bf16[128,2048]{1,0:T(8,128)(2,1)S(1)} %collective-permute-done.15.refs_1_), channel_id=1, source_target_pairs={{0,1},{1,0},{2,3},{3,2},{4,5},{5,4},{6,7},{7,6},{8,9},{9,8},{10,11... | collective-permute-start | bytes 1572872 | tf_op jit(solution)/shard_map/ppermute | solution.py:328
  92.8 14.5 %collective-permute-start.22 = (bf16[64,2048]{1,0:T(8,128)(2,1)S(1)}, bf16[64,2048]{1,0:T(8,128)(2,1)S(1)}, u32[]{:S(2)}, u32[]{:S(2)}) collective-permute-start(bf16[64,2048]{1,0:T(8,128)(2,1)S(1)} %get-tuple-element.126), channel_id=1, source_target_pairs={{0,2},{1,3},{2,4},{3,5},{4,6},{5,7},{6,0},{7,1},{8,10},{9,11},{10,... | collective-permute-start | bytes 786440 | tf_op jit(solution)/shard_map/ppermute | solution.py:331
  94.4 19.8 %collective-permute-start.21 = (bf16[128,2048]{1,0:T(8,128)(2,1)S(1)}, bf16[128,2048]{1,0:T(8,128)(2,1)S(1)}, u32[]{:S(2)}, u32[]{:S(2)}) collective-permute-start(bf16[128,2048]{1,0:T(8,128)(2,1)S(1)} %add_convert_fusion.2), channel_id=1, source_target_pairs={{0,6},{1,7},{2,0},{3,1},{4,2},{5,3},{6,4},{7,5},{8,14},{9,15},{10,... | collective-permute-start | bytes 1572872 | tf_op jit(solution)/shard_map/ppermute | solution.py:331
  106.6 1.6 %collective-permute-start.18 = (bf16[64,2048]{1,0:T(8,128)(2,1)S(1)}, bf16[64,2048]{1,0:T(8,128)(2,1)S(1)}, u32[]{:S(2)}, u32[]{:S(2)}) collective-permute-start(bf16[64,2048]{1,0:T(8,128)(2,1)S(1)} %get-tuple-element.115), channel_id=1, source_target_pairs={{0,1},{1,0},{2,3},{3,2},{4,5},{5,4},{6,7},{7,6},{8,9},{9,8},{10,11... | collective-permute-start | bytes 786440 | tf_op jit(solution)/shard_map/ppermute | solution.py:328
  106.7 1.9 %collective-permute-start.19 = (bf16[64,2048]{1,0:T(8,128)(2,1)S(1)}, bf16[64,2048]{1,0:T(8,128)(2,1)S(1)}, u32[]{:S(2)}, u32[]{:S(2)}) collective-permute-start(bf16[64,2048]{1,0:T(8,128)(2,1)S(1)} %get-tuple-element.116), channel_id=1, source_target_pairs={{0,1},{1,0},{2,3},{3,2},{4,5},{5,4},{6,7},{7,6},{8,9},{9,8},{10,11... | collective-permute-start | bytes 786440 | tf_op jit(solution)/shard_map/ppermute | solution.py:328
  107.2 8.7 %collective-permute-start.12 = (bf16[128,2048]{1,0:T(8,128)(2,1)S(1)}, bf16[128,2048]{1,0:T(8,128)(2,1)S(1)}, u32[]{:S(2)}, u32[]{:S(2)}) collective-permute-start(bf16[128,2048]{1,0:T(8,128)(2,1)S(1)} %get-tuple-element.105), channel_id=1, source_target_pairs={{0,1},{1,0},{2,3},{3,2},{4,5},{5,4},{6,7},{7,6},{8,9},{9,8},{10,11... | collective-permute-start | bytes 1572872 | tf_op jit(solution)/shard_map/ppermute | solution.py:328
  114.4 13.9 %collective-permute-start.23 = (bf16[128,2048]{1,0:T(8,128)(2,1)S(1)}, bf16[128,2048]{1,0:T(8,128)(2,1)S(1)}, u32[]{:S(2)}, u32[]{:S(2)}) collective-permute-start(bf16[128,2048]{1,0:T(8,128)(2,1)S(1)} %add_convert_fusion.1), channel_id=1, source_target_pairs={{0,6},{1,7},{2,0},{3,1},{4,2},{5,3},{6,4},{7,5},{8,14},{9,15},{10,... | collective-permute-start | bytes 1572872 | tf_op jit(solution)/shard_map/ppermute | solution.py:331

commit v9 on v8

--- a/solution.py
+++ b/solution.py
@@ -21,7 +21,7 @@
 
 
 SMALL = cost(0)
-OWN_COST, HEADS_COST, LEFT_COST, FAR_COST, RIGHT_COST = 30, 30, 0, 0, 30
+OWN_COST, HEADS_COST, LEFT_COST, FAR_COST, RIGHT_COST = 30, 30, 0, 0, 0
 NT = (((1,), (1,)), ((), ()))
 TN = (((0,), (0,)), ((), ()))
 
@@ -376,25 +376,27 @@
     carried = left_sums[-1].astype(jnp.bfloat16)
     for sums in reversed(left_sums[:-1]):
         carried = add_up(sums, hop(carried, 1)).astype(jnp.bfloat16)
-    left_halves = [hop(carried[: bins // 2], 1), hop(carried[bins // 2 :], 1)]
+    left_carried = hop(carried, 1)
     rights = [(right_rows, hop(right_grads, 1))]
     for d in range(2, half):
         rights.append(tuple(hop(member, 1) for member in rights[-1]))
-    kept, give, _ = work(left_pair, weights, FAR_COST)
-    left_halves[0], rights, kept, give = barrier((left_halves[0], rights, kept, give))
+    kept, give, _ = work(left_pair, weights, FAR_COST, 2)
+    rights, kept, give = barrier((rights, kept, give))
     carried = add_up(kept, joined([swap(piece) for piece in give]))
     for d in range(half - 1, 0, -1):
         carried = hop(carried.astype(jnp.bfloat16), -1)
-        right_pair = pair(*rights[d - 1])
+        rows, grads = rights[d - 1]
+        halves = [swap(grads[: bins // 2]), swap(grads[bins // 2 :])]
+        right_pair = [[rows, grads], [right_partner if d == 1 else swap(rows), *halves]]
         if d == 1:
-            right_pair[1][0] = right_partner
+            right_pair, left_carried = barrier((right_pair, left_carried))
         kept, give, _ = work(
             right_pair, weights, RIGHT_COST, 2, slopes=slopes if d == 1 else None
         )
         given = [swap(piece) for piece in give]
-        kept, given, carried, left_halves = barrier((kept, given, carried, left_halves))
+        kept, given, carried = barrier((kept, given, carried))
         carried = add_up(kept, joined(given), carried)
-    total = add_up(total, joined(left_halves))
+    total = add_up(total, left_carried)
     carried = hop(carried.astype(jnp.bfloat16), -1)
     outs = unpack_groups(mine, results)
     total = add_up(total, carried).astype(jnp.bfloat16)

time: 130 us -> 136 us (1.046)
  starting transfers between devices: 21.4 us -> 34 us
  waiting for transfers between devices: 42.5 us -> 35.7 us
    ppermute x8 -> x7, starting transfers between devices: 12.2 us -> 23.9 us  [hop(): lax.ppermute(block, 'exp', [(i, (i + 2 * step) % members) for i in range(...]
    ppermute x8 -> x7, waiting for transfers between devices: 32.8 us -> 26.3 us  [hop(): lax.ppermute(block, 'exp', [(i, (i + 2 * step) % members) for i in range(...]
    ppermute x10 -> x12, starting transfers between devices: 2.26 us -> 3.11 us  [swap(): return lax.ppermute(block, 'exp', [(i, i ^ 1) for i in range(members)])]
    ppermute x10 -> x12, waiting for transfers between devices: 4.8 us -> 4.62 us  [swap(): return lax.ppermute(block, 'exp', [(i, i ^ 1) for i in range(members)])]
  transfers between devices with their start and end apart: 24 -> 25, of which waited for: 12 -> 11; matrix products, arithmetic and copies ran while one was open for 0% -> 0% of each run, Pallas kernels for 47% -> 45%
where the time goes in v9:
time: 136 us; the launch traced here: 135 us
  Pallas kernels  60.3 us (44%)
  waiting for transfers between devices  35.7 us (26%)
  starting transfers between devices  34 us (25%)
  other arithmetic  4.39 us (3%)
    pallas_call x4, Pallas kernels, expert_back(): pl.pallas_call(functools.partial(expert_kernel, layout, len(ahead), later...  49.7 us
    ppermute x7, waiting for transfers between devices, hop(): lax.ppermute(block, 'exp', [(i, (i + 2 * step) % members) for i in range(...  26.3 us
    ppermute x7, starting transfers between devices, hop(): lax.ppermute(block, 'exp', [(i, (i + 2 * step) % members) for i in range(...  23.9 us
    ppermute x6, starting transfers between devices, exchange(): lax.ppermute(blocks[place], 'ctx', [(i, i ^ place) for i in range(groups)])  6.98 us
    pallas_call x1, Pallas kernels, heads_back(): pl.pallas_call(heads_kernel, grid=(heads,), out_shape=[jax.ShapeDtypeStru...  6.37 us
    ppermute x6, waiting for transfers between devices, exchange(): lax.ppermute(blocks[place], 'ctx', [(i, i ^ place) for i in range(groups)])  4.85 us
    ppermute x12, waiting for transfers between devices, swap(): return lax.ppermute(block, 'exp', [(i, i ^ 1) for i in range(members)])  4.62 us
    ppermute x12, starting transfers between devices, swap(): return lax.ppermute(block, 'exp', [(i, i ^ 1) for i in range(members)])  3.11 us
  transfers between devices with their start and end apart: 25, of which 11 were waited for; matrix products, arithmetic and copies ran while one was open for 0% of the time, Pallas kernels for 45%

profile of v9, /device:TPU:0, one launch (start us, length us, event | category | flops | bytes accessed | tf_op | source)
XLA Modules:
  0.0 135.3 jit_solution(587745807779983186)
XLA Ops:
  0.6 0.7 fusion.10
  1.4 0.7 reduce-precision_convert_fusion.1
  2.1 1.3 pad_maximum_fusion.refs_0_
  3.4 0.5 collective-permute-start
  3.9 4.7 %collective-permute-start.4 = (bf16[272,2048]{1,0:T(8,128)(2,1)S(1)}, bf16[272,2048]{1,0:T(8,128)(2,1)S(1)}, u32[]{:S(2)}, u32[]{:S(2)}) collective-permute-start(bf16[272,2048]{1,0:T(8,128)(2,1)S(1)} %pad_maximum_fusion.refs_0_), channel_id=1, source_target_pairs={{0,6},{1,7},{2,0},{3,1},{4,2},{5,3},{6,4},{7,5},{8,14},{9,15},{10,... | collective-permute-start | bytes 3342344 | tf_op jit(solution)/shard_map/ppermute | solution.py:331
  8.6 0.1 collective-permute-start.7
  8.7 3.0 %pack_groups.1 = (bf16[4,128,512]{2,1,0:T(8,128)(2,1)}, bf16[4,128,512]{2,1,0:T(8,128)(2,1)}, bf16[4,128,512]{2,1,0:T(8,128)(2,1)}, bf16[4,128,512]{2,1,0:T(8,128)(2,1)}) custom-call(s32[1]{0:T(128)} %bitcast.mine_ref, bf16[128,2048]{1,0:T(8,128)(2,1)} %bitcast.30, bf16[128,2048]{1,0:T(8,128)(2,1)} %bitcast.31, bf16[128,2048]{1,0:T(8,128)(2,1)} %bitcast.32, ...), custom_call_target="tpu_custom_call" | custom-call | tf_op jit(solution)/shard_map/pack_groups/pallas_call | solution.py:58
  11.7 1.5 %collective-permute-start.1 = (bf16[4,128,512]{2,1,0:T(8,128)(2,1)}, bf16[4,128,512]{2,1,0:T(8,128)(2,1)S(1)}, u32[]{:S(2)}, u32[]{:S(2)}) collective-permute-start(bf16[4,128,512]{2,1,0:T(8,128)(2,1)} %get-tuple-element.75), channel_id=1, source_target_pairs={{0,8},{8,0},{16,24},{24,16},{1,9},{9,1},{17,25},{25,17},{2,10},{10... | collective-permute-start | bytes 1572872 | tf_op jit(solution)/shard_map/ppermute | solution.py:140
  13.2 1.5 %collective-permute-start.2 = (bf16[4,128,512]{2,1,0:T(8,128)(2,1)}, bf16[4,128,512]{2,1,0:T(8,128)(2,1)S(1)}, u32[]{:S(2)}, u32[]{:S(2)}) collective-permute-start(bf16[4,128,512]{2,1,0:T(8,128)(2,1)} %get-tuple-element.76), channel_id=1, source_target_pairs={{0,16},{8,24},{16,0},{24,8},{1,17},{9,25},{17,1},{25,9},{2,18},{10... | collective-permute-start | bytes 1572872 | tf_op jit(solution)/shard_map/ppermute | solution.py:140
  14.7 0.5 collective-permute-start.3
  15.2 15.8 %expert_back.4 = (bf16[128,2048]{1,0:T(8,128)(2,1)S(1)}, bf16[128,2048]{1,0:T(8,128)(2,1)S(1)}, bf16[4,2048,768]{2,1,0:T(8,128)(2,1)S(1)}, bf16[4,768,2048]{2,1,0:T(8,128)(2,1)S(1)}) custom-call(s32[1]{0:T(128)} %bitcast.11.base_ref, bf16[272,2048]{1,0:T(8,128)(2,1)S(1)} %pad_maximum_fusion.refs_0_, bf16[272,2048]{1,0:T(8,128)(2,1)} %collective-permute-done.refs_1_, ...), custom_call_target="tpu_custom_call" | custom-call | flops 30000001024 | bytes 30000000 | tf_op jit(solution)/shard_map/expert_back/pallas_call | solution.py:294
  31.0 2.5 %collective-permute-done.4.refs_0_ = bf16[272,2048]{1,0:T(8,128)(2,1)S(1)} collective-permute-done((bf16[272,2048]{1,0:T(8,128)(2,1)S(1)}, bf16[272,2048]{1,0:T(8,128)(2,1)S(1)}, u32[]{:S(2)}, u32[]{:S(2)}) %collective-permute-start.4) | collective-permute-done | bytes 1114144 | tf_op jit(solution)/shard_map/ppermute | solution.py:331
  33.5 4.8 %collective-permute-done.2.refs_2_ = bf16[4,128,512]{2,1,0:T(8,128)(2,1)S(1)} collective-permute-done((bf16[4,128,512]{2,1,0:T(8,128)(2,1)}, bf16[4,128,512]{2,1,0:T(8,128)(2,1)S(1)}, u32[]{:S(2)}, u32[]{:S(2)}) %collective-permute-start.2) | collective-permute-done | bytes 524320 | tf_op jit(solution)/shard_map/ppermute | solution.py:140
  38.3 3.5 %collective-permute-start.5 = (bf16[272,2048]{1,0:T(8,128)(2,1)S(1)}, bf16[272,2048]{1,0:T(8,128)(2,1)S(1)}, u32[]{:S(2)}, u32[]{:S(2)}) collective-permute-start(bf16[272,2048]{1,0:T(8,128)(2,1)S(1)} %collective-permute-done.4.refs_0_), channel_id=1, source_target_pairs={{0,6},{1,7},{2,0},{3,1},{4,2},{5,3},{6,4},{7,5},{8,14},{9,15},{10,... | collective-permute-start | bytes 3342344 | tf_op jit(solution)/shard_map/ppermute | solution.py:331
  41.9 6.4 %heads_back.1 = (bf16[3,128,512]{2,1,0:T(8,128)(2,1)S(1)}, bf16[3,128,512]{2,1,0:T(8,128)(2,1)S(1)}, bf16[3,128,512]{2,1,0:T(8,128)(2,1)S(1)}, bf16[3,128,512]{2,1,0:T(8,128)(2,1)S(1)}) custom-call(bf16[4,128,512]{2,1,0:T(8,128)(2,1)S(1)} %copy-done, bf16[4,128,512]{2,1,0:T(8,128)(2,1)S(1)} %collective-permute-done.1.refs_1_, ...), custom_call_target="tpu_custom_call" | custom-call | flops 30000001024 | bytes 30000000 | tf_op jit(solution)/shard_map/heads_back/pallas_call | solution.py:125
  48.2 0.3 collective-permute-start.11
  48.5 1.2 collective-permute-start.8
  49.8 0.8 collective-permute-start.9
  50.6 1.4 %collective-permute-start.10 = (bf16[3,128,512]{2,1,0:T(8,128)(2,1)S(1)}, bf16[3,128,512]{2,1,0:T(8,128)(2,1)S(1)}, u32[]{:S(2)}, u32[]{:S(2)}) collective-permute-start(bf16[3,128,512]{2,1,0:T(8,128)(2,1)S(1)} %get-tuple-element.94), channel_id=1, source_target_pairs={{0,24},{8,16},{16,8},{24,0},{1,25},{9,17},{17,9},{25,1},{2,26},{10... | collective-permute-start | bytes 1179656 | tf_op jit(solution)/shard_map/ppermute | solution.py:140
  52.0 12.3 %expert_back.5 = (bf16[128,2048]{1,0:T(8,128)(2,1)S(1)}, bf16[128,2048]{1,0:T(8,128)(2,1)S(1)}, f32[192,768]{1,0:T(8,128)S(1)}) custom-call(s32[1]{0:T(128)} %bitcast.11.base_ref, bf16[272,2048]{1,0:T(8,128)(2,1)S(1)} %collective-permute-done.4.refs_0_, bf16[272,2048]{1,0:T(8,128)(2,1)S(1)} %collective-permute-done.6.refs_1_, ...), custom_call_target="tpu_custom_call" | custom-call | tf_op jit(solution)/shard_map/expert_back/pallas_call | solution.py:294
  64.4 6.1 %collective-permute-done.5.refs_0_ = bf16[272,2048]{1,0:T(8,128)(2,1)S(1)} collective-permute-done((bf16[272,2048]{1,0:T(8,128)(2,1)S(1)}, bf16[272,2048]{1,0:T(8,128)(2,1)S(1)}, u32[]{:S(2)}, u32[]{:S(2)}) %collective-permute-start.5) | collective-permute-done | bytes 1114144 | tf_op jit(solution)/shard_map/ppermute | solution.py:331
  70.5 0.1 collective-permute-start.14
  70.6 0.4 collective-permute-start.17
  71.1 0.5 collective-permute-start.13
  71.6 2.5 %collective-permute-done.17 = bf16[128,2048]{1,0:T(8,128)(2,1)S(1)} collective-permute-done((bf16[128,2048]{1,0:T(8,128)(2,1)S(1)}, bf16[128,2048]{1,0:T(8,128)(2,1)S(1)}, u32[]{:S(2)}, u32[]{:S(2)}) %collective-permute-start.17) | collective-permute-done | bytes 524320 | tf_op jit(solution)/shard_map/ppermute | solution.py:328
  74.1 0.1 add_convert_fusion.3
  74.2 0.5 collective-permute-start.18
  74.7 12.0 %expert_back.6 = (bf16[128,2048]{1,0:T(8,128)(2,1)S(1)}, bf16[64,2048]{1,0:T(8,128)(2,1)S(1)}, bf16[64,2048]{1,0:T(8,128)(2,1)S(1)}) custom-call(s32[1]{0:T(128)} %bitcast.11.base_ref, bf16[272,2048]{1,0:T(8,128)(2,1)S(1)} %collective-permute-done.5.refs_0_, bf16[272,2048]{1,0:T(8,128)(2,1)S(1)} %collective-permute-done.14.refs_1_, ...), custom_call_target="tpu_custom_call" | custom-call | tf_op jit(solution)/shard_map/expert_back/pallas_call | solution.py:294
  86.7 0.9 collective-permute-done.13.refs_1_
  87.7 0.5 collective-permute-start.22
  88.2 0.1 collective-permute-start.16
  88.3 0.5 collective-permute-start.15
  88.8 0.4 collective-permute-done.21
  89.2 0.4 collective-permute-done.22
  89.6 0.1 add_convert_fusion.2
  89.7 2.7 %collective-permute-start.23 = (bf16[128,2048]{1,0:T(8,128)(2,1)S(1)}, bf16[128,2048]{1,0:T(8,128)(2,1)S(1)}, u32[]{:S(2)}, u32[]{:S(2)}) collective-permute-start(bf16[128,2048]{1,0:T(8,128)(2,1)S(1)} %add_convert_fusion.2), channel_id=1, source_target_pairs={{0,6},{1,7},{2,0},{3,1},{4,2},{5,3},{6,4},{7,5},{8,14},{9,15},{10,... | collective-permute-start | bytes 1572872 | tf_op jit(solution)/shard_map/ppermute | solution.py:331
  92.4 6.5 %collective-permute-done.18 = bf16[128,2048]{1,0:T(8,128)(2,1)S(1)} collective-permute-done((bf16[128,2048]{1,0:T(8,128)(2,1)S(1)}, bf16[128,2048]{1,0:T(8,128)(2,1)S(1)}, u32[]{:S(2)}, u32[]{:S(2)}) %collective-permute-start.18) | collective-permute-done | bytes 524320 | tf_op jit(solution)/shard_map/ppermute | solution.py:331
  98.9 9.6 %expert_back.7 = (bf16[128,2048]{1,0:T(8,128)(2,1)S(1)}, bf16[64,2048]{1,0:T(8,128)(2,1)S(1)}, bf16[64,2048]{1,0:T(8,128)(2,1)S(1)}) custom-call(s32[1]{0:T(128)} %bitcast.11.base_ref, bf16[144,2048]{1,0:T(8,128)(2,1)S(1)} %collective-permute-done.7.refs_2_.refs_0_, bf16[128,2048]{1,0:T(8,128)(2,1)S(1)} %collective-permute-done.13.refs_1_, ...), custom_call_target="tpu_custom_call" | custom-call | tf_op jit(solution)/shard_map/expert_back/pallas_call | solution.py:294
  108.5 0.1 collective-permute-start.19
  108.6 0.5 collective-permute-start.20
  109.1 0.1 collective-permute-start.12
  109.2 0.9 collective-permute-done.19
  110.1 0.4 collective-permute-done.20
  110.5 0.2 add_convert_fusion.1
  110.8 11.9 %collective-permute-start.24 = (bf16[128,2048]{1,0:T(8,128)(2,1)S(1)}, bf16[128,2048]{1,0:T(8,128)(2,1)S(1)}, u32[]{:S(2)}, u32[]{:S(2)}) collective-permute-start(bf16[128,2048]{1,0:T(8,128)(2,1)S(1)} %add_convert_fusion.1), channel_id=1, source_target_pairs={{0,6},{1,7},{2,0},{3,1},{4,2},{5,3},{6,4},{7,5},{8,14},{9,15},{10,... | collective-permute-start | bytes 1572872 | tf_op jit(solution)/shard_map/ppermute | solution.py:331
  122.7 1.3 unpack_groups.1
  123.9 10.2 %collective-permute-done.24 = bf16[128,2048]{1,0:T(8,128)(2,1)S(1)} collective-permute-done((bf16[128,2048]{1,0:T(8,128)(2,1)S(1)}, bf16[128,2048]{1,0:T(8,128)(2,1)S(1)}, u32[]{:S(2)}, u32[]{:S(2)}) %collective-permute-start.24) | collective-permute-done | bytes 524320 | tf_op jit(solution)/shard_map/ppermute | solution.py:331
  134.2 1.1 fusion
  (25 shorter events, 0.2 us)
Async XLA Ops:
  0.6 7.9 %copy-start.2 = (bf16[1,128,2048]{2,1,0:T(8,128)(2,1)S(1)}, bf16[1,128,2048]{2,1,0:T(8,128)(2,1)}, u32[]{:S(2)}) copy-start(bf16[1,128,2048]{2,1,0:T(8,128)(2,1)} %param.13) | copy-start | bytes 1572868
  3.4 8.3 %collective-permute-start = (bf16[272,2048]{1,0:T(8,128)(2,1)S(1)}, bf16[272,2048]{1,0:T(8,128)(2,1)}, u32[]{:S(2)}, u32[]{:S(2)}) collective-permute-start(bf16[272,2048]{1,0:T(8,128)(2,1)S(1)} %pad_maximum_fusion.refs_0_), channel_id=1, source_target_pairs={{0,1},{1,0},{2,3},{3,2},{4,5},{5,4},{6,7},{7,6},{8,9},{9,8},{10,11... | collective-permute-start | bytes 3342344 | tf_op jit(solution)/shard_map/ppermute | solution.py:328
  3.9 29.6 %collective-permute-start.4 = (bf16[272,2048]{1,0:T(8,128)(2,1)S(1)}, bf16[272,2048]{1,0:T(8,128)(2,1)S(1)}, u32[]{:S(2)}, u32[]{:S(2)}) collective-permute-start(bf16[272,2048]{1,0:T(8,128)(2,1)S(1)} %pad_maximum_fusion.refs_0_), channel_id=1, source_target_pairs={{0,6},{1,7},{2,0},{3,1},{4,2},{5,3},{6,4},{7,5},{8,14},{9,15},{10,... | collective-permute-start | bytes 3342344 | tf_op jit(solution)/shard_map/ppermute | solution.py:331
  8.6 39.6 %collective-permute-start.7 = (bf16[144,2048]{1,0:T(8,128)(2,1)S(1)}, bf16[144,2048]{1,0:T(8,128)(2,1)S(1)}, u32[]{:S(2)}, u32[]{:S(2)}) collective-permute-start(bf16[144,2048]{1,0:T(8,128)(2,1)S(1)} %pad_maximum_fusion.1), channel_id=1, source_target_pairs={{0,2},{1,3},{2,4},{3,5},{4,6},{5,7},{6,0},{7,1},{8,10},{9,11},{10,... | collective-permute-start | bytes 1769480 | tf_op jit(solution)/shard_map/ppermute | solution.py:331
  11.7 21.8 %collective-permute-start.1 = (bf16[4,128,512]{2,1,0:T(8,128)(2,1)}, bf16[4,128,512]{2,1,0:T(8,128)(2,1)S(1)}, u32[]{:S(2)}, u32[]{:S(2)}) collective-permute-start(bf16[4,128,512]{2,1,0:T(8,128)(2,1)} %get-tuple-element.75), channel_id=1, source_target_pairs={{0,8},{8,0},{16,24},{24,16},{1,9},{9,1},{17,25},{25,17},{2,10},{10... | collective-permute-start | bytes 1572872 | tf_op jit(solution)/shard_map/ppermute | solution.py:140
  13.2 25.2 %collective-permute-start.2 = (bf16[4,128,512]{2,1,0:T(8,128)(2,1)}, bf16[4,128,512]{2,1,0:T(8,128)(2,1)S(1)}, u32[]{:S(2)}, u32[]{:S(2)}) collective-permute-start(bf16[4,128,512]{2,1,0:T(8,128)(2,1)} %get-tuple-element.76), channel_id=1, source_target_pairs={{0,16},{8,24},{16,0},{24,8},{1,17},{9,25},{17,1},{25,9},{2,18},{10... | collective-permute-start | bytes 1572872 | tf_op jit(solution)/shard_map/ppermute | solution.py:140
  14.7 23.6 %collective-permute-start.3 = (bf16[4,128,512]{2,1,0:T(8,128)(2,1)}, bf16[4,128,512]{2,1,0:T(8,128)(2,1)S(1)}, u32[]{:S(2)}, u32[]{:S(2)}) collective-permute-start(bf16[4,128,512]{2,1,0:T(8,128)(2,1)} %get-tuple-element.77), channel_id=1, source_target_pairs={{0,24},{8,16},{16,8},{24,0},{1,25},{9,17},{17,9},{25,1},{2,26},{10... | collective-permute-start | bytes 1572872 | tf_op jit(solution)/shard_map/ppermute | solution.py:140
  15.2 26.7 %copy-start = (bf16[4,128,512]{2,1,0:T(8,128)(2,1)S(1)}, bf16[4,128,512]{2,1,0:T(8,128)(2,1)}, u32[]{:S(2)}) copy-start(bf16[4,128,512]{2,1,0:T(8,128)(2,1)} %get-tuple-element.83.refs_0_) | copy-start | bytes 1572868
  38.3 9.9 %collective-permute-start.6 = (bf16[272,2048]{1,0:T(8,128)(2,1)S(1)}, bf16[272,2048]{1,0:T(8,128)(2,1)S(1)}, u32[]{:S(2)}, u32[]{:S(2)}) collective-permute-start(bf16[272,2048]{1,0:T(8,128)(2,1)S(1)} %collective-permute-done.4.refs_0_), channel_id=1, source_target_pairs={{0,1},{1,0},{2,3},{3,2},{4,5},{5,4},{6,7},{7,6},{8,9},{9,8},{10,11... | collective-permute-start | bytes 3342344 | tf_op jit(solution)/shard_map/ppermute | solution.py:328
  38.3 32.2 %collective-permute-start.5 = (bf16[272,2048]{1,0:T(8,128)(2,1)S(1)}, bf16[272,2048]{1,0:T(8,128)(2,1)S(1)}, u32[]{:S(2)}, u32[]{:S(2)}) collective-permute-start(bf16[272,2048]{1,0:T(8,128)(2,1)S(1)} %collective-permute-done.4.refs_0_), channel_id=1, source_target_pairs={{0,6},{1,7},{2,0},{3,1},{4,2},{5,3},{6,4},{7,5},{8,14},{9,15},{10,... | collective-permute-start | bytes 3342344 | tf_op jit(solution)/shard_map/ppermute | solution.py:331
  48.2 3.8 %collective-permute-start.11 = (bf16[144,2048]{1,0:T(8,128)(2,1)S(1)}, bf16[144,2048]{1,0:T(8,128)(2,1)S(1)}, u32[]{:S(2)}, u32[]{:S(2)}) collective-permute-start(bf16[144,2048]{1,0:T(8,128)(2,1)S(1)} %collective-permute-done.7.refs_2_.refs_0_), channel_id=1, source_target_pairs={{0,1},{1,0},{2,3},{3,2},{4,5},{5,4},{6,7},{7,6},{8,9},{9,8},{10,11... | collective-permute-start | bytes 1769480 | tf_op jit(solution)/shard_map/ppermute | solution.py:328
  48.5 21.9 %collective-permute-start.8 = (bf16[3,128,512]{2,1,0:T(8,128)(2,1)S(1)}, bf16[3,128,512]{2,1,0:T(8,128)(2,1)S(1)}, u32[]{:S(2)}, u32[]{:S(2)}) collective-permute-start(bf16[3,128,512]{2,1,0:T(8,128)(2,1)S(1)} %get-tuple-element.92), channel_id=1, source_target_pairs={{0,8},{8,0},{16,24},{24,16},{1,9},{9,1},{17,25},{25,17},{2,10},{10... | collective-permute-start | bytes 1179656 | tf_op jit(solution)/shard_map/ppermute | solution.py:140
  49.8 20.7 %collective-permute-start.9 = (bf16[3,128,512]{2,1,0:T(8,128)(2,1)S(1)}, bf16[3,128,512]{2,1,0:T(8,128)(2,1)S(1)}, u32[]{:S(2)}, u32[]{:S(2)}) collective-permute-start(bf16[3,128,512]{2,1,0:T(8,128)(2,1)S(1)} %get-tuple-element.93), channel_id=1, source_target_pairs={{0,16},{8,24},{16,0},{24,8},{1,17},{9,25},{17,1},{25,9},{2,18},{10... | collective-permute-start | bytes 1179656 | tf_op jit(solution)/shard_map/ppermute | solution.py:140
  50.6 19.9 %collective-permute-start.10 = (bf16[3,128,512]{2,1,0:T(8,128)(2,1)S(1)}, bf16[3,128,512]{2,1,0:T(8,128)(2,1)S(1)}, u32[]{:S(2)}, u32[]{:S(2)}) collective-permute-start(bf16[3,128,512]{2,1,0:T(8,128)(2,1)S(1)} %get-tuple-element.94), channel_id=1, source_target_pairs={{0,24},{8,16},{16,8},{24,0},{1,25},{9,17},{17,9},{25,1},{2,26},{10... | collective-permute-start | bytes 1179656 | tf_op jit(solution)/shard_map/ppermute | solution.py:140
  52.0 19.0 %copy-start.1 = (bf16[1,128,2048]{2,1,0:T(8,128)(2,1)S(1)}, bf16[1,128,2048]{2,1,0:T(8,128)(2,1)}, u32[]{:S(2)}) copy-start(bf16[1,128,2048]{2,1,0:T(8,128)(2,1)} %param.12) | copy-start | bytes 1572868
  70.5 4.2 %collective-permute-start.14 = (bf16[272,2048]{1,0:T(8,128)(2,1)S(1)}, bf16[272,2048]{1,0:T(8,128)(2,1)S(1)}, u32[]{:S(2)}, u32[]{:S(2)}) collective-permute-start(bf16[272,2048]{1,0:T(8,128)(2,1)S(1)} %collective-permute-done.5.refs_0_), channel_id=1, source_target_pairs={{0,1},{1,0},{2,3},{3,2},{4,5},{5,4},{6,7},{7,6},{8,9},{9,8},{10,11... | collective-permute-start | bytes 3342344 | tf_op jit(solution)/shard_map/ppermute | solution.py:328
  70.6 3.4 %collective-permute-start.17 = (bf16[128,2048]{1,0:T(8,128)(2,1)S(1)}, bf16[128,2048]{1,0:T(8,128)(2,1)S(1)}, u32[]{:S(2)}, u32[]{:S(2)}) collective-permute-start(bf16[128,2048]{1,0:T(8,128)(2,1)S(1)} %get-tuple-element.118), channel_id=1, source_target_pairs={{0,1},{1,0},{2,3},{3,2},{4,5},{5,4},{6,7},{7,6},{8,9},{9,8},{10,11... | collective-permute-start | bytes 1572872 | tf_op jit(solution)/shard_map/ppermute | solution.py:328
  71.1 16.6 %collective-permute-start.13 = (bf16[128,2048]{1,0:T(8,128)(2,1)S(1)}, bf16[128,2048]{1,0:T(8,128)(2,1)S(1)}, u32[]{:S(2)}, u32[]{:S(2)}) collective-permute-start(bf16[128,2048]{1,0:T(8,128)(2,1)S(1)} %bitcast.27), channel_id=1, source_target_pairs={{0,2},{1,3},{2,4},{3,5},{4,6},{5,7},{6,0},{7,1},{8,10},{9,11},{10,... | collective-permute-start | bytes 1572872 | tf_op jit(solution)/shard_map/ppermute | solution.py:331
  74.2 24.7 %collective-permute-start.18 = (bf16[128,2048]{1,0:T(8,128)(2,1)S(1)}, bf16[128,2048]{1,0:T(8,128)(2,1)S(1)}, u32[]{:S(2)}, u32[]{:S(2)}) collective-permute-start(bf16[128,2048]{1,0:T(8,128)(2,1)S(1)} %add_convert_fusion.3), channel_id=1, source_target_pairs={{0,2},{1,3},{2,4},{3,5},{4,6},{5,7},{6,0},{7,1},{8,10},{9,11},{10,... | collective-permute-start | bytes 1572872 | tf_op jit(solution)/shard_map/ppermute | solution.py:331
  87.6 1.5 %collective-permute-start.21 = (bf16[64,2048]{1,0:T(8,128)(2,1)S(1)}, bf16[64,2048]{1,0:T(8,128)(2,1)S(1)}, u32[]{:S(2)}, u32[]{:S(2)}) collective-permute-start(bf16[64,2048]{1,0:T(8,128)(2,1)S(1)} %get-tuple-element.130), channel_id=1, source_target_pairs={{0,1},{1,0},{2,3},{3,2},{4,5},{5,4},{6,7},{7,6},{8,9},{9,8},{10,11... | collective-permute-start | bytes 786440 | tf_op jit(solution)/shard_map/ppermute | solution.py:328
  87.7 1.9 %collective-permute-start.22 = (bf16[64,2048]{1,0:T(8,128)(2,1)S(1)}, bf16[64,2048]{1,0:T(8,128)(2,1)S(1)}, u32[]{:S(2)}, u32[]{:S(2)}) collective-permute-start(bf16[64,2048]{1,0:T(8,128)(2,1)S(1)} %get-tuple-element.131), channel_id=1, source_target_pairs={{0,1},{1,0},{2,3},{3,2},{4,5},{5,4},{6,7},{7,6},{8,9},{9,8},{10,11... | collective-permute-start | bytes 786440 | tf_op jit(solution)/shard_map/ppermute | solution.py:328
  88.2 10.7 %collective-permute-start.16 = (bf16[64,2048]{1,0:T(8,128)(2,1)S(1)}, bf16[64,2048]{1,0:T(8,128)(2,1)S(1)}, u32[]{:S(2)}, u32[]{:S(2)}) collective-permute-start(bf16[64,2048]{1,0:T(8,128)(2,1)S(1)} %get-tuple-element.136), channel_id=1, source_target_pairs={{0,1},{1,0},{2,3},{3,2},{4,5},{5,4},{6,7},{7,6},{8,9},{9,8},{10,11... | collective-permute-start | bytes 786440 | tf_op jit(solution)/shard_map/ppermute | solution.py:328
  88.3 10.6 %collective-permute-start.15 = (bf16[64,2048]{1,0:T(8,128)(2,1)S(1)}, bf16[64,2048]{1,0:T(8,128)(2,1)S(1)}, u32[]{:S(2)}, u32[]{:S(2)}) collective-permute-start(bf16[64,2048]{1,0:T(8,128)(2,1)S(1)} %get-tuple-element.137), channel_id=1, source_target_pairs={{0,1},{1,0},{2,3},{3,2},{4,5},{5,4},{6,7},{7,6},{8,9},{9,8},{10,11... | collective-permute-start | bytes 786440 | tf_op jit(solution)/shard_map/ppermute | solution.py:328
  89.7 20.8 %collective-permute-start.23 = (bf16[128,2048]{1,0:T(8,128)(2,1)S(1)}, bf16[128,2048]{1,0:T(8,128)(2,1)S(1)}, u32[]{:S(2)}, u32[]{:S(2)}) collective-permute-start(bf16[128,2048]{1,0:T(8,128)(2,1)S(1)} %add_convert_fusion.2), channel_id=1, source_target_pairs={{0,6},{1,7},{2,0},{3,1},{4,2},{5,3},{6,4},{7,5},{8,14},{9,15},{10,... | collective-permute-start | bytes 1572872 | tf_op jit(solution)/shard_map/ppermute | solution.py:331
  108.5 1.6 %collective-permute-start.19 = (bf16[64,2048]{1,0:T(8,128)(2,1)S(1)}, bf16[64,2048]{1,0:T(8,128)(2,1)S(1)}, u32[]{:S(2)}, u32[]{:S(2)}) collective-permute-start(bf16[64,2048]{1,0:T(8,128)(2,1)S(1)} %get-tuple-element.127), channel_id=1, source_target_pairs={{0,1},{1,0},{2,3},{3,2},{4,5},{5,4},{6,7},{7,6},{8,9},{9,8},{10,11... | collective-permute-start | bytes 786440 | tf_op jit(solution)/shard_map/ppermute | solution.py:328
  108.6 1.9 %collective-permute-start.20 = (bf16[64,2048]{1,0:T(8,128)(2,1)S(1)}, bf16[64,2048]{1,0:T(8,128)(2,1)S(1)}, u32[]{:S(2)}, u32[]{:S(2)}) collective-permute-start(bf16[64,2048]{1,0:T(8,128)(2,1)S(1)} %get-tuple-element.128), channel_id=1, source_target_pairs={{0,1},{1,0},{2,3},{3,2},{4,5},{5,4},{6,7},{7,6},{8,9},{9,8},{10,11... | collective-permute-start | bytes 786440 | tf_op jit(solution)/shard_map/ppermute | solution.py:328
  109.1 14.8 %collective-permute-start.12 = (bf16[128,2048]{1,0:T(8,128)(2,1)S(1)}, bf16[128,2048]{1,0:T(8,128)(2,1)S(1)}, u32[]{:S(2)}, u32[]{:S(2)}) collective-permute-start(bf16[128,2048]{1,0:T(8,128)(2,1)S(1)} %get-tuple-element.110), channel_id=1, source_target_pairs={{0,1},{1,0},{2,3},{3,2},{4,5},{5,4},{6,7},{7,6},{8,9},{9,8},{10,11... | collective-permute-start | bytes 1572872 | tf_op jit(solution)/shard_map/ppermute | solution.py:328
  110.8 23.4 %collective-permute-start.24 = (bf16[128,2048]{1,0:T(8,128)(2,1)S(1)}, bf16[128,2048]{1,0:T(8,128)(2,1)S(1)}, u32[]{:S(2)}, u32[]{:S(2)}) collective-permute-start(bf16[128,2048]{1,0:T(8,128)(2,1)S(1)} %add_convert_fusion.1), channel_id=1, source_target_pairs={{0,6},{1,7},{2,0},{3,1},{4,2},{5,3},{6,4},{7,5},{8,14},{9,15},{10,... | collective-permute-start | bytes 1572872 | tf_op jit(solution)/shard_map/ppermute | solution.py:331

commit v10 on v8

--- a/solution.py
+++ b/solution.py
@@ -392,12 +392,11 @@
             right_pair, weights, RIGHT_COST, 2, slopes=slopes if d == 1 else None
         )
         given = [swap(piece) for piece in give]
-        kept, given, carried, left_halves = barrier((kept, given, carried, left_halves))
+        kept, given, carried = barrier((kept, given, carried))
         carried = add_up(kept, joined(given), carried)
-    total = add_up(total, joined(left_halves))
     carried = hop(carried.astype(jnp.bfloat16), -1)
     outs = unpack_groups(mine, results)
-    total = add_up(total, carried).astype(jnp.bfloat16)
+    total = add_up(total, joined(left_halves), carried).astype(jnp.bfloat16)
     return tuple(out[None] for out in outs) + (total[None],)
 
 

time: 130 us -> 131 us (level)
  starting transfers between devices: 21.4 us -> 23.7 us
  waiting for transfers between devices: 42.5 us -> 41.1 us
    ppermute x8, starting transfers between devices: 12.2 us -> 14.4 us  [hop(): lax.ppermute(block, 'exp', [(i, (i + 2 * step) % members) for i in range(...]
    ppermute x8, waiting for transfers between devices: 32.8 us -> 31.5 us  [hop(): lax.ppermute(block, 'exp', [(i, (i + 2 * step) % members) for i in range(...]
  transfers between devices with their start and end apart: 24 -> 24, of which waited for: 12 -> 12; matrix products, arithmetic and copies ran while one was open for 0% -> 0% of each run, Pallas kernels for 47% -> 46%
where the time goes in v10:
time: 131 us; the launch traced here: 130 us
  Pallas kernels  60.3 us (46%)
  waiting for transfers between devices  41.1 us (31%)
  starting transfers between devices  23.7 us (18%)
  other arithmetic  4.39 us (3%)
    pallas_call x4, Pallas kernels, expert_back(): pl.pallas_call(functools.partial(expert_kernel, layout, len(ahead), later...  49.7 us
    ppermute x8, waiting for transfers between devices, hop(): lax.ppermute(block, 'exp', [(i, (i + 2 * step) % members) for i in range(...  31.5 us
    ppermute x8, starting transfers between devices, hop(): lax.ppermute(block, 'exp', [(i, (i + 2 * step) % members) for i in range(...  14.4 us
    ppermute x6, starting transfers between devices, exchange(): lax.ppermute(blocks[place], 'ctx', [(i, i ^ place) for i in range(groups)])  6.98 us
    pallas_call x1, Pallas kernels, heads_back(): pl.pallas_call(heads_kernel, grid=(heads,), out_shape=[jax.ShapeDtypeStru...  6.37 us
    ppermute x6, waiting for transfers between devices, exchange(): lax.ppermute(blocks[place], 'ctx', [(i, i ^ place) for i in range(groups)])  4.85 us
    ppermute x10, waiting for transfers between devices, swap(): return lax.ppermute(block, 'exp', [(i, i ^ 1) for i in range(members)])  4.8 us
    pallas_call x1, Pallas kernels, pack_groups(): pl.pallas_call(pack_kernel, out_shape=[block] * groups, in_specs=[pl.Bloc...  2.99 us
  transfers between devices with their start and end apart: 24, of which 12 were waited for; matrix products, arithmetic and copies ran while one was open for 0% of the time, Pallas kernels for 46%

profile of v10, /device:TPU:0, one launch (start us, length us, event | category | flops | bytes accessed | tf_op | source)
XLA Modules:
  0.0 130.3 jit_solution(8782636192280941243)
XLA Ops:
  0.6 0.0 copy-start.2
  0.6 0.7 fusion.10
  1.4 0.7 reduce-precision_convert_fusion.1
  2.1 1.3 pad_maximum_fusion.refs_0_
  3.4 0.5 collective-permute-start
  3.9 4.7 %collective-permute-start.4 = (bf16[272,2048]{1,0:T(8,128)(2,1)S(1)}, bf16[272,2048]{1,0:T(8,128)(2,1)S(1)}, u32[]{:S(2)}, u32[]{:S(2)}) collective-permute-start(bf16[272,2048]{1,0:T(8,128)(2,1)S(1)} %pad_maximum_fusion.refs_0_), channel_id=1, source_target_pairs={{0,6},{1,7},{2,0},{3,1},{4,2},{5,3},{6,4},{7,5},{8,14},{9,15},{10,... | collective-permute-start | bytes 3342344 | tf_op jit(solution)/shard_map/ppermute | solution.py:331
  8.6 0.1 collective-permute-start.7
  8.7 3.0 %pack_groups.1 = (bf16[4,128,512]{2,1,0:T(8,128)(2,1)}, bf16[4,128,512]{2,1,0:T(8,128)(2,1)}, bf16[4,128,512]{2,1,0:T(8,128)(2,1)}, bf16[4,128,512]{2,1,0:T(8,128)(2,1)}) custom-call(s32[1]{0:T(128)} %bitcast.mine_ref, bf16[128,2048]{1,0:T(8,128)(2,1)} %bitcast.30, bf16[128,2048]{1,0:T(8,128)(2,1)} %bitcast.31, bf16[128,2048]{1,0:T(8,128)(2,1)} %bitcast.32, ...), custom_call_target="tpu_custom_call" | custom-call | tf_op jit(solution)/shard_map/pack_groups/pallas_call | solution.py:58
  11.7 1.5 %collective-permute-start.1 = (bf16[4,128,512]{2,1,0:T(8,128)(2,1)}, bf16[4,128,512]{2,1,0:T(8,128)(2,1)S(1)}, u32[]{:S(2)}, u32[]{:S(2)}) collective-permute-start(bf16[4,128,512]{2,1,0:T(8,128)(2,1)} %get-tuple-element.68), channel_id=1, source_target_pairs={{0,8},{8,0},{16,24},{24,16},{1,9},{9,1},{17,25},{25,17},{2,10},{10... | collective-permute-start | bytes 1572872 | tf_op jit(solution)/shard_map/ppermute | solution.py:140
  13.2 1.5 %collective-permute-start.2 = (bf16[4,128,512]{2,1,0:T(8,128)(2,1)}, bf16[4,128,512]{2,1,0:T(8,128)(2,1)S(1)}, u32[]{:S(2)}, u32[]{:S(2)}) collective-permute-start(bf16[4,128,512]{2,1,0:T(8,128)(2,1)} %get-tuple-element.69), channel_id=1, source_target_pairs={{0,16},{8,24},{16,0},{24,8},{1,17},{9,25},{17,1},{25,9},{2,18},{10... | collective-permute-start | bytes 1572872 | tf_op jit(solution)/shard_map/ppermute | solution.py:140
  14.7 0.5 collective-permute-start.3
  15.2 15.8 %expert_back.4 = (bf16[128,2048]{1,0:T(8,128)(2,1)S(1)}, bf16[128,2048]{1,0:T(8,128)(2,1)S(1)}, bf16[4,2048,768]{2,1,0:T(8,128)(2,1)S(1)}, bf16[4,768,2048]{2,1,0:T(8,128)(2,1)S(1)}) custom-call(s32[1]{0:T(128)} %bitcast.11.base_ref, bf16[272,2048]{1,0:T(8,128)(2,1)S(1)} %pad_maximum_fusion.refs_0_, bf16[272,2048]{1,0:T(8,128)(2,1)} %collective-permute-done.refs_1_, ...), custom_call_target="tpu_custom_call" | custom-call | flops 30000001024 | bytes 30000000 | tf_op jit(solution)/shard_map/expert_back/pallas_call | solution.py:294
  31.0 2.5 %collective-permute-done.4.refs_0_ = bf16[272,2048]{1,0:T(8,128)(2,1)S(1)} collective-permute-done((bf16[272,2048]{1,0:T(8,128)(2,1)S(1)}, bf16[272,2048]{1,0:T(8,128)(2,1)S(1)}, u32[]{:S(2)}, u32[]{:S(2)}) %collective-permute-start.4) | collective-permute-done | bytes 1114144 | tf_op jit(solution)/shard_map/ppermute | solution.py:331
  33.5 4.8 %collective-permute-done.2.refs_2_ = bf16[4,128,512]{2,1,0:T(8,128)(2,1)S(1)} collective-permute-done((bf16[4,128,512]{2,1,0:T(8,128)(2,1)}, bf16[4,128,512]{2,1,0:T(8,128)(2,1)S(1)}, u32[]{:S(2)}, u32[]{:S(2)}) %collective-permute-start.2) | collective-permute-done | bytes 524320 | tf_op jit(solution)/shard_map/ppermute | solution.py:140
  38.3 3.5 %collective-permute-start.5 = (bf16[272,2048]{1,0:T(8,128)(2,1)S(1)}, bf16[272,2048]{1,0:T(8,128)(2,1)S(1)}, u32[]{:S(2)}, u32[]{:S(2)}) collective-permute-start(bf16[272,2048]{1,0:T(8,128)(2,1)S(1)} %collective-permute-done.4.refs_0_), channel_id=1, source_target_pairs={{0,6},{1,7},{2,0},{3,1},{4,2},{5,3},{6,4},{7,5},{8,14},{9,15},{10,... | collective-permute-start | bytes 3342344 | tf_op jit(solution)/shard_map/ppermute | solution.py:331
  41.9 6.4 %heads_back.1 = (bf16[3,128,512]{2,1,0:T(8,128)(2,1)S(1)}, bf16[3,128,512]{2,1,0:T(8,128)(2,1)S(1)}, bf16[3,128,512]{2,1,0:T(8,128)(2,1)S(1)}, bf16[3,128,512]{2,1,0:T(8,128)(2,1)S(1)}) custom-call(bf16[4,128,512]{2,1,0:T(8,128)(2,1)S(1)} %copy-done, bf16[4,128,512]{2,1,0:T(8,128)(2,1)S(1)} %collective-permute-done.1.refs_1_, ...), custom_call_target="tpu_custom_call" | custom-call | flops 30000001024 | bytes 30000000 | tf_op jit(solution)/shard_map/heads_back/pallas_call | solution.py:125
  48.2 0.3 collective-permute-start.11
  48.5 1.2 collective-permute-start.8
  49.8 0.8 collective-permute-start.9
  50.6 1.4 %collective-permute-start.10 = (bf16[3,128,512]{2,1,0:T(8,128)(2,1)S(1)}, bf16[3,128,512]{2,1,0:T(8,128)(2,1)S(1)}, u32[]{:S(2)}, u32[]{:S(2)}) collective-permute-start(bf16[3,128,512]{2,1,0:T(8,128)(2,1)S(1)} %get-tuple-element.87), channel_id=1, source_target_pairs={{0,24},{8,16},{16,8},{24,0},{1,25},{9,17},{17,9},{25,1},{2,26},{10... | collective-permute-start | bytes 1179656 | tf_op jit(solution)/shard_map/ppermute | solution.py:140
  52.0 12.3 %expert_back.5 = (bf16[128,2048]{1,0:T(8,128)(2,1)S(1)}, bf16[128,2048]{1,0:T(8,128)(2,1)S(1)}, f32[192,768]{1,0:T(8,128)S(1)}) custom-call(s32[1]{0:T(128)} %bitcast.11.base_ref, bf16[272,2048]{1,0:T(8,128)(2,1)S(1)} %collective-permute-done.4.refs_0_, bf16[272,2048]{1,0:T(8,128)(2,1)S(1)} %collective-permute-done.6.refs_1_, ...), custom_call_target="tpu_custom_call" | custom-call | tf_op jit(solution)/shard_map/expert_back/pallas_call | solution.py:294
  64.4 6.1 %collective-permute-done.5.refs_0_ = bf16[272,2048]{1,0:T(8,128)(2,1)S(1)} collective-permute-done((bf16[272,2048]{1,0:T(8,128)(2,1)S(1)}, bf16[272,2048]{1,0:T(8,128)(2,1)S(1)}, u32[]{:S(2)}, u32[]{:S(2)}) %collective-permute-start.5) | collective-permute-done | bytes 1114144 | tf_op jit(solution)/shard_map/ppermute | solution.py:331
  70.5 0.1 collective-permute-start.13
  70.6 0.5 collective-permute-start.15
  71.1 0.2 collective-permute-start.16
  71.3 1.2 collective-permute-done.13
  72.5 0.1 add_convert_fusion.3
  72.7 0.5 collective-permute-start.14
  73.2 0.9 collective-permute-done.16.refs_1_
  74.1 12.0 %expert_back.6 = (bf16[128,2048]{1,0:T(8,128)(2,1)S(1)}, bf16[128,2048]{1,0:T(8,128)(2,1)S(1)}) custom-call(s32[1]{0:T(128)} %bitcast.11.base_ref, bf16[272,2048]{1,0:T(8,128)(2,1)S(1)} %collective-permute-done.5.refs_0_, bf16[272,2048]{1,0:T(8,128)(2,1)S(1)} %collective-permute-done.16.refs_1_, ...), custom_call_target="tpu_custom_call" | custom-call | tf_op jit(solution)/shard_map/expert_back/pallas_call | solution.py:294
  86.1 1.1 collective-permute-done.15.refs_1_
  87.2 5.2 %collective-permute-done.14 = bf16[64,2048]{1,0:T(8,128)(2,1)S(1)} collective-permute-done((bf16[64,2048]{1,0:T(8,128)(2,1)S(1)}, bf16[64,2048]{1,0:T(8,128)(2,1)S(1)}, u32[]{:S(2)}, u32[]{:S(2)}) %collective-permute-start.14) | collective-permute-done | bytes 262176 | tf_op jit(solution)/shard_map/ppermute | solution.py:331
  92.3 0.5 collective-permute-start.18
  92.8 1.4 %collective-permute-done.21 = bf16[128,2048]{1,0:T(8,128)(2,1)S(1)} collective-permute-done((bf16[128,2048]{1,0:T(8,128)(2,1)S(1)}, bf16[128,2048]{1,0:T(8,128)(2,1)S(1)}, u32[]{:S(2)}, u32[]{:S(2)}) %collective-permute-start.21) | collective-permute-done | bytes 524320 | tf_op jit(solution)/shard_map/ppermute | solution.py:328
  94.2 0.1 add_convert_fusion.2
  94.4 1.8 %collective-permute-start.22 = (bf16[128,2048]{1,0:T(8,128)(2,1)S(1)}, bf16[128,2048]{1,0:T(8,128)(2,1)S(1)}, u32[]{:S(2)}, u32[]{:S(2)}) collective-permute-start(bf16[128,2048]{1,0:T(8,128)(2,1)S(1)} %add_convert_fusion.2), channel_id=1, source_target_pairs={{0,6},{1,7},{2,0},{3,1},{4,2},{5,3},{6,4},{7,5},{8,14},{9,15},{10,... | collective-permute-start | bytes 1572872 | tf_op jit(solution)/shard_map/ppermute | solution.py:331
  96.1 9.6 %expert_back.7 = (bf16[128,2048]{1,0:T(8,128)(2,1)S(1)}, bf16[64,2048]{1,0:T(8,128)(2,1)S(1)}, bf16[64,2048]{1,0:T(8,128)(2,1)S(1)}) custom-call(s32[1]{0:T(128)} %bitcast.11.base_ref, bf16[144,2048]{1,0:T(8,128)(2,1)S(1)} %collective-permute-done.7.refs_2_.refs_0_, bf16[128,2048]{1,0:T(8,128)(2,1)S(1)} %collective-permute-done.15.refs_1_, ...), custom_call_target="tpu_custom_call" | custom-call | flops 30000001024 | bytes 30000000 | tf_op jit(solution)/shard_map/expert_back/pallas_call | solution.py:294
  105.7 0.1 collective-permute-start.19
  105.8 0.5 collective-permute-start.20
  106.3 0.1 collective-permute-start.12
  106.4 0.9 collective-permute-done.19
  107.3 0.4 collective-permute-done.20
  107.7 0.8 collective-permute-done.22
  108.6 0.2 add_convert_fusion.1
  108.8 3.4 %collective-permute-start.23 = (bf16[128,2048]{1,0:T(8,128)(2,1)S(1)}, bf16[128,2048]{1,0:T(8,128)(2,1)S(1)}, u32[]{:S(2)}, u32[]{:S(2)}) collective-permute-start(bf16[128,2048]{1,0:T(8,128)(2,1)S(1)} %add_convert_fusion.1), channel_id=1, source_target_pairs={{0,6},{1,7},{2,0},{3,1},{4,2},{5,3},{6,4},{7,5},{8,14},{9,15},{10,... | collective-permute-start | bytes 1572872 | tf_op jit(solution)/shard_map/ppermute | solution.py:331
  112.2 1.3 unpack_groups.1
  113.5 15.8 %collective-permute-done.17 = bf16[64,2048]{1,0:T(8,128)(2,1)S(1)} collective-permute-done((bf16[64,2048]{1,0:T(8,128)(2,1)S(1)}, bf16[64,2048]{1,0:T(8,128)(2,1)S(1)}, u32[]{:S(2)}, u32[]{:S(2)}) %collective-permute-start.17) | collective-permute-done | bytes 262176 | tf_op jit(solution)/shard_map/ppermute | solution.py:331
  129.2 1.1 fusion
  (23 shorter events, 0.1 us)
Async XLA Ops:
  0.6 7.9 %copy-start.2 = (bf16[1,128,2048]{2,1,0:T(8,128)(2,1)S(1)}, bf16[1,128,2048]{2,1,0:T(8,128)(2,1)}, u32[]{:S(2)}) copy-start(bf16[1,128,2048]{2,1,0:T(8,128)(2,1)} %param.13) | copy-start | bytes 1572868
  3.4 8.3 %collective-permute-start = (bf16[272,2048]{1,0:T(8,128)(2,1)S(1)}, bf16[272,2048]{1,0:T(8,128)(2,1)}, u32[]{:S(2)}, u32[]{:S(2)}) collective-permute-start(bf16[272,2048]{1,0:T(8,128)(2,1)S(1)} %pad_maximum_fusion.refs_0_), channel_id=1, source_target_pairs={{0,1},{1,0},{2,3},{3,2},{4,5},{5,4},{6,7},{7,6},{8,9},{9,8},{10,11... | collective-permute-start | bytes 3342344 | tf_op jit(solution)/shard_map/ppermute | solution.py:328
  3.9 29.6 %collective-permute-start.4 = (bf16[272,2048]{1,0:T(8,128)(2,1)S(1)}, bf16[272,2048]{1,0:T(8,128)(2,1)S(1)}, u32[]{:S(2)}, u32[]{:S(2)}) collective-permute-start(bf16[272,2048]{1,0:T(8,128)(2,1)S(1)} %pad_maximum_fusion.refs_0_), channel_id=1, source_target_pairs={{0,6},{1,7},{2,0},{3,1},{4,2},{5,3},{6,4},{7,5},{8,14},{9,15},{10,... | collective-permute-start | bytes 3342344 | tf_op jit(solution)/shard_map/ppermute | solution.py:331
  8.6 39.6 %collective-permute-start.7 = (bf16[144,2048]{1,0:T(8,128)(2,1)S(1)}, bf16[144,2048]{1,0:T(8,128)(2,1)S(1)}, u32[]{:S(2)}, u32[]{:S(2)}) collective-permute-start(bf16[144,2048]{1,0:T(8,128)(2,1)S(1)} %pad_maximum_fusion.1), channel_id=1, source_target_pairs={{0,2},{1,3},{2,4},{3,5},{4,6},{5,7},{6,0},{7,1},{8,10},{9,11},{10,... | collective-permute-start | bytes 1769480 | tf_op jit(solution)/shard_map/ppermute | solution.py:331
  11.7 21.8 %collective-permute-start.1 = (bf16[4,128,512]{2,1,0:T(8,128)(2,1)}, bf16[4,128,512]{2,1,0:T(8,128)(2,1)S(1)}, u32[]{:S(2)}, u32[]{:S(2)}) collective-permute-start(bf16[4,128,512]{2,1,0:T(8,128)(2,1)} %get-tuple-element.68), channel_id=1, source_target_pairs={{0,8},{8,0},{16,24},{24,16},{1,9},{9,1},{17,25},{25,17},{2,10},{10... | collective-permute-start | bytes 1572872 | tf_op jit(solution)/shard_map/ppermute | solution.py:140
  13.2 25.2 %collective-permute-start.2 = (bf16[4,128,512]{2,1,0:T(8,128)(2,1)}, bf16[4,128,512]{2,1,0:T(8,128)(2,1)S(1)}, u32[]{:S(2)}, u32[]{:S(2)}) collective-permute-start(bf16[4,128,512]{2,1,0:T(8,128)(2,1)} %get-tuple-element.69), channel_id=1, source_target_pairs={{0,16},{8,24},{16,0},{24,8},{1,17},{9,25},{17,1},{25,9},{2,18},{10... | collective-permute-start | bytes 1572872 | tf_op jit(solution)/shard_map/ppermute | solution.py:140
  14.7 23.6 %collective-permute-start.3 = (bf16[4,128,512]{2,1,0:T(8,128)(2,1)}, bf16[4,128,512]{2,1,0:T(8,128)(2,1)S(1)}, u32[]{:S(2)}, u32[]{:S(2)}) collective-permute-start(bf16[4,128,512]{2,1,0:T(8,128)(2,1)} %get-tuple-element.70), channel_id=1, source_target_pairs={{0,24},{8,16},{16,8},{24,0},{1,25},{9,17},{17,9},{25,1},{2,26},{10... | collective-permute-start | bytes 1572872 | tf_op jit(solution)/shard_map/ppermute | solution.py:140
  15.2 26.7 %copy-start = (bf16[4,128,512]{2,1,0:T(8,128)(2,1)S(1)}, bf16[4,128,512]{2,1,0:T(8,128)(2,1)}, u32[]{:S(2)}) copy-start(bf16[4,128,512]{2,1,0:T(8,128)(2,1)} %get-tuple-element.76.refs_0_) | copy-start | bytes 1572868
  38.3 9.9 %collective-permute-start.6 = (bf16[272,2048]{1,0:T(8,128)(2,1)S(1)}, bf16[272,2048]{1,0:T(8,128)(2,1)S(1)}, u32[]{:S(2)}, u32[]{:S(2)}) collective-permute-start(bf16[272,2048]{1,0:T(8,128)(2,1)S(1)} %collective-permute-done.4.refs_0_), channel_id=1, source_target_pairs={{0,1},{1,0},{2,3},{3,2},{4,5},{5,4},{6,7},{7,6},{8,9},{9,8},{10,11... | collective-permute-start | bytes 3342344 | tf_op jit(solution)/shard_map/ppermute | solution.py:328
  38.3 32.2 %collective-permute-start.5 = (bf16[272,2048]{1,0:T(8,128)(2,1)S(1)}, bf16[272,2048]{1,0:T(8,128)(2,1)S(1)}, u32[]{:S(2)}, u32[]{:S(2)}) collective-permute-start(bf16[272,2048]{1,0:T(8,128)(2,1)S(1)} %collective-permute-done.4.refs_0_), channel_id=1, source_target_pairs={{0,6},{1,7},{2,0},{3,1},{4,2},{5,3},{6,4},{7,5},{8,14},{9,15},{10,... | collective-permute-start | bytes 3342344 | tf_op jit(solution)/shard_map/ppermute | solution.py:331
  48.2 3.8 %collective-permute-start.11 = (bf16[144,2048]{1,0:T(8,128)(2,1)S(1)}, bf16[144,2048]{1,0:T(8,128)(2,1)S(1)}, u32[]{:S(2)}, u32[]{:S(2)}) collective-permute-start(bf16[144,2048]{1,0:T(8,128)(2,1)S(1)} %collective-permute-done.7.refs_2_.refs_0_), channel_id=1, source_target_pairs={{0,1},{1,0},{2,3},{3,2},{4,5},{5,4},{6,7},{7,6},{8,9},{9,8},{10,11... | collective-permute-start | bytes 1769480 | tf_op jit(solution)/shard_map/ppermute | solution.py:328
  48.5 21.9 %collective-permute-start.8 = (bf16[3,128,512]{2,1,0:T(8,128)(2,1)S(1)}, bf16[3,128,512]{2,1,0:T(8,128)(2,1)S(1)}, u32[]{:S(2)}, u32[]{:S(2)}) collective-permute-start(bf16[3,128,512]{2,1,0:T(8,128)(2,1)S(1)} %get-tuple-element.85), channel_id=1, source_target_pairs={{0,8},{8,0},{16,24},{24,16},{1,9},{9,1},{17,25},{25,17},{2,10},{10... | collective-permute-start | bytes 1179656 | tf_op jit(solution)/shard_map/ppermute | solution.py:140
  49.8 20.7 %collective-permute-start.9 = (bf16[3,128,512]{2,1,0:T(8,128)(2,1)S(1)}, bf16[3,128,512]{2,1,0:T(8,128)(2,1)S(1)}, u32[]{:S(2)}, u32[]{:S(2)}) collective-permute-start(bf16[3,128,512]{2,1,0:T(8,128)(2,1)S(1)} %get-tuple-element.86), channel_id=1, source_target_pairs={{0,16},{8,24},{16,0},{24,8},{1,17},{9,25},{17,1},{25,9},{2,18},{10... | collective-permute-start | bytes 1179656 | tf_op jit(solution)/shard_map/ppermute | solution.py:140
  50.6 19.9 %collective-permute-start.10 = (bf16[3,128,512]{2,1,0:T(8,128)(2,1)S(1)}, bf16[3,128,512]{2,1,0:T(8,128)(2,1)S(1)}, u32[]{:S(2)}, u32[]{:S(2)}) collective-permute-start(bf16[3,128,512]{2,1,0:T(8,128)(2,1)S(1)} %get-tuple-element.87), channel_id=1, source_target_pairs={{0,24},{8,16},{16,8},{24,0},{1,25},{9,17},{17,9},{25,1},{2,26},{10... | collective-permute-start | bytes 1179656 | tf_op jit(solution)/shard_map/ppermute | solution.py:140
  52.0 18.6 %copy-start.1 = (bf16[1,128,2048]{2,1,0:T(8,128)(2,1)S(1)}, bf16[1,128,2048]{2,1,0:T(8,128)(2,1)}, u32[]{:S(2)}) copy-start(bf16[1,128,2048]{2,1,0:T(8,128)(2,1)} %param.12) | copy-start | bytes 1572868
  70.5 2.0 %collective-permute-start.13 = (bf16[128,2048]{1,0:T(8,128)(2,1)S(1)}, bf16[128,2048]{1,0:T(8,128)(2,1)S(1)}, u32[]{:S(2)}, u32[]{:S(2)}) collective-permute-start(bf16[128,2048]{1,0:T(8,128)(2,1)S(1)} %get-tuple-element.105), channel_id=1, source_target_pairs={{0,1},{1,0},{2,3},{3,2},{4,5},{5,4},{6,7},{7,6},{8,9},{9,8},{10,11... | collective-permute-start | bytes 1572872 | tf_op jit(solution)/shard_map/ppermute | solution.py:328
  70.6 16.5 %collective-permute-start.15 = (bf16[128,2048]{1,0:T(8,128)(2,1)S(1)}, bf16[128,2048]{1,0:T(8,128)(2,1)S(1)}, u32[]{:S(2)}, u32[]{:S(2)}) collective-permute-start(bf16[128,2048]{1,0:T(8,128)(2,1)S(1)} %bitcast.27), channel_id=1, source_target_pairs={{0,2},{1,3},{2,4},{3,5},{4,6},{5,7},{6,0},{7,1},{8,10},{9,11},{10,... | collective-permute-start | bytes 1572872 | tf_op jit(solution)/shard_map/ppermute | solution.py:331
  71.1 2.9 %collective-permute-start.16 = (bf16[272,2048]{1,0:T(8,128)(2,1)S(1)}, bf16[272,2048]{1,0:T(8,128)(2,1)S(1)}, u32[]{:S(2)}, u32[]{:S(2)}) collective-permute-start(bf16[272,2048]{1,0:T(8,128)(2,1)S(1)} %collective-permute-done.5.refs_0_), channel_id=1, source_target_pairs={{0,1},{1,0},{2,3},{3,2},{4,5},{5,4},{6,7},{7,6},{8,9},{9,8},{10,11... | collective-permute-start | bytes 3342344 | tf_op jit(solution)/shard_map/ppermute | solution.py:328
  72.7 19.7 %collective-permute-start.14 = (bf16[64,2048]{1,0:T(8,128)(2,1)S(1)}, bf16[64,2048]{1,0:T(8,128)(2,1)S(1)}, u32[]{:S(2)}, u32[]{:S(2)}) collective-permute-start(bf16[64,2048]{1,0:T(8,128)(2,1)S(1)} %get-tuple-element.123), channel_id=1, source_target_pairs={{0,2},{1,3},{2,4},{3,5},{4,6},{5,7},{6,0},{7,1},{8,10},{9,11},{10,... | collective-permute-start | bytes 786440 | tf_op jit(solution)/shard_map/ppermute | solution.py:331
  92.3 1.9 %collective-permute-start.21 = (bf16[128,2048]{1,0:T(8,128)(2,1)S(1)}, bf16[128,2048]{1,0:T(8,128)(2,1)S(1)}, u32[]{:S(2)}, u32[]{:S(2)}) collective-permute-start(bf16[128,2048]{1,0:T(8,128)(2,1)S(1)} %get-tuple-element.117), channel_id=1, source_target_pairs={{0,1},{1,0},{2,3},{3,2},{4,5},{5,4},{6,7},{7,6},{8,9},{9,8},{10,11... | collective-permute-start | bytes 1572872 | tf_op jit(solution)/shard_map/ppermute | solution.py:328
  92.3 3.8 %collective-permute-start.18 = (bf16[128,2048]{1,0:T(8,128)(2,1)S(1)}, bf16[128,2048]{1,0:T(8,128)(2,1)S(1)}, u32[]{:S(2)}, u32[]{:S(2)}) collective-permute-start(bf16[128,2048]{1,0:T(8,128)(2,1)S(1)} %collective-permute-done.15.refs_1_), channel_id=1, source_target_pairs={{0,1},{1,0},{2,3},{3,2},{4,5},{5,4},{6,7},{7,6},{8,9},{9,8},{10,11... | collective-permute-start | bytes 1572872 | tf_op jit(solution)/shard_map/ppermute | solution.py:328
  94.4 14.2 %collective-permute-start.22 = (bf16[128,2048]{1,0:T(8,128)(2,1)S(1)}, bf16[128,2048]{1,0:T(8,128)(2,1)S(1)}, u32[]{:S(2)}, u32[]{:S(2)}) collective-permute-start(bf16[128,2048]{1,0:T(8,128)(2,1)S(1)} %add_convert_fusion.2), channel_id=1, source_target_pairs={{0,6},{1,7},{2,0},{3,1},{4,2},{5,3},{6,4},{7,5},{8,14},{9,15},{10,... | collective-permute-start | bytes 1572872 | tf_op jit(solution)/shard_map/ppermute | solution.py:331
  105.7 1.6 %collective-permute-start.19 = (bf16[64,2048]{1,0:T(8,128)(2,1)S(1)}, bf16[64,2048]{1,0:T(8,128)(2,1)S(1)}, u32[]{:S(2)}, u32[]{:S(2)}) collective-permute-start(bf16[64,2048]{1,0:T(8,128)(2,1)S(1)} %get-tuple-element.114), channel_id=1, source_target_pairs={{0,1},{1,0},{2,3},{3,2},{4,5},{5,4},{6,7},{7,6},{8,9},{9,8},{10,11... | collective-permute-start | bytes 786440 | tf_op jit(solution)/shard_map/ppermute | solution.py:328
  105.8 1.9 %collective-permute-start.20 = (bf16[64,2048]{1,0:T(8,128)(2,1)S(1)}, bf16[64,2048]{1,0:T(8,128)(2,1)S(1)}, u32[]{:S(2)}, u32[]{:S(2)}) collective-permute-start(bf16[64,2048]{1,0:T(8,128)(2,1)S(1)} %get-tuple-element.115), channel_id=1, source_target_pairs={{0,1},{1,0},{2,3},{3,2},{4,5},{5,4},{6,7},{7,6},{8,9},{9,8},{10,11... | collective-permute-start | bytes 786440 | tf_op jit(solution)/shard_map/ppermute | solution.py:328
  106.3 7.1 %collective-permute-start.12 = (bf16[128,2048]{1,0:T(8,128)(2,1)S(1)}, bf16[128,2048]{1,0:T(8,128)(2,1)S(1)}, u32[]{:S(2)}, u32[]{:S(2)}) collective-permute-start(bf16[128,2048]{1,0:T(8,128)(2,1)S(1)} %get-tuple-element.103), channel_id=1, source_target_pairs={{0,1},{1,0},{2,3},{3,2},{4,5},{5,4},{6,7},{7,6},{8,9},{9,8},{10,11... | collective-permute-start | bytes 1572872 | tf_op jit(solution)/shard_map/ppermute | solution.py:328
  108.8 20.4 %collective-permute-start.23 = (bf16[128,2048]{1,0:T(8,128)(2,1)S(1)}, bf16[128,2048]{1,0:T(8,128)(2,1)S(1)}, u32[]{:S(2)}, u32[]{:S(2)}) collective-permute-start(bf16[128,2048]{1,0:T(8,128)(2,1)S(1)} %add_convert_fusion.1), channel_id=1, source_target_pairs={{0,6},{1,7},{2,0},{3,1},{4,2},{5,3},{6,4},{7,5},{8,14},{9,15},{10,... | collective-permute-start | bytes 1572872 | tf_op jit(solution)/shard_map/ppermute | solution.py:331
  112.2 17.0 %collective-permute-start.17 = (bf16[64,2048]{1,0:T(8,128)(2,1)S(1)}, bf16[64,2048]{1,0:T(8,128)(2,1)S(1)}, u32[]{:S(2)}, u32[]{:S(2)}) collective-permute-start(bf16[64,2048]{1,0:T(8,128)(2,1)S(1)} %get-tuple-element.122), channel_id=1, source_target_pairs={{0,2},{1,3},{2,4},{3,5},{4,6},{5,7},{6,0},{7,1},{8,10},{9,11},{10,... | collective-permute-start | bytes 786440 | tf_op jit(solution)/shard_map/ppermute | solution.py:331

commit v11 on v8

--- a/solution.py
+++ b/solution.py
@@ -384,20 +384,23 @@
     left_halves[0], rights, kept, give = barrier((left_halves[0], rights, kept, give))
     carried = add_up(kept, joined([swap(piece) for piece in give]))
     for d in range(half - 1, 0, -1):
-        carried = hop(carried.astype(jnp.bfloat16), -1)
+        cut = bins - bins // 4
+        carried = carried.astype(jnp.bfloat16)
+        most, last = hop(carried[:cut], -1), hop(carried[cut:], -1)
         right_pair = pair(*rights[d - 1])
         if d == 1:
             right_pair[1][0] = right_partner
         kept, give, _ = work(
-            right_pair, weights, RIGHT_COST, 2, slopes=slopes if d == 1 else None
+            right_pair, weights, RIGHT_COST, 4, slopes=slopes if d == 1 else None
         )
+        kept, give, left_halves = barrier((kept, give, left_halves))
         given = [swap(piece) for piece in give]
-        kept, given, carried, left_halves = barrier((kept, given, carried, left_halves))
-        carried = add_up(kept, joined(given), carried)
+        sums = [add_up(kept[:cut], joined(given[:3]), most), add_up(kept[cut:], given[3], last)]
+        carried = jnp.concatenate(sums, axis=0)
     total = add_up(total, joined(left_halves))
-    carried = hop(carried.astype(jnp.bfloat16), -1)
+    returned = [hop(part.astype(jnp.bfloat16), -1) for part in sums]
     outs = unpack_groups(mine, results)
-    total = add_up(total, carried).astype(jnp.bfloat16)
+    total = add_up(total, joined(returned)).astype(jnp.bfloat16)
     return tuple(out[None] for out in outs) + (total[None],)
 
 

time: 130 us -> 127 us (0.977)
  waiting for transfers between devices: 42.5 us -> 37 us
  starting transfers between devices: 21.4 us -> 24 us
    ppermute x8 -> x10, waiting for transfers between devices: 32.8 us -> 28.2 us  [hop(): lax.ppermute(block, 'exp', [(i, (i + 2 * step) % members) for i in range(...]
    ppermute x8 -> x10, starting transfers between devices: 12.2 us -> 14 us  [hop(): lax.ppermute(block, 'exp', [(i, (i + 2 * step) % members) for i in range(...]
    ppermute x10 -> x12, waiting for transfers between devices: 4.8 us -> 3.96 us  [swap(): return lax.ppermute(block, 'exp', [(i, i ^ 1) for i in range(members)])]
    ppermute x10 -> x12, starting transfers between devices: 2.26 us -> 3.01 us  [swap(): return lax.ppermute(block, 'exp', [(i, i ^ 1) for i in range(members)])]
  transfers between devices with their start and end apart: 24 -> 28, of which waited for: 12 -> 13; matrix products, arithmetic and copies ran while one was open for 0% -> 0% of each run, Pallas kernels for 47% -> 48%
where the time goes in v11:
time: 127 us
  Pallas kernels  60.3 us (47%)
  waiting for transfers between devices  37 us (29%)
  starting transfers between devices  24 us (19%)
  other arithmetic  4.34 us (3%)
    pallas_call x4, Pallas kernels, expert_back(): pl.pallas_call(functools.partial(expert_kernel, layout, len(ahead), later...  49.7 us
    ppermute x10, waiting for transfers between devices, hop(): lax.ppermute(block, 'exp', [(i, (i + 2 * step) % members) for i in range(...  28.2 us
    ppermute x10, starting transfers between devices, hop(): lax.ppermute(block, 'exp', [(i, (i + 2 * step) % members) for i in range(...  14 us
    ppermute x6, starting transfers between devices, exchange(): lax.ppermute(blocks[place], 'ctx', [(i, i ^ place) for i in range(groups)])  6.98 us
    pallas_call x1, Pallas kernels, heads_back(): pl.pallas_call(heads_kernel, grid=(heads,), out_shape=[jax.ShapeDtypeStru...  6.37 us
    ppermute x6, waiting for transfers between devices, exchange(): lax.ppermute(blocks[place], 'ctx', [(i, i ^ place) for i in range(groups)])  4.85 us
    ppermute x12, waiting for transfers between devices, swap(): return lax.ppermute(block, 'exp', [(i, i ^ 1) for i in range(members)])  3.96 us
    ppermute x12, starting transfers between devices, swap(): return lax.ppermute(block, 'exp', [(i, i ^ 1) for i in range(members)])  3.01 us
  transfers between devices with their start and end apart: 28, of which 13 were waited for; matrix products, arithmetic and copies ran while one was open for 0% of the time, Pallas kernels for 48%

profile of v11, /device:TPU:0, one launch (start us, length us, event | category | flops | bytes accessed | tf_op | source)
XLA Modules:
  0.0 126.6 jit_solution(4880535670674904231)
XLA Ops:
  0.6 0.7 fusion.10
  1.4 0.7 reduce-precision_convert_fusion.1
  2.1 1.3 %pad_maximum_fusion.refs_0_ = bf16[272,2048]{1,0:T(8,128)(2,1)S(1)} fusion(bf16[128,2048]{1,0:T(8,128)(2,1)} %bitcast.25, bf16[16,2048]{1,0:T(8,128)(2,1)S(1)} %fusion.7, bf16[128,2048]{1,0:T(8,128)(2,1)} %bitcast.28), kind=kLoop, calls=%fused_computation | loop fusion | flops 3342336 | bytes 2228224 | tf_op jit(solution)/shard_map/concatenate | solution.py:154
  3.4 0.5 collective-permute-start
  3.9 4.7 %collective-permute-start.4 = (bf16[272,2048]{1,0:T(8,128)(2,1)S(1)}, bf16[272,2048]{1,0:T(8,128)(2,1)S(1)}, u32[]{:S(2)}, u32[]{:S(2)}) collective-permute-start(bf16[272,2048]{1,0:T(8,128)(2,1)S(1)} %pad_maximum_fusion.refs_0_), channel_id=1, source_target_pairs={{0,6},{1,7},{2,0},{3,1},{4,2},{5,3},{6,4},{7,5},{8,14},{9,15},{10,... | collective-permute-start | bytes 3342344 | tf_op jit(solution)/shard_map/ppermute | solution.py:331
  8.7 3.0 %pack_groups.1 = (bf16[4,128,512]{2,1,0:T(8,128)(2,1)}, bf16[4,128,512]{2,1,0:T(8,128)(2,1)}, bf16[4,128,512]{2,1,0:T(8,128)(2,1)}, bf16[4,128,512]{2,1,0:T(8,128)(2,1)}) custom-call(s32[1]{0:T(128)} %bitcast.mine_ref, bf16[128,2048]{1,0:T(8,128)(2,1)} %bitcast.30, bf16[128,2048]{1,0:T(8,128)(2,1)} %bitcast.31, bf16[128,2048]{1,0:T(8,128)(2,1)} %bitcast.32, ...), custom_call_target="tpu_custom_call" | custom-call | tf_op jit(solution)/shard_map/pack_groups/pallas_call | solution.py:58
  11.7 1.5 %collective-permute-start.1 = (bf16[4,128,512]{2,1,0:T(8,128)(2,1)}, bf16[4,128,512]{2,1,0:T(8,128)(2,1)S(1)}, u32[]{:S(2)}, u32[]{:S(2)}) collective-permute-start(bf16[4,128,512]{2,1,0:T(8,128)(2,1)} %get-tuple-element.73), channel_id=1, source_target_pairs={{0,8},{8,0},{16,24},{24,16},{1,9},{9,1},{17,25},{25,17},{2,10},{10... | collective-permute-start | bytes 1572872 | tf_op jit(solution)/shard_map/ppermute | solution.py:140
  13.2 1.5 %collective-permute-start.2 = (bf16[4,128,512]{2,1,0:T(8,128)(2,1)}, bf16[4,128,512]{2,1,0:T(8,128)(2,1)S(1)}, u32[]{:S(2)}, u32[]{:S(2)}) collective-permute-start(bf16[4,128,512]{2,1,0:T(8,128)(2,1)} %get-tuple-element.74), channel_id=1, source_target_pairs={{0,16},{8,24},{16,0},{24,8},{1,17},{9,25},{17,1},{25,9},{2,18},{10... | collective-permute-start | bytes 1572872 | tf_op jit(solution)/shard_map/ppermute | solution.py:140
  14.7 0.5 collective-permute-start.3
  15.2 15.8 %expert_back.4 = (bf16[128,2048]{1,0:T(8,128)(2,1)S(1)}, bf16[128,2048]{1,0:T(8,128)(2,1)S(1)}, bf16[4,2048,768]{2,1,0:T(8,128)(2,1)S(1)}, bf16[4,768,2048]{2,1,0:T(8,128)(2,1)S(1)}) custom-call(s32[1]{0:T(128)} %bitcast.11.base_ref, bf16[272,2048]{1,0:T(8,128)(2,1)S(1)} %pad_maximum_fusion.refs_0_, bf16[272,2048]{1,0:T(8,128)(2,1)} %collective-permute-done.refs_1_, ...), custom_call_target="tpu_custom_call" | custom-call | flops 30000001024 | bytes 30000000 | tf_op jit(solution)/shard_map/expert_back/pallas_call | solution.py:294
  31.0 2.5 %collective-permute-done.4.refs_0_ = bf16[272,2048]{1,0:T(8,128)(2,1)S(1)} collective-permute-done((bf16[272,2048]{1,0:T(8,128)(2,1)S(1)}, bf16[272,2048]{1,0:T(8,128)(2,1)S(1)}, u32[]{:S(2)}, u32[]{:S(2)}) %collective-permute-start.4) | collective-permute-done | bytes 1114144 | tf_op jit(solution)/shard_map/ppermute | solution.py:331
  33.5 4.8 %collective-permute-done.2.refs_2_ = bf16[4,128,512]{2,1,0:T(8,128)(2,1)S(1)} collective-permute-done((bf16[4,128,512]{2,1,0:T(8,128)(2,1)}, bf16[4,128,512]{2,1,0:T(8,128)(2,1)S(1)}, u32[]{:S(2)}, u32[]{:S(2)}) %collective-permute-start.2) | collective-permute-done | bytes 524320 | tf_op jit(solution)/shard_map/ppermute | solution.py:140
  38.3 3.5 %collective-permute-start.5 = (bf16[272,2048]{1,0:T(8,128)(2,1)S(1)}, bf16[272,2048]{1,0:T(8,128)(2,1)S(1)}, u32[]{:S(2)}, u32[]{:S(2)}) collective-permute-start(bf16[272,2048]{1,0:T(8,128)(2,1)S(1)} %collective-permute-done.4.refs_0_), channel_id=1, source_target_pairs={{0,6},{1,7},{2,0},{3,1},{4,2},{5,3},{6,4},{7,5},{8,14},{9,15},{10,... | collective-permute-start | bytes 3342344 | tf_op jit(solution)/shard_map/ppermute | solution.py:331
  41.9 6.4 %heads_back.1 = (bf16[3,128,512]{2,1,0:T(8,128)(2,1)S(1)}, bf16[3,128,512]{2,1,0:T(8,128)(2,1)S(1)}, bf16[3,128,512]{2,1,0:T(8,128)(2,1)S(1)}, bf16[3,128,512]{2,1,0:T(8,128)(2,1)S(1)}) custom-call(bf16[4,128,512]{2,1,0:T(8,128)(2,1)S(1)} %copy-done, bf16[4,128,512]{2,1,0:T(8,128)(2,1)S(1)} %collective-permute-done.1.refs_1_, ...), custom_call_target="tpu_custom_call" | custom-call | flops 30000001024 | bytes 30000000 | tf_op jit(solution)/shard_map/heads_back/pallas_call | solution.py:125
  48.2 0.3 collective-permute-start.11
  48.5 1.2 collective-permute-start.8
  49.8 0.8 collective-permute-start.9
  50.6 1.4 %collective-permute-start.10 = (bf16[3,128,512]{2,1,0:T(8,128)(2,1)S(1)}, bf16[3,128,512]{2,1,0:T(8,128)(2,1)S(1)}, u32[]{:S(2)}, u32[]{:S(2)}) collective-permute-start(bf16[3,128,512]{2,1,0:T(8,128)(2,1)S(1)} %get-tuple-element.92), channel_id=1, source_target_pairs={{0,24},{8,16},{16,8},{24,0},{1,25},{9,17},{17,9},{25,1},{2,26},{10... | collective-permute-start | bytes 1179656 | tf_op jit(solution)/shard_map/ppermute | solution.py:140
  52.0 12.3 %expert_back.5 = (bf16[128,2048]{1,0:T(8,128)(2,1)S(1)}, bf16[128,2048]{1,0:T(8,128)(2,1)S(1)}, f32[192,768]{1,0:T(8,128)S(1)}) custom-call(s32[1]{0:T(128)} %bitcast.11.base_ref, bf16[272,2048]{1,0:T(8,128)(2,1)S(1)} %collective-permute-done.4.refs_0_, bf16[272,2048]{1,0:T(8,128)(2,1)S(1)} %collective-permute-done.6.refs_1_, ...), custom_call_target="tpu_custom_call" | custom-call | tf_op jit(solution)/shard_map/expert_back/pallas_call | solution.py:294
  64.4 6.1 %collective-permute-done.5.refs_0_ = bf16[272,2048]{1,0:T(8,128)(2,1)S(1)} collective-permute-done((bf16[272,2048]{1,0:T(8,128)(2,1)S(1)}, bf16[272,2048]{1,0:T(8,128)(2,1)S(1)}, u32[]{:S(2)}, u32[]{:S(2)}) %collective-permute-start.5) | collective-permute-done | bytes 1114144 | tf_op jit(solution)/shard_map/ppermute | solution.py:331
  70.5 0.1 collective-permute-start.13
  70.6 0.5 collective-permute-start.15
  71.1 0.2 collective-permute-start.16
  71.3 1.2 collective-permute-done.13
  72.5 0.1 add_convert_fusion.2
  72.7 0.5 collective-permute-start.14
  73.2 0.9 collective-permute-done.16.refs_1_
  74.1 12.0 %expert_back.6 = (bf16[128,2048]{1,0:T(8,128)(2,1)S(1)}, bf16[128,2048]{1,0:T(8,128)(2,1)S(1)}) custom-call(s32[1]{0:T(128)} %bitcast.11.base_ref, bf16[272,2048]{1,0:T(8,128)(2,1)S(1)} %collective-permute-done.5.refs_0_, bf16[272,2048]{1,0:T(8,128)(2,1)S(1)} %collective-permute-done.16.refs_1_, ...), custom_call_target="tpu_custom_call" | custom-call | tf_op jit(solution)/shard_map/expert_back/pallas_call | solution.py:294
  86.1 1.1 collective-permute-done.15.refs_1_
  87.2 5.2 %collective-permute-done.14 = bf16[64,2048]{1,0:T(8,128)(2,1)S(1)} collective-permute-done((bf16[64,2048]{1,0:T(8,128)(2,1)S(1)}, bf16[64,2048]{1,0:T(8,128)(2,1)S(1)}, u32[]{:S(2)}, u32[]{:S(2)}) %collective-permute-start.14) | collective-permute-done | bytes 262176 | tf_op jit(solution)/shard_map/ppermute | solution.py:331
  92.3 0.5 collective-permute-start.17
  92.8 1.4 %collective-permute-done.22 = bf16[128,2048]{1,0:T(8,128)(2,1)S(1)} collective-permute-done((bf16[128,2048]{1,0:T(8,128)(2,1)S(1)}, bf16[128,2048]{1,0:T(8,128)(2,1)S(1)}, u32[]{:S(2)}, u32[]{:S(2)}) %collective-permute-start.22) | collective-permute-done | bytes 524320 | tf_op jit(solution)/shard_map/ppermute | solution.py:328
  94.2 0.1 add_convert_fusion.1
  94.4 2.7 %collective-permute-start.23 = (bf16[96,2048]{1,0:T(8,128)(2,1)S(1)}, bf16[96,2048]{1,0:T(8,128)(2,1)S(1)}, u32[]{:S(2)}, u32[]{:S(2)}) collective-permute-start(bf16[96,2048]{1,0:T(8,128)(2,1)S(1)} %slice.28), channel_id=1, source_target_pairs={{0,6},{1,7},{2,0},{3,1},{4,2},{5,3},{6,4},{7,5},{8,14},{9,15},{10,... | collective-permute-start | bytes 1179656 | tf_op jit(solution)/shard_map/ppermute | solution.py:331
  97.1 9.6 %expert_back.7 = (bf16[128,2048]{1,0:T(8,128)(2,1)S(1)}, bf16[32,2048]{1,0:T(8,128)(2,1)S(1)}, bf16[32,2048]{1,0:T(8,128)(2,1)S(1)}, bf16[32,2048]{1,0:T(8,128)(2,1)S(1)}, bf16[32,2048]{1,0:T(8,128)(2,1)S(1)}) custom-call(s32[1]{0:T(128)} %bitcast.11.base_ref, bf16[144,2048]{1,0:T(8,128)(2,1)S(1)} %collective-permute-done.7.refs_2_.refs_0_, ...), custom_call_target="tpu_custom_call" | custom-call | flops 30000001024 | bytes 30000000 | tf_op jit(solution)/shard_map/expert_back/pallas_call | solution.py:294
  106.7 0.5 collective-permute-start.20
  107.3 0.4 collective-permute-start.12
  107.8 0.3 collective-permute-done.19
  108.1 0.2 collective-permute-done.20
  108.3 0.3 collective-permute-start.25
  108.6 2.9 %collective-permute-done.23 = bf16[96,2048]{1,0:T(8,128)(2,1)S(1)} collective-permute-done((bf16[96,2048]{1,0:T(8,128)(2,1)S(1)}, bf16[96,2048]{1,0:T(8,128)(2,1)S(1)}, u32[]{:S(2)}, u32[]{:S(2)}) %collective-permute-start.23) | collective-permute-done | bytes 393248 | tf_op jit(solution)/shard_map/ppermute | solution.py:331
  111.4 0.1 add_convert_fusion.3
  111.6 0.5 collective-permute-start.24
  112.1 2.1 %collective-permute-done.26 = bf16[32,2048]{1,0:T(8,128)(2,1)S(1)} collective-permute-done((bf16[32,2048]{1,0:T(8,128)(2,1)S(1)}, bf16[32,2048]{1,0:T(8,128)(2,1)S(1)}, u32[]{:S(2)}, u32[]{:S(2)}) %collective-permute-start.26) | collective-permute-done | bytes 131104 | tf_op jit(solution)/shard_map/ppermute | solution.py:331
  114.2 1.6 %collective-permute-start.27 = (bf16[32,2048]{1,0:T(8,128)(2,1)S(1)}, bf16[32,2048]{1,0:T(8,128)(2,1)S(1)}, u32[]{:S(2)}, u32[]{:S(2)}) collective-permute-start(bf16[32,2048]{1,0:T(8,128)(2,1)S(1)} %add_convert_fusion.4), channel_id=1, source_target_pairs={{0,6},{1,7},{2,0},{3,1},{4,2},{5,3},{6,4},{7,5},{8,14},{9,15},{10,... | collective-permute-start | bytes 393224 | tf_op jit(solution)/shard_map/ppermute | solution.py:331
  115.8 1.3 unpack_groups.1
  117.1 8.4 %collective-permute-done.27 = bf16[32,2048]{1,0:T(8,128)(2,1)S(1)} collective-permute-done((bf16[32,2048]{1,0:T(8,128)(2,1)S(1)}, bf16[32,2048]{1,0:T(8,128)(2,1)S(1)}, u32[]{:S(2)}, u32[]{:S(2)}) %collective-permute-start.27) | collective-permute-done | bytes 131104 | tf_op jit(solution)/shard_map/ppermute | solution.py:331
  125.4 1.1 fusion
  (34 shorter events, 0.5 us)
Async XLA Ops:
  0.6 7.9 %copy-start.2 = (bf16[1,128,2048]{2,1,0:T(8,128)(2,1)S(1)}, bf16[1,128,2048]{2,1,0:T(8,128)(2,1)}, u32[]{:S(2)}) copy-start(bf16[1,128,2048]{2,1,0:T(8,128)(2,1)} %param.13) | copy-start | bytes 1572868
  3.4 8.3 %collective-permute-start = (bf16[272,2048]{1,0:T(8,128)(2,1)S(1)}, bf16[272,2048]{1,0:T(8,128)(2,1)}, u32[]{:S(2)}, u32[]{:S(2)}) collective-permute-start(bf16[272,2048]{1,0:T(8,128)(2,1)S(1)} %pad_maximum_fusion.refs_0_), channel_id=1, source_target_pairs={{0,1},{1,0},{2,3},{3,2},{4,5},{5,4},{6,7},{7,6},{8,9},{9,8},{10,11... | collective-permute-start | bytes 3342344 | tf_op jit(solution)/shard_map/ppermute | solution.py:328
  3.9 29.6 %collective-permute-start.4 = (bf16[272,2048]{1,0:T(8,128)(2,1)S(1)}, bf16[272,2048]{1,0:T(8,128)(2,1)S(1)}, u32[]{:S(2)}, u32[]{:S(2)}) collective-permute-start(bf16[272,2048]{1,0:T(8,128)(2,1)S(1)} %pad_maximum_fusion.refs_0_), channel_id=1, source_target_pairs={{0,6},{1,7},{2,0},{3,1},{4,2},{5,3},{6,4},{7,5},{8,14},{9,15},{10,... | collective-permute-start | bytes 3342344 | tf_op jit(solution)/shard_map/ppermute | solution.py:331
  8.6 39.6 %collective-permute-start.7 = (bf16[144,2048]{1,0:T(8,128)(2,1)S(1)}, bf16[144,2048]{1,0:T(8,128)(2,1)S(1)}, u32[]{:S(2)}, u32[]{:S(2)}) collective-permute-start(bf16[144,2048]{1,0:T(8,128)(2,1)S(1)} %pad_maximum_fusion.1), channel_id=1, source_target_pairs={{0,2},{1,3},{2,4},{3,5},{4,6},{5,7},{6,0},{7,1},{8,10},{9,11},{10,... | collective-permute-start | bytes 1769480 | tf_op jit(solution)/shard_map/ppermute | solution.py:331
  11.7 21.8 %collective-permute-start.1 = (bf16[4,128,512]{2,1,0:T(8,128)(2,1)}, bf16[4,128,512]{2,1,0:T(8,128)(2,1)S(1)}, u32[]{:S(2)}, u32[]{:S(2)}) collective-permute-start(bf16[4,128,512]{2,1,0:T(8,128)(2,1)} %get-tuple-element.73), channel_id=1, source_target_pairs={{0,8},{8,0},{16,24},{24,16},{1,9},{9,1},{17,25},{25,17},{2,10},{10... | collective-permute-start | bytes 1572872 | tf_op jit(solution)/shard_map/ppermute | solution.py:140
  13.2 25.2 %collective-permute-start.2 = (bf16[4,128,512]{2,1,0:T(8,128)(2,1)}, bf16[4,128,512]{2,1,0:T(8,128)(2,1)S(1)}, u32[]{:S(2)}, u32[]{:S(2)}) collective-permute-start(bf16[4,128,512]{2,1,0:T(8,128)(2,1)} %get-tuple-element.74), channel_id=1, source_target_pairs={{0,16},{8,24},{16,0},{24,8},{1,17},{9,25},{17,1},{25,9},{2,18},{10... | collective-permute-start | bytes 1572872 | tf_op jit(solution)/shard_map/ppermute | solution.py:140
  14.7 23.6 %collective-permute-start.3 = (bf16[4,128,512]{2,1,0:T(8,128)(2,1)}, bf16[4,128,512]{2,1,0:T(8,128)(2,1)S(1)}, u32[]{:S(2)}, u32[]{:S(2)}) collective-permute-start(bf16[4,128,512]{2,1,0:T(8,128)(2,1)} %get-tuple-element.75), channel_id=1, source_target_pairs={{0,24},{8,16},{16,8},{24,0},{1,25},{9,17},{17,9},{25,1},{2,26},{10... | collective-permute-start | bytes 1572872 | tf_op jit(solution)/shard_map/ppermute | solution.py:140
  15.2 26.7 %copy-start = (bf16[4,128,512]{2,1,0:T(8,128)(2,1)S(1)}, bf16[4,128,512]{2,1,0:T(8,128)(2,1)}, u32[]{:S(2)}) copy-start(bf16[4,128,512]{2,1,0:T(8,128)(2,1)} %get-tuple-element.81.refs_0_) | copy-start | bytes 1572868
  38.3 9.9 %collective-permute-start.6 = (bf16[272,2048]{1,0:T(8,128)(2,1)S(1)}, bf16[272,2048]{1,0:T(8,128)(2,1)S(1)}, u32[]{:S(2)}, u32[]{:S(2)}) collective-permute-start(bf16[272,2048]{1,0:T(8,128)(2,1)S(1)} %collective-permute-done.4.refs_0_), channel_id=1, source_target_pairs={{0,1},{1,0},{2,3},{3,2},{4,5},{5,4},{6,7},{7,6},{8,9},{9,8},{10,11... | collective-permute-start | bytes 3342344 | tf_op jit(solution)/shard_map/ppermute | solution.py:328
  38.3 32.2 %collective-permute-start.5 = (bf16[272,2048]{1,0:T(8,128)(2,1)S(1)}, bf16[272,2048]{1,0:T(8,128)(2,1)S(1)}, u32[]{:S(2)}, u32[]{:S(2)}) collective-permute-start(bf16[272,2048]{1,0:T(8,128)(2,1)S(1)} %collective-permute-done.4.refs_0_), channel_id=1, source_target_pairs={{0,6},{1,7},{2,0},{3,1},{4,2},{5,3},{6,4},{7,5},{8,14},{9,15},{10,... | collective-permute-start | bytes 3342344 | tf_op jit(solution)/shard_map/ppermute | solution.py:331
  48.2 3.8 %collective-permute-start.11 = (bf16[144,2048]{1,0:T(8,128)(2,1)S(1)}, bf16[144,2048]{1,0:T(8,128)(2,1)S(1)}, u32[]{:S(2)}, u32[]{:S(2)}) collective-permute-start(bf16[144,2048]{1,0:T(8,128)(2,1)S(1)} %collective-permute-done.7.refs_2_.refs_0_), channel_id=1, source_target_pairs={{0,1},{1,0},{2,3},{3,2},{4,5},{5,4},{6,7},{7,6},{8,9},{9,8},{10,11... | collective-permute-start | bytes 1769480 | tf_op jit(solution)/shard_map/ppermute | solution.py:328
  48.5 21.9 %collective-permute-start.8 = (bf16[3,128,512]{2,1,0:T(8,128)(2,1)S(1)}, bf16[3,128,512]{2,1,0:T(8,128)(2,1)S(1)}, u32[]{:S(2)}, u32[]{:S(2)}) collective-permute-start(bf16[3,128,512]{2,1,0:T(8,128)(2,1)S(1)} %get-tuple-element.90), channel_id=1, source_target_pairs={{0,8},{8,0},{16,24},{24,16},{1,9},{9,1},{17,25},{25,17},{2,10},{10... | collective-permute-start | bytes 1179656 | tf_op jit(solution)/shard_map/ppermute | solution.py:140
  49.8 20.7 %collective-permute-start.9 = (bf16[3,128,512]{2,1,0:T(8,128)(2,1)S(1)}, bf16[3,128,512]{2,1,0:T(8,128)(2,1)S(1)}, u32[]{:S(2)}, u32[]{:S(2)}) collective-permute-start(bf16[3,128,512]{2,1,0:T(8,128)(2,1)S(1)} %get-tuple-element.91), channel_id=1, source_target_pairs={{0,16},{8,24},{16,0},{24,8},{1,17},{9,25},{17,1},{25,9},{2,18},{10... | collective-permute-start | bytes 1179656 | tf_op jit(solution)/shard_map/ppermute | solution.py:140
  50.6 19.9 %collective-permute-start.10 = (bf16[3,128,512]{2,1,0:T(8,128)(2,1)S(1)}, bf16[3,128,512]{2,1,0:T(8,128)(2,1)S(1)}, u32[]{:S(2)}, u32[]{:S(2)}) collective-permute-start(bf16[3,128,512]{2,1,0:T(8,128)(2,1)S(1)} %get-tuple-element.92), channel_id=1, source_target_pairs={{0,24},{8,16},{16,8},{24,0},{1,25},{9,17},{17,9},{25,1},{2,26},{10... | collective-permute-start | bytes 1179656 | tf_op jit(solution)/shard_map/ppermute | solution.py:140
  52.0 18.6 %copy-start.1 = (bf16[1,128,2048]{2,1,0:T(8,128)(2,1)S(1)}, bf16[1,128,2048]{2,1,0:T(8,128)(2,1)}, u32[]{:S(2)}) copy-start(bf16[1,128,2048]{2,1,0:T(8,128)(2,1)} %param.12) | copy-start | bytes 1572868
  70.5 2.0 %collective-permute-start.13 = (bf16[128,2048]{1,0:T(8,128)(2,1)S(1)}, bf16[128,2048]{1,0:T(8,128)(2,1)S(1)}, u32[]{:S(2)}, u32[]{:S(2)}) collective-permute-start(bf16[128,2048]{1,0:T(8,128)(2,1)S(1)} %get-tuple-element.110), channel_id=1, source_target_pairs={{0,1},{1,0},{2,3},{3,2},{4,5},{5,4},{6,7},{7,6},{8,9},{9,8},{10,11... | collective-permute-start | bytes 1572872 | tf_op jit(solution)/shard_map/ppermute | solution.py:328
  70.6 16.5 %collective-permute-start.15 = (bf16[128,2048]{1,0:T(8,128)(2,1)S(1)}, bf16[128,2048]{1,0:T(8,128)(2,1)S(1)}, u32[]{:S(2)}, u32[]{:S(2)}) collective-permute-start(bf16[128,2048]{1,0:T(8,128)(2,1)S(1)} %bitcast.27), channel_id=1, source_target_pairs={{0,2},{1,3},{2,4},{3,5},{4,6},{5,7},{6,0},{7,1},{8,10},{9,11},{10,... | collective-permute-start | bytes 1572872 | tf_op jit(solution)/shard_map/ppermute | solution.py:331
  71.1 2.9 %collective-permute-start.16 = (bf16[272,2048]{1,0:T(8,128)(2,1)S(1)}, bf16[272,2048]{1,0:T(8,128)(2,1)S(1)}, u32[]{:S(2)}, u32[]{:S(2)}) collective-permute-start(bf16[272,2048]{1,0:T(8,128)(2,1)S(1)} %collective-permute-done.5.refs_0_), channel_id=1, source_target_pairs={{0,1},{1,0},{2,3},{3,2},{4,5},{5,4},{6,7},{7,6},{8,9},{9,8},{10,11... | collective-permute-start | bytes 3342344 | tf_op jit(solution)/shard_map/ppermute | solution.py:328
  72.7 19.7 %collective-permute-start.14 = (bf16[64,2048]{1,0:T(8,128)(2,1)S(1)}, bf16[64,2048]{1,0:T(8,128)(2,1)S(1)}, u32[]{:S(2)}, u32[]{:S(2)}) collective-permute-start(bf16[64,2048]{1,0:T(8,128)(2,1)S(1)} %get-tuple-element.133), channel_id=1, source_target_pairs={{0,2},{1,3},{2,4},{3,5},{4,6},{5,7},{6,0},{7,1},{8,10},{9,11},{10,... | collective-permute-start | bytes 786440 | tf_op jit(solution)/shard_map/ppermute | solution.py:331
  92.3 1.9 %collective-permute-start.22 = (bf16[128,2048]{1,0:T(8,128)(2,1)S(1)}, bf16[128,2048]{1,0:T(8,128)(2,1)S(1)}, u32[]{:S(2)}, u32[]{:S(2)}) collective-permute-start(bf16[128,2048]{1,0:T(8,128)(2,1)S(1)} %get-tuple-element.130), channel_id=1, source_target_pairs={{0,1},{1,0},{2,3},{3,2},{4,5},{5,4},{6,7},{7,6},{8,9},{9,8},{10,11... | collective-permute-start | bytes 1572872 | tf_op jit(solution)/shard_map/ppermute | solution.py:328
  92.3 4.7 %collective-permute-start.17 = (bf16[128,2048]{1,0:T(8,128)(2,1)S(1)}, bf16[128,2048]{1,0:T(8,128)(2,1)S(1)}, u32[]{:S(2)}, u32[]{:S(2)}) collective-permute-start(bf16[128,2048]{1,0:T(8,128)(2,1)S(1)} %collective-permute-done.15.refs_1_), channel_id=1, source_target_pairs={{0,1},{1,0},{2,3},{3,2},{4,5},{5,4},{6,7},{7,6},{8,9},{9,8},{10,11... | collective-permute-start | bytes 1572872 | tf_op jit(solution)/shard_map/ppermute | solution.py:328
  92.8 13.8 %collective-permute-start.18 = (bf16[64,2048]{1,0:T(8,128)(2,1)S(1)}, bf16[64,2048]{1,0:T(8,128)(2,1)S(1)}, u32[]{:S(2)}, u32[]{:S(2)}) collective-permute-start(bf16[64,2048]{1,0:T(8,128)(2,1)S(1)} %get-tuple-element.132), channel_id=1, source_target_pairs={{0,2},{1,3},{2,4},{3,5},{4,6},{5,7},{6,0},{7,1},{8,10},{9,11},{10,... | collective-permute-start | bytes 786440 | tf_op jit(solution)/shard_map/ppermute | solution.py:331
  94.4 17.1 %collective-permute-start.23 = (bf16[96,2048]{1,0:T(8,128)(2,1)S(1)}, bf16[96,2048]{1,0:T(8,128)(2,1)S(1)}, u32[]{:S(2)}, u32[]{:S(2)}) collective-permute-start(bf16[96,2048]{1,0:T(8,128)(2,1)S(1)} %slice.28), channel_id=1, source_target_pairs={{0,6},{1,7},{2,0},{3,1},{4,2},{5,3},{6,4},{7,5},{8,14},{9,15},{10,... | collective-permute-start | bytes 1179656 | tf_op jit(solution)/shard_map/ppermute | solution.py:331
  106.7 1.4 %collective-permute-start.19 = (bf16[32,2048]{1,0:T(8,128)(2,1)S(1)}, bf16[32,2048]{1,0:T(8,128)(2,1)S(1)}, u32[]{:S(2)}, u32[]{:S(2)}) collective-permute-start(bf16[32,2048]{1,0:T(8,128)(2,1)S(1)} %get-tuple-element.126), channel_id=1, source_target_pairs={{0,1},{1,0},{2,3},{3,2},{4,5},{5,4},{6,7},{7,6},{8,9},{9,8},{10,11... | collective-permute-start | bytes 393224 | tf_op jit(solution)/shard_map/ppermute | solution.py:328
  106.7 1.5 %collective-permute-start.20 = (bf16[32,2048]{1,0:T(8,128)(2,1)S(1)}, bf16[32,2048]{1,0:T(8,128)(2,1)S(1)}, u32[]{:S(2)}, u32[]{:S(2)}) collective-permute-start(bf16[32,2048]{1,0:T(8,128)(2,1)S(1)} %get-tuple-element.127), channel_id=1, source_target_pairs={{0,1},{1,0},{2,3},{3,2},{4,5},{5,4},{6,7},{7,6},{8,9},{9,8},{10,11... | collective-permute-start | bytes 393224 | tf_op jit(solution)/shard_map/ppermute | solution.py:328
  107.2 1.4 %collective-permute-start.21 = (bf16[32,2048]{1,0:T(8,128)(2,1)S(1)}, bf16[32,2048]{1,0:T(8,128)(2,1)S(1)}, u32[]{:S(2)}, u32[]{:S(2)}) collective-permute-start(bf16[32,2048]{1,0:T(8,128)(2,1)S(1)} %get-tuple-element.128), channel_id=1, source_target_pairs={{0,1},{1,0},{2,3},{3,2},{4,5},{5,4},{6,7},{7,6},{8,9},{9,8},{10,11... | collective-permute-start | bytes 393224 | tf_op jit(solution)/shard_map/ppermute | solution.py:328
  107.3 9.8 %collective-permute-start.12 = (bf16[128,2048]{1,0:T(8,128)(2,1)S(1)}, bf16[128,2048]{1,0:T(8,128)(2,1)S(1)}, u32[]{:S(2)}, u32[]{:S(2)}) collective-permute-start(bf16[128,2048]{1,0:T(8,128)(2,1)S(1)} %get-tuple-element.108), channel_id=1, source_target_pairs={{0,1},{1,0},{2,3},{3,2},{4,5},{5,4},{6,7},{7,6},{8,9},{9,8},{10,11... | collective-permute-start | bytes 1572872 | tf_op jit(solution)/shard_map/ppermute | solution.py:328
  108.1 6.1 %collective-permute-start.26 = (bf16[32,2048]{1,0:T(8,128)(2,1)S(1)}, bf16[32,2048]{1,0:T(8,128)(2,1)S(1)}, u32[]{:S(2)}, u32[]{:S(2)}) collective-permute-start(bf16[32,2048]{1,0:T(8,128)(2,1)S(1)} %slice.29), channel_id=1, source_target_pairs={{0,6},{1,7},{2,0},{3,1},{4,2},{5,3},{6,4},{7,5},{8,14},{9,15},{10,... | collective-permute-start | bytes 393224 | tf_op jit(solution)/shard_map/ppermute | solution.py:331
  108.3 5.9 %collective-permute-start.25 = (bf16[32,2048]{1,0:T(8,128)(2,1)S(1)}, bf16[32,2048]{1,0:T(8,128)(2,1)S(1)}, u32[]{:S(2)}, u32[]{:S(2)}) collective-permute-start(bf16[32,2048]{1,0:T(8,128)(2,1)S(1)} %get-tuple-element.131), channel_id=1, source_target_pairs={{0,1},{1,0},{2,3},{3,2},{4,5},{5,4},{6,7},{7,6},{8,9},{9,8},{10,11... | collective-permute-start | bytes 393224 | tf_op jit(solution)/shard_map/ppermute | solution.py:328
  111.6 13.8 %collective-permute-start.24 = (bf16[96,2048]{1,0:T(8,128)(2,1)S(1)}, bf16[96,2048]{1,0:T(8,128)(2,1)S(1)}, u32[]{:S(2)}, u32[]{:S(2)}) collective-permute-start(bf16[96,2048]{1,0:T(8,128)(2,1)S(1)} %add_convert_fusion.3), channel_id=1, source_target_pairs={{0,6},{1,7},{2,0},{3,1},{4,2},{5,3},{6,4},{7,5},{8,14},{9,15},{10,... | collective-permute-start | bytes 1179656 | tf_op jit(solution)/shard_map/ppermute | solution.py:331
  114.2 11.2 %collective-permute-start.27 = (bf16[32,2048]{1,0:T(8,128)(2,1)S(1)}, bf16[32,2048]{1,0:T(8,128)(2,1)S(1)}, u32[]{:S(2)}, u32[]{:S(2)}) collective-permute-start(bf16[32,2048]{1,0:T(8,128)(2,1)S(1)} %add_convert_fusion.4), channel_id=1, source_target_pairs={{0,6},{1,7},{2,0},{3,1},{4,2},{5,3},{6,4},{7,5},{8,14},{9,15},{10,... | collective-permute-start | bytes 393224 | tf_op jit(solution)/shard_map/ppermute | solution.py:331

commit v12 on v11

--- a/solution.py
+++ b/solution.py
@@ -376,7 +376,7 @@
     carried = left_sums[-1].astype(jnp.bfloat16)
     for sums in reversed(left_sums[:-1]):
         carried = add_up(sums, hop(carried, 1)).astype(jnp.bfloat16)
-    left_halves = [hop(carried[: bins // 2], 1), hop(carried[bins // 2 :], 1)]
+    left_halves = [hop(carried[: bins // 4], 1), hop(carried[bins // 4 :], 1)]
     rights = [(right_rows, hop(right_grads, 1))]
     for d in range(2, half):
         rights.append(tuple(hop(member, 1) for member in rights[-1]))

time: 127 us -> 127 us (level)
  no operation moved by 1% of the time
where the time goes in v12:
time: 127 us
  Pallas kernels  60.3 us (47%)
  waiting for transfers between devices  37.5 us (30%)
  starting transfers between devices  23.6 us (19%)
  other arithmetic  4.34 us (3%)
    pallas_call x4, Pallas kernels, expert_back(): pl.pallas_call(functools.partial(expert_kernel, layout, len(ahead), later...  49.7 us
    ppermute x10, waiting for transfers between devices, hop(): lax.ppermute(block, 'exp', [(i, (i + 2 * step) % members) for i in range(...  29 us
    ppermute x10, starting transfers between devices, hop(): lax.ppermute(block, 'exp', [(i, (i + 2 * step) % members) for i in range(...  13.4 us
    ppermute x6, starting transfers between devices, exchange(): lax.ppermute(blocks[place], 'ctx', [(i, i ^ place) for i in range(groups)])  6.98 us
    pallas_call x1, Pallas kernels, heads_back(): pl.pallas_call(heads_kernel, grid=(heads,), out_shape=[jax.ShapeDtypeStru...  6.37 us
    ppermute x6, waiting for transfers between devices, exchange(): lax.ppermute(blocks[place], 'ctx', [(i, i ^ place) for i in range(groups)])  4.85 us
    ppermute x12, waiting for transfers between devices, swap(): return lax.ppermute(block, 'exp', [(i, i ^ 1) for i in range(members)])  3.62 us
    ppermute x12, starting transfers between devices, swap(): return lax.ppermute(block, 'exp', [(i, i ^ 1) for i in range(members)])  3.26 us
  transfers between devices with their start and end apart: 28, of which 13 were waited for; matrix products, arithmetic and copies ran while one was open for 0% of the time, Pallas kernels for 48%

profile of v12, /device:TPU:0, one launch (start us, length us, event | category | flops | bytes accessed | tf_op | source)
XLA Modules:
  0.0 126.7 jit_solution(9387666747211311083)
XLA Ops:
  0.6 0.7 fusion.10
  1.4 0.7 reduce-precision_convert_fusion.1
  2.1 1.3 %pad_maximum_fusion.refs_0_ = bf16[272,2048]{1,0:T(8,128)(2,1)S(1)} fusion(bf16[128,2048]{1,0:T(8,128)(2,1)} %bitcast.25, bf16[16,2048]{1,0:T(8,128)(2,1)S(1)} %fusion.7, bf16[128,2048]{1,0:T(8,128)(2,1)} %bitcast.28), kind=kLoop, calls=%fused_computation | loop fusion | flops 3342336 | bytes 2228224 | tf_op jit(solution)/shard_map/concatenate | solution.py:154
  3.4 0.5 collective-permute-start
  3.9 4.7 %collective-permute-start.4 = (bf16[272,2048]{1,0:T(8,128)(2,1)S(1)}, bf16[272,2048]{1,0:T(8,128)(2,1)S(1)}, u32[]{:S(2)}, u32[]{:S(2)}) collective-permute-start(bf16[272,2048]{1,0:T(8,128)(2,1)S(1)} %pad_maximum_fusion.refs_0_), channel_id=1, source_target_pairs={{0,6},{1,7},{2,0},{3,1},{4,2},{5,3},{6,4},{7,5},{8,14},{9,15},{10,... | collective-permute-start | bytes 3342344 | tf_op jit(solution)/shard_map/ppermute | solution.py:331
  8.7 3.0 %pack_groups.1 = (bf16[4,128,512]{2,1,0:T(8,128)(2,1)}, bf16[4,128,512]{2,1,0:T(8,128)(2,1)}, bf16[4,128,512]{2,1,0:T(8,128)(2,1)}, bf16[4,128,512]{2,1,0:T(8,128)(2,1)}) custom-call(s32[1]{0:T(128)} %bitcast.mine_ref, bf16[128,2048]{1,0:T(8,128)(2,1)} %bitcast.30, bf16[128,2048]{1,0:T(8,128)(2,1)} %bitcast.31, bf16[128,2048]{1,0:T(8,128)(2,1)} %bitcast.32, ...), custom_call_target="tpu_custom_call" | custom-call | tf_op jit(solution)/shard_map/pack_groups/pallas_call | solution.py:58
  11.7 1.5 %collective-permute-start.1 = (bf16[4,128,512]{2,1,0:T(8,128)(2,1)}, bf16[4,128,512]{2,1,0:T(8,128)(2,1)S(1)}, u32[]{:S(2)}, u32[]{:S(2)}) collective-permute-start(bf16[4,128,512]{2,1,0:T(8,128)(2,1)} %get-tuple-element.73), channel_id=1, source_target_pairs={{0,8},{8,0},{16,24},{24,16},{1,9},{9,1},{17,25},{25,17},{2,10},{10... | collective-permute-start | bytes 1572872 | tf_op jit(solution)/shard_map/ppermute | solution.py:140
  13.2 1.5 %collective-permute-start.2 = (bf16[4,128,512]{2,1,0:T(8,128)(2,1)}, bf16[4,128,512]{2,1,0:T(8,128)(2,1)S(1)}, u32[]{:S(2)}, u32[]{:S(2)}) collective-permute-start(bf16[4,128,512]{2,1,0:T(8,128)(2,1)} %get-tuple-element.74), channel_id=1, source_target_pairs={{0,16},{8,24},{16,0},{24,8},{1,17},{9,25},{17,1},{25,9},{2,18},{10... | collective-permute-start | bytes 1572872 | tf_op jit(solution)/shard_map/ppermute | solution.py:140
  14.7 0.5 collective-permute-start.3
  15.2 15.8 %expert_back.4 = (bf16[128,2048]{1,0:T(8,128)(2,1)S(1)}, bf16[128,2048]{1,0:T(8,128)(2,1)S(1)}, bf16[4,2048,768]{2,1,0:T(8,128)(2,1)S(1)}, bf16[4,768,2048]{2,1,0:T(8,128)(2,1)S(1)}) custom-call(s32[1]{0:T(128)} %bitcast.11.base_ref, bf16[272,2048]{1,0:T(8,128)(2,1)S(1)} %pad_maximum_fusion.refs_0_, bf16[272,2048]{1,0:T(8,128)(2,1)} %collective-permute-done.refs_1_, ...), custom_call_target="tpu_custom_call" | custom-call | flops 30000001024 | bytes 30000000 | tf_op jit(solution)/shard_map/expert_back/pallas_call | solution.py:294
  31.0 2.5 %collective-permute-done.4.refs_0_ = bf16[272,2048]{1,0:T(8,128)(2,1)S(1)} collective-permute-done((bf16[272,2048]{1,0:T(8,128)(2,1)S(1)}, bf16[272,2048]{1,0:T(8,128)(2,1)S(1)}, u32[]{:S(2)}, u32[]{:S(2)}) %collective-permute-start.4) | collective-permute-done | bytes 1114144 | tf_op jit(solution)/shard_map/ppermute | solution.py:331
  33.5 4.8 %collective-permute-done.2.refs_2_ = bf16[4,128,512]{2,1,0:T(8,128)(2,1)S(1)} collective-permute-done((bf16[4,128,512]{2,1,0:T(8,128)(2,1)}, bf16[4,128,512]{2,1,0:T(8,128)(2,1)S(1)}, u32[]{:S(2)}, u32[]{:S(2)}) %collective-permute-start.2) | collective-permute-done | bytes 524320 | tf_op jit(solution)/shard_map/ppermute | solution.py:140
  38.3 3.5 %collective-permute-start.5 = (bf16[272,2048]{1,0:T(8,128)(2,1)S(1)}, bf16[272,2048]{1,0:T(8,128)(2,1)S(1)}, u32[]{:S(2)}, u32[]{:S(2)}) collective-permute-start(bf16[272,2048]{1,0:T(8,128)(2,1)S(1)} %collective-permute-done.4.refs_0_), channel_id=1, source_target_pairs={{0,6},{1,7},{2,0},{3,1},{4,2},{5,3},{6,4},{7,5},{8,14},{9,15},{10,... | collective-permute-start | bytes 3342344 | tf_op jit(solution)/shard_map/ppermute | solution.py:331
  41.9 6.4 %heads_back.1 = (bf16[3,128,512]{2,1,0:T(8,128)(2,1)S(1)}, bf16[3,128,512]{2,1,0:T(8,128)(2,1)S(1)}, bf16[3,128,512]{2,1,0:T(8,128)(2,1)S(1)}, bf16[3,128,512]{2,1,0:T(8,128)(2,1)S(1)}) custom-call(bf16[4,128,512]{2,1,0:T(8,128)(2,1)S(1)} %copy-done, bf16[4,128,512]{2,1,0:T(8,128)(2,1)S(1)} %collective-permute-done.1.refs_1_, ...), custom_call_target="tpu_custom_call" | custom-call | flops 30000001024 | bytes 30000000 | tf_op jit(solution)/shard_map/heads_back/pallas_call | solution.py:125
  48.2 0.3 collective-permute-start.11
  48.5 1.2 collective-permute-start.8
  49.8 0.8 collective-permute-start.9
  50.6 1.4 %collective-permute-start.10 = (bf16[3,128,512]{2,1,0:T(8,128)(2,1)S(1)}, bf16[3,128,512]{2,1,0:T(8,128)(2,1)S(1)}, u32[]{:S(2)}, u32[]{:S(2)}) collective-permute-start(bf16[3,128,512]{2,1,0:T(8,128)(2,1)S(1)} %get-tuple-element.92), channel_id=1, source_target_pairs={{0,24},{8,16},{16,8},{24,0},{1,25},{9,17},{17,9},{25,1},{2,26},{10... | collective-permute-start | bytes 1179656 | tf_op jit(solution)/shard_map/ppermute | solution.py:140
  52.0 12.3 %expert_back.5 = (bf16[128,2048]{1,0:T(8,128)(2,1)S(1)}, bf16[128,2048]{1,0:T(8,128)(2,1)S(1)}, f32[192,768]{1,0:T(8,128)S(1)}) custom-call(s32[1]{0:T(128)} %bitcast.11.base_ref, bf16[272,2048]{1,0:T(8,128)(2,1)S(1)} %collective-permute-done.4.refs_0_, bf16[272,2048]{1,0:T(8,128)(2,1)S(1)} %collective-permute-done.6.refs_1_, ...), custom_call_target="tpu_custom_call" | custom-call | tf_op jit(solution)/shard_map/expert_back/pallas_call | solution.py:294
  64.4 6.1 %collective-permute-done.5.refs_0_ = bf16[272,2048]{1,0:T(8,128)(2,1)S(1)} collective-permute-done((bf16[272,2048]{1,0:T(8,128)(2,1)S(1)}, bf16[272,2048]{1,0:T(8,128)(2,1)S(1)}, u32[]{:S(2)}, u32[]{:S(2)}) %collective-permute-start.5) | collective-permute-done | bytes 1114144 | tf_op jit(solution)/shard_map/ppermute | solution.py:331
  70.5 0.1 collective-permute-start.13
  70.6 0.4 collective-permute-start.16
  71.1 0.5 collective-permute-start.15
  71.6 0.9 collective-permute-done.13
  72.5 0.1 add_convert_fusion.2
  72.6 0.5 collective-permute-start.14
  73.2 0.9 collective-permute-done.16.refs_1_
  74.1 12.0 %expert_back.6 = (bf16[128,2048]{1,0:T(8,128)(2,1)S(1)}, bf16[128,2048]{1,0:T(8,128)(2,1)S(1)}) custom-call(s32[1]{0:T(128)} %bitcast.11.base_ref, bf16[272,2048]{1,0:T(8,128)(2,1)S(1)} %collective-permute-done.5.refs_0_, bf16[272,2048]{1,0:T(8,128)(2,1)S(1)} %collective-permute-done.16.refs_1_, ...), custom_call_target="tpu_custom_call" | custom-call | tf_op jit(solution)/shard_map/expert_back/pallas_call | solution.py:294
  86.1 1.6 %collective-permute-done.15.refs_1_ = bf16[128,2048]{1,0:T(8,128)(2,1)S(1)} collective-permute-done((bf16[128,2048]{1,0:T(8,128)(2,1)S(1)}, bf16[128,2048]{1,0:T(8,128)(2,1)S(1)}, u32[]{:S(2)}, u32[]{:S(2)}) %collective-permute-start.15) | collective-permute-done | bytes 524320 | tf_op jit(solution)/shard_map/ppermute | solution.py:331
  87.6 1.9 %collective-permute-done.14 = bf16[32,2048]{1,0:T(8,128)(2,1)S(1)} collective-permute-done((bf16[32,2048]{1,0:T(8,128)(2,1)S(1)}, bf16[32,2048]{1,0:T(8,128)(2,1)S(1)}, u32[]{:S(2)}, u32[]{:S(2)}) %collective-permute-start.14) | collective-permute-done | bytes 131104 | tf_op jit(solution)/shard_map/ppermute | solution.py:331
  89.6 0.5 collective-permute-start.17
  90.2 1.3 %collective-permute-done.22 = bf16[128,2048]{1,0:T(8,128)(2,1)S(1)} collective-permute-done((bf16[128,2048]{1,0:T(8,128)(2,1)S(1)}, bf16[128,2048]{1,0:T(8,128)(2,1)S(1)}, u32[]{:S(2)}, u32[]{:S(2)}) %collective-permute-start.22) | collective-permute-done | bytes 524320 | tf_op jit(solution)/shard_map/ppermute | solution.py:328
  91.5 0.1 add_convert_fusion.1
  91.7 2.7 %collective-permute-start.23 = (bf16[96,2048]{1,0:T(8,128)(2,1)S(1)}, bf16[96,2048]{1,0:T(8,128)(2,1)S(1)}, u32[]{:S(2)}, u32[]{:S(2)}) collective-permute-start(bf16[96,2048]{1,0:T(8,128)(2,1)S(1)} %slice.28), channel_id=1, source_target_pairs={{0,6},{1,7},{2,0},{3,1},{4,2},{5,3},{6,4},{7,5},{8,14},{9,15},{10,... | collective-permute-start | bytes 1179656 | tf_op jit(solution)/shard_map/ppermute | solution.py:331
  94.4 9.6 %expert_back.7 = (bf16[128,2048]{1,0:T(8,128)(2,1)S(1)}, bf16[32,2048]{1,0:T(8,128)(2,1)S(1)}, bf16[32,2048]{1,0:T(8,128)(2,1)S(1)}, bf16[32,2048]{1,0:T(8,128)(2,1)S(1)}, bf16[32,2048]{1,0:T(8,128)(2,1)S(1)}) custom-call(s32[1]{0:T(128)} %bitcast.11.base_ref, bf16[144,2048]{1,0:T(8,128)(2,1)S(1)} %collective-permute-done.7.refs_2_.refs_0_, ...), custom_call_target="tpu_custom_call" | custom-call | flops 30000001024 | bytes 30000000 | tf_op jit(solution)/shard_map/expert_back/pallas_call | solution.py:294
  104.1 0.5 collective-permute-start.20
  104.7 0.4 collective-permute-start.12
  105.1 0.3 collective-permute-done.19
  105.5 0.2 collective-permute-done.20
  105.6 0.3 collective-permute-start.25
  105.9 5.7 %collective-permute-done.23 = bf16[96,2048]{1,0:T(8,128)(2,1)S(1)} collective-permute-done((bf16[96,2048]{1,0:T(8,128)(2,1)S(1)}, bf16[96,2048]{1,0:T(8,128)(2,1)S(1)}, u32[]{:S(2)}, u32[]{:S(2)}) %collective-permute-start.23) | collective-permute-done | bytes 393248 | tf_op jit(solution)/shard_map/ppermute | solution.py:331
  111.6 0.1 add_convert_fusion.3
  111.8 0.8 collective-permute-start.24
  112.6 1.7 %collective-permute-done.26 = bf16[32,2048]{1,0:T(8,128)(2,1)S(1)} collective-permute-done((bf16[32,2048]{1,0:T(8,128)(2,1)S(1)}, bf16[32,2048]{1,0:T(8,128)(2,1)S(1)}, u32[]{:S(2)}, u32[]{:S(2)}) %collective-permute-start.26) | collective-permute-done | bytes 131104 | tf_op jit(solution)/shard_map/ppermute | solution.py:331
  114.3 0.5 collective-permute-start.27
  114.8 1.3 unpack_groups.1
  116.1 9.4 %collective-permute-done.27 = bf16[32,2048]{1,0:T(8,128)(2,1)S(1)} collective-permute-done((bf16[32,2048]{1,0:T(8,128)(2,1)S(1)}, bf16[32,2048]{1,0:T(8,128)(2,1)S(1)}, u32[]{:S(2)}, u32[]{:S(2)}) %collective-permute-start.27) | collective-permute-done | bytes 131104 | tf_op jit(solution)/shard_map/ppermute | solution.py:331
  125.5 1.1 fusion
  (35 shorter events, 0.5 us)
Async XLA Ops:
  0.6 7.9 %copy-start.2 = (bf16[1,128,2048]{2,1,0:T(8,128)(2,1)S(1)}, bf16[1,128,2048]{2,1,0:T(8,128)(2,1)}, u32[]{:S(2)}) copy-start(bf16[1,128,2048]{2,1,0:T(8,128)(2,1)} %param.13) | copy-start | bytes 1572868
  3.4 8.3 %collective-permute-start = (bf16[272,2048]{1,0:T(8,128)(2,1)S(1)}, bf16[272,2048]{1,0:T(8,128)(2,1)}, u32[]{:S(2)}, u32[]{:S(2)}) collective-permute-start(bf16[272,2048]{1,0:T(8,128)(2,1)S(1)} %pad_maximum_fusion.refs_0_), channel_id=1, source_target_pairs={{0,1},{1,0},{2,3},{3,2},{4,5},{5,4},{6,7},{7,6},{8,9},{9,8},{10,11... | collective-permute-start | bytes 3342344 | tf_op jit(solution)/shard_map/ppermute | solution.py:328
  3.9 29.6 %collective-permute-start.4 = (bf16[272,2048]{1,0:T(8,128)(2,1)S(1)}, bf16[272,2048]{1,0:T(8,128)(2,1)S(1)}, u32[]{:S(2)}, u32[]{:S(2)}) collective-permute-start(bf16[272,2048]{1,0:T(8,128)(2,1)S(1)} %pad_maximum_fusion.refs_0_), channel_id=1, source_target_pairs={{0,6},{1,7},{2,0},{3,1},{4,2},{5,3},{6,4},{7,5},{8,14},{9,15},{10,... | collective-permute-start | bytes 3342344 | tf_op jit(solution)/shard_map/ppermute | solution.py:331
  8.6 39.6 %collective-permute-start.7 = (bf16[144,2048]{1,0:T(8,128)(2,1)S(1)}, bf16[144,2048]{1,0:T(8,128)(2,1)S(1)}, u32[]{:S(2)}, u32[]{:S(2)}) collective-permute-start(bf16[144,2048]{1,0:T(8,128)(2,1)S(1)} %pad_maximum_fusion.1), channel_id=1, source_target_pairs={{0,2},{1,3},{2,4},{3,5},{4,6},{5,7},{6,0},{7,1},{8,10},{9,11},{10,... | collective-permute-start | bytes 1769480 | tf_op jit(solution)/shard_map/ppermute | solution.py:331
  11.7 21.8 %collective-permute-start.1 = (bf16[4,128,512]{2,1,0:T(8,128)(2,1)}, bf16[4,128,512]{2,1,0:T(8,128)(2,1)S(1)}, u32[]{:S(2)}, u32[]{:S(2)}) collective-permute-start(bf16[4,128,512]{2,1,0:T(8,128)(2,1)} %get-tuple-element.73), channel_id=1, source_target_pairs={{0,8},{8,0},{16,24},{24,16},{1,9},{9,1},{17,25},{25,17},{2,10},{10... | collective-permute-start | bytes 1572872 | tf_op jit(solution)/shard_map/ppermute | solution.py:140
  13.2 25.2 %collective-permute-start.2 = (bf16[4,128,512]{2,1,0:T(8,128)(2,1)}, bf16[4,128,512]{2,1,0:T(8,128)(2,1)S(1)}, u32[]{:S(2)}, u32[]{:S(2)}) collective-permute-start(bf16[4,128,512]{2,1,0:T(8,128)(2,1)} %get-tuple-element.74), channel_id=1, source_target_pairs={{0,16},{8,24},{16,0},{24,8},{1,17},{9,25},{17,1},{25,9},{2,18},{10... | collective-permute-start | bytes 1572872 | tf_op jit(solution)/shard_map/ppermute | solution.py:140
  14.7 23.6 %collective-permute-start.3 = (bf16[4,128,512]{2,1,0:T(8,128)(2,1)}, bf16[4,128,512]{2,1,0:T(8,128)(2,1)S(1)}, u32[]{:S(2)}, u32[]{:S(2)}) collective-permute-start(bf16[4,128,512]{2,1,0:T(8,128)(2,1)} %get-tuple-element.75), channel_id=1, source_target_pairs={{0,24},{8,16},{16,8},{24,0},{1,25},{9,17},{17,9},{25,1},{2,26},{10... | collective-permute-start | bytes 1572872 | tf_op jit(solution)/shard_map/ppermute | solution.py:140
  15.2 26.7 %copy-start = (bf16[4,128,512]{2,1,0:T(8,128)(2,1)S(1)}, bf16[4,128,512]{2,1,0:T(8,128)(2,1)}, u32[]{:S(2)}) copy-start(bf16[4,128,512]{2,1,0:T(8,128)(2,1)} %get-tuple-element.81.refs_0_) | copy-start | bytes 1572868
  38.3 9.9 %collective-permute-start.6 = (bf16[272,2048]{1,0:T(8,128)(2,1)S(1)}, bf16[272,2048]{1,0:T(8,128)(2,1)S(1)}, u32[]{:S(2)}, u32[]{:S(2)}) collective-permute-start(bf16[272,2048]{1,0:T(8,128)(2,1)S(1)} %collective-permute-done.4.refs_0_), channel_id=1, source_target_pairs={{0,1},{1,0},{2,3},{3,2},{4,5},{5,4},{6,7},{7,6},{8,9},{9,8},{10,11... | collective-permute-start | bytes 3342344 | tf_op jit(solution)/shard_map/ppermute | solution.py:328
  38.3 32.2 %collective-permute-start.5 = (bf16[272,2048]{1,0:T(8,128)(2,1)S(1)}, bf16[272,2048]{1,0:T(8,128)(2,1)S(1)}, u32[]{:S(2)}, u32[]{:S(2)}) collective-permute-start(bf16[272,2048]{1,0:T(8,128)(2,1)S(1)} %collective-permute-done.4.refs_0_), channel_id=1, source_target_pairs={{0,6},{1,7},{2,0},{3,1},{4,2},{5,3},{6,4},{7,5},{8,14},{9,15},{10,... | collective-permute-start | bytes 3342344 | tf_op jit(solution)/shard_map/ppermute | solution.py:331
  48.2 3.8 %collective-permute-start.11 = (bf16[144,2048]{1,0:T(8,128)(2,1)S(1)}, bf16[144,2048]{1,0:T(8,128)(2,1)S(1)}, u32[]{:S(2)}, u32[]{:S(2)}) collective-permute-start(bf16[144,2048]{1,0:T(8,128)(2,1)S(1)} %collective-permute-done.7.refs_2_.refs_0_), channel_id=1, source_target_pairs={{0,1},{1,0},{2,3},{3,2},{4,5},{5,4},{6,7},{7,6},{8,9},{9,8},{10,11... | collective-permute-start | bytes 1769480 | tf_op jit(solution)/shard_map/ppermute | solution.py:328
  48.5 21.9 %collective-permute-start.8 = (bf16[3,128,512]{2,1,0:T(8,128)(2,1)S(1)}, bf16[3,128,512]{2,1,0:T(8,128)(2,1)S(1)}, u32[]{:S(2)}, u32[]{:S(2)}) collective-permute-start(bf16[3,128,512]{2,1,0:T(8,128)(2,1)S(1)} %get-tuple-element.90), channel_id=1, source_target_pairs={{0,8},{8,0},{16,24},{24,16},{1,9},{9,1},{17,25},{25,17},{2,10},{10... | collective-permute-start | bytes 1179656 | tf_op jit(solution)/shard_map/ppermute | solution.py:140
  49.8 20.7 %collective-permute-start.9 = (bf16[3,128,512]{2,1,0:T(8,128)(2,1)S(1)}, bf16[3,128,512]{2,1,0:T(8,128)(2,1)S(1)}, u32[]{:S(2)}, u32[]{:S(2)}) collective-permute-start(bf16[3,128,512]{2,1,0:T(8,128)(2,1)S(1)} %get-tuple-element.91), channel_id=1, source_target_pairs={{0,16},{8,24},{16,0},{24,8},{1,17},{9,25},{17,1},{25,9},{2,18},{10... | collective-permute-start | bytes 1179656 | tf_op jit(solution)/shard_map/ppermute | solution.py:140
  50.6 19.9 %collective-permute-start.10 = (bf16[3,128,512]{2,1,0:T(8,128)(2,1)S(1)}, bf16[3,128,512]{2,1,0:T(8,128)(2,1)S(1)}, u32[]{:S(2)}, u32[]{:S(2)}) collective-permute-start(bf16[3,128,512]{2,1,0:T(8,128)(2,1)S(1)} %get-tuple-element.92), channel_id=1, source_target_pairs={{0,24},{8,16},{16,8},{24,0},{1,25},{9,17},{17,9},{25,1},{2,26},{10... | collective-permute-start | bytes 1179656 | tf_op jit(solution)/shard_map/ppermute | solution.py:140
  52.0 19.0 %copy-start.1 = (bf16[1,128,2048]{2,1,0:T(8,128)(2,1)S(1)}, bf16[1,128,2048]{2,1,0:T(8,128)(2,1)}, u32[]{:S(2)}) copy-start(bf16[1,128,2048]{2,1,0:T(8,128)(2,1)} %param.12) | copy-start | bytes 1572868
  70.5 2.0 %collective-permute-start.13 = (bf16[128,2048]{1,0:T(8,128)(2,1)S(1)}, bf16[128,2048]{1,0:T(8,128)(2,1)S(1)}, u32[]{:S(2)}, u32[]{:S(2)}) collective-permute-start(bf16[128,2048]{1,0:T(8,128)(2,1)S(1)} %get-tuple-element.110), channel_id=1, source_target_pairs={{0,1},{1,0},{2,3},{3,2},{4,5},{5,4},{6,7},{7,6},{8,9},{9,8},{10,11... | collective-permute-start | bytes 1572872 | tf_op jit(solution)/shard_map/ppermute | solution.py:328
  70.6 3.4 %collective-permute-start.16 = (bf16[272,2048]{1,0:T(8,128)(2,1)S(1)}, bf16[272,2048]{1,0:T(8,128)(2,1)S(1)}, u32[]{:S(2)}, u32[]{:S(2)}) collective-permute-start(bf16[272,2048]{1,0:T(8,128)(2,1)S(1)} %collective-permute-done.5.refs_0_), channel_id=1, source_target_pairs={{0,1},{1,0},{2,3},{3,2},{4,5},{5,4},{6,7},{7,6},{8,9},{9,8},{10,11... | collective-permute-start | bytes 3342344 | tf_op jit(solution)/shard_map/ppermute | solution.py:328
  71.1 16.6 %collective-permute-start.15 = (bf16[128,2048]{1,0:T(8,128)(2,1)S(1)}, bf16[128,2048]{1,0:T(8,128)(2,1)S(1)}, u32[]{:S(2)}, u32[]{:S(2)}) collective-permute-start(bf16[128,2048]{1,0:T(8,128)(2,1)S(1)} %bitcast.27), channel_id=1, source_target_pairs={{0,2},{1,3},{2,4},{3,5},{4,6},{5,7},{6,0},{7,1},{8,10},{9,11},{10,... | collective-permute-start | bytes 1572872 | tf_op jit(solution)/shard_map/ppermute | solution.py:331
  72.6 17.0 %collective-permute-start.14 = (bf16[32,2048]{1,0:T(8,128)(2,1)S(1)}, bf16[32,2048]{1,0:T(8,128)(2,1)S(1)}, u32[]{:S(2)}, u32[]{:S(2)}) collective-permute-start(bf16[32,2048]{1,0:T(8,128)(2,1)S(1)} %slice.26), channel_id=1, source_target_pairs={{0,2},{1,3},{2,4},{3,5},{4,6},{5,7},{6,0},{7,1},{8,10},{9,11},{10,... | collective-permute-start | bytes 393224 | tf_op jit(solution)/shard_map/ppermute | solution.py:331
  89.6 1.9 %collective-permute-start.22 = (bf16[128,2048]{1,0:T(8,128)(2,1)S(1)}, bf16[128,2048]{1,0:T(8,128)(2,1)S(1)}, u32[]{:S(2)}, u32[]{:S(2)}) collective-permute-start(bf16[128,2048]{1,0:T(8,128)(2,1)S(1)} %get-tuple-element.130), channel_id=1, source_target_pairs={{0,1},{1,0},{2,3},{3,2},{4,5},{5,4},{6,7},{7,6},{8,9},{9,8},{10,11... | collective-permute-start | bytes 1572872 | tf_op jit(solution)/shard_map/ppermute | solution.py:328
  89.6 4.8 %collective-permute-start.17 = (bf16[128,2048]{1,0:T(8,128)(2,1)S(1)}, bf16[128,2048]{1,0:T(8,128)(2,1)S(1)}, u32[]{:S(2)}, u32[]{:S(2)}) collective-permute-start(bf16[128,2048]{1,0:T(8,128)(2,1)S(1)} %collective-permute-done.15.refs_1_), channel_id=1, source_target_pairs={{0,1},{1,0},{2,3},{3,2},{4,5},{5,4},{6,7},{7,6},{8,9},{9,8},{10,11... | collective-permute-start | bytes 1572872 | tf_op jit(solution)/shard_map/ppermute | solution.py:328
  90.1 13.9 %collective-permute-start.18 = (bf16[96,2048]{1,0:T(8,128)(2,1)S(1)}, bf16[96,2048]{1,0:T(8,128)(2,1)S(1)}, u32[]{:S(2)}, u32[]{:S(2)}) collective-permute-start(bf16[96,2048]{1,0:T(8,128)(2,1)S(1)} %slice.27), channel_id=1, source_target_pairs={{0,2},{1,3},{2,4},{3,5},{4,6},{5,7},{6,0},{7,1},{8,10},{9,11},{10,... | collective-permute-start | bytes 1179656 | tf_op jit(solution)/shard_map/ppermute | solution.py:331
  91.7 20.0 %collective-permute-start.23 = (bf16[96,2048]{1,0:T(8,128)(2,1)S(1)}, bf16[96,2048]{1,0:T(8,128)(2,1)S(1)}, u32[]{:S(2)}, u32[]{:S(2)}) collective-permute-start(bf16[96,2048]{1,0:T(8,128)(2,1)S(1)} %slice.28), channel_id=1, source_target_pairs={{0,6},{1,7},{2,0},{3,1},{4,2},{5,3},{6,4},{7,5},{8,14},{9,15},{10,... | collective-permute-start | bytes 1179656 | tf_op jit(solution)/shard_map/ppermute | solution.py:331
  104.1 1.4 %collective-permute-start.19 = (bf16[32,2048]{1,0:T(8,128)(2,1)S(1)}, bf16[32,2048]{1,0:T(8,128)(2,1)S(1)}, u32[]{:S(2)}, u32[]{:S(2)}) collective-permute-start(bf16[32,2048]{1,0:T(8,128)(2,1)S(1)} %get-tuple-element.126), channel_id=1, source_target_pairs={{0,1},{1,0},{2,3},{3,2},{4,5},{5,4},{6,7},{7,6},{8,9},{9,8},{10,11... | collective-permute-start | bytes 393224 | tf_op jit(solution)/shard_map/ppermute | solution.py:328
  104.1 1.5 %collective-permute-start.20 = (bf16[32,2048]{1,0:T(8,128)(2,1)S(1)}, bf16[32,2048]{1,0:T(8,128)(2,1)S(1)}, u32[]{:S(2)}, u32[]{:S(2)}) collective-permute-start(bf16[32,2048]{1,0:T(8,128)(2,1)S(1)} %get-tuple-element.127), channel_id=1, source_target_pairs={{0,1},{1,0},{2,3},{3,2},{4,5},{5,4},{6,7},{7,6},{8,9},{9,8},{10,11... | collective-permute-start | bytes 393224 | tf_op jit(solution)/shard_map/ppermute | solution.py:328
  104.6 1.4 %collective-permute-start.21 = (bf16[32,2048]{1,0:T(8,128)(2,1)S(1)}, bf16[32,2048]{1,0:T(8,128)(2,1)S(1)}, u32[]{:S(2)}, u32[]{:S(2)}) collective-permute-start(bf16[32,2048]{1,0:T(8,128)(2,1)S(1)} %get-tuple-element.128), channel_id=1, source_target_pairs={{0,1},{1,0},{2,3},{3,2},{4,5},{5,4},{6,7},{7,6},{8,9},{9,8},{10,11... | collective-permute-start | bytes 393224 | tf_op jit(solution)/shard_map/ppermute | solution.py:328
  104.7 11.4 %collective-permute-start.12 = (bf16[128,2048]{1,0:T(8,128)(2,1)S(1)}, bf16[128,2048]{1,0:T(8,128)(2,1)S(1)}, u32[]{:S(2)}, u32[]{:S(2)}) collective-permute-start(bf16[128,2048]{1,0:T(8,128)(2,1)S(1)} %get-tuple-element.108), channel_id=1, source_target_pairs={{0,1},{1,0},{2,3},{3,2},{4,5},{5,4},{6,7},{7,6},{8,9},{9,8},{10,11... | collective-permute-start | bytes 1572872 | tf_op jit(solution)/shard_map/ppermute | solution.py:328
  105.4 8.8 %collective-permute-start.26 = (bf16[32,2048]{1,0:T(8,128)(2,1)S(1)}, bf16[32,2048]{1,0:T(8,128)(2,1)S(1)}, u32[]{:S(2)}, u32[]{:S(2)}) collective-permute-start(bf16[32,2048]{1,0:T(8,128)(2,1)S(1)} %slice.29), channel_id=1, source_target_pairs={{0,6},{1,7},{2,0},{3,1},{4,2},{5,3},{6,4},{7,5},{8,14},{9,15},{10,... | collective-permute-start | bytes 393224 | tf_op jit(solution)/shard_map/ppermute | solution.py:331
  105.6 8.7 %collective-permute-start.25 = (bf16[32,2048]{1,0:T(8,128)(2,1)S(1)}, bf16[32,2048]{1,0:T(8,128)(2,1)S(1)}, u32[]{:S(2)}, u32[]{:S(2)}) collective-permute-start(bf16[32,2048]{1,0:T(8,128)(2,1)S(1)} %get-tuple-element.131), channel_id=1, source_target_pairs={{0,1},{1,0},{2,3},{3,2},{4,5},{5,4},{6,7},{7,6},{8,9},{9,8},{10,11... | collective-permute-start | bytes 393224 | tf_op jit(solution)/shard_map/ppermute | solution.py:328
  111.8 13.7 %collective-permute-start.24 = (bf16[96,2048]{1,0:T(8,128)(2,1)S(1)}, bf16[96,2048]{1,0:T(8,128)(2,1)S(1)}, u32[]{:S(2)}, u32[]{:S(2)}) collective-permute-start(bf16[96,2048]{1,0:T(8,128)(2,1)S(1)} %add_convert_fusion.3), channel_id=1, source_target_pairs={{0,6},{1,7},{2,0},{3,1},{4,2},{5,3},{6,4},{7,5},{8,14},{9,15},{10,... | collective-permute-start | bytes 1179656 | tf_op jit(solution)/shard_map/ppermute | solution.py:331
  114.3 11.2 %collective-permute-start.27 = (bf16[32,2048]{1,0:T(8,128)(2,1)S(1)}, bf16[32,2048]{1,0:T(8,128)(2,1)S(1)}, u32[]{:S(2)}, u32[]{:S(2)}) collective-permute-start(bf16[32,2048]{1,0:T(8,128)(2,1)S(1)} %add_convert_fusion.4), channel_id=1, source_target_pairs={{0,6},{1,7},{2,0},{3,1},{4,2},{5,3},{6,4},{7,5},{8,14},{9,15},{10,... | collective-permute-start | bytes 393224 | tf_op jit(solution)/shard_map/ppermute | solution.py:331

commit v13 on v11

--- a/solution.py
+++ b/solution.py
@@ -398,6 +398,7 @@
         sums = [add_up(kept[:cut], joined(given[:3]), most), add_up(kept[cut:], given[3], last)]
         carried = jnp.concatenate(sums, axis=0)
     total = add_up(total, joined(left_halves))
+    total, sums[1] = barrier((total, sums[1]))
     returned = [hop(part.astype(jnp.bfloat16), -1) for part in sums]
     outs = unpack_groups(mine, results)
     total = add_up(total, joined(returned)).astype(jnp.bfloat16)

time: 127 us -> 129 us (1.016)
  waiting for transfers between devices: 37 us -> 38.8 us
    ppermute x10, waiting for transfers between devices: 28.2 us -> 29.6 us  [hop(): lax.ppermute(block, 'exp', [(i, (i + 2 * step) % members) for i in range(...]
  transfers between devices with their start and end apart: 28 -> 28, of which waited for: 13 -> 12; matrix products, arithmetic and copies ran while one was open for 0% -> 1% of each run, Pallas kernels for 48% -> 47%
where the time goes in v13:
time: 129 us; the launch traced here: 128 us
  Pallas kernels  60.3 us (47%)
  waiting for transfers between devices  38.8 us (30%)
  starting transfers between devices  24.1 us (19%)
  other arithmetic  4.32 us (3%)
    pallas_call x4, Pallas kernels, expert_back(): pl.pallas_call(functools.partial(expert_kernel, layout, len(ahead), later...  49.7 us
    ppermute x10, waiting for transfers between devices, hop(): lax.ppermute(block, 'exp', [(i, (i + 2 * step) % members) for i in range(...  29.6 us
    ppermute x10, starting transfers between devices, hop(): lax.ppermute(block, 'exp', [(i, (i + 2 * step) % members) for i in range(...  14.7 us
    ppermute x6, starting transfers between devices, exchange(): lax.ppermute(blocks[place], 'ctx', [(i, i ^ place) for i in range(groups)])  6.98 us
    pallas_call x1, Pallas kernels, heads_back(): pl.pallas_call(heads_kernel, grid=(heads,), out_shape=[jax.ShapeDtypeStru...  6.37 us
    ppermute x6, waiting for transfers between devices, exchange(): lax.ppermute(blocks[place], 'ctx', [(i, i ^ place) for i in range(groups)])  4.85 us
    ppermute x12, waiting for transfers between devices, swap(): return lax.ppermute(block, 'exp', [(i, i ^ 1) for i in range(members)])  4.38 us
    pallas_call x1, Pallas kernels, pack_groups(): pl.pallas_call(pack_kernel, out_shape=[block] * groups, in_specs=[pl.Bloc...  2.99 us
  transfers between devices with their start and end apart: 28, of which 12 were waited for; matrix products, arithmetic and copies ran while one was open for 1% of the time, Pallas kernels for 47%

profile of v13, /device:TPU:0, one launch (start us, length us, event | category | flops | bytes accessed | tf_op | source)
XLA Modules:
  0.0 128.5 jit_solution(13982671333872107616)
XLA Ops:
  0.6 0.7 fusion.10
  1.4 0.7 reduce-precision_convert_fusion.1
  2.1 1.3 pad_maximum_fusion.refs_0_
  3.4 0.5 collective-permute-start
  3.9 4.7 %collective-permute-start.4 = (bf16[272,2048]{1,0:T(8,128)(2,1)S(1)}, bf16[272,2048]{1,0:T(8,128)(2,1)S(1)}, u32[]{:S(2)}, u32[]{:S(2)}) collective-permute-start(bf16[272,2048]{1,0:T(8,128)(2,1)S(1)} %pad_maximum_fusion.refs_0_), channel_id=1, source_target_pairs={{0,6},{1,7},{2,0},{3,1},{4,2},{5,3},{6,4},{7,5},{8,14},{9,15},{10,... | collective-permute-start | bytes 3342344 | tf_op jit(solution)/shard_map/ppermute | solution.py:331
  8.7 3.0 %pack_groups.1 = (bf16[4,128,512]{2,1,0:T(8,128)(2,1)}, bf16[4,128,512]{2,1,0:T(8,128)(2,1)}, bf16[4,128,512]{2,1,0:T(8,128)(2,1)}, bf16[4,128,512]{2,1,0:T(8,128)(2,1)}) custom-call(s32[1]{0:T(128)} %bitcast.mine_ref, bf16[128,2048]{1,0:T(8,128)(2,1)} %bitcast.30, bf16[128,2048]{1,0:T(8,128)(2,1)} %bitcast.31, bf16[128,2048]{1,0:T(8,128)(2,1)} %bitcast.32, ...), custom_call_target="tpu_custom_call" | custom-call | tf_op jit(solution)/shard_map/pack_groups/pallas_call | solution.py:58
  11.7 1.5 %collective-permute-start.1 = (bf16[4,128,512]{2,1,0:T(8,128)(2,1)}, bf16[4,128,512]{2,1,0:T(8,128)(2,1)S(1)}, u32[]{:S(2)}, u32[]{:S(2)}) collective-permute-start(bf16[4,128,512]{2,1,0:T(8,128)(2,1)} %get-tuple-element.75), channel_id=1, source_target_pairs={{0,8},{8,0},{16,24},{24,16},{1,9},{9,1},{17,25},{25,17},{2,10},{10... | collective-permute-start | bytes 1572872 | tf_op jit(solution)/shard_map/ppermute | solution.py:140
  13.2 1.5 %collective-permute-start.2 = (bf16[4,128,512]{2,1,0:T(8,128)(2,1)}, bf16[4,128,512]{2,1,0:T(8,128)(2,1)S(1)}, u32[]{:S(2)}, u32[]{:S(2)}) collective-permute-start(bf16[4,128,512]{2,1,0:T(8,128)(2,1)} %get-tuple-element.76), channel_id=1, source_target_pairs={{0,16},{8,24},{16,0},{24,8},{1,17},{9,25},{17,1},{25,9},{2,18},{10... | collective-permute-start | bytes 1572872 | tf_op jit(solution)/shard_map/ppermute | solution.py:140
  14.7 0.5 collective-permute-start.3
  15.2 15.8 %expert_back.4 = (bf16[128,2048]{1,0:T(8,128)(2,1)S(1)}, bf16[128,2048]{1,0:T(8,128)(2,1)S(1)}, bf16[4,2048,768]{2,1,0:T(8,128)(2,1)S(1)}, bf16[4,768,2048]{2,1,0:T(8,128)(2,1)S(1)}) custom-call(s32[1]{0:T(128)} %bitcast.11.base_ref, bf16[272,2048]{1,0:T(8,128)(2,1)S(1)} %pad_maximum_fusion.refs_0_, bf16[272,2048]{1,0:T(8,128)(2,1)} %collective-permute-done.refs_1_, ...), custom_call_target="tpu_custom_call" | custom-call | flops 30000001024 | bytes 30000000 | tf_op jit(solution)/shard_map/expert_back/pallas_call | solution.py:294
  31.0 2.5 %collective-permute-done.4.refs_0_ = bf16[272,2048]{1,0:T(8,128)(2,1)S(1)} collective-permute-done((bf16[272,2048]{1,0:T(8,128)(2,1)S(1)}, bf16[272,2048]{1,0:T(8,128)(2,1)S(1)}, u32[]{:S(2)}, u32[]{:S(2)}) %collective-permute-start.4) | collective-permute-done | bytes 1114144 | tf_op jit(solution)/shard_map/ppermute | solution.py:331
  33.5 4.8 %collective-permute-done.2.refs_2_ = bf16[4,128,512]{2,1,0:T(8,128)(2,1)S(1)} collective-permute-done((bf16[4,128,512]{2,1,0:T(8,128)(2,1)}, bf16[4,128,512]{2,1,0:T(8,128)(2,1)S(1)}, u32[]{:S(2)}, u32[]{:S(2)}) %collective-permute-start.2) | collective-permute-done | bytes 524320 | tf_op jit(solution)/shard_map/ppermute | solution.py:140
  38.3 3.5 %collective-permute-start.5 = (bf16[272,2048]{1,0:T(8,128)(2,1)S(1)}, bf16[272,2048]{1,0:T(8,128)(2,1)S(1)}, u32[]{:S(2)}, u32[]{:S(2)}) collective-permute-start(bf16[272,2048]{1,0:T(8,128)(2,1)S(1)} %collective-permute-done.4.refs_0_), channel_id=1, source_target_pairs={{0,6},{1,7},{2,0},{3,1},{4,2},{5,3},{6,4},{7,5},{8,14},{9,15},{10,... | collective-permute-start | bytes 3342344 | tf_op jit(solution)/shard_map/ppermute | solution.py:331
  41.9 6.4 %heads_back.1 = (bf16[3,128,512]{2,1,0:T(8,128)(2,1)S(1)}, bf16[3,128,512]{2,1,0:T(8,128)(2,1)S(1)}, bf16[3,128,512]{2,1,0:T(8,128)(2,1)S(1)}, bf16[3,128,512]{2,1,0:T(8,128)(2,1)S(1)}) custom-call(bf16[4,128,512]{2,1,0:T(8,128)(2,1)S(1)} %copy-done, bf16[4,128,512]{2,1,0:T(8,128)(2,1)S(1)} %collective-permute-done.1.refs_1_, ...), custom_call_target="tpu_custom_call" | custom-call | flops 30000001024 | bytes 30000000 | tf_op jit(solution)/shard_map/heads_back/pallas_call | solution.py:125
  48.2 0.3 collective-permute-start.11
  48.5 1.2 collective-permute-start.8
  49.8 0.8 collective-permute-start.9
  50.6 1.4 %collective-permute-start.10 = (bf16[3,128,512]{2,1,0:T(8,128)(2,1)S(1)}, bf16[3,128,512]{2,1,0:T(8,128)(2,1)S(1)}, u32[]{:S(2)}, u32[]{:S(2)}) collective-permute-start(bf16[3,128,512]{2,1,0:T(8,128)(2,1)S(1)} %get-tuple-element.94), channel_id=1, source_target_pairs={{0,24},{8,16},{16,8},{24,0},{1,25},{9,17},{17,9},{25,1},{2,26},{10... | collective-permute-start | bytes 1179656 | tf_op jit(solution)/shard_map/ppermute | solution.py:140
  52.0 12.3 %expert_back.5 = (bf16[128,2048]{1,0:T(8,128)(2,1)S(1)}, bf16[128,2048]{1,0:T(8,128)(2,1)S(1)}, f32[192,768]{1,0:T(8,128)S(1)}) custom-call(s32[1]{0:T(128)} %bitcast.11.base_ref, bf16[272,2048]{1,0:T(8,128)(2,1)S(1)} %collective-permute-done.4.refs_0_, bf16[272,2048]{1,0:T(8,128)(2,1)S(1)} %collective-permute-done.6.refs_1_, ...), custom_call_target="tpu_custom_call" | custom-call | tf_op jit(solution)/shard_map/expert_back/pallas_call | solution.py:294
  64.4 6.1 %collective-permute-done.5.refs_0_ = bf16[272,2048]{1,0:T(8,128)(2,1)S(1)} collective-permute-done((bf16[272,2048]{1,0:T(8,128)(2,1)S(1)}, bf16[272,2048]{1,0:T(8,128)(2,1)S(1)}, u32[]{:S(2)}, u32[]{:S(2)}) %collective-permute-start.5) | collective-permute-done | bytes 1114144 | tf_op jit(solution)/shard_map/ppermute | solution.py:331
  70.5 0.1 collective-permute-start.13
  70.6 0.5 collective-permute-start.15
  71.1 0.2 collective-permute-start.16
  71.3 1.2 collective-permute-done.13
  72.5 0.1 add_convert_fusion.2
  72.7 0.5 collective-permute-start.14
  73.2 0.9 collective-permute-done.16.refs_1_
  74.1 12.0 %expert_back.6 = (bf16[128,2048]{1,0:T(8,128)(2,1)S(1)}, bf16[128,2048]{1,0:T(8,128)(2,1)S(1)}) custom-call(s32[1]{0:T(128)} %bitcast.11.base_ref, bf16[272,2048]{1,0:T(8,128)(2,1)S(1)} %collective-permute-done.5.refs_0_, bf16[272,2048]{1,0:T(8,128)(2,1)S(1)} %collective-permute-done.16.refs_1_, ...), custom_call_target="tpu_custom_call" | custom-call | tf_op jit(solution)/shard_map/expert_back/pallas_call | solution.py:294
  86.1 1.1 collective-permute-done.15.refs_1_
  87.2 5.2 %collective-permute-done.14 = bf16[64,2048]{1,0:T(8,128)(2,1)S(1)} collective-permute-done((bf16[64,2048]{1,0:T(8,128)(2,1)S(1)}, bf16[64,2048]{1,0:T(8,128)(2,1)S(1)}, u32[]{:S(2)}, u32[]{:S(2)}) %collective-permute-start.14) | collective-permute-done | bytes 262176 | tf_op jit(solution)/shard_map/ppermute | solution.py:331
  92.3 0.5 collective-permute-start.17
  92.8 1.4 %collective-permute-done.20 = bf16[128,2048]{1,0:T(8,128)(2,1)S(1)} collective-permute-done((bf16[128,2048]{1,0:T(8,128)(2,1)S(1)}, bf16[128,2048]{1,0:T(8,128)(2,1)S(1)}, u32[]{:S(2)}, u32[]{:S(2)}) %collective-permute-start.20) | collective-permute-done | bytes 524320 | tf_op jit(solution)/shard_map/ppermute | solution.py:328
  94.2 0.1 add_convert_fusion.1
  94.4 2.5 %collective-permute-start.21 = (bf16[32,2048]{1,0:T(8,128)(2,1)S(1)}, bf16[32,2048]{1,0:T(8,128)(2,1)S(1)}, u32[]{:S(2)}, u32[]{:S(2)}) collective-permute-start(bf16[32,2048]{1,0:T(8,128)(2,1)S(1)} %slice.28), channel_id=1, source_target_pairs={{0,6},{1,7},{2,0},{3,1},{4,2},{5,3},{6,4},{7,5},{8,14},{9,15},{10,... | collective-permute-start | bytes 393224 | tf_op jit(solution)/shard_map/ppermute | solution.py:331
  96.9 0.2 collective-permute-start.25
  97.1 9.6 %expert_back.7 = (bf16[128,2048]{1,0:T(8,128)(2,1)S(1)}, bf16[32,2048]{1,0:T(8,128)(2,1)S(1)}, bf16[32,2048]{1,0:T(8,128)(2,1)S(1)}, bf16[32,2048]{1,0:T(8,128)(2,1)S(1)}, bf16[32,2048]{1,0:T(8,128)(2,1)S(1)}) custom-call(s32[1]{0:T(128)} %bitcast.11.base_ref, bf16[144,2048]{1,0:T(8,128)(2,1)S(1)} %collective-permute-done.7.refs_2_.refs_0_, ...), custom_call_target="tpu_custom_call" | custom-call | flops 30000001024 | bytes 30000000 | tf_op jit(solution)/shard_map/expert_back/pallas_call | solution.py:294
  106.8 0.5 collective-permute-start.23
  107.4 0.2 convert_add_fusion
  107.6 0.5 collective-permute-done.22
  108.2 0.1 collective-permute-start.19
  108.4 0.3 collective-permute-done.24
  108.7 5.4 %collective-permute-done.25 = bf16[96,2048]{1,0:T(8,128)(2,1)S(1)} collective-permute-done((bf16[96,2048]{1,0:T(8,128)(2,1)S(1)}, bf16[96,2048]{1,0:T(8,128)(2,1)S(1)}, u32[]{:S(2)}, u32[]{:S(2)}) %collective-permute-start.25) | collective-permute-done | bytes 393248 | tf_op jit(solution)/shard_map/ppermute | solution.py:331
  114.0 0.1 add_convert_fusion.3
  114.2 0.9 collective-permute-start.26
  115.1 1.8 %collective-permute-start.27 = (bf16[32,2048]{1,0:T(8,128)(2,1)S(1)}, bf16[32,2048]{1,0:T(8,128)(2,1)S(1)}, u32[]{:S(2)}, u32[]{:S(2)}) collective-permute-start(bf16[32,2048]{1,0:T(8,128)(2,1)S(1)} %convert_add_fusion.1), channel_id=1, source_target_pairs={{0,6},{1,7},{2,0},{3,1},{4,2},{5,3},{6,4},{7,5},{8,14},{9,15},{10,... | collective-permute-start | bytes 393224 | tf_op jit(solution)/shard_map/ppermute | solution.py:331
  117.0 1.3 unpack_groups.1
  118.2 9.3 %collective-permute-done.27 = bf16[32,2048]{1,0:T(8,128)(2,1)S(1)} collective-permute-done((bf16[32,2048]{1,0:T(8,128)(2,1)S(1)}, bf16[32,2048]{1,0:T(8,128)(2,1)S(1)}, u32[]{:S(2)}, u32[]{:S(2)}) %collective-permute-start.27) | collective-permute-done | bytes 131104 | tf_op jit(solution)/shard_map/ppermute | solution.py:331
  127.6 0.9 fusion
  (35 shorter events, 0.5 us)
Async XLA Ops:
  0.6 7.9 %copy-start.2 = (bf16[1,128,2048]{2,1,0:T(8,128)(2,1)S(1)}, bf16[1,128,2048]{2,1,0:T(8,128)(2,1)}, u32[]{:S(2)}) copy-start(bf16[1,128,2048]{2,1,0:T(8,128)(2,1)} %param.13) | copy-start | bytes 1572868
  3.4 8.3 %collective-permute-start = (bf16[272,2048]{1,0:T(8,128)(2,1)S(1)}, bf16[272,2048]{1,0:T(8,128)(2,1)}, u32[]{:S(2)}, u32[]{:S(2)}) collective-permute-start(bf16[272,2048]{1,0:T(8,128)(2,1)S(1)} %pad_maximum_fusion.refs_0_), channel_id=1, source_target_pairs={{0,1},{1,0},{2,3},{3,2},{4,5},{5,4},{6,7},{7,6},{8,9},{9,8},{10,11... | collective-permute-start | bytes 3342344 | tf_op jit(solution)/shard_map/ppermute | solution.py:328
  3.9 29.6 %collective-permute-start.4 = (bf16[272,2048]{1,0:T(8,128)(2,1)S(1)}, bf16[272,2048]{1,0:T(8,128)(2,1)S(1)}, u32[]{:S(2)}, u32[]{:S(2)}) collective-permute-start(bf16[272,2048]{1,0:T(8,128)(2,1)S(1)} %pad_maximum_fusion.refs_0_), channel_id=1, source_target_pairs={{0,6},{1,7},{2,0},{3,1},{4,2},{5,3},{6,4},{7,5},{8,14},{9,15},{10,... | collective-permute-start | bytes 3342344 | tf_op jit(solution)/shard_map/ppermute | solution.py:331
  8.6 39.6 %collective-permute-start.7 = (bf16[144,2048]{1,0:T(8,128)(2,1)S(1)}, bf16[144,2048]{1,0:T(8,128)(2,1)S(1)}, u32[]{:S(2)}, u32[]{:S(2)}) collective-permute-start(bf16[144,2048]{1,0:T(8,128)(2,1)S(1)} %pad_maximum_fusion.1), channel_id=1, source_target_pairs={{0,2},{1,3},{2,4},{3,5},{4,6},{5,7},{6,0},{7,1},{8,10},{9,11},{10,... | collective-permute-start | bytes 1769480 | tf_op jit(solution)/shard_map/ppermute | solution.py:331
  11.7 21.8 %collective-permute-start.1 = (bf16[4,128,512]{2,1,0:T(8,128)(2,1)}, bf16[4,128,512]{2,1,0:T(8,128)(2,1)S(1)}, u32[]{:S(2)}, u32[]{:S(2)}) collective-permute-start(bf16[4,128,512]{2,1,0:T(8,128)(2,1)} %get-tuple-element.75), channel_id=1, source_target_pairs={{0,8},{8,0},{16,24},{24,16},{1,9},{9,1},{17,25},{25,17},{2,10},{10... | collective-permute-start | bytes 1572872 | tf_op jit(solution)/shard_map/ppermute | solution.py:140
  13.2 25.2 %collective-permute-start.2 = (bf16[4,128,512]{2,1,0:T(8,128)(2,1)}, bf16[4,128,512]{2,1,0:T(8,128)(2,1)S(1)}, u32[]{:S(2)}, u32[]{:S(2)}) collective-permute-start(bf16[4,128,512]{2,1,0:T(8,128)(2,1)} %get-tuple-element.76), channel_id=1, source_target_pairs={{0,16},{8,24},{16,0},{24,8},{1,17},{9,25},{17,1},{25,9},{2,18},{10... | collective-permute-start | bytes 1572872 | tf_op jit(solution)/shard_map/ppermute | solution.py:140
  14.7 23.6 %collective-permute-start.3 = (bf16[4,128,512]{2,1,0:T(8,128)(2,1)}, bf16[4,128,512]{2,1,0:T(8,128)(2,1)S(1)}, u32[]{:S(2)}, u32[]{:S(2)}) collective-permute-start(bf16[4,128,512]{2,1,0:T(8,128)(2,1)} %get-tuple-element.77), channel_id=1, source_target_pairs={{0,24},{8,16},{16,8},{24,0},{1,25},{9,17},{17,9},{25,1},{2,26},{10... | collective-permute-start | bytes 1572872 | tf_op jit(solution)/shard_map/ppermute | solution.py:140
  15.2 26.7 %copy-start = (bf16[4,128,512]{2,1,0:T(8,128)(2,1)S(1)}, bf16[4,128,512]{2,1,0:T(8,128)(2,1)}, u32[]{:S(2)}) copy-start(bf16[4,128,512]{2,1,0:T(8,128)(2,1)} %get-tuple-element.83.refs_0_) | copy-start | bytes 1572868
  38.3 9.9 %collective-permute-start.6 = (bf16[272,2048]{1,0:T(8,128)(2,1)S(1)}, bf16[272,2048]{1,0:T(8,128)(2,1)S(1)}, u32[]{:S(2)}, u32[]{:S(2)}) collective-permute-start(bf16[272,2048]{1,0:T(8,128)(2,1)S(1)} %collective-permute-done.4.refs_0_), channel_id=1, source_target_pairs={{0,1},{1,0},{2,3},{3,2},{4,5},{5,4},{6,7},{7,6},{8,9},{9,8},{10,11... | collective-permute-start | bytes 3342344 | tf_op jit(solution)/shard_map/ppermute | solution.py:328
  38.3 32.2 %collective-permute-start.5 = (bf16[272,2048]{1,0:T(8,128)(2,1)S(1)}, bf16[272,2048]{1,0:T(8,128)(2,1)S(1)}, u32[]{:S(2)}, u32[]{:S(2)}) collective-permute-start(bf16[272,2048]{1,0:T(8,128)(2,1)S(1)} %collective-permute-done.4.refs_0_), channel_id=1, source_target_pairs={{0,6},{1,7},{2,0},{3,1},{4,2},{5,3},{6,4},{7,5},{8,14},{9,15},{10,... | collective-permute-start | bytes 3342344 | tf_op jit(solution)/shard_map/ppermute | solution.py:331
  48.2 3.8 %collective-permute-start.11 = (bf16[144,2048]{1,0:T(8,128)(2,1)S(1)}, bf16[144,2048]{1,0:T(8,128)(2,1)S(1)}, u32[]{:S(2)}, u32[]{:S(2)}) collective-permute-start(bf16[144,2048]{1,0:T(8,128)(2,1)S(1)} %collective-permute-done.7.refs_2_.refs_0_), channel_id=1, source_target_pairs={{0,1},{1,0},{2,3},{3,2},{4,5},{5,4},{6,7},{7,6},{8,9},{9,8},{10,11... | collective-permute-start | bytes 1769480 | tf_op jit(solution)/shard_map/ppermute | solution.py:328
  48.5 21.9 %collective-permute-start.8 = (bf16[3,128,512]{2,1,0:T(8,128)(2,1)S(1)}, bf16[3,128,512]{2,1,0:T(8,128)(2,1)S(1)}, u32[]{:S(2)}, u32[]{:S(2)}) collective-permute-start(bf16[3,128,512]{2,1,0:T(8,128)(2,1)S(1)} %get-tuple-element.92), channel_id=1, source_target_pairs={{0,8},{8,0},{16,24},{24,16},{1,9},{9,1},{17,25},{25,17},{2,10},{10... | collective-permute-start | bytes 1179656 | tf_op jit(solution)/shard_map/ppermute | solution.py:140
  49.8 20.7 %collective-permute-start.9 = (bf16[3,128,512]{2,1,0:T(8,128)(2,1)S(1)}, bf16[3,128,512]{2,1,0:T(8,128)(2,1)S(1)}, u32[]{:S(2)}, u32[]{:S(2)}) collective-permute-start(bf16[3,128,512]{2,1,0:T(8,128)(2,1)S(1)} %get-tuple-element.93), channel_id=1, source_target_pairs={{0,16},{8,24},{16,0},{24,8},{1,17},{9,25},{17,1},{25,9},{2,18},{10... | collective-permute-start | bytes 1179656 | tf_op jit(solution)/shard_map/ppermute | solution.py:140
  50.6 19.9 %collective-permute-start.10 = (bf16[3,128,512]{2,1,0:T(8,128)(2,1)S(1)}, bf16[3,128,512]{2,1,0:T(8,128)(2,1)S(1)}, u32[]{:S(2)}, u32[]{:S(2)}) collective-permute-start(bf16[3,128,512]{2,1,0:T(8,128)(2,1)S(1)} %get-tuple-element.94), channel_id=1, source_target_pairs={{0,24},{8,16},{16,8},{24,0},{1,25},{9,17},{17,9},{25,1},{2,26},{10... | collective-permute-start | bytes 1179656 | tf_op jit(solution)/shard_map/ppermute | solution.py:140
  52.0 18.6 %copy-start.1 = (bf16[1,128,2048]{2,1,0:T(8,128)(2,1)S(1)}, bf16[1,128,2048]{2,1,0:T(8,128)(2,1)}, u32[]{:S(2)}) copy-start(bf16[1,128,2048]{2,1,0:T(8,128)(2,1)} %param.12) | copy-start | bytes 1572868
  70.5 2.0 %collective-permute-start.13 = (bf16[128,2048]{1,0:T(8,128)(2,1)S(1)}, bf16[128,2048]{1,0:T(8,128)(2,1)S(1)}, u32[]{:S(2)}, u32[]{:S(2)}) collective-permute-start(bf16[128,2048]{1,0:T(8,128)(2,1)S(1)} %get-tuple-element.112), channel_id=1, source_target_pairs={{0,1},{1,0},{2,3},{3,2},{4,5},{5,4},{6,7},{7,6},{8,9},{9,8},{10,11... | collective-permute-start | bytes 1572872 | tf_op jit(solution)/shard_map/ppermute | solution.py:328
  70.6 16.5 %collective-permute-start.15 = (bf16[128,2048]{1,0:T(8,128)(2,1)S(1)}, bf16[128,2048]{1,0:T(8,128)(2,1)S(1)}, u32[]{:S(2)}, u32[]{:S(2)}) collective-permute-start(bf16[128,2048]{1,0:T(8,128)(2,1)S(1)} %bitcast.27), channel_id=1, source_target_pairs={{0,2},{1,3},{2,4},{3,5},{4,6},{5,7},{6,0},{7,1},{8,10},{9,11},{10,... | collective-permute-start | bytes 1572872 | tf_op jit(solution)/shard_map/ppermute | solution.py:331
  71.1 2.9 %collective-permute-start.16 = (bf16[272,2048]{1,0:T(8,128)(2,1)S(1)}, bf16[272,2048]{1,0:T(8,128)(2,1)S(1)}, u32[]{:S(2)}, u32[]{:S(2)}) collective-permute-start(bf16[272,2048]{1,0:T(8,128)(2,1)S(1)} %collective-permute-done.5.refs_0_), channel_id=1, source_target_pairs={{0,1},{1,0},{2,3},{3,2},{4,5},{5,4},{6,7},{7,6},{8,9},{9,8},{10,11... | collective-permute-start | bytes 3342344 | tf_op jit(solution)/shard_map/ppermute | solution.py:328
  72.7 19.7 %collective-permute-start.14 = (bf16[64,2048]{1,0:T(8,128)(2,1)S(1)}, bf16[64,2048]{1,0:T(8,128)(2,1)S(1)}, u32[]{:S(2)}, u32[]{:S(2)}) collective-permute-start(bf16[64,2048]{1,0:T(8,128)(2,1)S(1)} %get-tuple-element.137), channel_id=1, source_target_pairs={{0,2},{1,3},{2,4},{3,5},{4,6},{5,7},{6,0},{7,1},{8,10},{9,11},{10,... | collective-permute-start | bytes 786440 | tf_op jit(solution)/shard_map/ppermute | solution.py:331
  92.3 1.9 %collective-permute-start.20 = (bf16[128,2048]{1,0:T(8,128)(2,1)S(1)}, bf16[128,2048]{1,0:T(8,128)(2,1)S(1)}, u32[]{:S(2)}, u32[]{:S(2)}) collective-permute-start(bf16[128,2048]{1,0:T(8,128)(2,1)S(1)} %get-tuple-element.130), channel_id=1, source_target_pairs={{0,1},{1,0},{2,3},{3,2},{4,5},{5,4},{6,7},{7,6},{8,9},{9,8},{10,11... | collective-permute-start | bytes 1572872 | tf_op jit(solution)/shard_map/ppermute | solution.py:328
  92.3 4.8 %collective-permute-start.17 = (bf16[128,2048]{1,0:T(8,128)(2,1)S(1)}, bf16[128,2048]{1,0:T(8,128)(2,1)S(1)}, u32[]{:S(2)}, u32[]{:S(2)}) collective-permute-start(bf16[128,2048]{1,0:T(8,128)(2,1)S(1)} %collective-permute-done.15.refs_1_), channel_id=1, source_target_pairs={{0,1},{1,0},{2,3},{3,2},{4,5},{5,4},{6,7},{7,6},{8,9},{9,8},{10,11... | collective-permute-start | bytes 1572872 | tf_op jit(solution)/shard_map/ppermute | solution.py:328
  92.8 14.5 %collective-permute-start.12 = (bf16[128,2048]{1,0:T(8,128)(2,1)S(1)}, bf16[128,2048]{1,0:T(8,128)(2,1)S(1)}, u32[]{:S(2)}, u32[]{:S(2)}) collective-permute-start(bf16[128,2048]{1,0:T(8,128)(2,1)S(1)} %get-tuple-element.110), channel_id=1, source_target_pairs={{0,1},{1,0},{2,3},{3,2},{4,5},{5,4},{6,7},{7,6},{8,9},{9,8},{10,11... | collective-permute-start | bytes 1572872 | tf_op jit(solution)/shard_map/ppermute | solution.py:328
  92.8 13.9 %collective-permute-start.18 = (bf16[64,2048]{1,0:T(8,128)(2,1)S(1)}, bf16[64,2048]{1,0:T(8,128)(2,1)S(1)}, u32[]{:S(2)}, u32[]{:S(2)}) collective-permute-start(bf16[64,2048]{1,0:T(8,128)(2,1)S(1)} %get-tuple-element.136), channel_id=1, source_target_pairs={{0,2},{1,3},{2,4},{3,5},{4,6},{5,7},{6,0},{7,1},{8,10},{9,11},{10,... | collective-permute-start | bytes 786440 | tf_op jit(solution)/shard_map/ppermute | solution.py:331
  94.4 20.7 %collective-permute-start.21 = (bf16[32,2048]{1,0:T(8,128)(2,1)S(1)}, bf16[32,2048]{1,0:T(8,128)(2,1)S(1)}, u32[]{:S(2)}, u32[]{:S(2)}) collective-permute-start(bf16[32,2048]{1,0:T(8,128)(2,1)S(1)} %slice.28), channel_id=1, source_target_pairs={{0,6},{1,7},{2,0},{3,1},{4,2},{5,3},{6,4},{7,5},{8,14},{9,15},{10,... | collective-permute-start | bytes 393224 | tf_op jit(solution)/shard_map/ppermute | solution.py:331
  96.9 17.2 %collective-permute-start.25 = (bf16[96,2048]{1,0:T(8,128)(2,1)S(1)}, bf16[96,2048]{1,0:T(8,128)(2,1)S(1)}, u32[]{:S(2)}, u32[]{:S(2)}) collective-permute-start(bf16[96,2048]{1,0:T(8,128)(2,1)S(1)} %slice.29), channel_id=1, source_target_pairs={{0,6},{1,7},{2,0},{3,1},{4,2},{5,3},{6,4},{7,5},{8,14},{9,15},{10,... | collective-permute-start | bytes 1179656 | tf_op jit(solution)/shard_map/ppermute | solution.py:331
  106.8 1.4 %collective-permute-start.22 = (bf16[32,2048]{1,0:T(8,128)(2,1)S(1)}, bf16[32,2048]{1,0:T(8,128)(2,1)S(1)}, u32[]{:S(2)}, u32[]{:S(2)}) collective-permute-start(bf16[32,2048]{1,0:T(8,128)(2,1)S(1)} %get-tuple-element.132), channel_id=1, source_target_pairs={{0,1},{1,0},{2,3},{3,2},{4,5},{5,4},{6,7},{7,6},{8,9},{9,8},{10,11... | collective-permute-start | bytes 393224 | tf_op jit(solution)/shard_map/ppermute | solution.py:328
  106.8 1.5 %collective-permute-start.23 = (bf16[32,2048]{1,0:T(8,128)(2,1)S(1)}, bf16[32,2048]{1,0:T(8,128)(2,1)S(1)}, u32[]{:S(2)}, u32[]{:S(2)}) collective-permute-start(bf16[32,2048]{1,0:T(8,128)(2,1)S(1)} %get-tuple-element.133), channel_id=1, source_target_pairs={{0,1},{1,0},{2,3},{3,2},{4,5},{5,4},{6,7},{7,6},{8,9},{9,8},{10,11... | collective-permute-start | bytes 393224 | tf_op jit(solution)/shard_map/ppermute | solution.py:328
  107.3 1.3 %collective-permute-start.24 = (bf16[32,2048]{1,0:T(8,128)(2,1)S(1)}, bf16[32,2048]{1,0:T(8,128)(2,1)S(1)}, u32[]{:S(2)}, u32[]{:S(2)}) collective-permute-start(bf16[32,2048]{1,0:T(8,128)(2,1)S(1)} %get-tuple-element.134), channel_id=1, source_target_pairs={{0,1},{1,0},{2,3},{3,2},{4,5},{5,4},{6,7},{7,6},{8,9},{9,8},{10,11... | collective-permute-start | bytes 393224 | tf_op jit(solution)/shard_map/ppermute | solution.py:328
  108.2 6.9 %collective-permute-start.19 = (bf16[32,2048]{1,0:T(8,128)(2,1)S(1)}, bf16[32,2048]{1,0:T(8,128)(2,1)S(1)}, u32[]{:S(2)}, u32[]{:S(2)}) collective-permute-start(bf16[32,2048]{1,0:T(8,128)(2,1)S(1)} %get-tuple-element.128), channel_id=1, source_target_pairs={{0,1},{1,0},{2,3},{3,2},{4,5},{5,4},{6,7},{7,6},{8,9},{9,8},{10,11... | collective-permute-start | bytes 393224 | tf_op jit(solution)/shard_map/ppermute | solution.py:328
  114.2 13.4 %collective-permute-start.26 = (bf16[96,2048]{1,0:T(8,128)(2,1)S(1)}, bf16[96,2048]{1,0:T(8,128)(2,1)S(1)}, u32[]{:S(2)}, u32[]{:S(2)}) collective-permute-start(bf16[96,2048]{1,0:T(8,128)(2,1)S(1)} %add_convert_fusion.3), channel_id=1, source_target_pairs={{0,6},{1,7},{2,0},{3,1},{4,2},{5,3},{6,4},{7,5},{8,14},{9,15},{10,... | collective-permute-start | bytes 1179656 | tf_op jit(solution)/shard_map/ppermute | solution.py:331
  115.1 12.4 %collective-permute-start.27 = (bf16[32,2048]{1,0:T(8,128)(2,1)S(1)}, bf16[32,2048]{1,0:T(8,128)(2,1)S(1)}, u32[]{:S(2)}, u32[]{:S(2)}) collective-permute-start(bf16[32,2048]{1,0:T(8,128)(2,1)S(1)} %convert_add_fusion.1), channel_id=1, source_target_pairs={{0,6},{1,7},{2,0},{3,1},{4,2},{5,3},{6,4},{7,5},{8,14},{9,15},{10,... | collective-permute-start | bytes 393224 | tf_op jit(solution)/shard_map/ppermute | solution.py:331
